TPU v7x, 32 devices: a whole 2x2x4 slice. The times are simulated.
32 devices in a mesh: gz: 4 (over z), gy: 8 (over y, x, core).
Axes of the slice: x: 2, y: 2, z: 4, core: 2. Of those that a mesh axis runs over, the one named last changes fastest.
Arguments:
- tracer: float32 [128, 256, 128], P('gz', 'gy'), may hold values from 0.1 to 10
- y_speed: float32 [128, 256, 128], P('gz', 'gy'), may hold values from -0.4 to 0.4
- z_speed: float32 [128, 256, 128], P('gz', 'gy'), may hold values from -0.4 to 0.4
- kappa: float32 [128, 256, 128], P('gz', 'gy'), may hold values from 0.5 to 8
Outputs:
- updated: float32 [128, 256, 128], P('gz', 'gy')
All inputs are finite; a program needn't handle non-finite values.
Results may differ from a plain program's by a relative error of at most 0.0003.
Values sent between devices are 32-bit elements; how exact they have to be, the bound alone decides.
No kernel may reach another device: no remote copies, remote signals or barrier semaphores. Data moves between devices by JAX's collectives and lax.ppermute only.
A program may use at most 64 MiB of HBM per device.

v0:
```python
import jax
import jax.numpy as jnp
from jax import lax
from jax.sharding import PartitionSpec as P

NSUB = 4


rate_const = 500.0


def padded_2(x, sides, width):
    for axis, dim in sides:
        peers, length = (lax.axis_size(axis), x.shape[dim])
        up = [(i, (i + 1) % peers) for i in range(peers - 1)]
        down = [(j, i) for i, j in up]
        last = lax.slice_in_dim(x, length - width, length, axis=dim)
        leading = lax.slice_in_dim(x, 0, width, axis=dim)
        before = lax.ppermute(last, axis, up)
        after = lax.ppermute(leading, axis, down)
        x = jnp.concatenate([before, x, after], axis=dim)
    return x


def from_behind(x, axis, by):
    peers = lax.axis_size(axis)
    pairs = [(i, i + by) for i in range(peers) if 0 <= i + by < peers]
    return lax.ppermute(x, axis, pairs)


def advect_once(tracer, y_speed, z_speed):
    face_y = 0.5 * (y_speed[:, 1:] + y_speed[:, :-1])
    flux_y = jnp.maximum(face_y, 0.0) * tracer[:, :-1] + jnp.minimum(face_y, 0.0) * tracer[:, 1:]
    diff_y = flux_y[:, 1:] - flux_y[:, :-1]
    face_z = 0.5 * (z_speed[1:] + z_speed[:-1])
    flux_z = jnp.maximum(face_z, 0.0) * tracer[:-1] + jnp.minimum(face_z, 0.0) * tracer[1:]
    diff_z = flux_z[1:] - flux_z[:-1]
    return tracer[1:-1, 1:-1] - diff_y[1:-1] - diff_z[:, 1:-1]


def move_down(values, offset, axis, fill):
    count = values.shape[axis]
    kept = lax.slice_in_dim(values, 0, count - offset, axis=axis)
    padding = jnp.full_like(lax.slice_in_dim(values, 0, offset, axis=axis), fill)
    return jnp.concatenate([padding, kept], axis=axis)


def move_up(values, offset, axis, fill):
    count = values.shape[axis]
    kept = lax.slice_in_dim(values, offset, count, axis=axis)
    padding = jnp.full_like(lax.slice_in_dim(values, 0, offset, axis=axis), fill)
    return jnp.concatenate([kept, padding], axis=axis)


def reduce_lines(sub_diag, main_diag, sup_diag, rights, axis):
    count = main_diag.shape[axis]
    offset = 1
    while offset < count:
        factor_low = -sub_diag / move_down(main_diag, offset, axis, 1.0)
        factor_high = -sup_diag / move_up(main_diag, offset, axis, 1.0)
        new_main = (
            main_diag
            + factor_low * move_down(sup_diag, offset, axis, 0.0)
            + factor_high * move_up(sub_diag, offset, axis, 0.0)
        )
        new_sub = factor_low * move_down(sub_diag, offset, axis, 0.0)
        new_sup = factor_high * move_up(sup_diag, offset, axis, 0.0)
        rights = tuple(
            (
                right
                + factor_low * move_down(right, offset, axis, 0.0)
                + factor_high * move_up(right, offset, axis, 0.0)
                for right in rights
            )
        )
        sub_diag, main_diag, sup_diag = (new_sub, new_main, new_sup)
        offset = offset * 2
    return tuple((right / main_diag for right in rights))


def solve_rows(items):
    tracer_part, kappa_part = items
    count = kappa_part.shape[1]
    inner = rate_const * 0.5 * (kappa_part[:, 1:] + kappa_part[:, :-1])
    lower = jnp.concatenate([rate_const * kappa_part[:, :1], inner], axis=1)
    upper = jnp.concatenate([inner, rate_const * kappa_part[:, count - 1 :]], axis=1)
    main_diag = 1.0 + lower + upper
    zero_row = jnp.zeros_like(kappa_part[:, :1])
    sub_diag = jnp.concatenate([zero_row, -inner], axis=1)
    sup_diag = jnp.concatenate([-inner, zero_row], axis=1)
    solved = reduce_lines(sub_diag, main_diag, sup_diag, (tracer_part,), 1)[0]
    return lax.all_to_all(solved, "gy", split_axis=1, concat_axis=0, tiled=True)


def local(tracer, y_speed, z_speed, kappa):
    depth_z, depth_y, band = tracer.shape
    z_index = lax.axis_index("gz")
    z_count = lax.axis_size("gz")
    fields = jnp.stack([y_speed, z_speed, kappa])
    width = 1
    padded = padded_2(fields, (("gz", 1), ("gy", 2)), 1)
    state = tracer
    for step in range(NSUB):
        rimmed = padded_2(state, (("gz", 0), ("gy", 1)), 1)
        state = advect_once(rimmed, padded[0], padded[1])
    kappa_below = padded[2, width - 1 : width, width : width + depth_y]
    kappa_above = padded[2, width + depth_z : width + depth_z + 1, width : width + depth_y]
    lines = solve_rows(
        (
            lax.all_to_all(state, "gy", split_axis=0, concat_axis=1, tiled=True),
            lax.all_to_all(kappa, "gy", split_axis=0, concat_axis=1, tiled=True),
        )
    )
    inner = rate_const * 0.5 * (kappa[1:] + kappa[:-1])
    low_edge = jnp.where(
        z_index == 0, rate_const * kappa[:1], rate_const * 0.5 * (kappa[:1] + kappa_below)
    )
    high_edge = jnp.where(
        z_index == z_count - 1,
        rate_const * kappa[depth_z - 1 :],
        rate_const * 0.5 * (kappa[depth_z - 1 :] + kappa_above),
    )
    lower = jnp.concatenate([low_edge, inner], axis=0)
    upper = jnp.concatenate([inner, high_edge], axis=0)
    main_diag = 1.0 + lower + upper
    inner_count = depth_z - 1
    zero_row = jnp.zeros_like(kappa[:1])
    sub_local = jnp.concatenate([zero_row, -lower[1:inner_count]], axis=0)
    sup_local = jnp.concatenate([-upper[: inner_count - 1], zero_row], axis=0)
    zero_rows = jnp.zeros_like(kappa[: inner_count - 1])
    first_right = jnp.concatenate([lower[:1], zero_rows], axis=0)
    last_right = jnp.concatenate([zero_rows, upper[inner_count - 1 : inner_count]], axis=0)
    base, toward_low, toward_high = reduce_lines(
        sub_local,
        main_diag[:inner_count],
        sup_local,
        (lines[:inner_count], first_right, last_right),
        0,
    )
    following = from_behind(jnp.stack([base[0], toward_low[0], toward_high[0]]), "gz", -1)
    sep_low = lower[depth_z - 1]
    sep_high = upper[depth_z - 1]
    sub_red = jnp.where(z_index == 0, 0.0, -sep_low * toward_low[inner_count - 1])
    diag_red = (
        main_diag[depth_z - 1] - sep_low * toward_high[inner_count - 1] - sep_high * following[1]
    )
    sup_red = -sep_high * following[2]
    rhs_red = lines[depth_z - 1] + sep_low * base[inner_count - 1] + sep_high * following[0]
    equations = jnp.stack([sub_red, diag_red, sup_red, rhs_red])
    collected = lax.all_gather(equations[None], "gz", axis=0, tiled=True)
    values = reduce_lines(collected[:, 0], collected[:, 1], collected[:, 2], (collected[:, 3],), 0)[
        0
    ]
    sep_here = lax.dynamic_index_in_dim(values, z_index, axis=0, keepdims=False)
    previous = lax.dynamic_index_in_dim(values, jnp.maximum(z_index - 1, 0), axis=0, keepdims=False)
    sep_prev = jnp.where(z_index > 0, previous, 0.0)
    interior = base + sep_prev[None] * toward_low + sep_here[None] * toward_high
    return jnp.concatenate([interior, sep_here[None]], axis=0)


def solution(mesh):
    return jax.shard_map(
        local,
        mesh=mesh,
        in_specs=(
            P("gz", "gy", None),
            P("gz", "gy", None),
            P("gz", "gy", None),
            P("gz", "gy", None),
        ),
        out_specs=P("gz", "gy", None),
        check_vma=False,
    )
```

profile of v0, /device:TPU:0, one launch (start us, length us, event | category | flops | bytes accessed | tf_op | source)
XLA Modules:
  0.0 159.7 jit_solution(17583239569676999479)
XLA Ops:
  0.0 0.9 fusion.92
  0.9 4.9 %collective-permute-start.4 = (f32[1,32,128]{2,1,0:T(8,128)S(1)}, f32[1,32,128]{2,1,0:T(8,128)S(1)}, u32[]{:S(2)}, u32[]{:S(2)}) collective-permute-start(f32[1,32,128]{2,1,0:T(8,128)S(1)} %get-tuple-element.166), channel_id=1, source_target_pairs={{0,8},{8,16},{16,24},{1,9},{9,17},{17,25},{2,10},{10,18},{18,26},{... | collective-permute-start | bytes 49160 | tf_op jit(solution)/shard_map/ppermute | solution.py:19
  6.6 3.5 %collective-permute-start = (f32[3,1,32,128]{3,2,1,0:T(8,128)S(1)}, f32[3,1,32,128]{3,2,1,0:T(8,128)S(1)}, u32[]{:S(2)}, u32[]{:S(2)}) collective-permute-start(f32[3,1,32,128]{3,2,1,0:T(8,128)S(1)} %get-tuple-element.53), channel_id=1, source_target_pairs={{0,8},{8,16},{16,24},{1,9},{9,17},{17,25},{2,10},{10,18},{18,26},{... | collective-permute-start | bytes 147464 | tf_op jit(solution)/shard_map/ppermute | solution.py:19
  10.1 1.3 collective-permute-start.1
  11.4 1.3 collective-permute-start.5
  12.8 4.9 %collective-permute-done.5 = f32[1,32,128]{2,1,0:T(8,128)S(1)} collective-permute-done((f32[1,32,128]{2,1,0:T(8,128)S(1)}, f32[1,32,128]{2,1,0:T(8,128)S(1)}, u32[]{:S(2)}, u32[]{:S(2)}) %collective-permute-start.5) | collective-permute-done | bytes 16416 | tf_op jit(solution)/shard_map/ppermute | solution.py:20
  17.7 1.3 collective-permute-start.6
  19.0 1.3 collective-permute-start.7
  20.3 1.1 pad_maximum_fusion.11
  21.4 4.8 %collective-permute-start.2 = (f32[3,34,1,128]{3,2,1,0:T(1,128)S(1)}, f32[3,34,1,128]{3,2,1,0:T(1,128)S(1)}, u32[]{:S(2)}, u32[]{:S(2)}) collective-permute-start(f32[3,34,1,128]{3,2,1,0:T(1,128)S(1)} %get-tuple-element.49), channel_id=1, source_target_pairs={{0,1},{1,2},{2,3},{3,4},{4,5},{5,6},{6,7},{8,9},{9,10},{10,11},{11... | collective-permute-start | bytes 156680 | tf_op jit(solution)/shard_map/ppermute | solution.py:19
  26.2 1.3 collective-permute-start.3
  27.6 2.9 %collective-permute-done.3 = f32[3,34,1,128]{3,2,1,0:T(1,128)S(1)} collective-permute-done((f32[3,34,1,128]{3,2,1,0:T(1,128)S(1)}, f32[3,34,1,128]{3,2,1,0:T(1,128)S(1)}, u32[]{:S(2)}, u32[]{:S(2)}) %collective-permute-start.3) | collective-permute-done | bytes 52256 | tf_op jit(solution)/shard_map/ppermute | solution.py:20
  30.5 1.4 pad_maximum_fusion
  33.0 3.9 %collective-permute-start.8 = (f32[1,32,128]{2,1,0:T(8,128)S(1)}, f32[1,32,128]{2,1,0:T(8,128)S(1)}, u32[]{:S(2)}, u32[]{:S(2)}) collective-permute-start(f32[1,32,128]{2,1,0:T(8,128)S(1)} %get-tuple-element.163), channel_id=1, source_target_pairs={{0,8},{8,16},{16,24},{1,9},{9,17},{17,25},{2,10},{10,18},{18,26},{... | collective-permute-start | bytes 49160 | tf_op jit(solution)/shard_map/ppermute | solution.py:19
  36.9 1.3 collective-permute-start.9
  38.4 4.2 %collective-permute-done.9 = f32[1,32,128]{2,1,0:T(8,128)S(1)} collective-permute-done((f32[1,32,128]{2,1,0:T(8,128)S(1)}, f32[1,32,128]{2,1,0:T(8,128)S(1)}, u32[]{:S(2)}, u32[]{:S(2)}) %collective-permute-start.9) | collective-permute-done | bytes 16416 | tf_op jit(solution)/shard_map/ppermute | solution.py:20
  42.6 3.3 %collective-permute-start.10 = (f32[34,1,128]{2,1,0:T(1,128)S(1)}, f32[34,1,128]{2,1,0:T(1,128)S(1)}, u32[]{:S(2)}, u32[]{:S(2)}) collective-permute-start(f32[34,1,128]{2,1,0:T(1,128)S(1)} %get-tuple-element.89), channel_id=1, source_target_pairs={{0,1},{1,2},{2,3},{3,4},{4,5},{5,6},{6,7},{8,9},{9,10},{10,11},{11... | collective-permute-start | bytes 52232 | tf_op jit(solution)/shard_map/ppermute | solution.py:19
  45.9 1.3 collective-permute-start.11
  47.2 7.7 %all-to-all-start.1 = ((f32[32,32,128]{2,1,0:T(8,128)}), f32[32,32,128]{2,1,0:T(8,128)S(1)}, u32[]{:S(2)}, u32[]{:S(2)}) async-start(f32[32,32,128]{2,1,0:T(8,128)} %param.7), calls=%async_computation.1 | async-start | bytes 1048576 | tf_op jit(solution)/shard_map/all_to_all | solution.py:111
  55.8 3.5 %collective-permute-start.12 = (f32[1,32,128]{2,1,0:T(8,128)S(1)}, f32[1,32,128]{2,1,0:T(8,128)S(1)}, u32[]{:S(2)}, u32[]{:S(2)}) collective-permute-start(f32[1,32,128]{2,1,0:T(8,128)S(1)} %get-tuple-element.161), channel_id=1, source_target_pairs={{0,8},{8,16},{16,24},{1,9},{9,17},{17,25},{2,10},{10,18},{18,26},{... | collective-permute-start | bytes 49160 | tf_op jit(solution)/shard_map/ppermute | solution.py:19
  59.3 1.3 collective-permute-start.13
  60.6 1.3 add_multiply_fusion
  61.9 3.0 %collective-permute-done.13 = f32[1,32,128]{2,1,0:T(8,128)S(1)} collective-permute-done((f32[1,32,128]{2,1,0:T(8,128)S(1)}, f32[1,32,128]{2,1,0:T(8,128)S(1)}, u32[]{:S(2)}, u32[]{:S(2)}) %collective-permute-start.13) | collective-permute-done | bytes 16416 | tf_op jit(solution)/shard_map/ppermute | solution.py:20
  65.0 1.3 collective-permute-start.14
  66.2 1.3 collective-permute-start.15
  67.6 4.0 %collective-permute-done.15 = f32[34,1,128]{2,1,0:T(1,128)S(1)} collective-permute-done((f32[34,1,128]{2,1,0:T(1,128)S(1)}, f32[34,1,128]{2,1,0:T(1,128)S(1)}, u32[]{:S(2)}, u32[]{:S(2)}) %collective-permute-start.15) | collective-permute-done | bytes 17440 | tf_op jit(solution)/shard_map/ppermute | solution.py:20
  72.5 1.9 %collective-permute-start.16 = (f32[1,32,128]{2,1,0:T(8,128)S(1)}, f32[1,32,128]{2,1,0:T(8,128)S(1)}, u32[]{:S(2)}, u32[]{:S(2)}) collective-permute-start(f32[1,32,128]{2,1,0:T(8,128)S(1)} %get-tuple-element.159), channel_id=1, source_target_pairs={{0,8},{8,16},{16,24},{1,9},{9,17},{17,25},{2,10},{10,18},{18,26},{... | collective-permute-start | bytes 49160 | tf_op jit(solution)/shard_map/ppermute | solution.py:19
  74.4 1.3 collective-permute-start.17
  75.7 1.3 pad_slice_fusion.2
  77.6 2.4 %collective-permute-done.17 = f32[1,32,128]{2,1,0:T(8,128)S(1)} collective-permute-done((f32[1,32,128]{2,1,0:T(8,128)S(1)}, f32[1,32,128]{2,1,0:T(8,128)S(1)}, u32[]{:S(2)}, u32[]{:S(2)}) %collective-permute-start.17) | collective-permute-done | bytes 16416 | tf_op jit(solution)/shard_map/ppermute | solution.py:20
  80.1 3.0 %collective-permute-start.18 = (f32[34,1,128]{2,1,0:T(1,128)S(1)}, f32[34,1,128]{2,1,0:T(1,128)S(1)}, u32[]{:S(2)}, u32[]{:S(2)}) collective-permute-start(f32[34,1,128]{2,1,0:T(1,128)S(1)} %get-tuple-element.85), channel_id=1, source_target_pairs={{0,1},{1,2},{2,3},{3,4},{4,5},{5,6},{6,7},{8,9},{9,10},{10,11},{11... | collective-permute-start | bytes 52232 | tf_op jit(solution)/shard_map/ppermute | solution.py:19
  83.0 1.3 collective-permute-start.19
  85.1 2.0 %collective-permute-done.19 = f32[34,1,128]{2,1,0:T(1,128)S(1)} collective-permute-done((f32[34,1,128]{2,1,0:T(1,128)S(1)}, f32[34,1,128]{2,1,0:T(1,128)S(1)}, u32[]{:S(2)}, u32[]{:S(2)}) %collective-permute-start.19) | collective-permute-done | bytes 17440 | tf_op jit(solution)/shard_map/ppermute | solution.py:20
  87.7 1.1 fusion.11
  88.8 6.8 %all-to-all-start = ((f32[32,32,128]{2,1,0:T(8,128)}), f32[32,32,128]{2,1,0:T(8,128)}, u32[]{:S(2)}, u32[]{:S(2)}) async-start(f32[32,32,128]{2,1,0:T(8,128)} %fusion.11), calls=%async_computation | async-start | bytes 1048576 | tf_op jit(solution)/shard_map/all_to_all | solution.py:110
  95.8 1.1 pad_slice_fusion.5
  97.0 8.5 %all-to-all-done = f32[32,32,128]{2,1,0:T(8,128)} async-done(((f32[32,32,128]{2,1,0:T(8,128)}), f32[32,32,128]{2,1,0:T(8,128)}, u32[]{:S(2)}, u32[]{:S(2)}) %all-to-all-start) | async-done | bytes 524320 | tf_op jit(solution)/shard_map/all_to_all | solution.py:110
  105.5 1.1 copy.49
  107.2 0.8 copy-done.7
  114.8 1.1 copy.51
  115.9 3.7 %all-to-all-start.2 = ((f32[4,256,128]{2,0,1:T(4,128)}), f32[4,256,128]{2,0,1:T(4,128)S(1)}, u32[]{:S(2)}, u32[]{:S(2)}) async-start(f32[4,256,128]{2,0,1:T(4,128)} %copy.51), calls=%async_computation.2 | async-start | bytes 1048576 | tf_op jit(solution)/shard_map/all_to_all | solution.py:92
  119.9 9.2 %all-to-all-done.2 = f32[4,256,128]{2,0,1:T(4,128)S(1)} async-done(((f32[4,256,128]{2,0,1:T(4,128)}), f32[4,256,128]{2,0,1:T(4,128)S(1)}, u32[]{:S(2)}, u32[]{:S(2)}) %all-to-all-start.2) | async-done | bytes 524320 | tf_op jit(solution)/shard_map/all_to_all | solution.py:92
  132.8 0.9 multiply_add_fusion.25
  134.5 0.8 multiply_add_fusion.23
  137.9 1.3 collective-permute-start.20
  139.2 4.7 %collective-permute-done.20 = f32[3,32,128]{2,1,0:T(8,128)S(1)} collective-permute-done((f32[3,32,128]{2,1,0:T(8,128)S(1)}, f32[3,32,128]{2,1,0:T(8,128)S(1)}, u32[]{:S(2)}, u32[]{:S(2)}) %collective-permute-start.20) | collective-permute-done | bytes 49184 | tf_op jit(solution)/shard_map/ppermute | solution.py:28
  144.6 13.8 %all-gather = f32[16,32,128]{2,1,0:T(8,128)S(1)} all-gather(f32[4,32,128]{2,1,0:T(8,128)S(1)} %pad_maximum_fusion.6), channel_id=2, replica_groups=mesh['gz'=4,'gy'=8] {'gz'}, dimensions={0}, use_global_device_ids=true | all-gather | bytes 327680 | tf_op jit(solution)/shard_map/all_gather | solution.py:150
  158.9 0.8 pad_maximum_fusion.5
  (184 shorter events, 21.5 us)
Async XLA Ops:
  0.0 12.7 %copy-start.4 = (f32[32,32,128]{2,1,0:T(8,128)S(1)}, f32[32,32,128]{2,1,0:T(8,128)}, u32[]{:S(2)}) copy-start(f32[32,32,128]{2,1,0:T(8,128)} %param.4) | copy-start | bytes 1572868
  0.0 20.3 %copy-start.1 = (f32[32,32,128]{2,1,0:T(8,128)S(1)}, f32[32,32,128]{2,1,0:T(8,128)}, u32[]{:S(2)}) copy-start(f32[32,32,128]{2,1,0:T(8,128)} %param.5) | copy-start | bytes 1572868
  0.0 20.3 %copy-start = (f32[32,32,128]{2,1,0:T(8,128)S(1)}, f32[32,32,128]{2,1,0:T(8,128)}, u32[]{:S(2)}) copy-start(f32[32,32,128]{2,1,0:T(8,128)} %param.6) | copy-start | bytes 1572868
  0.9 11.8 %collective-permute-start.4 = (f32[1,32,128]{2,1,0:T(8,128)S(1)}, f32[1,32,128]{2,1,0:T(8,128)S(1)}, u32[]{:S(2)}, u32[]{:S(2)}) collective-permute-start(f32[1,32,128]{2,1,0:T(8,128)S(1)} %get-tuple-element.166), channel_id=1, source_target_pairs={{0,8},{8,16},{16,24},{1,9},{9,17},{17,25},{2,10},{10,18},{18,26},{... | collective-permute-start | bytes 49160 | tf_op jit(solution)/shard_map/ppermute | solution.py:19
  6.6 13.7 %collective-permute-start = (f32[3,1,32,128]{3,2,1,0:T(8,128)S(1)}, f32[3,1,32,128]{3,2,1,0:T(8,128)S(1)}, u32[]{:S(2)}, u32[]{:S(2)}) collective-permute-start(f32[3,1,32,128]{3,2,1,0:T(8,128)S(1)} %get-tuple-element.53), channel_id=1, source_target_pairs={{0,8},{8,16},{16,24},{1,9},{9,17},{17,25},{2,10},{10,18},{18,26},{... | collective-permute-start | bytes 147464 | tf_op jit(solution)/shard_map/ppermute | solution.py:19
  10.1 10.2 %collective-permute-start.1 = (f32[3,1,32,128]{3,2,1,0:T(8,128)S(1)}, f32[3,1,32,128]{3,2,1,0:T(8,128)S(1)}, u32[]{:S(2)}, u32[]{:S(2)}) collective-permute-start(f32[3,1,32,128]{3,2,1,0:T(8,128)S(1)} %get-tuple-element.54), channel_id=1, source_target_pairs={{8,0},{16,8},{24,16},{9,1},{17,9},{25,17},{10,2},{18,10},{26,18},{... | collective-permute-start | bytes 147464 | tf_op jit(solution)/shard_map/ppermute | solution.py:20
  11.4 6.3 %collective-permute-start.5 = (f32[1,32,128]{2,1,0:T(8,128)S(1)}, f32[1,32,128]{2,1,0:T(8,128)S(1)}, u32[]{:S(2)}, u32[]{:S(2)}) collective-permute-start(f32[1,32,128]{2,1,0:T(8,128)S(1)} %get-tuple-element.165), channel_id=1, source_target_pairs={{8,0},{16,8},{24,16},{9,1},{17,9},{25,17},{10,2},{18,10},{26,18},{... | collective-permute-start | bytes 49160 | tf_op jit(solution)/shard_map/ppermute | solution.py:20
  17.7 9.8 %collective-permute-start.6 = (f32[34,1,128]{2,1,0:T(1,128)S(1)}, f32[34,1,128]{2,1,0:T(1,128)S(1)}, u32[]{:S(2)}, u32[]{:S(2)}) collective-permute-start(f32[34,1,128]{2,1,0:T(1,128)S(1)} %get-tuple-element.91), channel_id=1, source_target_pairs={{0,1},{1,2},{2,3},{3,4},{4,5},{5,6},{6,7},{8,9},{9,10},{10,11},{11... | collective-permute-start | bytes 52232 | tf_op jit(solution)/shard_map/ppermute | solution.py:19
  19.0 8.5 %collective-permute-start.7 = (f32[34,1,128]{2,1,0:T(1,128)S(1)}, f32[34,1,128]{2,1,0:T(1,128)S(1)}, u32[]{:S(2)}, u32[]{:S(2)}) collective-permute-start(f32[34,1,128]{2,1,0:T(1,128)S(1)} %get-tuple-element.92), channel_id=1, source_target_pairs={{1,0},{2,1},{3,2},{4,3},{5,4},{6,5},{7,6},{9,8},{10,9},{11,10},{12... | collective-permute-start | bytes 52232 | tf_op jit(solution)/shard_map/ppermute | solution.py:20
  21.4 6.2 %collective-permute-start.2 = (f32[3,34,1,128]{3,2,1,0:T(1,128)S(1)}, f32[3,34,1,128]{3,2,1,0:T(1,128)S(1)}, u32[]{:S(2)}, u32[]{:S(2)}) collective-permute-start(f32[3,34,1,128]{3,2,1,0:T(1,128)S(1)} %get-tuple-element.49), channel_id=1, source_target_pairs={{0,1},{1,2},{2,3},{3,4},{4,5},{5,6},{6,7},{8,9},{9,10},{10,11},{11... | collective-permute-start | bytes 156680 | tf_op jit(solution)/shard_map/ppermute | solution.py:19
  26.2 4.4 %collective-permute-start.3 = (f32[3,34,1,128]{3,2,1,0:T(1,128)S(1)}, f32[3,34,1,128]{3,2,1,0:T(1,128)S(1)}, u32[]{:S(2)}, u32[]{:S(2)}) collective-permute-start(f32[3,34,1,128]{3,2,1,0:T(1,128)S(1)} %get-tuple-element.50), channel_id=1, source_target_pairs={{1,0},{2,1},{3,2},{4,3},{5,4},{6,5},{7,6},{9,8},{10,9},{11,10},{12... | collective-permute-start | bytes 156680 | tf_op jit(solution)/shard_map/ppermute | solution.py:20
  33.0 5.4 %collective-permute-start.8 = (f32[1,32,128]{2,1,0:T(8,128)S(1)}, f32[1,32,128]{2,1,0:T(8,128)S(1)}, u32[]{:S(2)}, u32[]{:S(2)}) collective-permute-start(f32[1,32,128]{2,1,0:T(8,128)S(1)} %get-tuple-element.163), channel_id=1, source_target_pairs={{0,8},{8,16},{16,24},{1,9},{9,17},{17,25},{2,10},{10,18},{18,26},{... | collective-permute-start | bytes 49160 | tf_op jit(solution)/shard_map/ppermute | solution.py:19
  36.9 5.6 %collective-permute-start.9 = (f32[1,32,128]{2,1,0:T(8,128)S(1)}, f32[1,32,128]{2,1,0:T(8,128)S(1)}, u32[]{:S(2)}, u32[]{:S(2)}) collective-permute-start(f32[1,32,128]{2,1,0:T(8,128)S(1)} %get-tuple-element.164), channel_id=1, source_target_pairs={{8,0},{16,8},{24,16},{9,1},{17,9},{25,17},{10,2},{18,10},{26,18},{... | collective-permute-start | bytes 49160 | tf_op jit(solution)/shard_map/ppermute | solution.py:20
  42.6 12.3 %collective-permute-start.10 = (f32[34,1,128]{2,1,0:T(1,128)S(1)}, f32[34,1,128]{2,1,0:T(1,128)S(1)}, u32[]{:S(2)}, u32[]{:S(2)}) collective-permute-start(f32[34,1,128]{2,1,0:T(1,128)S(1)} %get-tuple-element.89), channel_id=1, source_target_pairs={{0,1},{1,2},{2,3},{3,4},{4,5},{5,6},{6,7},{8,9},{9,10},{10,11},{11... | collective-permute-start | bytes 52232 | tf_op jit(solution)/shard_map/ppermute | solution.py:19
  45.9 9.0 %collective-permute-start.11 = (f32[34,1,128]{2,1,0:T(1,128)S(1)}, f32[34,1,128]{2,1,0:T(1,128)S(1)}, u32[]{:S(2)}, u32[]{:S(2)}) collective-permute-start(f32[34,1,128]{2,1,0:T(1,128)S(1)} %get-tuple-element.90), channel_id=1, source_target_pairs={{1,0},{2,1},{3,2},{4,3},{5,4},{6,5},{7,6},{9,8},{10,9},{11,10},{12... | collective-permute-start | bytes 52232 | tf_op jit(solution)/shard_map/ppermute | solution.py:20
  47.2 41.6 %all-to-all-start.1 = ((f32[32,32,128]{2,1,0:T(8,128)}), f32[32,32,128]{2,1,0:T(8,128)S(1)}, u32[]{:S(2)}, u32[]{:S(2)}) async-start(f32[32,32,128]{2,1,0:T(8,128)} %param.7), calls=%async_computation.1 | async-start | bytes 1048576 | tf_op jit(solution)/shard_map/all_to_all | solution.py:111
  55.8 6.1 %collective-permute-start.12 = (f32[1,32,128]{2,1,0:T(8,128)S(1)}, f32[1,32,128]{2,1,0:T(8,128)S(1)}, u32[]{:S(2)}, u32[]{:S(2)}) collective-permute-start(f32[1,32,128]{2,1,0:T(8,128)S(1)} %get-tuple-element.161), channel_id=1, source_target_pairs={{0,8},{8,16},{16,24},{1,9},{9,17},{17,25},{2,10},{10,18},{18,26},{... | collective-permute-start | bytes 49160 | tf_op jit(solution)/shard_map/ppermute | solution.py:19
  59.3 5.6 %collective-permute-start.13 = (f32[1,32,128]{2,1,0:T(8,128)S(1)}, f32[1,32,128]{2,1,0:T(8,128)S(1)}, u32[]{:S(2)}, u32[]{:S(2)}) collective-permute-start(f32[1,32,128]{2,1,0:T(8,128)S(1)} %get-tuple-element.162), channel_id=1, source_target_pairs={{8,0},{16,8},{24,16},{9,1},{17,9},{25,17},{10,2},{18,10},{26,18},{... | collective-permute-start | bytes 49160 | tf_op jit(solution)/shard_map/ppermute | solution.py:20
  61.9 5.7 %copy-start.2 = (f32[31,32,128]{2,1,0:T(8,128)}, f32[31,32,128]{2,1,0:T(8,128)S(1)}, u32[]{:S(2)}) copy-start(f32[31,32,128]{2,1,0:T(8,128)S(1)} %add_multiply_fusion) | copy-start | bytes 1523716
  65.0 2.7 %collective-permute-start.14 = (f32[34,1,128]{2,1,0:T(1,128)S(1)}, f32[34,1,128]{2,1,0:T(1,128)S(1)}, u32[]{:S(2)}, u32[]{:S(2)}) collective-permute-start(f32[34,1,128]{2,1,0:T(1,128)S(1)} %get-tuple-element.87), channel_id=1, source_target_pairs={{0,1},{1,2},{2,3},{3,4},{4,5},{5,6},{6,7},{8,9},{9,10},{10,11},{11... | collective-permute-start | bytes 52232 | tf_op jit(solution)/shard_map/ppermute | solution.py:19
  66.2 5.3 %collective-permute-start.15 = (f32[34,1,128]{2,1,0:T(1,128)S(1)}, f32[34,1,128]{2,1,0:T(1,128)S(1)}, u32[]{:S(2)}, u32[]{:S(2)}) collective-permute-start(f32[34,1,128]{2,1,0:T(1,128)S(1)} %get-tuple-element.88), channel_id=1, source_target_pairs={{1,0},{2,1},{3,2},{4,3},{5,4},{6,5},{7,6},{9,8},{10,9},{11,10},{12... | collective-permute-start | bytes 52232 | tf_op jit(solution)/shard_map/ppermute | solution.py:20
  72.5 5.1 %collective-permute-start.16 = (f32[1,32,128]{2,1,0:T(8,128)S(1)}, f32[1,32,128]{2,1,0:T(8,128)S(1)}, u32[]{:S(2)}, u32[]{:S(2)}) collective-permute-start(f32[1,32,128]{2,1,0:T(8,128)S(1)} %get-tuple-element.159), channel_id=1, source_target_pairs={{0,8},{8,16},{16,24},{1,9},{9,17},{17,25},{2,10},{10,18},{18,26},{... | collective-permute-start | bytes 49160 | tf_op jit(solution)/shard_map/ppermute | solution.py:19
  74.4 5.6 %collective-permute-start.17 = (f32[1,32,128]{2,1,0:T(8,128)S(1)}, f32[1,32,128]{2,1,0:T(8,128)S(1)}, u32[]{:S(2)}, u32[]{:S(2)}) collective-permute-start(f32[1,32,128]{2,1,0:T(8,128)S(1)} %get-tuple-element.160), channel_id=1, source_target_pairs={{8,0},{16,8},{24,16},{9,1},{17,9},{25,17},{10,2},{18,10},{26,18},{... | collective-permute-start | bytes 49160 | tf_op jit(solution)/shard_map/ppermute | solution.py:20
  80.1 5.0 %collective-permute-start.18 = (f32[34,1,128]{2,1,0:T(1,128)S(1)}, f32[34,1,128]{2,1,0:T(1,128)S(1)}, u32[]{:S(2)}, u32[]{:S(2)}) collective-permute-start(f32[34,1,128]{2,1,0:T(1,128)S(1)} %get-tuple-element.85), channel_id=1, source_target_pairs={{0,1},{1,2},{2,3},{3,4},{4,5},{5,6},{6,7},{8,9},{9,10},{10,11},{11... | collective-permute-start | bytes 52232 | tf_op jit(solution)/shard_map/ppermute | solution.py:19
  83.0 4.0 %collective-permute-start.19 = (f32[34,1,128]{2,1,0:T(1,128)S(1)}, f32[34,1,128]{2,1,0:T(1,128)S(1)}, u32[]{:S(2)}, u32[]{:S(2)}) collective-permute-start(f32[34,1,128]{2,1,0:T(1,128)S(1)} %get-tuple-element.86), channel_id=1, source_target_pairs={{1,0},{2,1},{3,2},{4,3},{5,4},{6,5},{7,6},{9,8},{10,9},{11,10},{12... | collective-permute-start | bytes 52232 | tf_op jit(solution)/shard_map/ppermute | solution.py:20
  85.1 34.6 %copy-start.12 = (f32[1,32,128]{2,1,0:T(8,128)}, f32[1,32,128]{2,1,0:T(8,128)S(1)}, u32[]{:S(2)}) copy-start(f32[1,32,128]{2,1,0:T(8,128)S(1)} %get-tuple-element.96) | copy-start | bytes 49156
  88.8 16.6 %all-to-all-start = ((f32[32,32,128]{2,1,0:T(8,128)}), f32[32,32,128]{2,1,0:T(8,128)}, u32[]{:S(2)}, u32[]{:S(2)}) async-start(f32[32,32,128]{2,1,0:T(8,128)} %fusion.11), calls=%async_computation | async-start | bytes 1048576 | tf_op jit(solution)/shard_map/all_to_all | solution.py:110
  107.0 1.0 copy-start.7
  107.1 1.2 copy-start.8
  114.7 4.9 %copy-start.3 = (f32[31,32,128]{2,1,0:T(8,128)S(1)}, f32[31,32,128]{2,1,0:T(8,128)}, u32[]{:S(2)}) copy-start(f32[31,32,128]{2,1,0:T(8,128)} %copy-done.2) | copy-start | bytes 1523716
  115.9 13.2 %all-to-all-start.2 = ((f32[4,256,128]{2,0,1:T(4,128)}), f32[4,256,128]{2,0,1:T(4,128)S(1)}, u32[]{:S(2)}, u32[]{:S(2)}) async-start(f32[4,256,128]{2,0,1:T(4,128)} %copy.51), calls=%async_computation.2 | async-start | bytes 1048576 | tf_op jit(solution)/shard_map/all_to_all | solution.py:92
  129.9 1.0 copy-start.9
  129.9 1.2 copy-start.10
  129.9 1.3 copy-start.11
  129.9 1.3 copy-start.14
  137.1 0.8 copy-start.5
  137.2 6.7 %copy-start.13 = (f32[1,32,128]{2,1,0:T(8,128)S(1)}, f32[1,32,128]{2,1,0:T(8,128)}, u32[]{:S(2)}) copy-start(f32[1,32,128]{2,1,0:T(8,128)} %copy-done.12) | copy-start | bytes 49156
  137.9 6.0 %collective-permute-start.20 = (f32[3,32,128]{2,1,0:T(8,128)S(1)}, f32[3,32,128]{2,1,0:T(8,128)S(1)}, u32[]{:S(2)}, u32[]{:S(2)}) collective-permute-start(f32[3,32,128]{2,1,0:T(8,128)S(1)} %pad_maximum_fusion.15), channel_id=1, source_target_pairs={{8,0},{16,8},{24,16},{9,1},{17,9},{25,17},{10,2},{18,10},{26,18},{... | collective-permute-start | bytes 147464 | tf_op jit(solution)/shard_map/ppermute | solution.py:28
  139.2 19.5 %copy-start.6 = (f32[31,32,128]{2,1,0:T(8,128)S(1)}, f32[31,32,128]{2,1,0:T(8,128)}, u32[]{:S(2)}) copy-start(f32[31,32,128]{2,1,0:T(8,128)} %copy-done.5) | copy-start | bytes 1523716
where the time goes:
time: 161 us; the launch traced here: 160 us
  starting transfers between devices  63.7 us (40%)
  waiting for transfers between devices  45.9 us (29%)
  other arithmetic  21.7 us (13%)
  blocking collectives  13.8 us (9%)
  local copies, waits for them, and re-layouts  13.3 us (8%)
    ppermute x10, starting transfers between devices, padded_2(): before = lax.ppermute(last, axis, up)  31.3 us
    ppermute x10, waiting for transfers between devices, padded_2(): after = lax.ppermute(leading, axis, down)  23.4 us
    all_gather x1, blocking collectives, local(): collected = lax.all_gather(equations[None], 'gz', axis=0, tiled=True)  13.8 us
    ppermute x10, starting transfers between devices, padded_2(): after = lax.ppermute(leading, axis, down)  12.9 us
    all_to_all x1, waiting for transfers between devices, solve_rows(): return lax.all_to_all(solved, 'gy', split_axis=1, concat_axis=0, tiled=True)  9.2 us
    all_to_all x1, waiting for transfers between devices, local(): lax.all_to_all(state, 'gy', split_axis=0, concat_axis=1, tiled=True)  8.47 us
    all_to_all x1, starting transfers between devices, local(): lax.all_to_all(kappa, 'gy', split_axis=0, concat_axis=1, tiled=True)  7.67 us
    all_to_all x1, starting transfers between devices, local(): lax.all_to_all(state, 'gy', split_axis=0, concat_axis=1, tiled=True)  6.8 us
  transfers between devices with their start and end apart: 24, of which 11 were waited for; matrix products, arithmetic and copies ran while one was open for 7% of the time, Pallas kernels for 0%

commit v1 on v0

v1 whole, which is shorter than its diff:
```python
import functools

import jax
import jax.numpy as jnp
from jax import lax
from jax.experimental import pallas as pl
from jax.experimental.pallas import tpu as pltpu
from jax.sharding import PartitionSpec as P

NSUB = 4
RATE = 500.0
AXES = ("gz", "gy")
F32 = jnp.float32


def vmem(count):
    return [pl.BlockSpec(memory_space=pltpu.VMEM)] * count


def shape(*dims):
    return jax.ShapeDtypeStruct(dims, F32)


def place():
    return (
        lax.axis_index("gz"),
        lax.axis_index("gy"),
        lax.axis_size("gz"),
        lax.axis_size("gy"),
    )


def pair_up(index):
    return index ^ 1


def pair_other(index, count):
    return (index + 1 if index % 2 else index - 1) % count


def permutation(z_partner, y_partner):
    z_count, y_count = lax.axis_size("gz"), lax.axis_size("gy")
    pairs = []
    for z in range(z_count):
        for y in range(y_count):
            to_z, to_y = z_partner(z), y_partner(y)
            if not 0 <= to_z < z_count:
                to_z, to_y = z, pair_up(y)
            pairs.append((z * y_count + y, to_z * y_count + to_y))
    return pairs


def same(index):
    return index


def z_other(index):
    return index + 1 if index % 2 else index - 1


def y_other(index):
    return pair_other(index, lax.axis_size("gy"))


def send(x, z_partner=same, y_partner=same):
    return lax.ppermute(x, AXES, permutation(z_partner, y_partner))


def pack_kernel(c, ys, zs, a_ref, b_ref, o_ref, e_ref, oa_ref, ob_ref):
    z, y, _, _ = place()
    depth, width = c.shape[0], c.shape[1]
    z_odd, y_odd = lax.rem(z, 2), lax.rem(y, 2)
    for ref, low in ((a_ref, z_odd), (b_ref, 1 - z_odd)):
        four, three = (1 - low) * (depth - 4), (1 - low) * (depth - 3)
        ref[0:4] = c[pl.ds(four, 4)]
        ref[4:8] = zs[pl.ds(four, 4)]
        ref[8:11] = ys[pl.ds(three, 3)]

    def rims(o_start, e_start):
        for ref, start in ((o_ref, o_start), (e_ref, e_start)):
            high = int(start > 0)
            for k in range(4):
                ref[k] = c[:, start + k, :]
                ref[4 + k] = ys[:, start + k, :]
            for k in range(3):
                ref[8 + k] = zs[:, start + high + k, :]

        def corner(ref, z_start):
            high = int(o_start > 0)
            for f, field in enumerate((c, ys, zs)):
                for k in range(3):
                    ref[3 * f + k] = field[z_start : z_start + 8, o_start + high + k, :]

        @pl.when(z_odd == 0)
        def _():
            corner(oa_ref, depth - 8)
            corner(ob_ref, 0)

        @pl.when(z_odd == 1)
        def _():
            corner(oa_ref, 0)
            corner(ob_ref, depth - 8)

    @pl.when(y_odd == 0)
    def _():
        rims(0, width - 4)

    @pl.when(y_odd == 1)
    def _():
        rims(width - 4, 0)


def pack(tracer, y_speed, z_speed):
    depth, width, band = tracer.shape
    return pl.pallas_call(
        pack_kernel,
        out_shape=(
            shape(11, width, band),
            shape(11, width, band),
            shape(11, depth, band),
            shape(11, depth, band),
            shape(9, 8, band),
            shape(9, 8, band),
        ),
        in_specs=vmem(3),
        out_specs=vmem(6),
        name="pack",
    )(tracer, y_speed, z_speed)


def rim_kernel(a, b, out):
    _, y, _, _ = place()
    width = a.shape[1]

    def fill(start):
        for half, ref in enumerate((a, b)):
            for k in range(11):
                out[11 * half + k] = ref[k, start : start + 8, :]

    @pl.when(lax.rem(y, 2) == 0)
    def _():
        fill(width - 8)

    @pl.when(lax.rem(y, 2) == 1)
    def _():
        fill(0)


def rim(a, b):
    return pl.pallas_call(
        rim_kernel,
        out_shape=shape(22, 8, a.shape[2]),
        in_specs=vmem(2),
        out_specs=vmem(1)[0],
        name="rim",
    )(a, b)


def advect_kernel(
    tracer, y_speed, z_speed, a, b, o, e, oa, ob, ab, weight_y, first_y,
    forward, ports, c, ys, zs, yp, yn, zp, zn,
):
    z, y, z_count, y_count = place()
    depth, width, band = tracer.shape
    rows, cols = depth + 8, width + 8
    z_odd, y_odd = lax.rem(z, 2), lax.rem(y, 2)
    keep_b = jnp.where((z_odd == 0) & (z == 0) | (z_odd == 1) & (z == z_count - 1), 0.0, 1.0)
    keep_o = jnp.where((y_odd == 0) & (y == 0) | (y_odd == 1) & (y == y_count - 1), 0.0, 1.0)
    column = lax.broadcasted_iota(jnp.int32, (8, band), 0)
    outside = (column < 4) & (y == y_count - 1) | (column >= 4) & (y == 0)
    inside = jnp.where(outside, 0.0, 1.0)

    for field, own in ((c, tracer), (ys, y_speed), (zs, z_speed)):
        field[4 : 4 + depth, 0:width, :] = own[...]
        field[0:4, width:cols, :] = jnp.zeros((4, 8, band), F32)
        field[4 + depth : rows, width:cols, :] = jnp.zeros((4, 8, band), F32)
    ys[0:1, 0:width, :] = jnp.zeros((1, width, band), F32)
    ys[rows - 1 : rows, 0:width, :] = jnp.zeros((1, width, band), F32)
    for ref, low, keep in ((a, z_odd, None), (b, 1 - z_odd, keep_b)):
        scale = (lambda v: v) if keep is None else (lambda v: v * keep)
        four = jnp.where(low == 1, 0, depth + 4)
        three = jnp.where(low == 1, 1, depth + 4)
        c[pl.ds(four, 4), 0:width, :] = scale(ref[0:4])
        zs[pl.ds(four, 4), 0:width, :] = scale(ref[4:8])
        ys[pl.ds(three, 3), 0:width, :] = scale(ref[8:11])

    def sides(o_low):
        def columns(ref, low, scale):
            start = width + 4 * int(low)
            shift = int(low)
            for k in range(4):
                c[4 : 4 + depth, start + k, :] = scale(ref[k])
                ys[4 : 4 + depth, start + k, :] = scale(ref[4 + k])
            for k in range(3):
                zs[4 : 4 + depth, start + shift + k, :] = scale(ref[8 + k])
            far = start if low else start + 3
            zs[4 : 4 + depth, far, :] = jnp.zeros((depth, band), F32)

        columns(o, o_low, lambda v: v * keep_o)
        columns(e, not o_low, lambda v: v)

        def from_pair(half, z_low):
            start = width + 4 * int(o_low is False)
            low = not o_low
            from_col = 0 if not low else 4
            zr = 0 if z_low else depth + 4
            z3 = 1 if z_low else depth + 4
            keep = 1.0 if half == 0 else keep_b
            block = slice(from_col, from_col + 4)
            c[zr : zr + 4, start : start + 4, :] = ab[11 * half : 11 * half + 4, block, :] * keep
            zs[zr : zr + 4, start : start + 4, :] = ab[11 * half + 4 : 11 * half + 8, block, :] * keep
            ys[z3 : z3 + 3, start : start + 4, :] = ab[11 * half + 8 : 11 * half + 11, block, :] * keep

        def from_corner(ref, z_low, keep):
            start = width + (5 if o_low else 0)
            zr = 1 if z_low else depth + 4
            src = 5 if z_low else 0
            for f, field in enumerate((c, ys, zs)):
                for k in range(3):
                    field[zr : zr + 3, start + k, :] = ref[3 * f + k, src : src + 3, :] * keep

        @pl.when(z_odd == 0)
        def _():
            from_pair(0, False)
            from_pair(1, True)
            from_corner(oa, False, keep_o)
            from_corner(ob, True, keep_o * keep_b)

        @pl.when(z_odd == 1)
        def _():
            from_pair(0, True)
            from_pair(1, False)
            from_corner(oa, True, keep_o)
            from_corner(ob, False, keep_o * keep_b)

    @pl.when(y_odd == 0)
    def _():
        sides(True)

    @pl.when(y_odd == 1)
    def _():
        sides(False)

    def up(v):
        return pltpu.roll(v, cols - 1, 0)

    def down(v):
        return pltpu.roll(v, 1, 0)

    def faces(r, _):
        v = ys[r]
        s = 0.5 * (v + up(v))
        yp[r] = jnp.maximum(s, 0.0)
        yn[r] = jnp.minimum(s, 0.0)
        s = 0.5 * (zs[r] + zs[jnp.minimum(r + 1, rows - 1)])
        zp[r] = jnp.maximum(s, 0.0)
        zn[r] = jnp.minimum(s, 0.0)
        return 0

    lax.fori_loop(0, rows, faces, 0, unroll=4)

    for step in range(1, NSUB + 1):
        low = jnp.where(z == 0, 4, step)
        high = jnp.where(z == z_count - 1, rows - 4, rows - step)
        here = c[low]
        flux = zp[low - 1] * c[low - 1] + zn[low - 1] * here

        def row(r, carry):
            here, below = carry
            after = c[r + 1]
            above = zp[r] * here + zn[r] * after
            across = yp[r] * here + yn[r] * up(here)
            new = here - (across - down(across)) - (above - below)
            c[r, 0:width, :] = new[0:width]
            c[r, width:cols, :] = new[width:cols] * inside
            return after, above

        lax.fori_loop(low, high, row, (here, flux))

    total = jnp.zeros((depth, band), F32)
    carry = jnp.zeros((depth, band), F32)
    for j in range(width):
        value = c[4 : 4 + depth, j, :]
        total = total + first_y[j] * value
        carry = value + weight_y[j] * carry
        forward[j] = carry
    ports[0] = total
    ports[1] = carry


def advect(tracer, y_speed, z_speed, halos, weight_y, first_y):
    depth, width, band = tracer.shape
    padded = pltpu.VMEM((depth + 8, width + 8, band), F32)
    return pl.pallas_call(
        advect_kernel,
        out_shape=(shape(width, depth, band), shape(2, depth, band)),
        in_specs=vmem(12),
        out_specs=vmem(2),
        scratch_shapes=[padded] * 7,
        name="advect",
    )(tracer, y_speed, z_speed, *halos, weight_y, first_y)


def factor_rows(read, count, edge_low, edge_high, weight, inverse, first, last, ports):
    face = [None] * (count + 1)
    before = read(0)
    low_kappa = before
    for j in range(1, count):
        here = read(j)
        face[j] = 0.5 * RATE * (before + here)
        before = here
    high_kappa = before
    left = 1.0 + edge_low * (RATE * low_kappa)
    right = 1.0 + edge_high * (RATE * high_kappa)
    ratios = [None] * count
    weight[0] = jnp.zeros_like(low_kappa)
    for j in range(1, count):
        inv = 1.0 / (face[j] + left)
        ratio = face[j] * inv
        inverse[j - 1] = inv
        weight[j] = ratio
        left = 1.0 + left * ratio
        back = count - j
        ratio = face[back] / (face[back] + right)
        ratios[back] = ratio
        right = 1.0 + right * ratio
    end = 1.0 / (left + edge_high * (RATE * high_kappa))
    inverse[count - 1] = end
    start = 1.0 / (right + edge_low * (RATE * low_kappa))
    ports[0] = start
    ports[2] = end
    ports[3] = low_kappa
    ports[4] = high_kappa
    value = start
    first[0] = value
    back_value = end
    last[count - 1] = end
    for j in range(1, count):
        value = value * ratios[j]
        first[j] = value
        back = count - j
        back_value = back_value * weight[back]
        last[back - 1] = back_value
    ports[1] = value


def factor_kernel(kappa, wy, py, fy, ly, ports_y, wz, pz, fz, lz, ports_z):
    z, y, z_count, y_count = place()
    depth, width, _ = kappa.shape

    def flag(condition):
        return jnp.where(condition, 1.0, 0.0)

    factor_rows(
        lambda j: kappa[:, j, :], width, flag(y == 0), flag(y == y_count - 1), wy, py, fy, ly, ports_y
    )
    factor_rows(
        lambda j: kappa[j], depth, flag(z == 0), flag(z == z_count - 1), wz, pz, fz, lz, ports_z
    )


def factor(kappa):
    depth, width, band = kappa.shape
    along_y = [shape(width, depth, band)] * 4 + [shape(5, depth, band)]
    along_z = [shape(depth, width, band)] * 4 + [shape(5, width, band)]
    return pl.pallas_call(
        factor_kernel,
        out_shape=tuple(along_y + along_z),
        in_specs=vmem(1),
        out_specs=vmem(10),
        name="factor",
    )(kappa)


def backward_kernel(forward, weight, inverse, out):
    count = forward.shape[0]
    value = forward[count - 1] * inverse[count - 1]
    out[count - 1] = value
    for j in range(count - 2, -1, -1):
        value = forward[j] * inverse[j] + weight[j + 1] * value
        out[j] = value


def backward(forward, weight, inverse):
    return pl.pallas_call(
        backward_kernel,
        out_shape=shape(*forward.shape),
        in_specs=vmem(3),
        out_specs=vmem(1)[0],
        name="backward",
    )(forward, weight, inverse)


def turn_kernel(base, first_y, last_y, currents, weight_z, first_z, forward, ports, u):
    width, depth, band = base.shape
    low, high = currents[0], currents[1]
    for j in range(width):
        u[:, j, :] = base[j] + low * first_y[j] + high * last_y[j]
    total = jnp.zeros((width, band), F32)
    carry = jnp.zeros((width, band), F32)
    for k in range(depth):
        value = u[k]
        total = total + first_z[k] * value
        carry = value + weight_z[k] * carry
        forward[k] = carry
    ports[0] = total
    ports[1] = carry


def turn(base, first_y, last_y, currents, weight_z, first_z):
    width, depth, band = base.shape
    return pl.pallas_call(
        turn_kernel,
        out_shape=(shape(depth, width, band), shape(2, width, band)),
        in_specs=vmem(6),
        out_specs=vmem(2),
        scratch_shapes=[pltpu.VMEM((depth, width, band), F32)],
        name="turn",
    )(base, first_y, last_y, currents, weight_z, first_z)


def finish_kernel(base, first, last, currents, out):
    low, high = currents[0], currents[1]
    for k in range(base.shape[0]):
        out[k] = base[k] + low * first[k] + high * last[k]


def finish(base, first, last, currents):
    return pl.pallas_call(
        finish_kernel,
        out_shape=shape(*base.shape),
        in_specs=vmem(4),
        out_specs=vmem(1)[0],
        name="finish",
    )(base, first, last, currents)


def xor_exchange(x, axis, level):
    step = 1 << level
    return lax.ppermute(x, axis, [(i, i ^ step) for i in range(lax.axis_size(axis))])


def levels_of(axis):
    return (lax.axis_size(axis) - 1).bit_length()


def join_ports(ports, axis):
    index = lax.axis_index(axis)
    joins = []
    for level in range(levels_of(axis)):
        theirs = xor_exchange(ports, axis, level)
        is_left = (lax.shift_right_logical(index, level) & 1) == 0
        left = jnp.where(is_left, ports, theirs)
        right = jnp.where(is_left, theirs, ports)
        face = 0.5 * RATE * (left[4] + right[3])
        d = 1.0 / (1.0 / face + left[2] + right[0])
        joins.append((is_left, d, left[1], right[1]))
        ports = jnp.stack(
            [
                left[0] - left[1] * left[1] * d,
                left[1] * right[1] * d,
                right[2] - right[1] * right[1] * d,
                left[3],
                right[4],
            ]
        )
    return joins


def port_currents(sources, joins, axis):
    found = []
    count = len(joins)
    for level, (is_left, d, z_left, z_right) in enumerate(joins):
        theirs = xor_exchange(sources, axis, level)
        left = jnp.where(is_left, sources, theirs)
        right = jnp.where(is_left, theirs, sources)
        flow = (left[1] - right[0]) * d
        found.append(flow)
        if level + 1 < count:
            sources = jnp.stack([left[0] - z_left * flow, right[1] + z_right * flow])
    low = jnp.zeros_like(found[0])
    high = low
    for (is_left, d, z_left, z_right), flow in zip(joins[::-1], found[::-1]):
        flow = flow + (z_left * low - z_right * high) * d
        low, high = jnp.where(is_left, low, flow), jnp.where(is_left, -flow, high)
    return jnp.stack([low, high])


def local(tracer, y_speed, z_speed, kappa):
    a, b, o, e, oa, ob = pack(tracer, y_speed, z_speed)
    a = send(a, z_partner=pair_up)
    b = send(b, z_partner=z_other)
    o = send(o, y_partner=y_other)
    e = send(e, y_partner=pair_up)
    oa = send(oa, z_partner=pair_up, y_partner=y_other)
    ob = send(ob, z_partner=z_other, y_partner=y_other)
    ab = send(rim(a, b), y_partner=pair_up)
    wy, py, fy, ly, ports_y, wz, pz, fz, lz, ports_z = factor(kappa)
    joins_y = join_ports(ports_y, "gy")
    joins_z = join_ports(ports_z, "gz")
    forward, sources = advect(tracer, y_speed, z_speed, (a, b, o, e, oa, ob, ab), wy, fy)
    sources = jnp.stack([sources[0], sources[1] * py[-1]])
    currents = port_currents(sources, joins_y, "gy")
    base = backward(forward, wy, py)
    forward, sources = turn(base, fy, ly, currents, wz, fz)
    sources = jnp.stack([sources[0], sources[1] * pz[-1]])
    currents = port_currents(sources, joins_z, "gz")
    base = backward(forward, wz, pz)
    return finish(base, fz, lz, currents)


def solution(mesh):
    spec = P("gz", "gy", None)
    return jax.shard_map(
        local, mesh=mesh, in_specs=(spec,) * 4, out_specs=spec, check_vma=False
    )
```

time: 161 us -> 66.9 us (0.42)
  starting transfers between devices: 63.7 us -> 22.3 us
  waiting for transfers between devices: 45.9 us -> 13.5 us
  Pallas kernels: 0 us -> 26 us
  other arithmetic: 21.7 us -> 3.11 us
  blocking collectives: 13.8 us -> 0 us
  local copies, waits for them, and re-layouts: 13.3 us -> 1.24 us
    pallas_call x0 -> x8, Pallas kernels: none -> 26 us  [the longest x1 6.07 us: factor(): pl.pallas_call(factor_kernel, out_shape=tuple(along_y + along_z), in_spec...]
    ppermute x21 -> x17, starting transfers between devices: 45.5 us -> 22.3 us  [the longest x10 14.2 us: xor_exchange(): lax.ppermute(x, axis, [(i, i ^ step) for i in range(lax.axis_size(axis))])]
    all_to_all x3 -> x0, starting transfers between devices: 18.2 us -> none  [the longest x1 7.67 us: local(): lax.all_to_all(kappa, 'gy', split_axis=0, concat_axis=1, tiled=True)]
    all_to_all x3 -> x0, waiting for transfers between devices: 17.7 us -> none  [the longest x1 9.2 us: solve_rows(): return lax.all_to_all(solved, 'gy', split_axis=1, concat_axis=0, tiled=True)]
    ppermute x21 -> x17, waiting for transfers between devices: 28.2 us -> 13.5 us  [the longest x10 11.9 us: xor_exchange(): lax.ppermute(x, axis, [(i, i ^ step) for i in range(lax.axis_size(axis))])]
    all_gather x1 -> x0, blocking collectives: 13.8 us -> none  [local(): collected = lax.all_gather(equations[None], 'gz', axis=0, tiled=True)]
    add x32 -> x2, other arithmetic: 10.7 us -> 0.02 us  [port_currents(): sources = jnp.stack([left[0] - z_left * flow, right[1] + z_right * flow])]
    slice x80 -> x0, local copies, waits for them, and re-layouts: 7.97 us -> none  [the longest x36 3.23 us: move_down(): kept = lax.slice_in_dim(values, 0, count - offset, axis=axis)]
  transfers between devices with their start and end apart: 24 -> 17, of which waited for: 11 -> 8; matrix products, arithmetic and copies ran while one was open for 7% -> 0% of each run, Pallas kernels for 0% -> 13%
where the time goes in v1:
time: 66.9 us; the launch traced here: 66.4 us
  Pallas kernels  26 us (39%)
  starting transfers between devices  22.3 us (33%)
  waiting for transfers between devices  13.5 us (20%)
  other arithmetic  3.11 us (5%)
  local copies, waits for them, and re-layouts  1.24 us (2%)
    ppermute x10, starting transfers between devices, xor_exchange(): lax.ppermute(x, axis, [(i, i ^ step) for i in range(lax.axis_size(axis))])  14.2 us
    ppermute x10, waiting for transfers between devices, xor_exchange(): lax.ppermute(x, axis, [(i, i ^ step) for i in range(lax.axis_size(axis))])  11.9 us
    ppermute x7, starting transfers between devices, send(): return lax.ppermute(x, AXES, permutation(z_partner, y_partner))  8.16 us
    pallas_call x1, Pallas kernels, factor(): pl.pallas_call(factor_kernel, out_shape=tuple(along_y + along_z), in_spec...  6.07 us
    pallas_call x1, Pallas kernels, advect(): pl.pallas_call(advect_kernel, out_shape=(shape(width, depth, band), shape...  5.8 us
    pallas_call x2, Pallas kernels, backward(): pl.pallas_call(backward_kernel, out_shape=shape(*forward.shape), in_specs...  4.45 us
    pallas_call x1, Pallas kernels, turn(): pl.pallas_call(turn_kernel, out_shape=(shape(depth, width, band), shape(2...  3.12 us
    pallas_call x1, Pallas kernels, pack(): pl.pallas_call(pack_kernel, out_shape=(shape(11, width, band), shape(11,...  2.62 us
  transfers between devices with their start and end apart: 17, of which 8 were waited for; matrix products, arithmetic and copies ran while one was open for 0% of the time, Pallas kernels for 13%

profile of v1, /device:TPU:0, one launch (start us, length us, event | category | flops | bytes accessed | tf_op | source)
XLA Modules:
  0.0 66.4 jit_solution(16844076619708522053)
XLA Ops:
  0.0 6.1 %factor.1 = (f32[32,32,128]{2,1,0:T(8,128)}, f32[32,32,128]{2,1,0:T(8,128)}, f32[32,32,128]{2,1,0:T(8,128)}, f32[32,32,128]{2,1,0:T(8,128)}, f32[5,32,128]{2,1,0...) custom-call(f32[32,32,128]{2,1,0:T(8,128)} %kappa.1), custom_call_target="tpu_custom_call" | custom-call | tf_op jit(solution)/shard_map/factor/pallas_call | solution.py:366
  6.1 0.5 collective-permute-start.8
  6.5 2.6 %pack.1 = (f32[11,32,128]{2,1,0:T(8,128)}, f32[11,32,128]{2,1,0:T(8,128)}, f32[11,32,128]{2,1,0:T(8,128)}, f32[11,32,128]{2,1,0:T(8,128)}, f32[9,8,128]{2,1,0:T(8,128)}, /*index=5*/f32[9,8,128]{2,1,0:T(8,128)}) custom-call(f32[32,32,128]{2,1,0:T(8,128)} %tracer.1, f32[32,32,128]{2,1,0:T(8,128)} %y_speed.1, f32[32,32,128]{2,1,0:T(8,128)} %z_speed.1), custom_call_target="tpu_custom_call" | custom-call | tf_op jit(solution)/shard_map/pack/pallas_call | solution.py:115
  9.1 2.6 %collective-permute-start = (f32[11,32,128]{2,1,0:T(8,128)}, f32[11,32,128]{2,1,0:T(8,128)S(1)}, u32[]{:S(2)}, u32[]{:S(2)}) collective-permute-start(f32[11,32,128]{2,1,0:T(8,128)} %get-tuple-element.25), channel_id=1, source_target_pairs={{0,8},{1,9},{2,10},{3,11},{4,12},{5,13},{6,14},{7,15},{8,0},{9,1},... | collective-permute-start | bytes 540680 | tf_op jit(solution)/shard_map/ppermute | solution.py:66
  11.7 0.2 collective-permute-start.1
  11.9 2.4 %collective-permute-start.2 = (f32[11,32,128]{2,1,0:T(8,128)}, f32[11,32,128]{2,1,0:T(8,128)S(1)}, u32[]{:S(2)}, u32[]{:S(2)}) collective-permute-start(f32[11,32,128]{2,1,0:T(8,128)} %get-tuple-element.27), channel_id=1, source_target_pairs={{0,7},{1,2},{2,1},{3,4},{4,3},{5,6},{6,5},{7,0},{8,15},{9,10},{10,... | collective-permute-start | bytes 540680 | tf_op jit(solution)/shard_map/ppermute | solution.py:66
  14.3 0.0 collective-permute-start.3
  14.3 0.0 collective-permute-done.8
  14.3 2.6 %collective-permute-start.14 = (f32[5,32,128]{2,1,0:T(8,128)S(1)}, f32[5,32,128]{2,1,0:T(8,128)S(1)}, u32[]{:S(2)}, u32[]{:S(2)}) collective-permute-start(f32[5,32,128]{2,1,0:T(8,128)S(1)} %copy-done.5), channel_id=1, source_target_pairs={{0,8},{8,0},{16,24},{24,16},{1,9},{9,1},{17,25},{25,17},{2,10},{10... | collective-permute-start | bytes 245768 | tf_op jit(solution)/shard_map/ppermute | solution.py:440
  17.0 0.2 collective-permute-done.a
  17.2 2.9 %collective-permute-start.4 = (f32[9,8,128]{2,1,0:T(8,128)S(1)}, f32[9,8,128]{2,1,0:T(8,128)S(1)}, u32[]{:S(2)}, u32[]{:S(2)}) collective-permute-start(f32[9,8,128]{2,1,0:T(8,128)S(1)} %copy-done.10), channel_id=1, source_target_pairs={{0,15},{1,10},{2,9},{3,12},{4,11},{5,14},{6,13},{7,8},{8,7},{9,2},... | collective-permute-start | bytes 110600 | tf_op jit(solution)/shard_map/ppermute | solution.py:66
  20.1 0.0 collective-permute-done.1.b
  20.1 0.1 collective-permute-start.5
  20.2 0.6 copy-done.1
  20.8 1.7 %rim.1 = f32[22,8,128]{2,1,0:T(8,128)} custom-call(f32[11,32,128]{2,1,0:T(8,128)} %copy-done, f32[11,32,128]{2,1,0:T(8,128)} %copy-done.1), custom_call_target="tpu_custom_call" | custom-call | tf_op jit(solution)/shard_map/rim/pallas_call | solution.py:150
  22.4 0.0 collective-permute-done.14
  22.4 0.0 collective-permute-start.6
  22.4 0.0 collective-permute-done.4.oa
  22.5 0.0 collective-permute-done.5.ob
  22.5 0.0 collective-permute-done.2.o
  22.5 0.0 collective-permute-done.3.e
  22.5 1.4 %collective-permute-done.6.ab = f32[22,8,128]{2,1,0:T(8,128)S(1)} collective-permute-done((f32[22,8,128]{2,1,0:T(8,128)}, f32[22,8,128]{2,1,0:T(8,128)S(1)}, u32[]{:S(2)}, u32[]{:S(2)}) %collective-permute-start.6) | collective-permute-done | bytes 90144 | tf_op jit(solution)/shard_map/ppermute | solution.py:66
  23.9 0.6 copy-done.4
  24.6 5.8 %advect.1 = (f32[32,32,128]{2,1,0:T(8,128)}, f32[2,32,128]{2,1,0:T(8,128)}) custom-call(f32[32,32,128]{2,1,0:T(8,128)} %tracer.1, f32[32,32,128]{2,1,0:T(8,128)} %y_speed.1, f32[32,32,128]{2,1,0:T(8,128)} %z_speed.1, f32[11,32,128]{2,1,0:T(8,128)} %copy-done, f32[11,32,128]{2,1,0:T(8,128)} %copy-done.1, f32[11,32,128]{2,1,0:T(8,128)} %copy-done.2, ...), custom_call_target="tpu_custom_call" | custom-call | tf_op jit(solution)/shard_map/advect/pallas_call | solution.py:294
  30.4 0.8 %fusion.43 = (f32[1,32,128]{2,1,0:T(8,128)S(1)}, f32[1,32,128]{2,1,0:T(8,128)S(1)}) fusion(f32[2,32,128]{2,1,0:T(8,128)} %get-tuple-element.36, f32[32,32,128]{2,1,0:T(8,128)} %get-tuple-element.34.inverse), kind=kLoop, calls=%fused_computation.128 | loop fusion | flops 4096 | bytes 81920 | tf_op jit(solution)/shard_map/slice | solution.py:502
  31.1 0.2 collective-permute-start.7
  31.4 1.0 %collective-permute-done.7 = f32[2,32,128]{2,1,0:T(8,128)S(1)} collective-permute-done((f32[2,32,128]{2,1,0:T(8,128)S(1)}, f32[2,32,128]{2,1,0:T(8,128)S(1)}, u32[]{:S(2)}, u32[]{:S(2)}) %collective-permute-start.7) | collective-permute-done | bytes 32800 | tf_op jit(solution)/shard_map/ppermute | solution.py:440
  32.5 1.1 %collective-permute-start.9 = (f32[2,32,128]{2,1,0:T(8,128)S(1)}, f32[2,32,128]{2,1,0:T(8,128)S(1)}, u32[]{:S(2)}, u32[]{:S(2)}) collective-permute-start(f32[2,32,128]{2,1,0:T(8,128)S(1)} %pad_maximum_fusion.3), channel_id=1, source_target_pairs={{0,2},{1,3},{2,0},{3,1},{4,6},{5,7},{6,4},{7,5},{8,10},{9,11},{10,... | collective-permute-start | bytes 98312 | tf_op jit(solution)/shard_map/ppermute | solution.py:440
  33.6 2.2 %backward.2.base = f32[32,32,128]{2,1,0:T(8,128)} custom-call(f32[32,32,128]{2,1,0:T(8,128)} %get-tuple-element.33.forward, f32[32,32,128]{2,1,0:T(8,128)} %get-tuple-element.31.weight_y.weight, f32[32,32,128]{2,1,0:T(8,128)} %get-tuple-element.34.inverse), custom_call_target="tpu_custom_call" | custom-call | tf_op jit(solution)/shard_map/backward/pallas_call | solution.py:385
  35.8 1.0 %collective-permute-start.10 = (f32[5,32,128]{2,1,0:T(8,128)S(1)}, f32[5,32,128]{2,1,0:T(8,128)S(1)}, u32[]{:S(2)}, u32[]{:S(2)}) collective-permute-start(f32[5,32,128]{2,1,0:T(8,128)S(1)} %get-tuple-element.78), channel_id=1, source_target_pairs={{0,2},{1,3},{2,0},{3,1},{4,6},{5,7},{6,4},{7,5},{8,10},{9,11},{10,... | collective-permute-start | bytes 245768 | tf_op jit(solution)/shard_map/ppermute | solution.py:440
  36.8 0.0 collective-permute-done.9
  36.8 3.4 %collective-permute-done.10 = f32[5,32,128]{2,1,0:T(8,128)S(1)} collective-permute-done((f32[5,32,128]{2,1,0:T(8,128)S(1)}, f32[5,32,128]{2,1,0:T(8,128)S(1)}, u32[]{:S(2)}, u32[]{:S(2)}) %collective-permute-start.10) | collective-permute-done | bytes 81952 | tf_op jit(solution)/shard_map/ppermute | solution.py:440
  40.3 0.8 %collective-permute-start.12 = (f32[5,32,128]{2,1,0:T(8,128)S(1)}, f32[5,32,128]{2,1,0:T(8,128)S(1)}, u32[]{:S(2)}, u32[]{:S(2)}) collective-permute-start(f32[5,32,128]{2,1,0:T(8,128)S(1)} %constant_dynamic-update-slice_fusion.5), channel_id=1, source_target_pairs={{0,4},{1,5},{2,6},{3,7},{4,0},{5,1},{6,2},{7,3},{8,12},{9,13},{10,... | collective-permute-start | bytes 245768 | tf_op jit(solution)/shard_map/ppermute | solution.py:440
  41.1 1.3 %collective-permute-start.11 = (f32[2,32,128]{2,1,0:T(8,128)S(1)}, f32[2,32,128]{2,1,0:T(8,128)S(1)}, u32[]{:S(2)}, u32[]{:S(2)}) collective-permute-start(f32[2,32,128]{2,1,0:T(8,128)S(1)} %pad_maximum_fusion), channel_id=1, source_target_pairs={{0,4},{1,5},{2,6},{3,7},{4,0},{5,1},{6,2},{7,3},{8,12},{9,13},{10,... | collective-permute-start | bytes 98312 | tf_op jit(solution)/shard_map/ppermute | solution.py:440
  42.4 2.4 %collective-permute-done.12 = f32[5,32,128]{2,1,0:T(8,128)S(1)} collective-permute-done((f32[5,32,128]{2,1,0:T(8,128)S(1)}, f32[5,32,128]{2,1,0:T(8,128)S(1)}, u32[]{:S(2)}, u32[]{:S(2)}) %collective-permute-start.12) | collective-permute-done | bytes 81952 | tf_op jit(solution)/shard_map/ppermute | solution.py:440
  44.9 0.3 collective-permute-done.11
  45.3 0.6 pad_maximum_fusion.4.currents
  45.9 3.1 %turn.1 = (f32[32,32,128]{2,1,0:T(8,128)}, f32[2,32,128]{2,1,0:T(8,128)}) custom-call(f32[32,32,128]{2,1,0:T(8,128)} %backward.2.base, f32[32,32,128]{2,1,0:T(8,128)} %get-tuple-element.32.first_y, f32[32,32,128]{2,1,0:T(8,128)} %get-tuple-element.35.last_y, f32[2,32,128]{2,1,0:T(8,128)} %pad_maximum_fusion.4.currents, ...), custom_call_target="tpu_custom_call" | custom-call | tf_op jit(solution)/shard_map/turn/pallas_call | solution.py:412
  49.0 0.8 %fusion.42 = (f32[1,32,128]{2,1,0:T(8,128)S(1)}, f32[1,32,128]{2,1,0:T(8,128)S(1)}) fusion(f32[2,32,128]{2,1,0:T(8,128)} %get-tuple-element.43, f32[32,32,128]{2,1,0:T(8,128)} %get-tuple-element.41.inverse), kind=kLoop, calls=%fused_computation.127 | loop fusion | flops 4096 | bytes 81920 | tf_op jit(solution)/shard_map/slice | solution.py:506
  49.8 3.7 %collective-permute-start.13 = (f32[2,32,128]{2,1,0:T(8,128)S(1)}, f32[2,32,128]{2,1,0:T(8,128)S(1)}, u32[]{:S(2)}, u32[]{:S(2)}) collective-permute-start(f32[2,32,128]{2,1,0:T(8,128)S(1)} %pad_maximum_fusion.5), channel_id=1, source_target_pairs={{0,8},{8,0},{16,24},{24,16},{1,9},{9,1},{17,25},{25,17},{2,10},{10... | collective-permute-start | bytes 98312 | tf_op jit(solution)/shard_map/ppermute | solution.py:440
  53.5 2.2 %backward.3.base = f32[32,32,128]{2,1,0:T(8,128)} custom-call(f32[32,32,128]{2,1,0:T(8,128)} %get-tuple-element.40.forward, f32[32,32,128]{2,1,0:T(8,128)} %get-tuple-element.38.weight_z.weight, f32[32,32,128]{2,1,0:T(8,128)} %get-tuple-element.41.inverse), custom_call_target="tpu_custom_call" | custom-call | tf_op jit(solution)/shard_map/backward/pallas_call | solution.py:385
  55.7 0.0 collective-permute-done.13
  55.8 2.8 %collective-permute-start.16 = (f32[5,32,128]{2,1,0:T(8,128)S(1)}, f32[5,32,128]{2,1,0:T(8,128)S(1)}, u32[]{:S(2)}, u32[]{:S(2)}) collective-permute-start(f32[5,32,128]{2,1,0:T(8,128)S(1)} %constant_dynamic-update-slice_fusion.10), channel_id=1, source_target_pairs={{0,16},{8,24},{16,0},{24,8},{1,17},{9,25},{17,1},{25,9},{2,18},{10... | collective-permute-start | bytes 245768 | tf_op jit(solution)/shard_map/ppermute | solution.py:440
  58.6 0.2 collective-permute-start.15
  58.8 2.4 %collective-permute-done.16 = f32[5,32,128]{2,1,0:T(8,128)S(1)} collective-permute-done((f32[5,32,128]{2,1,0:T(8,128)S(1)}, f32[5,32,128]{2,1,0:T(8,128)S(1)}, u32[]{:S(2)}, u32[]{:S(2)}) %collective-permute-start.16) | collective-permute-done | bytes 81952 | tf_op jit(solution)/shard_map/ppermute | solution.py:440
  61.2 2.3 %collective-permute-done.15 = f32[2,32,128]{2,1,0:T(8,128)S(1)} collective-permute-done((f32[2,32,128]{2,1,0:T(8,128)S(1)}, f32[2,32,128]{2,1,0:T(8,128)S(1)}, u32[]{:S(2)}, u32[]{:S(2)}) %collective-permute-start.15) | collective-permute-done | bytes 32800 | tf_op jit(solution)/shard_map/ppermute | solution.py:440
  63.6 0.6 pad_maximum_fusion.6.currents
  64.2 2.2 %finish.1 = f32[32,32,128]{2,1,0:T(8,128)} custom-call(f32[32,32,128]{2,1,0:T(8,128)} %backward.3.base, f32[32,32,128]{2,1,0:T(8,128)} %get-tuple-element.39.first_z.first, f32[32,32,128]{2,1,0:T(8,128)} %get-tuple-element.42.last, f32[2,32,128]{2,1,0:T(8,128)} %pad_maximum_fusion.6.currents), custom_call_target="tpu_custom_call" | custom-call | tf_op jit(solution)/shard_map/finish/pallas_call | solution.py:429
  (52 shorter events, 0.4 us)
Async XLA Ops:
  6.1 8.2 %copy-start.5 = (f32[5,32,128]{2,1,0:T(8,128)S(1)}, f32[5,32,128]{2,1,0:T(8,128)}, u32[]{:S(2)}) copy-start(f32[5,32,128]{2,1,0:T(8,128)} %get-tuple-element.44) | copy-start | bytes 245764
  6.1 8.2 %collective-permute-start.8 = (f32[5,32,128]{2,1,0:T(8,128)}, f32[5,32,128]{2,1,0:T(8,128)S(1)}, u32[]{:S(2)}, u32[]{:S(2)}) collective-permute-start(f32[5,32,128]{2,1,0:T(8,128)} %get-tuple-element.37), channel_id=1, source_target_pairs={{0,1},{1,0},{2,3},{3,2},{4,5},{5,4},{6,7},{7,6},{8,9},{9,8},{10,11... | collective-permute-start | bytes 245768 | tf_op jit(solution)/shard_map/ppermute | solution.py:440
  6.5 10.4 %copy-start.6 = (f32[5,32,128]{2,1,0:T(8,128)S(1)}, f32[5,32,128]{2,1,0:T(8,128)}, u32[]{:S(2)}) copy-start(f32[5,32,128]{2,1,0:T(8,128)} %get-tuple-element.37) | copy-start | bytes 245764
  9.1 8.0 %collective-permute-start = (f32[11,32,128]{2,1,0:T(8,128)}, f32[11,32,128]{2,1,0:T(8,128)S(1)}, u32[]{:S(2)}, u32[]{:S(2)}) collective-permute-start(f32[11,32,128]{2,1,0:T(8,128)} %get-tuple-element.25), channel_id=1, source_target_pairs={{0,8},{1,9},{2,10},{3,11},{4,12},{5,13},{6,14},{7,15},{8,0},{9,1},... | collective-permute-start | bytes 540680 | tf_op jit(solution)/shard_map/ppermute | solution.py:66
  11.7 8.3 %collective-permute-start.1 = (f32[11,32,128]{2,1,0:T(8,128)}, f32[11,32,128]{2,1,0:T(8,128)S(1)}, u32[]{:S(2)}, u32[]{:S(2)}) collective-permute-start(f32[11,32,128]{2,1,0:T(8,128)} %get-tuple-element.26), channel_id=1, source_target_pairs={{0,1},{1,0},{2,3},{3,2},{4,5},{5,4},{6,7},{7,6},{8,16},{9,17},{10,... | collective-permute-start | bytes 540680 | tf_op jit(solution)/shard_map/ppermute | solution.py:66
  11.9 10.5 %collective-permute-start.2 = (f32[11,32,128]{2,1,0:T(8,128)}, f32[11,32,128]{2,1,0:T(8,128)S(1)}, u32[]{:S(2)}, u32[]{:S(2)}) collective-permute-start(f32[11,32,128]{2,1,0:T(8,128)} %get-tuple-element.27), channel_id=1, source_target_pairs={{0,7},{1,2},{2,1},{3,4},{4,3},{5,6},{6,5},{7,0},{8,15},{9,10},{10,... | collective-permute-start | bytes 540680 | tf_op jit(solution)/shard_map/ppermute | solution.py:66
  14.3 8.2 %collective-permute-start.3 = (f32[11,32,128]{2,1,0:T(8,128)}, f32[11,32,128]{2,1,0:T(8,128)S(1)}, u32[]{:S(2)}, u32[]{:S(2)}) collective-permute-start(f32[11,32,128]{2,1,0:T(8,128)} %get-tuple-element.28), channel_id=1, source_target_pairs={{0,1},{1,0},{2,3},{3,2},{4,5},{5,4},{6,7},{7,6},{8,9},{9,8},{10,11... | collective-permute-start | bytes 540680 | tf_op jit(solution)/shard_map/ppermute | solution.py:66
  14.3 2.8 %copy-start.10 = (f32[9,8,128]{2,1,0:T(8,128)S(1)}, f32[9,8,128]{2,1,0:T(8,128)}, u32[]{:S(2)}) copy-start(f32[9,8,128]{2,1,0:T(8,128)} %get-tuple-element.29) | copy-start | bytes 110596
  14.3 5.8 %copy-start.9 = (f32[9,8,128]{2,1,0:T(8,128)S(1)}, f32[9,8,128]{2,1,0:T(8,128)}, u32[]{:S(2)}) copy-start(f32[9,8,128]{2,1,0:T(8,128)} %get-tuple-element.30) | copy-start | bytes 110596
  14.3 8.1 %collective-permute-start.14 = (f32[5,32,128]{2,1,0:T(8,128)S(1)}, f32[5,32,128]{2,1,0:T(8,128)S(1)}, u32[]{:S(2)}, u32[]{:S(2)}) collective-permute-start(f32[5,32,128]{2,1,0:T(8,128)S(1)} %copy-done.5), channel_id=1, source_target_pairs={{0,8},{8,0},{16,24},{24,16},{1,9},{9,1},{17,25},{25,17},{2,10},{10... | collective-permute-start | bytes 245768 | tf_op jit(solution)/shard_map/ppermute | solution.py:440
  17.1 3.0 %copy-start = (f32[11,32,128]{2,1,0:T(8,128)}, f32[11,32,128]{2,1,0:T(8,128)S(1)}, u32[]{:S(2)}) copy-start(f32[11,32,128]{2,1,0:T(8,128)S(1)} %collective-permute-done.a) | copy-start | bytes 540676
  17.2 5.3 %collective-permute-start.4 = (f32[9,8,128]{2,1,0:T(8,128)S(1)}, f32[9,8,128]{2,1,0:T(8,128)S(1)}, u32[]{:S(2)}, u32[]{:S(2)}) collective-permute-start(f32[9,8,128]{2,1,0:T(8,128)S(1)} %copy-done.10), channel_id=1, source_target_pairs={{0,15},{1,10},{2,9},{3,12},{4,11},{5,14},{6,13},{7,8},{8,7},{9,2},... | collective-permute-start | bytes 110600 | tf_op jit(solution)/shard_map/ppermute | solution.py:66
  20.1 0.7 %copy-start.1 = (f32[11,32,128]{2,1,0:T(8,128)}, f32[11,32,128]{2,1,0:T(8,128)S(1)}, u32[]{:S(2)}) copy-start(f32[11,32,128]{2,1,0:T(8,128)S(1)} %collective-permute-done.1.b) | copy-start | bytes 540676
  20.1 2.4 %collective-permute-start.5 = (f32[9,8,128]{2,1,0:T(8,128)S(1)}, f32[9,8,128]{2,1,0:T(8,128)S(1)}, u32[]{:S(2)}, u32[]{:S(2)}) collective-permute-start(f32[9,8,128]{2,1,0:T(8,128)S(1)} %copy-done.9), channel_id=1, source_target_pairs={{0,1},{1,0},{2,3},{3,2},{4,5},{5,4},{6,7},{7,6},{8,23},{9,18},{10,... | collective-permute-start | bytes 110600 | tf_op jit(solution)/shard_map/ppermute | solution.py:66
  22.4 1.5 %collective-permute-start.6 = (f32[22,8,128]{2,1,0:T(8,128)}, f32[22,8,128]{2,1,0:T(8,128)S(1)}, u32[]{:S(2)}, u32[]{:S(2)}) collective-permute-start(f32[22,8,128]{2,1,0:T(8,128)} %rim.1), channel_id=1, source_target_pairs={{0,1},{1,0},{2,3},{3,2},{4,5},{5,4},{6,7},{7,6},{8,9},{9,8},{10,11... | collective-permute-start | bytes 270344 | tf_op jit(solution)/shard_map/ppermute | solution.py:66
  22.5 1.5 %copy-start.7 = (f32[9,8,128]{2,1,0:T(8,128)}, f32[9,8,128]{2,1,0:T(8,128)S(1)}, u32[]{:S(2)}) copy-start(f32[9,8,128]{2,1,0:T(8,128)S(1)} %collective-permute-done.4.oa) | copy-start | bytes 110596
  22.5 1.5 %copy-start.8 = (f32[9,8,128]{2,1,0:T(8,128)}, f32[9,8,128]{2,1,0:T(8,128)S(1)}, u32[]{:S(2)}) copy-start(f32[9,8,128]{2,1,0:T(8,128)S(1)} %collective-permute-done.5.ob) | copy-start | bytes 110596
  22.5 1.4 %copy-start.2 = (f32[11,32,128]{2,1,0:T(8,128)}, f32[11,32,128]{2,1,0:T(8,128)S(1)}, u32[]{:S(2)}) copy-start(f32[11,32,128]{2,1,0:T(8,128)S(1)} %collective-permute-done.2.o) | copy-start | bytes 540676
  22.5 1.4 %copy-start.3 = (f32[11,32,128]{2,1,0:T(8,128)}, f32[11,32,128]{2,1,0:T(8,128)S(1)}, u32[]{:S(2)}) copy-start(f32[11,32,128]{2,1,0:T(8,128)S(1)} %collective-permute-done.3.e) | copy-start | bytes 540676
  23.9 0.6 copy-start.4
  31.1 1.3 %collective-permute-start.7 = (f32[2,32,128]{2,1,0:T(8,128)S(1)}, f32[2,32,128]{2,1,0:T(8,128)S(1)}, u32[]{:S(2)}, u32[]{:S(2)}) collective-permute-start(f32[2,32,128]{2,1,0:T(8,128)S(1)} %pad_maximum_fusion.2), channel_id=1, source_target_pairs={{0,1},{1,0},{2,3},{3,2},{4,5},{5,4},{6,7},{7,6},{8,9},{9,8},{10,11... | collective-permute-start | bytes 98312 | tf_op jit(solution)/shard_map/ppermute | solution.py:440
  32.5 4.3 %collective-permute-start.9 = (f32[2,32,128]{2,1,0:T(8,128)S(1)}, f32[2,32,128]{2,1,0:T(8,128)S(1)}, u32[]{:S(2)}, u32[]{:S(2)}) collective-permute-start(f32[2,32,128]{2,1,0:T(8,128)S(1)} %pad_maximum_fusion.3), channel_id=1, source_target_pairs={{0,2},{1,3},{2,0},{3,1},{4,6},{5,7},{6,4},{7,5},{8,10},{9,11},{10,... | collective-permute-start | bytes 98312 | tf_op jit(solution)/shard_map/ppermute | solution.py:440
  35.8 4.4 %collective-permute-start.10 = (f32[5,32,128]{2,1,0:T(8,128)S(1)}, f32[5,32,128]{2,1,0:T(8,128)S(1)}, u32[]{:S(2)}, u32[]{:S(2)}) collective-permute-start(f32[5,32,128]{2,1,0:T(8,128)S(1)} %get-tuple-element.78), channel_id=1, source_target_pairs={{0,2},{1,3},{2,0},{3,1},{4,6},{5,7},{6,4},{7,5},{8,10},{9,11},{10,... | collective-permute-start | bytes 245768 | tf_op jit(solution)/shard_map/ppermute | solution.py:440
  40.3 4.5 %collective-permute-start.12 = (f32[5,32,128]{2,1,0:T(8,128)S(1)}, f32[5,32,128]{2,1,0:T(8,128)S(1)}, u32[]{:S(2)}, u32[]{:S(2)}) collective-permute-start(f32[5,32,128]{2,1,0:T(8,128)S(1)} %constant_dynamic-update-slice_fusion.5), channel_id=1, source_target_pairs={{0,4},{1,5},{2,6},{3,7},{4,0},{5,1},{6,2},{7,3},{8,12},{9,13},{10,... | collective-permute-start | bytes 245768 | tf_op jit(solution)/shard_map/ppermute | solution.py:440
  41.1 4.1 %collective-permute-start.11 = (f32[2,32,128]{2,1,0:T(8,128)S(1)}, f32[2,32,128]{2,1,0:T(8,128)S(1)}, u32[]{:S(2)}, u32[]{:S(2)}) collective-permute-start(f32[2,32,128]{2,1,0:T(8,128)S(1)} %pad_maximum_fusion), channel_id=1, source_target_pairs={{0,4},{1,5},{2,6},{3,7},{4,0},{5,1},{6,2},{7,3},{8,12},{9,13},{10,... | collective-permute-start | bytes 98312 | tf_op jit(solution)/shard_map/ppermute | solution.py:440
  49.8 5.9 %collective-permute-start.13 = (f32[2,32,128]{2,1,0:T(8,128)S(1)}, f32[2,32,128]{2,1,0:T(8,128)S(1)}, u32[]{:S(2)}, u32[]{:S(2)}) collective-permute-start(f32[2,32,128]{2,1,0:T(8,128)S(1)} %pad_maximum_fusion.5), channel_id=1, source_target_pairs={{0,8},{8,0},{16,24},{24,16},{1,9},{9,1},{17,25},{25,17},{2,10},{10... | collective-permute-start | bytes 98312 | tf_op jit(solution)/shard_map/ppermute | solution.py:440
  55.8 5.4 %collective-permute-start.16 = (f32[5,32,128]{2,1,0:T(8,128)S(1)}, f32[5,32,128]{2,1,0:T(8,128)S(1)}, u32[]{:S(2)}, u32[]{:S(2)}) collective-permute-start(f32[5,32,128]{2,1,0:T(8,128)S(1)} %constant_dynamic-update-slice_fusion.10), channel_id=1, source_target_pairs={{0,16},{8,24},{16,0},{24,8},{1,17},{9,25},{17,1},{25,9},{2,18},{10... | collective-permute-start | bytes 245768 | tf_op jit(solution)/shard_map/ppermute | solution.py:440
  58.6 4.9 %collective-permute-start.15 = (f32[2,32,128]{2,1,0:T(8,128)S(1)}, f32[2,32,128]{2,1,0:T(8,128)S(1)}, u32[]{:S(2)}, u32[]{:S(2)}) collective-permute-start(f32[2,32,128]{2,1,0:T(8,128)S(1)} %pad_maximum_fusion.1), channel_id=1, source_target_pairs={{0,16},{8,24},{16,0},{24,8},{1,17},{9,25},{17,1},{25,9},{2,18},{10... | collective-permute-start | bytes 98312 | tf_op jit(solution)/shard_map/ppermute | solution.py:440

commit v2 on v0

v2 whole, which is shorter than its diff:
```python
import jax
import jax.numpy as jnp
from jax import lax
from jax.experimental import pallas as pl
from jax.experimental.pallas import tpu as pltpu
from jax.sharding import PartitionSpec as P

NSUB = 4
RATE = 500.0
AXES = ("gz", "gy")
F32 = jnp.float32
VMEM_BYTES = 12 << 20


def near(*dims):
    return pltpu.VMEM(dims, F32)


def far(*dims):
    return pltpu.HBM(dims, F32)


def call(kernel, name, outs, operands, scratch=(), cycles=0):
    whole, away = pl.BlockSpec(memory_space=pltpu.VMEM), pl.BlockSpec(memory_space=pltpu.HBM)
    inputs, in_specs = [], []
    for operand in operands:
        where, x = operand if isinstance(operand, tuple) else ("near", operand)
        x = pltpu.with_memory_space_constraint(x, pltpu.VMEM if where == "near" else pltpu.HBM)
        inputs.append(x)
        in_specs.append(away if where == "far" else whole)
    out_specs = [away if isinstance(out, tuple) else whole for out in outs]
    result = pl.pallas_call(
        kernel,
        out_shape=[out[1] if isinstance(out, tuple) else out for out in outs],
        in_specs=in_specs,
        out_specs=out_specs,
        scratch_shapes=scratch,
        compiler_params=pltpu.CompilerParams(vmem_limit_bytes=VMEM_BYTES),
        cost_estimate=pl.CostEstimate(flops=0, bytes_accessed=cycles * 1024, transcendentals=0) if cycles else None,
        name=name,
    )(*inputs)
    return result if len(outs) > 1 else result[0]


def place():
    return (
        lax.axis_index("gz"),
        lax.axis_index("gy"),
        lax.axis_size("gz"),
        lax.axis_size("gy"),
    )


def pair_up(index):
    return index ^ 1


def same(index):
    return index


def z_other(index):
    return index + 1 if index % 2 else index - 1


def y_other(index):
    return (index + 1 if index % 2 else index - 1) % lax.axis_size("gy")


def permutation(z_partner, y_partner):
    z_count, y_count = lax.axis_size("gz"), lax.axis_size("gy")
    pairs = []
    for z in range(z_count):
        for y in range(y_count):
            to_z, to_y = z_partner(z), y_partner(y)
            if not 0 <= to_z < z_count:
                to_z, to_y = z, pair_up(y)
            pairs.append((z * y_count + y, to_z * y_count + to_y))
    return pairs


def send(x, z_partner=same, y_partner=same):
    return lax.ppermute(x, AXES, permutation(z_partner, y_partner))


def swap(x, axis, level):
    step = 1 << level
    if axis == "gy":
        step |= 1
    return lax.ppermute(x, axis, [(i, i ^ step) for i in range(lax.axis_size(axis))])


def levels_of(axis):
    return (lax.axis_size(axis) - 1).bit_length()


def rim_kernel(a, b, oa, ob, out):
    _, y, _, _ = place()
    width = a.shape[1]
    start = pl.multiple_of((1 - lax.rem(y, 2)) * (width - 8), 8)
    for half, ref in enumerate((a, b)):
        for k in range(11):
            out[11 * half + k] = ref[k, pl.ds(start, 8), :]


def rim(a, b, oa, ob):
    return call(rim_kernel, "rim", [near(22, 8, a.shape[2])], [a, b, oa, ob], cycles=200)


def reciprocal(x):
    r = pl.reciprocal(x, approx=True)
    return r * (2.0 - x * r)


def factor(sides):
    state = []
    for read, count, r, phi, psi, ports, edge_low, edge_high in sides:
        first = read(0)
        before = first
        for j in range(1, count):
            here = read(j)
            r[j] = reciprocal((0.5 * RATE) * (before + here))
            before = here
        ports[3] = first
        ports[4] = before
        one = jnp.ones_like(first)
        phi[0] = one
        psi[count - 1] = one
        state.append([one, 1.0 + edge_low * first, one, 1.0 + edge_high * before])
    for j in range(1, max(side[1] for side in sides)):
        for (_, count, r, phi, psi, _, _, _), s in zip(sides, state):
            if j < count:
                s[0] = s[0] + r[j] * s[1]
                s[1] = s[1] + s[0]
                phi[j] = s[0]
                s[2] = s[2] + r[count - j] * s[3]
                s[3] = s[3] + s[2]
                psi[count - 1 - j] = s[2]
    for (_, _, _, _, _, ports, _, edge_high), s in zip(sides, state):
        inverse = reciprocal(s[1] + edge_high * ports[4] * s[0])
        ports[0] = s[2] * inverse
        ports[1] = inverse
        ports[2] = s[0] * inverse


def begin_kernel(
    tracer, y_speed, z_speed, kappa_far, a_ref, b_ref, o_ref, e_ref, oa_ref, ob_ref,
    phi_y_far, psi_y_far, phi_z_far, psi_z_far,
    c, ys, zs, kappa, r_y, r_z, phi_y, psi_y, phi_z, psi_z, sem,
):
    arrivals = [
        pltpu.make_async_copy(source, target, sem.at[k])
        for k, (source, target) in enumerate(((kappa_far, kappa), (tracer, c), (y_speed, ys), (z_speed, zs)))
    ]
    for copy in arrivals:
        copy.start()
    z, y, z_count, y_count = place()
    depth, width, _ = c.shape

    def flag(condition):
        return jnp.where(condition, RATE, 0.0)

    arrivals[0].wait()
    factor((
        (lambda j: kappa[:, j, :], width, r_y, phi_y, psi_y, e_ref.at[11:16], flag(y == 0), flag(y == y_count - 1)),
        (lambda j: kappa[j], depth, r_z, phi_z, psi_z, a_ref.at[11:16], flag(z == 0), flag(z == z_count - 1)),
    ))
    results = [
        pltpu.make_async_copy(source, target, sem.at[4 + k])
        for k, (source, target) in enumerate(
            ((phi_y, phi_y_far), (psi_y, psi_y_far), (phi_z, phi_z_far), (psi_z, psi_z_far))
        )
    ]
    for copy in results:
        copy.start()
    for copy in arrivals[1:]:
        copy.wait()

    z_odd, y_odd = lax.rem(z, 2), lax.rem(y, 2)
    for ref, low in ((a_ref, z_odd), (b_ref, 1 - z_odd)):
        four, three = (1 - low) * (depth - 4), (1 - low) * (depth - 3)
        ref[0:4] = c[pl.ds(four, 4)]
        ref[4:8] = zs[pl.ds(four, 4)]
        ref[8:11] = ys[pl.ds(three, 3)]

    def rims(o_start, e_start):
        for ref, start in ((o_ref, o_start), (e_ref, e_start)):
            high = int(start > 0)
            for k in range(4):
                ref[k] = c[:, start + k, :]
                ref[4 + k] = ys[:, start + k, :]
            for k in range(3):
                ref[8 + k] = zs[:, start + high + k, :]
        high = int(o_start > 0)
        oa_start = pl.multiple_of((1 - z_odd) * (depth - 8), 8)
        ob_start = pl.multiple_of(z_odd * (depth - 8), 8)
        for f, field in enumerate((c, ys, zs)):
            for k in range(3):
                oa_ref[3 * f + k] = field[pl.ds(oa_start, 8), o_start + high + k, :]
                ob_ref[3 * f + k] = field[pl.ds(ob_start, 8), o_start + high + k, :]

    @pl.when(y_odd == 0)
    def _():
        rims(0, width - 4)

    @pl.when(y_odd == 1)
    def _():
        rims(width - 4, 0)

    for copy in results:
        copy.wait()


def begin(tracer, y_speed, z_speed, kappa):
    depth, width, band = tracer.shape
    along_y, along_z = (width, depth, band), (depth, width, band)
    return call(
        begin_kernel,
        "begin",
        [near(16, width, band), near(11, width, band), near(11, depth, band), near(16, depth, band)]
        + [near(9, 8, band)] * 2
        + [("far", far(*along_y))] * 2
        + [("far", far(*along_z))] * 2,
        [("far", x) for x in (tracer, y_speed, z_speed, kappa)],
        scratch=[near(*along_z)] * 4 + [near(*along_y), near(*along_z)] + [near(*along_y)] * 2
        + [near(*along_z)] * 2 + [pltpu.SemaphoreType.DMA((8,))],
        cycles=4000,
    )


def ports_kernel(axis, level, first_row, mine, theirs, out, joint):
    is_left = (lax.shift_right_logical(lax.axis_index(axis), level) & 1) == 0
    pairs = [(mine[first_row + k], theirs[first_row + k]) for k in range(5)]
    left = [jnp.where(is_left, m, t) for m, t in pairs]
    right = [jnp.where(is_left, t, m) for m, t in pairs]
    d = reciprocal(reciprocal((0.5 * RATE) * (left[4] + right[3])) + left[2] + right[0])
    out[0] = left[0] - left[1] * left[1] * d
    out[1] = left[1] * right[1] * d
    out[2] = right[2] - right[1] * right[1] * d
    out[3] = left[3]
    out[4] = right[4]
    joint[0] = d
    joint[1] = left[1]
    joint[2] = right[1]


def join_ports(mine, theirs, axis, level, first_row=0):
    _, lines, band = mine.shape

    def kernel(*refs):
        ports_kernel(axis, level, first_row, *refs)

    return call(kernel, "join_ports", [near(5, lines, band), near(3, lines, band)], [mine, theirs], cycles=100)


def join_levels(mine, theirs, axis):
    ports, joint = join_ports(mine, theirs, axis, 0, first_row=11)
    joints = [joint]
    for level in range(1, levels_of(axis) - 1):
        ports, joint = join_ports(ports, swap(ports, axis, level), axis, level)
        joints.append(joint)
    return ports, joints


def source_kernel(axis, level, last, mine, theirs, joint, ports, out, flow_ref):
    index = lax.axis_index(axis)
    is_left = (lax.shift_right_logical(index, level) & 1) == 0
    pairs = [(mine[k], theirs[k]) for k in range(2)]
    left = [jnp.where(is_left, m, t) for m, t in pairs]
    right = [jnp.where(is_left, t, m) for m, t in pairs]
    flow = (left[1] - right[0]) * joint[0]
    flow_ref[0] = flow
    low, high = left[0] - joint[1] * flow, right[1] + joint[2] * flow
    if not last:
        out[0] = low
        out[1] = high
        return
    next_left = (lax.shift_right_logical(index, level + 1) & 1) == 0
    out[0] = jnp.where(next_left, high, low)
    out[1] = jnp.where(next_left, ports[2], ports[0])
    out[2] = jnp.where(next_left, ports[4], ports[3])


def join_sources(mine, theirs, joint, ports, axis, level):
    _, lines, band = mine.shape
    last = level + 2 == levels_of(axis)

    def kernel(*refs):
        source_kernel(axis, level, last, *refs)

    outs = [near(3 if last else 2, lines, band), near(1, lines, band)]
    return call(kernel, "join_sources", outs, [mine, theirs, joint, ports], cycles=100)


def end_currents(axis, mine, theirs, joints, flows):
    index = lax.axis_index(axis)
    level = len(joints)
    is_left = (lax.shift_right_logical(index, level) & 1) == 0
    d = reciprocal(reciprocal((0.5 * RATE) * (mine[2] + theirs[2])) + mine[1] + theirs[1])
    flow = (mine[0] - theirs[0]) * d
    zero = jnp.zeros_like(flow)
    low, high = jnp.where(is_left, zero, -flow), jnp.where(is_left, -flow, zero)
    for level in range(level - 1, -1, -1):
        joint = joints[level]
        is_left = (lax.shift_right_logical(index, level) & 1) == 0
        flow = flows[level][0] + (joint[1] * low - joint[2] * high) * joint[0]
        low, high = jnp.where(is_left, low, flow), jnp.where(is_left, -flow, high)
    return low, high


def solve_open(read, phi, psi, scale, base, ports, kept):
    count = base.shape[0]
    total = jnp.zeros(base.shape[1:], F32)
    for j in range(count):
        value = scale * read(j)
        kept[j] = value
        total = total + phi[j] * value
        base[j] = psi[j] * total
    ports[1] = total
    total = jnp.zeros(base.shape[1:], F32)
    for j in range(count - 1, -1, -1):
        base[j] = base[j] + phi[j] * total
        total = total + psi[j] * kept[j]
    ports[0] = total


def advect_kernel(
    tracer, y_speed, z_speed, a, b, o, e, oa, ob, ab, e_mine, phi_far, psi_far,
    base, sources, phi, psi, c, ys, zs, sy, sz, kept, sem,
):
    z, y, z_count, y_count = place()
    depth, width, band = tracer.shape
    rows, cols = depth + 8, width + 8
    copies = [
        pltpu.make_async_copy(own, field.at[pl.ds(4, depth), pl.ds(0, width), :], sem.at[k])
        for k, (field, own) in enumerate(((c, tracer), (ys, y_speed), (zs, z_speed)))
    ]
    copies += [
        pltpu.make_async_copy(phi_far, phi, sem.at[3]),
        pltpu.make_async_copy(psi_far, psi, sem.at[4]),
    ]
    for copy in copies:
        copy.start()
    z_odd, y_odd = lax.rem(z, 2), lax.rem(y, 2)
    keep_b = jnp.where((z_odd == 0) & (z == 0) | (z_odd == 1) & (z == z_count - 1), 0.0, 1.0)
    keep_o = jnp.where((y_odd == 0) & (y == 0) | (y_odd == 1) & (y == y_count - 1), 0.0, 1.0)
    column = lax.broadcasted_iota(jnp.int32, (8, band), 0)
    outside = (column < 4) & (y == y_count - 1) | (column >= 4) & (y == 0)
    inside = jnp.where(outside, 0.0, 1.0)

    for field in (c, ys, zs):
        field[0:4, width:cols, :] = jnp.zeros((4, 8, band), F32)
        field[4 + depth : rows, width:cols, :] = jnp.zeros((4, 8, band), F32)
    ys[0:1, 0:width, :] = jnp.zeros((1, width, band), F32)
    ys[rows - 1 : rows, 0:width, :] = jnp.zeros((1, width, band), F32)
    for ref, low, keep in ((a, z_odd, None), (b, 1 - z_odd, keep_b)):
        scale = (lambda v: v) if keep is None else (lambda v: v * keep)
        four = jnp.where(low == 1, 0, depth + 4)
        three = jnp.where(low == 1, 1, depth + 4)
        c[pl.ds(four, 4), 0:width, :] = scale(ref[0:4])
        zs[pl.ds(four, 4), 0:width, :] = scale(ref[4:8])
        ys[pl.ds(three, 3), 0:width, :] = scale(ref[8:11])

    def sides(o_low):
        def columns(ref, low, scale):
            start = width + 4 * int(low)
            shift = int(low)
            for k in range(4):
                c[4 : 4 + depth, start + k, :] = scale(ref[k])
                ys[4 : 4 + depth, start + k, :] = scale(ref[4 + k])
            for k in range(3):
                zs[4 : 4 + depth, start + shift + k, :] = scale(ref[8 + k])
            far_column = start if low else start + 3
            zs[4 : 4 + depth, far_column, :] = jnp.zeros((depth, band), F32)

        columns(o, o_low, lambda v: v * keep_o)
        columns(e, not o_low, lambda v: v)

        def from_pair(half, z_low):
            start = width if o_low else width + 4
            block = slice(0, 4) if o_low else slice(4, 8)
            zr = 0 if z_low else depth + 4
            z3 = 1 if z_low else depth + 4
            keep = 1.0 if half == 0 else keep_b
            c[zr : zr + 4, start : start + 4, :] = ab[11 * half : 11 * half + 4, block, :] * keep
            zs[zr : zr + 4, start : start + 4, :] = ab[11 * half + 4 : 11 * half + 8, block, :] * keep
            ys[z3 : z3 + 3, start : start + 4, :] = ab[11 * half + 8 : 11 * half + 11, block, :] * keep

        def from_corner(ref, z_low, keep):
            start = width + (5 if o_low else 0)
            zr = 1 if z_low else depth + 4
            src = 5 if z_low else 0
            for f, field in enumerate((c, ys, zs)):
                for k in range(3):
                    field[zr : zr + 3, start + k, :] = ref[3 * f + k, src : src + 3, :] * keep

        @pl.when(z_odd == 0)
        def _():
            from_pair(0, False)
            from_pair(1, True)
            from_corner(oa, False, keep_o)
            from_corner(ob, True, keep_o * keep_b)

        @pl.when(z_odd == 1)
        def _():
            from_pair(0, True)
            from_pair(1, False)
            from_corner(oa, True, keep_o)
            from_corner(ob, False, keep_o * keep_b)

    @pl.when(y_odd == 0)
    def _():
        sides(True)

    @pl.when(y_odd == 1)
    def _():
        sides(False)

    for copy in copies[:3]:
        copy.wait()

    def up(v):
        return pltpu.roll(v, cols - 1, 0)

    def down(v):
        return pltpu.roll(v, 1, 0)

    def flux(speed, here, after):
        return speed * jnp.where(speed > 0.0, here, after)

    def faces(r, before):
        v = ys[r]
        sy[r] = 0.5 * (v + up(v))
        after = zs[r + 1]
        sz[r] = 0.5 * (before + after)
        return after

    lax.fori_loop(0, rows - 1, faces, zs[0], unroll=3)

    keep_low = jnp.where(z == 0, 0.0, 1.0)
    keep_high = jnp.where(z == z_count - 1, 0.0, 1.0)
    for step in range(1, NSUB + 1):
        here = c[step]

        def row(r, carry):
            here, below = carry
            after = c[r + 1]
            above = flux(sz[r], here, after)
            across = flux(sy[r], here, up(here))
            new = here - (across - down(across)) - (above - below)
            c[r, 0:width, :] = new[0:width]
            c[r, width:cols, :] = new[width:cols] * inside
            return after, above

        lax.fori_loop(step, rows - step, row, (here, flux(sz[step - 1], c[step - 1], here)), unroll=4)
        if step < NSUB:
            c[3] = c[3] * keep_low
            c[4 + depth] = c[4 + depth] * keep_high

    for copy in copies[3:]:
        copy.wait()
    solve_open(lambda j: c[4 : 4 + depth, j, :], phi, psi, e_mine[12], base, sources, kept)


def advect(tracer, y_speed, z_speed, halos, e_mine, phi, psi):
    depth, width, band = tracer.shape
    padded = near(depth + 8, width + 8, band)
    along_y = near(width, depth, band)
    return call(
        advect_kernel,
        "advect",
        [along_y, near(2, depth, band), along_y, along_y],
        [("far", x) for x in (tracer, y_speed, z_speed)]
        + list(halos)
        + [e_mine, ("far", phi), ("far", psi)],
        scratch=[padded] * 5 + [along_y, pltpu.SemaphoreType.DMA((5,))],
        cycles=5000,
    )


def turn_kernel(levels, *refs):
    mine, theirs = refs[0:2]
    joints, flows = refs[2 : 2 + levels], refs[2 + levels : 2 + 2 * levels]
    (
        ports_y, base_y, phi_y, psi_y, ports_z, phi_far, psi_far,
        base, sources, phi, psi, u, kept, sem,
    ) = refs[2 + 2 * levels :]
    copies = [
        pltpu.make_async_copy(phi_far, phi, sem.at[0]),
        pltpu.make_async_copy(psi_far, psi, sem.at[1]),
    ]
    for copy in copies:
        copy.start()
    low, high = end_currents("gy", mine, theirs, joints, flows)
    scale = ports_y[12]
    low, high = low * scale, high * scale
    for j in range(base_y.shape[0]):
        u[:, j, :] = base_y[j] + low * psi_y[j] + high * phi_y[j]
    for copy in copies:
        copy.wait()
    solve_open(lambda k: u[k], phi, psi, ports_z[12], base, sources, kept)


def turn(mine, theirs, joints, flows, ports_y, base_y, phi_y, psi_y, ports_z, phi_z, psi_z):
    width, depth, band = base_y.shape
    along_z = near(depth, width, band)

    def kernel(*refs):
        turn_kernel(len(joints), *refs)

    return call(
        kernel,
        "turn",
        [along_z, near(2, width, band), along_z, along_z],
        [mine, theirs, *joints, *flows, ports_y, base_y, phi_y, psi_y, ports_z]
        + [("far", phi_z), ("far", psi_z)],
        scratch=[along_z, along_z, pltpu.SemaphoreType.DMA((2,))],
        cycles=1500,
    )


def finish_kernel(levels, *refs):
    mine, theirs = refs[0:2]
    joints, flows = refs[2 : 2 + levels], refs[2 + levels : 2 + 2 * levels]
    ports_z, base, phi, psi, out, u, sem = refs[2 + 2 * levels :]
    low, high = end_currents("gz", mine, theirs, joints, flows)
    scale = ports_z[12]
    low, high = low * scale, high * scale
    depth = base.shape[0]
    part = depth // 4
    copies = []
    for p in range(4):
        for k in range(p * part, (p + 1) * part):
            u[k] = base[k] + low * psi[k] + high * phi[k]
        block = pl.ds(p * part, part)
        copies.append(pltpu.make_async_copy(u.at[block], out.at[block], sem.at[p]))
        copies[-1].start()
    for copy in copies:
        copy.wait()


def finish(mine, theirs, joints, flows, ports_z, base, phi, psi):
    def kernel(*refs):
        finish_kernel(len(joints), *refs)

    return call(
        kernel,
        "finish",
        [("far", jax.ShapeDtypeStruct(base.shape, F32))],
        [mine, theirs, *joints, *flows, ports_z, base, phi, psi],
        scratch=[near(*base.shape), pltpu.SemaphoreType.DMA((4,))],
        cycles=1000,
    )


def exchange_sources(sources, ports, joints, axis):
    flows = []
    for level, joint in enumerate(joints):
        theirs = swap(sources, axis, level)
        sources, flow = join_sources(sources, theirs, joint, ports, axis, level)
        flows.append(flow)
    return sources, swap(sources, axis, len(joints)), flows


def local(tracer, y_speed, z_speed, kappa):
    a_mine, b, o, e_mine, oa, ob, phi_y, psi_y, phi_z, psi_z = begin(tracer, y_speed, z_speed, kappa)
    a = send(a_mine, z_partner=pair_up)
    b = send(b, z_partner=z_other)
    o = send(o, y_partner=y_other)
    oa = send(oa, z_partner=pair_up, y_partner=y_other)
    ob = send(ob, z_partner=z_other, y_partner=y_other)
    e = swap(e_mine, "gy", 0)
    ab = send(rim(a, b, oa, ob), y_partner=pair_up)

    ports_y, joints_y = join_levels(e_mine, e, "gy")
    ports_z, joints_z = join_levels(a_mine, a, "gz")

    base, sources, phi_y, psi_y = advect(
        tracer, y_speed, z_speed, (a, b, o, e, oa, ob, ab), e_mine, phi_y, psi_y
    )
    mine, theirs, flows = exchange_sources(sources, ports_y, joints_y, "gy")
    base, sources, phi_z, psi_z = turn(
        mine, theirs, joints_y, flows, e_mine, base, phi_y, psi_y, a_mine, phi_z, psi_z
    )
    mine, theirs, flows = exchange_sources(sources, ports_z, joints_z, "gz")
    return finish(mine, theirs, joints_z, flows, a_mine, base, phi_z, psi_z)


def solution(mesh):
    spec = P("gz", "gy", None)
    return jax.shard_map(
        local, mesh=mesh, in_specs=(spec,) * 4, out_specs=spec, check_vma=False
    )
```

time: 161 us -> 46.3 us (0.29)
  starting transfers between devices: 63.7 us -> 21.3 us
  waiting for transfers between devices: 45.9 us -> 14.6 us
  other arithmetic: 21.7 us -> 0 us
  blocking collectives: 13.8 us -> 0 us
  local copies, waits for them, and re-layouts: 13.3 us -> 0 us
  Pallas kernels: 0 us -> 10.2 us
    ppermute x21 -> x13, starting transfers between devices: 45.5 us -> 21.3 us  [the longest x7 12.6 us: swap(): lax.ppermute(x, axis, [(i, i ^ step) for i in range(lax.axis_size(axis))])]
    all_to_all x3 -> x0, starting transfers between devices: 18.2 us -> none  [the longest x1 7.67 us: local(): lax.all_to_all(kappa, 'gy', split_axis=0, concat_axis=1, tiled=True)]
    all_to_all x3 -> x0, waiting for transfers between devices: 17.7 us -> none  [the longest x1 9.2 us: solve_rows(): return lax.all_to_all(solved, 'gy', split_axis=1, concat_axis=0, tiled=True)]
    all_gather x1 -> x0, blocking collectives: 13.8 us -> none  [local(): collected = lax.all_gather(equations[None], 'gz', axis=0, tiled=True)]
    ppermute x21 -> x13, waiting for transfers between devices: 28.2 us -> 14.6 us  [the longest x7 10.5 us: swap(): lax.ppermute(x, axis, [(i, i ^ step) for i in range(lax.axis_size(axis))])]
    add x32 -> x0, other arithmetic: 10.7 us -> none  [the longest x12 6.36 us: reduce_lines(): right + factor_low * move_down(right, offset, axis, 0.0)]
    pallas_call x0 -> x11, Pallas kernels: none -> 10.2 us  [call(): pl.pallas_call(kernel, out_shape=[out[1] if isinstance(out, tuple) else o...]
    slice x80 -> x0, local copies, waits for them, and re-layouts: 7.97 us -> none  [the longest x36 3.23 us: move_down(): kept = lax.slice_in_dim(values, 0, count - offset, axis=axis)]
  transfers between devices with their start and end apart: 24 -> 13, of which waited for: 11 -> 7; matrix products, arithmetic and copies ran while one was open for 7% -> 0% of each run, Pallas kernels for 0% -> 8%
where the time goes in v2:
time: 46.3 us; the launch traced here: 46.2 us
  starting transfers between devices  21.3 us (46%)
  waiting for transfers between devices  14.6 us (32%)
  Pallas kernels  10.2 us (22%)
    ppermute x7, starting transfers between devices, swap(): lax.ppermute(x, axis, [(i, i ^ step) for i in range(lax.axis_size(axis))])  12.6 us
    ppermute x7, waiting for transfers between devices, swap(): lax.ppermute(x, axis, [(i, i ^ step) for i in range(lax.axis_size(axis))])  10.5 us
    pallas_call x11, Pallas kernels, call(): pl.pallas_call(kernel, out_shape=[out[1] if isinstance(out, tuple) else o...  10.2 us
    ppermute x6, starting transfers between devices, send(): return lax.ppermute(x, AXES, permutation(z_partner, y_partner))  8.65 us
    ppermute x6, waiting for transfers between devices, send(): return lax.ppermute(x, AXES, permutation(z_partner, y_partner))  4.11 us
  transfers between devices with their start and end apart: 13, of which 7 were waited for; matrix products, arithmetic and copies ran while one was open for 0% of the time, Pallas kernels for 8%

profile of v2, /device:TPU:0, one launch (start us, length us, event | category | flops | bytes accessed | tf_op | source)
XLA Modules:
  0.0 46.2 jit_solution(16279657636979087513)
XLA Ops:
  0.0 4.2 %begin.1 = (f32[16,32,128]{2,1,0:T(8,128)S(1)}, f32[11,32,128]{2,1,0:T(8,128)S(1)}, f32[11,32,128]{2,1,0:T(8,128)S(1)}, f32[16,32,128]{2,1,0:T(8,128)S(1)}, f32[...) custom-call(f32[32,32,128]{2,1,0:T(8,128)} %tracer.3, ...), custom_call_target="tpu_custom_call" | custom-call | bytes 4096000 | tf_op jit(solution)/shard_map/begin/pallas_call | solution.py:32
  4.2 3.1 %collective-permute-start = (f32[16,32,128]{2,1,0:T(8,128)S(1)}, f32[16,32,128]{2,1,0:T(8,128)S(1)}, u32[]{:S(2)}, u32[]{:S(2)}) collective-permute-start(f32[16,32,128]{2,1,0:T(8,128)S(1)} %get-tuple-element.35.refs_10_.refs_0_.refs_4_), channel_id=1, source_target_pairs={{0,8},{1,9},{2,10},{3,11},{4,12},{5,13},{6,14},{7,15},{8,0},{9,1},... | collective-permute-start | bytes 786440 | tf_op jit(solution)/shard_map/ppermute | solution.py:83
  7.3 0.0 collective-permute-start.3
  7.3 0.5 %collective-permute-start.1 = (f32[11,32,128]{2,1,0:T(8,128)S(1)}, f32[11,32,128]{2,1,0:T(8,128)S(1)}, u32[]{:S(2)}, u32[]{:S(2)}) collective-permute-start(f32[11,32,128]{2,1,0:T(8,128)S(1)} %get-tuple-element.36), channel_id=1, source_target_pairs={{0,1},{1,0},{2,3},{3,2},{4,5},{5,4},{6,7},{7,6},{8,16},{9,17},{10,... | collective-permute-start | bytes 540680 | tf_op jit(solution)/shard_map/ppermute | solution.py:83
  7.8 2.1 %collective-permute-start.2 = (f32[11,32,128]{2,1,0:T(8,128)S(1)}, f32[11,32,128]{2,1,0:T(8,128)S(1)}, u32[]{:S(2)}, u32[]{:S(2)}) collective-permute-start(f32[11,32,128]{2,1,0:T(8,128)S(1)} %get-tuple-element.37), channel_id=1, source_target_pairs={{0,7},{1,2},{2,1},{3,4},{4,3},{5,6},{6,5},{7,0},{8,15},{9,10},{10,... | collective-permute-start | bytes 540680 | tf_op jit(solution)/shard_map/ppermute | solution.py:83
  9.9 2.7 %collective-permute-start.4 = (f32[9,8,128]{2,1,0:T(8,128)S(1)}, f32[9,8,128]{2,1,0:T(8,128)S(1)}, u32[]{:S(2)}, u32[]{:S(2)}) collective-permute-start(f32[9,8,128]{2,1,0:T(8,128)S(1)} %get-tuple-element.39), channel_id=1, source_target_pairs={{0,15},{1,10},{2,9},{3,12},{4,11},{5,14},{6,13},{7,8},{8,7},{9,2},... | collective-permute-start | bytes 110600 | tf_op jit(solution)/shard_map/ppermute | solution.py:83
  12.6 3.0 %collective-permute-done.4.oa = f32[9,8,128]{2,1,0:T(8,128)S(1)} collective-permute-done((f32[9,8,128]{2,1,0:T(8,128)S(1)}, f32[9,8,128]{2,1,0:T(8,128)S(1)}, u32[]{:S(2)}, u32[]{:S(2)}) %collective-permute-start.4) | collective-permute-done | bytes 36896 | tf_op jit(solution)/shard_map/ppermute | solution.py:83
  15.5 0.1 collective-permute-start.5
  15.6 1.1 %collective-permute-done.5.ob = f32[9,8,128]{2,1,0:T(8,128)S(1)} collective-permute-done((f32[9,8,128]{2,1,0:T(8,128)S(1)}, f32[9,8,128]{2,1,0:T(8,128)S(1)}, u32[]{:S(2)}, u32[]{:S(2)}) %collective-permute-start.5) | collective-permute-done | bytes 36896 | tf_op jit(solution)/shard_map/ppermute | solution.py:83
  16.7 0.0 collective-permute-done.1.b
  16.7 0.0 collective-permute-done.a.refs_1_
  16.8 0.2 collective-permute-start.6
  17.0 0.0 collective-permute-done.3.e.refs_1_
  17.0 1.1 %collective-permute-start.8 = (f32[5,32,128]{2,1,0:T(8,128)S(1)}, f32[5,32,128]{2,1,0:T(8,128)S(1)}, u32[]{:S(2)}, u32[]{:S(2)}) collective-permute-start(f32[5,32,128]{2,1,0:T(8,128)S(1)} %get-tuple-element.45.refs_0_), channel_id=1, source_target_pairs={{0,3},{1,2},{2,1},{3,0},{4,7},{5,6},{6,5},{7,4},{8,11},{9,10},{10,... | collective-permute-start | bytes 245768 | tf_op jit(solution)/shard_map/ppermute | solution.py:90
  18.1 0.0 collective-permute-done.2.o
  18.1 0.0 collective-permute-done.6.ab
  18.1 3.6 %advect.1 = (f32[32,32,128]{2,1,0:T(8,128)S(1)}, f32[2,32,128]{2,1,0:T(8,128)S(1)}, f32[32,32,128]{2,1,0:T(8,128)S(1)}, f32[32,32,128]{2,1,0:T(8,128)S(1)}) custom-call(f32[32,32,128]{2,1,0:T(8,128)} %tracer.3, f32[32,32,128]{2,1,0:T(8,128)} %y_speed.3, f32[32,32,128]{2,1,0:T(8,128)} %z_speed.3, f32[16,32,128]{2,1,0:T(8,128)S(1)} %collective-permute-done.a.refs_1_, ...), custom_call_target="tpu_custom_call" | custom-call | bytes 5120000 | tf_op jit(solution)/shard_map/advect/pallas_call | solution.py:32
  21.7 0.4 collective-permute-start.7
  22.1 0.0 collective-permute-done.8.refs_1_
  22.1 0.8 %collective-permute-done.7.refs_1_ = f32[2,32,128]{2,1,0:T(8,128)S(1)} collective-permute-done((f32[2,32,128]{2,1,0:T(8,128)S(1)}, f32[2,32,128]{2,1,0:T(8,128)S(1)}, u32[]{:S(2)}, u32[]{:S(2)}) %collective-permute-start.7) | collective-permute-done | bytes 32800 | tf_op jit(solution)/shard_map/ppermute | solution.py:90
  23.0 1.1 %collective-permute-start.9 = (f32[2,32,128]{2,1,0:T(8,128)S(1)}, f32[2,32,128]{2,1,0:T(8,128)S(1)}, u32[]{:S(2)}, u32[]{:S(2)}) collective-permute-start(f32[2,32,128]{2,1,0:T(8,128)S(1)} %get-tuple-element.47.refs_0_), channel_id=1, source_target_pairs={{0,3},{1,2},{2,1},{3,0},{4,7},{5,6},{6,5},{7,4},{8,11},{9,10},{10,... | collective-permute-start | bytes 98312 | tf_op jit(solution)/shard_map/ppermute | solution.py:90
  24.0 2.3 %collective-permute-done.9.refs_1_ = f32[2,32,128]{2,1,0:T(8,128)S(1)} collective-permute-done((f32[2,32,128]{2,1,0:T(8,128)S(1)}, f32[2,32,128]{2,1,0:T(8,128)S(1)}, u32[]{:S(2)}, u32[]{:S(2)}) %collective-permute-start.9) | collective-permute-done | bytes 32800 | tf_op jit(solution)/shard_map/ppermute | solution.py:90
  26.4 1.3 %collective-permute-start.10 = (f32[3,32,128]{2,1,0:T(8,128)S(1)}, f32[3,32,128]{2,1,0:T(8,128)S(1)}, u32[]{:S(2)}, u32[]{:S(2)}) collective-permute-start(f32[3,32,128]{2,1,0:T(8,128)S(1)} %get-tuple-element.49.refs_0_), channel_id=1, source_target_pairs={{0,5},{1,4},{2,7},{3,6},{4,1},{5,0},{6,3},{7,2},{8,13},{9,12},{10,... | collective-permute-start | bytes 147464 | tf_op jit(solution)/shard_map/ppermute | solution.py:90
  27.7 2.4 %collective-permute-done.10.refs_1_ = f32[3,32,128]{2,1,0:T(8,128)S(1)} collective-permute-done((f32[3,32,128]{2,1,0:T(8,128)S(1)}, f32[3,32,128]{2,1,0:T(8,128)S(1)}, u32[]{:S(2)}, u32[]{:S(2)}) %collective-permute-start.10) | collective-permute-done | bytes 49184 | tf_op jit(solution)/shard_map/ppermute | solution.py:90
  30.1 1.4 %turn.1 = (f32[32,32,128]{2,1,0:T(8,128)S(1)}, f32[2,32,128]{2,1,0:T(8,128)S(1)}, f32[32,32,128]{2,1,0:T(8,128)S(1)}, f32[32,32,128]{2,1,0:T(8,128)S(1)}) custom-call(f32[3,32,128]{2,1,0:T(8,128)S(1)} %get-tuple-element.49.refs_0_, f32[3,32,128]{2,1,0:T(8,128)S(1)} %collective-permute-done.10.refs_1_, f32[3,32,128]{2,1,0:T(8,128)S(1)} %get-tuple-element.44.refs_2_, ...), custom_call_target="tpu_custom_call" | custom-call | bytes 1536000 | tf_op jit(solution)/shard_map/turn/pallas_call | solution.py:32
  31.5 6.8 %collective-permute-start.11 = (f32[2,32,128]{2,1,0:T(8,128)S(1)}, f32[2,32,128]{2,1,0:T(8,128)S(1)}, u32[]{:S(2)}, u32[]{:S(2)}) collective-permute-start(f32[2,32,128]{2,1,0:T(8,128)S(1)} %get-tuple-element.57.refs_0_), channel_id=1, source_target_pairs={{0,8},{8,0},{16,24},{24,16},{1,9},{9,1},{17,25},{25,17},{2,10},{10... | collective-permute-start | bytes 98312 | tf_op jit(solution)/shard_map/ppermute | solution.py:90
  38.4 1.9 %collective-permute-done.11.refs_1_ = f32[2,32,128]{2,1,0:T(8,128)S(1)} collective-permute-done((f32[2,32,128]{2,1,0:T(8,128)S(1)}, f32[2,32,128]{2,1,0:T(8,128)S(1)}, u32[]{:S(2)}, u32[]{:S(2)}) %collective-permute-start.11) | collective-permute-done | bytes 32800 | tf_op jit(solution)/shard_map/ppermute | solution.py:90
  40.2 2.0 %collective-permute-start.12 = (f32[3,32,128]{2,1,0:T(8,128)S(1)}, f32[3,32,128]{2,1,0:T(8,128)S(1)}, u32[]{:S(2)}, u32[]{:S(2)}) collective-permute-start(f32[3,32,128]{2,1,0:T(8,128)S(1)} %get-tuple-element.60.refs_0_), channel_id=1, source_target_pairs={{0,16},{8,24},{16,0},{24,8},{1,17},{9,25},{17,1},{25,9},{2,18},{10... | collective-permute-start | bytes 147464 | tf_op jit(solution)/shard_map/ppermute | solution.py:90
  42.2 3.1 %collective-permute-done.12.refs_1_ = f32[3,32,128]{2,1,0:T(8,128)S(1)} collective-permute-done((f32[3,32,128]{2,1,0:T(8,128)S(1)}, f32[3,32,128]{2,1,0:T(8,128)S(1)}, u32[]{:S(2)}, u32[]{:S(2)}) %collective-permute-start.12) | collective-permute-done | bytes 49184 | tf_op jit(solution)/shard_map/ppermute | solution.py:90
  45.3 0.9 %finish.1 = f32[32,32,128]{2,1,0:T(8,128)} custom-call(f32[3,32,128]{2,1,0:T(8,128)S(1)} %get-tuple-element.60.refs_0_, f32[3,32,128]{2,1,0:T(8,128)S(1)} %collective-permute-done.12.refs_1_, f32[3,32,128]{2,1,0:T(8,128)S(1)} %get-tuple-element.58.refs_2_, f32[1,32,128]{2,1,0:T(8,128)S(1)} %get-tuple-element.61.refs_3_, ...), custom_call_target="tpu_custom_call" | custom-call | bytes 1024000 | tf_op jit(solution)/shard_map/finish/pallas_call | solution.py:32
  (7 shorter events, 0.2 us)
Async XLA Ops:
  4.2 12.5 %collective-permute-start = (f32[16,32,128]{2,1,0:T(8,128)S(1)}, f32[16,32,128]{2,1,0:T(8,128)S(1)}, u32[]{:S(2)}, u32[]{:S(2)}) collective-permute-start(f32[16,32,128]{2,1,0:T(8,128)S(1)} %get-tuple-element.35.refs_10_.refs_0_.refs_4_), channel_id=1, source_target_pairs={{0,8},{1,9},{2,10},{3,11},{4,12},{5,13},{6,14},{7,15},{8,0},{9,1},... | collective-permute-start | bytes 786440 | tf_op jit(solution)/shard_map/ppermute | solution.py:83
  7.3 9.7 %collective-permute-start.3 = (f32[16,32,128]{2,1,0:T(8,128)S(1)}, f32[16,32,128]{2,1,0:T(8,128)S(1)}, u32[]{:S(2)}, u32[]{:S(2)}) collective-permute-start(f32[16,32,128]{2,1,0:T(8,128)S(1)} %get-tuple-element.38.e_mine.refs_0_.refs_6_), channel_id=1, source_target_pairs={{0,1},{1,0},{2,3},{3,2},{4,5},{5,4},{6,7},{7,6},{8,9},{9,8},{10,11... | collective-permute-start | bytes 786440 | tf_op jit(solution)/shard_map/ppermute | solution.py:90
  7.3 9.4 %collective-permute-start.1 = (f32[11,32,128]{2,1,0:T(8,128)S(1)}, f32[11,32,128]{2,1,0:T(8,128)S(1)}, u32[]{:S(2)}, u32[]{:S(2)}) collective-permute-start(f32[11,32,128]{2,1,0:T(8,128)S(1)} %get-tuple-element.36), channel_id=1, source_target_pairs={{0,1},{1,0},{2,3},{3,2},{4,5},{5,4},{6,7},{7,6},{8,16},{9,17},{10,... | collective-permute-start | bytes 540680 | tf_op jit(solution)/shard_map/ppermute | solution.py:83
  7.8 10.3 %collective-permute-start.2 = (f32[11,32,128]{2,1,0:T(8,128)S(1)}, f32[11,32,128]{2,1,0:T(8,128)S(1)}, u32[]{:S(2)}, u32[]{:S(2)}) collective-permute-start(f32[11,32,128]{2,1,0:T(8,128)S(1)} %get-tuple-element.37), channel_id=1, source_target_pairs={{0,7},{1,2},{2,1},{3,4},{4,3},{5,6},{6,5},{7,0},{8,15},{9,10},{10,... | collective-permute-start | bytes 540680 | tf_op jit(solution)/shard_map/ppermute | solution.py:83
  9.9 5.6 %collective-permute-start.4 = (f32[9,8,128]{2,1,0:T(8,128)S(1)}, f32[9,8,128]{2,1,0:T(8,128)S(1)}, u32[]{:S(2)}, u32[]{:S(2)}) collective-permute-start(f32[9,8,128]{2,1,0:T(8,128)S(1)} %get-tuple-element.39), channel_id=1, source_target_pairs={{0,15},{1,10},{2,9},{3,12},{4,11},{5,14},{6,13},{7,8},{8,7},{9,2},... | collective-permute-start | bytes 110600 | tf_op jit(solution)/shard_map/ppermute | solution.py:83
  15.5 1.2 %collective-permute-start.5 = (f32[9,8,128]{2,1,0:T(8,128)S(1)}, f32[9,8,128]{2,1,0:T(8,128)S(1)}, u32[]{:S(2)}, u32[]{:S(2)}) collective-permute-start(f32[9,8,128]{2,1,0:T(8,128)S(1)} %get-tuple-element.40), channel_id=1, source_target_pairs={{0,1},{1,0},{2,3},{3,2},{4,5},{5,4},{6,7},{7,6},{8,23},{9,18},{10,... | collective-permute-start | bytes 110600 | tf_op jit(solution)/shard_map/ppermute | solution.py:83
  16.8 1.4 %collective-permute-start.6 = (f32[22,8,128]{2,1,0:T(8,128)S(1)}, f32[22,8,128]{2,1,0:T(8,128)S(1)}, u32[]{:S(2)}, u32[]{:S(2)}) collective-permute-start(f32[22,8,128]{2,1,0:T(8,128)S(1)} %rim.1), channel_id=1, source_target_pairs={{0,1},{1,0},{2,3},{3,2},{4,5},{5,4},{6,7},{7,6},{8,9},{9,8},{10,11... | collective-permute-start | bytes 270344 | tf_op jit(solution)/shard_map/ppermute | solution.py:83
  17.0 5.1 %collective-permute-start.8 = (f32[5,32,128]{2,1,0:T(8,128)S(1)}, f32[5,32,128]{2,1,0:T(8,128)S(1)}, u32[]{:S(2)}, u32[]{:S(2)}) collective-permute-start(f32[5,32,128]{2,1,0:T(8,128)S(1)} %get-tuple-element.45.refs_0_), channel_id=1, source_target_pairs={{0,3},{1,2},{2,1},{3,0},{4,7},{5,6},{6,5},{7,4},{8,11},{9,10},{10,... | collective-permute-start | bytes 245768 | tf_op jit(solution)/shard_map/ppermute | solution.py:90
  21.7 1.3 %collective-permute-start.7 = (f32[2,32,128]{2,1,0:T(8,128)S(1)}, f32[2,32,128]{2,1,0:T(8,128)S(1)}, u32[]{:S(2)}, u32[]{:S(2)}) collective-permute-start(f32[2,32,128]{2,1,0:T(8,128)S(1)} %get-tuple-element.43.refs_0_), channel_id=1, source_target_pairs={{0,1},{1,0},{2,3},{3,2},{4,5},{5,4},{6,7},{7,6},{8,9},{9,8},{10,11... | collective-permute-start | bytes 98312 | tf_op jit(solution)/shard_map/ppermute | solution.py:90
  23.0 3.4 %collective-permute-start.9 = (f32[2,32,128]{2,1,0:T(8,128)S(1)}, f32[2,32,128]{2,1,0:T(8,128)S(1)}, u32[]{:S(2)}, u32[]{:S(2)}) collective-permute-start(f32[2,32,128]{2,1,0:T(8,128)S(1)} %get-tuple-element.47.refs_0_), channel_id=1, source_target_pairs={{0,3},{1,2},{2,1},{3,0},{4,7},{5,6},{6,5},{7,4},{8,11},{9,10},{10,... | collective-permute-start | bytes 98312 | tf_op jit(solution)/shard_map/ppermute | solution.py:90
  26.4 3.7 %collective-permute-start.10 = (f32[3,32,128]{2,1,0:T(8,128)S(1)}, f32[3,32,128]{2,1,0:T(8,128)S(1)}, u32[]{:S(2)}, u32[]{:S(2)}) collective-permute-start(f32[3,32,128]{2,1,0:T(8,128)S(1)} %get-tuple-element.49.refs_0_), channel_id=1, source_target_pairs={{0,5},{1,4},{2,7},{3,6},{4,1},{5,0},{6,3},{7,2},{8,13},{9,12},{10,... | collective-permute-start | bytes 147464 | tf_op jit(solution)/shard_map/ppermute | solution.py:90
  31.5 8.7 %collective-permute-start.11 = (f32[2,32,128]{2,1,0:T(8,128)S(1)}, f32[2,32,128]{2,1,0:T(8,128)S(1)}, u32[]{:S(2)}, u32[]{:S(2)}) collective-permute-start(f32[2,32,128]{2,1,0:T(8,128)S(1)} %get-tuple-element.57.refs_0_), channel_id=1, source_target_pairs={{0,8},{8,0},{16,24},{24,16},{1,9},{9,1},{17,25},{25,17},{2,10},{10... | collective-permute-start | bytes 98312 | tf_op jit(solution)/shard_map/ppermute | solution.py:90
  40.2 5.1 %collective-permute-start.12 = (f32[3,32,128]{2,1,0:T(8,128)S(1)}, f32[3,32,128]{2,1,0:T(8,128)S(1)}, u32[]{:S(2)}, u32[]{:S(2)}) collective-permute-start(f32[3,32,128]{2,1,0:T(8,128)S(1)} %get-tuple-element.60.refs_0_), channel_id=1, source_target_pairs={{0,16},{8,24},{16,0},{24,8},{1,17},{9,25},{17,1},{25,9},{2,18},{10... | collective-permute-start | bytes 147464 | tf_op jit(solution)/shard_map/ppermute | solution.py:90

commit v3 on v2

--- a/solution.py
+++ b/solution.py
@@ -25,7 +25,8 @@
     inputs, in_specs = [], []
     for operand in operands:
         where, x = operand if isinstance(operand, tuple) else ("near", operand)
-        x = pltpu.with_memory_space_constraint(x, pltpu.VMEM if where == "near" else pltpu.HBM)
+        if where != "plain":
+            x = pltpu.with_memory_space_constraint(x, pltpu.VMEM if where == "near" else pltpu.HBM)
         inputs.append(x)
         in_specs.append(away if where == "far" else whole)
     out_specs = [away if isinstance(out, tuple) else whole for out in outs]
@@ -94,7 +95,7 @@
     return (lax.axis_size(axis) - 1).bit_length()
 
 
-def rim_kernel(a, b, oa, ob, out):
+def rim_kernel(a, b, oa, ob, _, out):
     _, y, _, _ = place()
     width = a.shape[1]
     start = pl.multiple_of((1 - lax.rem(y, 2)) * (width - 8), 8)
@@ -103,8 +104,8 @@
             out[11 * half + k] = ref[k, pl.ds(start, 8), :]
 
 
-def rim(a, b, oa, ob):
-    return call(rim_kernel, "rim", [near(22, 8, a.shape[2])], [a, b, oa, ob], cycles=200)
+def rim(a, b, oa, ob, after):
+    return call(rim_kernel, "rim", [near(22, 8, a.shape[2])], [a, b, oa, ob, ("far", after)], cycles=200)
 
 
 def reciprocal(x):
@@ -117,36 +118,79 @@
     for read, count, r, phi, psi, ports, edge_low, edge_high in sides:
         first = read(0)
         before = first
+        following = read(1)
         for j in range(1, count):
-            here = read(j)
+            here = following
+            if j + 1 < count:
+                following = read(j + 1)
             r[j] = reciprocal((0.5 * RATE) * (before + here))
             before = here
-        ports[3] = first
-        ports[4] = before
         one = jnp.ones_like(first)
-        phi[0] = one
-        psi[count - 1] = one
-        state.append([one, 1.0 + edge_low * first, one, 1.0 + edge_high * before])
-    for j in range(1, max(side[1] for side in sides)):
-        for (_, count, r, phi, psi, _, _, _), s in zip(sides, state):
-            if j < count:
-                s[0] = s[0] + r[j] * s[1]
+        if phi is not None:
+            phi[0] = one
+            psi[count - 1] = one
+        state.append([one, 1.0 + edge_low * first, one, 1.0 + edge_high * before, first, before])
+
+    def faces(j):
+        return [(r[j], r[count - j]) if j < count else None for _, count, r, _, _, _, _, _ in sides]
+
+    longest = max(side[1] for side in sides)
+    following = faces(1)
+    for j in range(1, longest):
+        here, following = following, faces(j + 1)
+        for (_, count, _, _, _, _, _, _), s, pair in zip(sides, state, here):
+            if pair is not None:
+                s[0] = s[0] + pair[0] * s[1]
                 s[1] = s[1] + s[0]
+                s[2] = s[2] + pair[1] * s[3]
+                s[3] = s[3] + s[2]
+        for (_, count, _, phi, psi, _, _, _), s, pair in zip(sides, state, here):
+            if pair is not None and phi is not None:
                 phi[j] = s[0]
-                s[2] = s[2] + r[count - j] * s[3]
-                s[3] = s[3] + s[2]
                 psi[count - 1 - j] = s[2]
     for (_, _, _, _, _, ports, _, edge_high), s in zip(sides, state):
-        inverse = reciprocal(s[1] + edge_high * ports[4] * s[0])
-        ports[0] = s[2] * inverse
-        ports[1] = inverse
-        ports[2] = s[0] * inverse
+        if ports is not None:
+            inverse = reciprocal(s[1] + edge_high * s[5] * s[0])
+            ports[0] = s[2] * inverse
+            ports[1] = inverse
+            ports[2] = s[0] * inverse
+            ports[3] = s[4]
+            ports[4] = s[5]
+
+
+def factor_sides(kappa, r_y, r_z, wanted_y, wanted_z):
+    z, y, z_count, y_count = place()
+    depth, width, _ = kappa.shape
+
+    def flag(condition):
+        return jnp.where(condition, RATE, 0.0)
+
+    return (
+        (lambda j: kappa[:, j, :], width, r_y, *wanted_y, flag(y == 0), flag(y == y_count - 1)),
+        (lambda j: kappa[j], depth, r_z, *wanted_z, flag(z == 0), flag(z == z_count - 1)),
+    )
+
+
+def factor_kernel(kappa, _, phi_y, psi_y, phi_z, psi_z, r_y, r_z):
+    factor(factor_sides(kappa, r_y, r_z, (phi_y, psi_y, None), (phi_z, psi_z, None)))
+
+
+def factor_again(kappa, after):
+    depth, width, band = kappa.shape
+    along_y, along_z = (width, depth, band), (depth, width, band)
+    return call(
+        factor_kernel,
+        "factor",
+        [far(*along_y)] * 2 + [far(*along_z)] * 2,
+        [("plain", kappa), after],
+        scratch=[near(*along_y), near(*along_z)],
+        cycles=4000,
+    )
 
 
 def begin_kernel(
     tracer, y_speed, z_speed, kappa_far, a_ref, b_ref, o_ref, e_ref, oa_ref, ob_ref,
-    phi_y_far, psi_y_far, phi_z_far, psi_z_far,
-    c, ys, zs, kappa, r_y, r_z, phi_y, psi_y, phi_z, psi_z, sem,
+    c, ys, zs, kappa, r_y, r_z, sem,
 ):
     arrivals = [
         pltpu.make_async_copy(source, target, sem.at[k])
@@ -154,25 +198,10 @@
     ]
     for copy in arrivals:
         copy.start()
-    z, y, z_count, y_count = place()
+    z, y, _, _ = place()
     depth, width, _ = c.shape
-
-    def flag(condition):
-        return jnp.where(condition, RATE, 0.0)
-
     arrivals[0].wait()
-    factor((
-        (lambda j: kappa[:, j, :], width, r_y, phi_y, psi_y, e_ref.at[11:16], flag(y == 0), flag(y == y_count - 1)),
-        (lambda j: kappa[j], depth, r_z, phi_z, psi_z, a_ref.at[11:16], flag(z == 0), flag(z == z_count - 1)),
-    ))
-    results = [
-        pltpu.make_async_copy(source, target, sem.at[4 + k])
-        for k, (source, target) in enumerate(
-            ((phi_y, phi_y_far), (psi_y, psi_y_far), (phi_z, phi_z_far), (psi_z, psi_z_far))
-        )
-    ]
-    for copy in results:
-        copy.start()
+    factor(factor_sides(kappa, r_y, r_z, (None, None, e_ref.at[11:16]), (None, None, a_ref.at[11:16])))
     for copy in arrivals[1:]:
         copy.wait()
 
@@ -207,9 +236,6 @@
     def _():
         rims(width - 4, 0)
 
-    for copy in results:
-        copy.wait()
-
 
 def begin(tracer, y_speed, z_speed, kappa):
     depth, width, band = tracer.shape
@@ -218,12 +244,9 @@
         begin_kernel,
         "begin",
         [near(16, width, band), near(11, width, band), near(11, depth, band), near(16, depth, band)]
-        + [near(9, 8, band)] * 2
-        + [("far", far(*along_y))] * 2
-        + [("far", far(*along_z))] * 2,
+        + [near(9, 8, band)] * 2,
         [("far", x) for x in (tracer, y_speed, z_speed, kappa)],
-        scratch=[near(*along_z)] * 4 + [near(*along_y), near(*along_z)] + [near(*along_y)] * 2
-        + [near(*along_z)] * 2 + [pltpu.SemaphoreType.DMA((8,))],
+        scratch=[near(*along_z)] * 4 + [near(*along_y), near(*along_z), pltpu.SemaphoreType.DMA((4,))],
         cycles=4000,
     )
 
@@ -253,13 +276,29 @@
     return call(kernel, "join_ports", [near(5, lines, band), near(3, lines, band)], [mine, theirs], cycles=100)
 
 
-def join_levels(mine, theirs, axis):
-    ports, joint = join_ports(mine, theirs, axis, 0, first_row=11)
-    joints = [joint]
-    for level in range(1, levels_of(axis) - 1):
+def join_levels(ports, axis, done):
+    joints = []
+    for level in range(done, levels_of(axis) - 1):
         ports, joint = join_ports(ports, swap(ports, axis, level), axis, level)
         joints.append(joint)
     return ports, joints
+
+
+def first_join_kernel(mine, theirs, oa, ob, out, joint, oa_out, ob_out):
+    ports_kernel("gy", 0, 11, mine, theirs, out, joint)
+    oa_out[...] = oa[...]
+    ob_out[...] = ob[...]
+
+
+def first_join(mine, theirs, oa, ob):
+    _, lines, band = mine.shape
+    return call(
+        first_join_kernel,
+        "first_join",
+        [near(5, lines, band), near(3, lines, band), near(*oa.shape), near(*ob.shape)],
+        [mine, theirs, oa, ob],
+        cycles=100,
+    )
 
 
 def source_kernel(axis, level, last, mine, theirs, joint, ports, out, flow_ref):
@@ -563,17 +602,22 @@
 
 
 def local(tracer, y_speed, z_speed, kappa):
-    a_mine, b, o, e_mine, oa, ob, phi_y, psi_y, phi_z, psi_z = begin(tracer, y_speed, z_speed, kappa)
+    a_mine, b, o, e_mine, oa, ob = begin(tracer, y_speed, z_speed, kappa)
+    o = send(o, y_partner=y_other)
+    e = swap(e_mine, "gy", 0)
     a = send(a_mine, z_partner=pair_up)
     b = send(b, z_partner=z_other)
-    o = send(o, y_partner=y_other)
+    ports_y, joint_y, oa, ob = first_join(e_mine, e, oa, ob)
     oa = send(oa, z_partner=pair_up, y_partner=y_other)
     ob = send(ob, z_partner=z_other, y_partner=y_other)
-    e = swap(e_mine, "gy", 0)
-    ab = send(rim(a, b, oa, ob), y_partner=pair_up)
-
-    ports_y, joints_y = join_levels(e_mine, e, "gy")
-    ports_z, joints_z = join_levels(a_mine, a, "gz")
+    phi_y, psi_y, phi_z, psi_z = factor_again(kappa, ports_y)
+    ab = send(rim(a, b, oa, ob, phi_y), y_partner=pair_up)
+
+    ports_y, joints = join_levels(ports_y, "gy", 1)
+    joints_y = [joint_y] + joints
+    ports_z, joint_z = join_ports(a_mine, a, "gz", 0, first_row=11)
+    ports_z, joints = join_levels(ports_z, "gz", 1)
+    joints_z = [joint_z] + joints
 
     base, sources, phi_y, psi_y = advect(
         tracer, y_speed, z_speed, (a, b, o, e, oa, ob, ab), e_mine, phi_y, psi_y

time: 46.3 us -> 40.4 us (0.87)
  starting transfers between devices: 21.3 us -> 15.4 us
  Pallas kernels: 10.2 us -> 11.7 us
  waiting for transfers between devices: 14.6 us -> 13.1 us
    ppermute x7, starting transfers between devices: 12.6 us -> 7.33 us  [swap(): lax.ppermute(x, axis, [(i, i ^ step) for i in range(lax.axis_size(axis))])]
    ppermute x6, waiting for transfers between devices: 4.11 us -> 1.99 us  [send(): return lax.ppermute(x, AXES, permutation(z_partner, y_partner))]
    pallas_call x11 -> x12, Pallas kernels: 10.2 us -> 11.7 us  [call(): pl.pallas_call(kernel, out_shape=[out[1] if isinstance(out, tuple) else o...]
    ppermute x7, waiting for transfers between devices: 10.5 us -> 11.2 us  [swap(): lax.ppermute(x, axis, [(i, i ^ step) for i in range(lax.axis_size(axis))])]
    ppermute x6, starting transfers between devices: 8.65 us -> 8.02 us  [send(): return lax.ppermute(x, AXES, permutation(z_partner, y_partner))]
  transfers between devices with their start and end apart: 13 -> 13, of which waited for: 7 -> 7; matrix products, arithmetic and copies ran while one was open for 0% -> 0% of each run, Pallas kernels for 8% -> 16%
where the time goes in v3:
time: 40.4 us; the launch traced here: 40.2 us
  starting transfers between devices  15.4 us (38%)
  waiting for transfers between devices  13.1 us (32%)
  Pallas kernels  11.7 us (29%)
    pallas_call x12, Pallas kernels, call(): pl.pallas_call(kernel, out_shape=[out[1] if isinstance(out, tuple) else o...  11.7 us
    ppermute x7, waiting for transfers between devices, swap(): lax.ppermute(x, axis, [(i, i ^ step) for i in range(lax.axis_size(axis))])  11.2 us
    ppermute x6, starting transfers between devices, send(): return lax.ppermute(x, AXES, permutation(z_partner, y_partner))  8.02 us
    ppermute x7, starting transfers between devices, swap(): lax.ppermute(x, axis, [(i, i ^ step) for i in range(lax.axis_size(axis))])  7.33 us
    ppermute x6, waiting for transfers between devices, send(): return lax.ppermute(x, AXES, permutation(z_partner, y_partner))  1.99 us
  transfers between devices with their start and end apart: 13, of which 7 were waited for; matrix products, arithmetic and copies ran while one was open for 0% of the time, Pallas kernels for 16%

profile of v3, /device:TPU:0, one launch (start us, length us, event | category | flops | bytes accessed | tf_op | source)
XLA Modules:
  0.0 40.2 jit_solution(12995645375823903531)
XLA Ops:
  0.0 2.9 %begin.1 = (f32[16,32,128]{2,1,0:T(8,128)S(1)}, f32[11,32,128]{2,1,0:T(8,128)S(1)}, f32[11,32,128]{2,1,0:T(8,128)S(1)}, f32[16,32,128]{2,1,0:T(8,128)S(1)}, f32[...) custom-call(f32[32,32,128]{2,1,0:T(8,128)} %tracer.3, f32[32,32,128]{2,1,0:T(8,128)} %y_speed.3, f32[32,32,128]{2,1,0:T(8,128)} %z_speed.3, ...), custom_call_target="tpu_custom_call" | custom-call | bytes 4096000 | tf_op jit(solution)/shard_map/begin/pallas_call | solution.py:33
  2.9 0.0 copy-start
  2.9 0.5 %collective-permute-start.3 = (f32[16,32,128]{2,1,0:T(8,128)S(1)}, f32[16,32,128]{2,1,0:T(8,128)S(1)}, u32[]{:S(2)}, u32[]{:S(2)}) collective-permute-start(f32[16,32,128]{2,1,0:T(8,128)S(1)} %get-tuple-element.40.mine.e_mine.refs_6_), channel_id=1, source_target_pairs={{0,1},{1,0},{2,3},{3,2},{4,5},{5,4},{6,7},{7,6},{8,9},{9,8},{10,11... | collective-permute-start | bytes 786440 | tf_op jit(solution)/shard_map/ppermute | solution.py:91
  3.4 2.6 %collective-permute-start = (f32[16,32,128]{2,1,0:T(8,128)S(1)}, f32[16,32,128]{2,1,0:T(8,128)S(1)}, u32[]{:S(2)}, u32[]{:S(2)}) collective-permute-start(f32[16,32,128]{2,1,0:T(8,128)S(1)} %get-tuple-element.37.refs_10_.refs_0_.refs_4_), channel_id=1, source_target_pairs={{0,8},{1,9},{2,10},{3,11},{4,12},{5,13},{6,14},{7,15},{8,0},{9,1},... | collective-permute-start | bytes 786440 | tf_op jit(solution)/shard_map/ppermute | solution.py:84
  6.1 0.2 collective-permute-start.1
  6.3 2.4 %collective-permute-start.2 = (f32[11,32,128]{2,1,0:T(8,128)S(1)}, f32[11,32,128]{2,1,0:T(8,128)S(1)}, u32[]{:S(2)}, u32[]{:S(2)}) collective-permute-start(f32[11,32,128]{2,1,0:T(8,128)S(1)} %get-tuple-element.39), channel_id=1, source_target_pairs={{0,7},{1,2},{2,1},{3,4},{4,3},{5,6},{6,5},{7,0},{8,15},{9,10},{10,... | collective-permute-start | bytes 540680 | tf_op jit(solution)/shard_map/ppermute | solution.py:84
  8.7 0.0 collective-permute-done.3.theirs.e
  8.7 2.7 %collective-permute-start.4 = (f32[9,8,128]{2,1,0:T(8,128)S(1)}, f32[9,8,128]{2,1,0:T(8,128)S(1)}, u32[]{:S(2)}, u32[]{:S(2)}) collective-permute-start(f32[9,8,128]{2,1,0:T(8,128)S(1)} %get-tuple-element.43), channel_id=1, source_target_pairs={{0,15},{1,10},{2,9},{3,12},{4,11},{5,14},{6,13},{7,8},{8,7},{9,2},... | collective-permute-start | bytes 110600 | tf_op jit(solution)/shard_map/ppermute | solution.py:84
  11.4 0.0 collective-permute-start.5
  11.4 0.0 copy-done
  11.4 2.8 %factor.1 = (f32[32,32,128]{2,1,0:T(8,128)}, f32[32,32,128]{2,1,0:T(8,128)}, f32[32,32,128]{2,1,0:T(8,128)}, f32[32,32,128]{2,1,0:T(8,128)}) custom-call(f32[32,32,128]{2,1,0:T(8,128)S(1)} %copy-done, f32[5,32,128]{2,1,0:T(8,128)S(1)} %get-tuple-element.45._.refs_0_), custom_call_target="tpu_custom_call" | custom-call | bytes 4096000 | tf_op jit(solution)/shard_map/factor/pallas_call | solution.py:33
  14.2 0.0 collective-permute-done.1.b
  14.2 0.0 collective-permute-done.a.refs_1_
  14.2 1.2 %collective-permute-done.4.oa = f32[9,8,128]{2,1,0:T(8,128)S(1)} collective-permute-done((f32[9,8,128]{2,1,0:T(8,128)S(1)}, f32[9,8,128]{2,1,0:T(8,128)S(1)}, u32[]{:S(2)}, u32[]{:S(2)}) %collective-permute-start.4) | collective-permute-done | bytes 36896 | tf_op jit(solution)/shard_map/ppermute | solution.py:84
  15.4 0.0 collective-permute-done.5.ob
  15.4 0.1 collective-permute-start.6
  15.5 0.5 %collective-permute-start.8 = (f32[5,32,128]{2,1,0:T(8,128)S(1)}, f32[5,32,128]{2,1,0:T(8,128)S(1)}, u32[]{:S(2)}, u32[]{:S(2)}) collective-permute-start(f32[5,32,128]{2,1,0:T(8,128)S(1)} %get-tuple-element.45._.refs_0_), channel_id=1, source_target_pairs={{0,3},{1,2},{2,1},{3,0},{4,7},{5,6},{6,5},{7,4},{8,11},{9,10},{10,... | collective-permute-start | bytes 245768 | tf_op jit(solution)/shard_map/ppermute | solution.py:91
  16.0 0.0 collective-permute-done.2.o
  16.0 0.8 %collective-permute-done.6.ab = f32[22,8,128]{2,1,0:T(8,128)S(1)} collective-permute-done((f32[22,8,128]{2,1,0:T(8,128)S(1)}, f32[22,8,128]{2,1,0:T(8,128)S(1)}, u32[]{:S(2)}, u32[]{:S(2)}) %collective-permute-start.6) | collective-permute-done | bytes 90144 | tf_op jit(solution)/shard_map/ppermute | solution.py:84
  16.8 3.6 %advect.1 = (f32[32,32,128]{2,1,0:T(8,128)S(1)}, f32[2,32,128]{2,1,0:T(8,128)S(1)}, f32[32,32,128]{2,1,0:T(8,128)S(1)}, f32[32,32,128]{2,1,0:T(8,128)S(1)}) custom-call(f32[32,32,128]{2,1,0:T(8,128)} %tracer.3, f32[32,32,128]{2,1,0:T(8,128)} %y_speed.3, f32[32,32,128]{2,1,0:T(8,128)} %z_speed.3, f32[16,32,128]{2,1,0:T(8,128)S(1)} %collective-permute-done.a.refs_1_, ...), custom_call_target="tpu_custom_call" | custom-call | bytes 5120000 | tf_op jit(solution)/shard_map/advect/pallas_call | solution.py:33
  20.3 0.2 collective-permute-start.7
  20.6 0.0 collective-permute-done.8.refs_1_
  20.6 1.0 %collective-permute-done.7.refs_1_ = f32[2,32,128]{2,1,0:T(8,128)S(1)} collective-permute-done((f32[2,32,128]{2,1,0:T(8,128)S(1)}, f32[2,32,128]{2,1,0:T(8,128)S(1)}, u32[]{:S(2)}, u32[]{:S(2)}) %collective-permute-start.7) | collective-permute-done | bytes 32800 | tf_op jit(solution)/shard_map/ppermute | solution.py:91
  21.6 0.7 %collective-permute-start.9 = (f32[2,32,128]{2,1,0:T(8,128)S(1)}, f32[2,32,128]{2,1,0:T(8,128)S(1)}, u32[]{:S(2)}, u32[]{:S(2)}) collective-permute-start(f32[2,32,128]{2,1,0:T(8,128)S(1)} %get-tuple-element.51.refs_0_), channel_id=1, source_target_pairs={{0,3},{1,2},{2,1},{3,0},{4,7},{5,6},{6,5},{7,4},{8,11},{9,10},{10,... | collective-permute-start | bytes 98312 | tf_op jit(solution)/shard_map/ppermute | solution.py:91
  22.3 2.7 %collective-permute-done.9.refs_1_ = f32[2,32,128]{2,1,0:T(8,128)S(1)} collective-permute-done((f32[2,32,128]{2,1,0:T(8,128)S(1)}, f32[2,32,128]{2,1,0:T(8,128)S(1)}, u32[]{:S(2)}, u32[]{:S(2)}) %collective-permute-start.9) | collective-permute-done | bytes 32800 | tf_op jit(solution)/shard_map/ppermute | solution.py:91
  25.1 0.5 %collective-permute-start.10 = (f32[3,32,128]{2,1,0:T(8,128)S(1)}, f32[3,32,128]{2,1,0:T(8,128)S(1)}, u32[]{:S(2)}, u32[]{:S(2)}) collective-permute-start(f32[3,32,128]{2,1,0:T(8,128)S(1)} %get-tuple-element.53.refs_0_), channel_id=1, source_target_pairs={{0,5},{1,4},{2,7},{3,6},{4,1},{5,0},{6,3},{7,2},{8,13},{9,12},{10,... | collective-permute-start | bytes 147464 | tf_op jit(solution)/shard_map/ppermute | solution.py:91
  25.6 3.3 %collective-permute-done.10.refs_1_ = f32[3,32,128]{2,1,0:T(8,128)S(1)} collective-permute-done((f32[3,32,128]{2,1,0:T(8,128)S(1)}, f32[3,32,128]{2,1,0:T(8,128)S(1)}, u32[]{:S(2)}, u32[]{:S(2)}) %collective-permute-start.10) | collective-permute-done | bytes 49184 | tf_op jit(solution)/shard_map/ppermute | solution.py:91
  28.9 1.4 %turn.1 = (f32[32,32,128]{2,1,0:T(8,128)S(1)}, f32[2,32,128]{2,1,0:T(8,128)S(1)}, f32[32,32,128]{2,1,0:T(8,128)S(1)}, f32[32,32,128]{2,1,0:T(8,128)S(1)}) custom-call(f32[3,32,128]{2,1,0:T(8,128)S(1)} %get-tuple-element.53.refs_0_, f32[3,32,128]{2,1,0:T(8,128)S(1)} %collective-permute-done.10.refs_1_, f32[3,32,128]{2,1,0:T(8,128)S(1)} %get-tuple-element.49.refs_2_, ...), custom_call_target="tpu_custom_call" | custom-call | bytes 1536000 | tf_op jit(solution)/shard_map/turn/pallas_call | solution.py:33
  30.3 2.0 %collective-permute-start.11 = (f32[2,32,128]{2,1,0:T(8,128)S(1)}, f32[2,32,128]{2,1,0:T(8,128)S(1)}, u32[]{:S(2)}, u32[]{:S(2)}) collective-permute-start(f32[2,32,128]{2,1,0:T(8,128)S(1)} %get-tuple-element.61.refs_0_), channel_id=1, source_target_pairs={{0,8},{8,0},{16,24},{24,16},{1,9},{9,1},{17,25},{25,17},{2,10},{10... | collective-permute-start | bytes 98312 | tf_op jit(solution)/shard_map/ppermute | solution.py:91
  32.4 1.9 %collective-permute-done.11.refs_1_ = f32[2,32,128]{2,1,0:T(8,128)S(1)} collective-permute-done((f32[2,32,128]{2,1,0:T(8,128)S(1)}, f32[2,32,128]{2,1,0:T(8,128)S(1)}, u32[]{:S(2)}, u32[]{:S(2)}) %collective-permute-start.11) | collective-permute-done | bytes 32800 | tf_op jit(solution)/shard_map/ppermute | solution.py:91
  34.3 2.9 %collective-permute-start.12 = (f32[3,32,128]{2,1,0:T(8,128)S(1)}, f32[3,32,128]{2,1,0:T(8,128)S(1)}, u32[]{:S(2)}, u32[]{:S(2)}) collective-permute-start(f32[3,32,128]{2,1,0:T(8,128)S(1)} %get-tuple-element.64.refs_0_), channel_id=1, source_target_pairs={{0,16},{8,24},{16,0},{24,8},{1,17},{9,25},{17,1},{25,9},{2,18},{10... | collective-permute-start | bytes 147464 | tf_op jit(solution)/shard_map/ppermute | solution.py:91
  37.2 2.2 %collective-permute-done.12.refs_1_ = f32[3,32,128]{2,1,0:T(8,128)S(1)} collective-permute-done((f32[3,32,128]{2,1,0:T(8,128)S(1)}, f32[3,32,128]{2,1,0:T(8,128)S(1)}, u32[]{:S(2)}, u32[]{:S(2)}) %collective-permute-start.12) | collective-permute-done | bytes 49184 | tf_op jit(solution)/shard_map/ppermute | solution.py:91
  39.4 0.9 %finish.1 = f32[32,32,128]{2,1,0:T(8,128)} custom-call(f32[3,32,128]{2,1,0:T(8,128)S(1)} %get-tuple-element.64.refs_0_, f32[3,32,128]{2,1,0:T(8,128)S(1)} %collective-permute-done.12.refs_1_, f32[3,32,128]{2,1,0:T(8,128)S(1)} %get-tuple-element.62.refs_2_, f32[1,32,128]{2,1,0:T(8,128)S(1)} %get-tuple-element.65.refs_3_, ...), custom_call_target="tpu_custom_call" | custom-call | bytes 1024000 | tf_op jit(solution)/shard_map/finish/pallas_call | solution.py:33
  (7 shorter events, 0.2 us)
Async XLA Ops:
  2.9 8.5 %copy-start = (f32[32,32,128]{2,1,0:T(8,128)S(1)}, f32[32,32,128]{2,1,0:T(8,128)}, u32[]{:S(2)}) copy-start(f32[32,32,128]{2,1,0:T(8,128)} %kappa.1) | copy-start | bytes 1572868
  2.9 5.7 %collective-permute-start.3 = (f32[16,32,128]{2,1,0:T(8,128)S(1)}, f32[16,32,128]{2,1,0:T(8,128)S(1)}, u32[]{:S(2)}, u32[]{:S(2)}) collective-permute-start(f32[16,32,128]{2,1,0:T(8,128)S(1)} %get-tuple-element.40.mine.e_mine.refs_6_), channel_id=1, source_target_pairs={{0,1},{1,0},{2,3},{3,2},{4,5},{5,4},{6,7},{7,6},{8,9},{9,8},{10,11... | collective-permute-start | bytes 786440 | tf_op jit(solution)/shard_map/ppermute | solution.py:91
  3.4 10.8 %collective-permute-start = (f32[16,32,128]{2,1,0:T(8,128)S(1)}, f32[16,32,128]{2,1,0:T(8,128)S(1)}, u32[]{:S(2)}, u32[]{:S(2)}) collective-permute-start(f32[16,32,128]{2,1,0:T(8,128)S(1)} %get-tuple-element.37.refs_10_.refs_0_.refs_4_), channel_id=1, source_target_pairs={{0,8},{1,9},{2,10},{3,11},{4,12},{5,13},{6,14},{7,15},{8,0},{9,1},... | collective-permute-start | bytes 786440 | tf_op jit(solution)/shard_map/ppermute | solution.py:84
  6.1 8.1 %collective-permute-start.1 = (f32[11,32,128]{2,1,0:T(8,128)S(1)}, f32[11,32,128]{2,1,0:T(8,128)S(1)}, u32[]{:S(2)}, u32[]{:S(2)}) collective-permute-start(f32[11,32,128]{2,1,0:T(8,128)S(1)} %get-tuple-element.38), channel_id=1, source_target_pairs={{0,1},{1,0},{2,3},{3,2},{4,5},{5,4},{6,7},{7,6},{8,16},{9,17},{10,... | collective-permute-start | bytes 540680 | tf_op jit(solution)/shard_map/ppermute | solution.py:84
  6.3 9.7 %collective-permute-start.2 = (f32[11,32,128]{2,1,0:T(8,128)S(1)}, f32[11,32,128]{2,1,0:T(8,128)S(1)}, u32[]{:S(2)}, u32[]{:S(2)}) collective-permute-start(f32[11,32,128]{2,1,0:T(8,128)S(1)} %get-tuple-element.39), channel_id=1, source_target_pairs={{0,7},{1,2},{2,1},{3,4},{4,3},{5,6},{6,5},{7,0},{8,15},{9,10},{10,... | collective-permute-start | bytes 540680 | tf_op jit(solution)/shard_map/ppermute | solution.py:84
  8.7 6.7 %collective-permute-start.4 = (f32[9,8,128]{2,1,0:T(8,128)S(1)}, f32[9,8,128]{2,1,0:T(8,128)S(1)}, u32[]{:S(2)}, u32[]{:S(2)}) collective-permute-start(f32[9,8,128]{2,1,0:T(8,128)S(1)} %get-tuple-element.43), channel_id=1, source_target_pairs={{0,15},{1,10},{2,9},{3,12},{4,11},{5,14},{6,13},{7,8},{8,7},{9,2},... | collective-permute-start | bytes 110600 | tf_op jit(solution)/shard_map/ppermute | solution.py:84
  11.4 4.0 %collective-permute-start.5 = (f32[9,8,128]{2,1,0:T(8,128)S(1)}, f32[9,8,128]{2,1,0:T(8,128)S(1)}, u32[]{:S(2)}, u32[]{:S(2)}) collective-permute-start(f32[9,8,128]{2,1,0:T(8,128)S(1)} %get-tuple-element.44), channel_id=1, source_target_pairs={{0,1},{1,0},{2,3},{3,2},{4,5},{5,4},{6,7},{7,6},{8,23},{9,18},{10,... | collective-permute-start | bytes 110600 | tf_op jit(solution)/shard_map/ppermute | solution.py:84
  15.4 1.4 %collective-permute-start.6 = (f32[22,8,128]{2,1,0:T(8,128)S(1)}, f32[22,8,128]{2,1,0:T(8,128)S(1)}, u32[]{:S(2)}, u32[]{:S(2)}) collective-permute-start(f32[22,8,128]{2,1,0:T(8,128)S(1)} %rim.1), channel_id=1, source_target_pairs={{0,1},{1,0},{2,3},{3,2},{4,5},{5,4},{6,7},{7,6},{8,9},{9,8},{10,11... | collective-permute-start | bytes 270344 | tf_op jit(solution)/shard_map/ppermute | solution.py:84
  15.5 5.1 %collective-permute-start.8 = (f32[5,32,128]{2,1,0:T(8,128)S(1)}, f32[5,32,128]{2,1,0:T(8,128)S(1)}, u32[]{:S(2)}, u32[]{:S(2)}) collective-permute-start(f32[5,32,128]{2,1,0:T(8,128)S(1)} %get-tuple-element.45._.refs_0_), channel_id=1, source_target_pairs={{0,3},{1,2},{2,1},{3,0},{4,7},{5,6},{6,5},{7,4},{8,11},{9,10},{10,... | collective-permute-start | bytes 245768 | tf_op jit(solution)/shard_map/ppermute | solution.py:91
  20.3 1.3 %collective-permute-start.7 = (f32[2,32,128]{2,1,0:T(8,128)S(1)}, f32[2,32,128]{2,1,0:T(8,128)S(1)}, u32[]{:S(2)}, u32[]{:S(2)}) collective-permute-start(f32[2,32,128]{2,1,0:T(8,128)S(1)} %get-tuple-element.48.refs_0_), channel_id=1, source_target_pairs={{0,1},{1,0},{2,3},{3,2},{4,5},{5,4},{6,7},{7,6},{8,9},{9,8},{10,11... | collective-permute-start | bytes 98312 | tf_op jit(solution)/shard_map/ppermute | solution.py:91
  21.6 3.4 %collective-permute-start.9 = (f32[2,32,128]{2,1,0:T(8,128)S(1)}, f32[2,32,128]{2,1,0:T(8,128)S(1)}, u32[]{:S(2)}, u32[]{:S(2)}) collective-permute-start(f32[2,32,128]{2,1,0:T(8,128)S(1)} %get-tuple-element.51.refs_0_), channel_id=1, source_target_pairs={{0,3},{1,2},{2,1},{3,0},{4,7},{5,6},{6,5},{7,4},{8,11},{9,10},{10,... | collective-permute-start | bytes 98312 | tf_op jit(solution)/shard_map/ppermute | solution.py:91
  25.1 3.8 %collective-permute-start.10 = (f32[3,32,128]{2,1,0:T(8,128)S(1)}, f32[3,32,128]{2,1,0:T(8,128)S(1)}, u32[]{:S(2)}, u32[]{:S(2)}) collective-permute-start(f32[3,32,128]{2,1,0:T(8,128)S(1)} %get-tuple-element.53.refs_0_), channel_id=1, source_target_pairs={{0,5},{1,4},{2,7},{3,6},{4,1},{5,0},{6,3},{7,2},{8,13},{9,12},{10,... | collective-permute-start | bytes 147464 | tf_op jit(solution)/shard_map/ppermute | solution.py:91
  30.3 4.0 %collective-permute-start.11 = (f32[2,32,128]{2,1,0:T(8,128)S(1)}, f32[2,32,128]{2,1,0:T(8,128)S(1)}, u32[]{:S(2)}, u32[]{:S(2)}) collective-permute-start(f32[2,32,128]{2,1,0:T(8,128)S(1)} %get-tuple-element.61.refs_0_), channel_id=1, source_target_pairs={{0,8},{8,0},{16,24},{24,16},{1,9},{9,1},{17,25},{25,17},{2,10},{10... | collective-permute-start | bytes 98312 | tf_op jit(solution)/shard_map/ppermute | solution.py:91
  34.3 5.1 %collective-permute-start.12 = (f32[3,32,128]{2,1,0:T(8,128)S(1)}, f32[3,32,128]{2,1,0:T(8,128)S(1)}, u32[]{:S(2)}, u32[]{:S(2)}) collective-permute-start(f32[3,32,128]{2,1,0:T(8,128)S(1)} %get-tuple-element.64.refs_0_), channel_id=1, source_target_pairs={{0,16},{8,24},{16,0},{24,8},{1,17},{9,25},{17,1},{25,9},{2,18},{10... | collective-permute-start | bytes 147464 | tf_op jit(solution)/shard_map/ppermute | solution.py:91

commit v4 on v3

v4 whole, which is shorter than its diff:
```python
import jax
import jax.numpy as jnp
from jax import lax
from jax.experimental import pallas as pl
from jax.experimental.pallas import tpu as pltpu
from jax.sharding import PartitionSpec as P

NSUB = 4
RATE = 500.0
AXES = ("gz", "gy")
F32 = jnp.float32
VMEM_BYTES = 12 << 20


def near(*dims):
    return pltpu.VMEM(dims, F32)


def far(*dims):
    return pltpu.HBM(dims, F32)


def call(kernel, name, outs, operands, scratch=(), cycles=0):
    whole, away = pl.BlockSpec(memory_space=pltpu.VMEM), pl.BlockSpec(memory_space=pltpu.HBM)
    inputs, in_specs = [], []
    for operand in operands:
        where, x = operand if isinstance(operand, tuple) else ("near", operand)
        if where != "plain":
            x = pltpu.with_memory_space_constraint(x, pltpu.VMEM if where == "near" else pltpu.HBM)
        inputs.append(x)
        in_specs.append(away if where == "far" else whole)
    out_specs = [away if isinstance(out, tuple) else whole for out in outs]
    result = pl.pallas_call(
        kernel,
        out_shape=[out[1] if isinstance(out, tuple) else out for out in outs],
        in_specs=in_specs,
        out_specs=out_specs,
        scratch_shapes=scratch,
        compiler_params=pltpu.CompilerParams(vmem_limit_bytes=VMEM_BYTES),
        cost_estimate=pl.CostEstimate(flops=0, bytes_accessed=cycles * 1024, transcendentals=0) if cycles else None,
        name=name,
    )(*inputs)
    return result if len(outs) > 1 else result[0]


def place():
    return (
        lax.axis_index("gz"),
        lax.axis_index("gy"),
        lax.axis_size("gz"),
        lax.axis_size("gy"),
    )


def pair_up(index):
    return index ^ 1


def same(index):
    return index


def z_other(index):
    return index + 1 if index % 2 else index - 1


def y_other(index):
    return (index + 1 if index % 2 else index - 1) % lax.axis_size("gy")


def permutation(z_partner, y_partner):
    z_count, y_count = lax.axis_size("gz"), lax.axis_size("gy")
    pairs = []
    for z in range(z_count):
        for y in range(y_count):
            to_z, to_y = z_partner(z), y_partner(y)
            if not 0 <= to_z < z_count:
                to_z, to_y = z, pair_up(y)
            pairs.append((z * y_count + y, to_z * y_count + to_y))
    return pairs


def send(x, z_partner=same, y_partner=same):
    return lax.ppermute(x, AXES, permutation(z_partner, y_partner))


def swap(x, axis, level):
    step = 1 << level
    if axis == "gy":
        step |= 1
    return lax.ppermute(x, axis, [(i, i ^ step) for i in range(lax.axis_size(axis))])


def levels_of(axis):
    return (lax.axis_size(axis) - 1).bit_length()


def begin_kernel(tracer, y_speed, z_speed, kappa_far, a_ref, b_ref, o_ref, e_ref, c, ys, zs, kappa, kappa_y, r_y, sem):
    arrivals = [
        pltpu.make_async_copy(source, target, sem.at[k])
        for k, (source, target) in enumerate(((kappa_far, kappa), (tracer, c), (z_speed, zs), (y_speed, ys)))
    ]
    for copy in arrivals:
        copy.start()
    z, y, _, y_count = place()
    depth, width, _ = c.shape
    z_odd, y_odd = lax.rem(z, 2), lax.rem(y, 2)
    arrivals[0].wait()
    ports = e_ref.at[11:16]
    kappa_y[...] = turned(kappa[...])
    ports[3], ports[4] = resistances(kappa_y, r_y)
    factor(((lambda j: r_y[j], width, *outer(ports, y, y_count), None, ports),))
    for copy in arrivals[1:]:
        copy.wait()
    for ref, low in ((a_ref, z_odd), (b_ref, 1 - z_odd)):
        four, three = (1 - low) * (depth - 4), (1 - low) * (depth - 3)
        ref[0:4] = c[pl.ds(four, 4)]
        ref[4:8] = zs[pl.ds(four, 4)]
        ref[8:11] = ys[pl.ds(three, 3)]

    def rims(o_low):
        for ref, low in ((o_ref, o_low), (e_ref, not o_low)):
            tile = slice(0, 8) if low else slice(width - 8, width)
            four, three = (0, 0) if low else (4, 5)
            ref[0:4] = turned(c[:, tile, :])[four : four + 4]
            ref[4:8] = turned(ys[:, tile, :])[four : four + 4]
            ref[8:11] = turned(zs[:, tile, :])[three : three + 3]

    @pl.when(y_odd == 0)
    def _():
        rims(True)

    @pl.when(y_odd == 1)
    def _():
        rims(False)


def begin(tracer, y_speed, z_speed, kappa):
    depth, width, band = tracer.shape
    return call(
        begin_kernel,
        "begin",
        [near(11, width, band)] * 2 + [near(11, depth, band), near(16, depth, band)],
        [("far", x) for x in (tracer, y_speed, z_speed, kappa)],
        scratch=[near(depth, width, band)] * 4 + [near(width, depth, band)] * 2 + [pltpu.SemaphoreType.DMA((4,))],
        cycles=2000,
    )


RIM_ROWS = 22


def rim_kernel(a, b, _, for_pair, for_other):
    z, y, _, _ = place()
    width = a.shape[1]
    z_odd, y_odd = lax.rem(z, 2) == 1, lax.rem(y, 2)
    start = pl.multiple_of((1 - y_odd) * (width - 8), 8)

    def corners(first):
        for f, (row, count) in enumerate(((0, 4), (8, 3), (4, 4))):
            for k in range(3):
                column_a, column_b = (ref[row : row + count, first + k, :] for ref in (a, b))
                for_other[3 * f + k, 4 - count : 4, :] = jnp.where(z_odd, column_a, column_b)
                for_other[3 * f + k, 4 : 4 + count, :] = jnp.where(z_odd, column_b, column_a)

    for tile in range(3, 6):
        for_other[tile] = jnp.zeros(for_other.shape[1:], F32)

    @pl.when(y_odd == 0)
    def _():
        corners(0)

    @pl.when(y_odd == 1)
    def _():
        corners(width - 3)

    for half, ref in enumerate((a, b)):
        for k in range(11):
            for_pair[11 * half + k] = ref[k, pl.ds(start, 8), :]


def rim(a, b, after):
    band = a.shape[2]
    return call(rim_kernel, "rim", [near(22, 8, band), near(9, 8, band)], [a, b, after], cycles=200)


def reciprocal(x):
    r = pl.reciprocal(x, approx=True)
    return r * (2.0 - x * r)


def turned(x):
    return jnp.swapaxes(x, 0, 1)


def resistances(kappa, r):
    count = kappa.shape[0]
    before, following = kappa[0], kappa[1]
    r[0] = jnp.zeros_like(before)
    for j in range(1, count):
        here = following
        if j + 1 < count:
            following = kappa[j + 1]
        r[j] = reciprocal((0.5 * RATE) * (before + here))
        before = here
    return kappa[0], before


def factor(sides):
    state = []
    for read, count, edge_low, edge_high, keep, _ in sides:
        one = jnp.ones_like(edge_low)
        if keep:
            keep[0][0] = one
            keep[1][count - 1] = one
        state.append([one, 1.0 + edge_low, one, 1.0 + edge_high])

    def faces(j):
        return [(read(j), read(count - j)) if j < count else None for read, count, _, _, _, _ in sides]

    longest = max(side[1] for side in sides)
    following = faces(1)
    for j in range(1, longest):
        here, following = following, faces(j + 1)
        for s, pair in zip(state, here):
            if pair is not None:
                s[0] = s[0] + pair[0] * s[1]
                s[1] = s[1] + s[0]
                s[2] = s[2] + pair[1] * s[3]
                s[3] = s[3] + s[2]
        for (_, count, _, _, keep, _), s, pair in zip(sides, state, here):
            if pair is not None and keep:
                keep[0][j] = s[0]
                keep[1][count - 1 - j] = s[2]
    for (_, _, _, edge_high, _, ports), s in zip(sides, state):
        if ports is not None:
            inverse = reciprocal(s[1] + edge_high * s[0])
            ports[0] = s[2] * inverse
            ports[1] = inverse
            ports[2] = s[0] * inverse


def outer(ports, index, count):
    return jnp.where(index == 0, RATE, 0.0) * ports[3], jnp.where(index == count - 1, RATE, 0.0) * ports[4]


def factor_kernel(kappa, r_y_far, r_z_far, ports_z, kappa_y, r_y, r_z, sem):
    z, _, z_count, _ = place()
    depth = kappa.shape[0]
    y_copy = pltpu.make_async_copy(r_y, r_y_far, sem.at[0])
    z_copy = pltpu.make_async_copy(r_z, r_z_far, sem.at[1])
    ports_z[3], ports_z[4] = resistances(kappa, r_z)
    z_copy.start()
    kappa_y[...] = turned(kappa[...])
    resistances(kappa_y, r_y)
    y_copy.start()
    factor(((lambda j: r_z[j], depth, *outer(ports_z, z, z_count), None, ports_z),))
    y_copy.wait()
    z_copy.wait()


def factor_lines(kappa):
    depth, width, band = kappa.shape
    along_y, along_z = (width, depth, band), (depth, width, band)
    return call(
        factor_kernel,
        "factor",
        [("far", far(*along_y)), ("far", far(*along_z)), near(5, width, band)],
        [("plain", kappa)],
        scratch=[near(*along_y), near(*along_y), near(*along_z), pltpu.SemaphoreType.DMA((2,))],
        cycles=4000,
    )


def ports_kernel(axis, level, first_row, mine, theirs, out, joint):
    is_left = (lax.shift_right_logical(lax.axis_index(axis), level) & 1) == 0
    pairs = [(mine[first_row + k], theirs[first_row + k]) for k in range(5)]
    left = [jnp.where(is_left, m, t) for m, t in pairs]
    right = [jnp.where(is_left, t, m) for m, t in pairs]
    d = reciprocal(reciprocal((0.5 * RATE) * (left[4] + right[3])) + left[2] + right[0])
    out[0] = left[0] - left[1] * left[1] * d
    out[1] = left[1] * right[1] * d
    out[2] = right[2] - right[1] * right[1] * d
    out[3] = left[3]
    out[4] = right[4]
    joint[0] = d
    joint[1] = left[1]
    joint[2] = right[1]


def join_ports(mine, theirs, axis, level, first_row=0):
    _, lines, band = mine.shape

    def kernel(*refs):
        ports_kernel(axis, level, first_row, *refs)

    return call(kernel, "join_ports", [near(5, lines, band), near(3, lines, band)], [mine, theirs], cycles=100)


def join_levels(ports, axis, done):
    joints = []
    for level in range(done, levels_of(axis) - 1):
        ports, joint = join_ports(ports, swap(ports, axis, level), axis, level)
        joints.append(joint)
    return ports, joints


def source_kernel(axis, level, mine, theirs, joint, *refs):
    *ports, out, flow_ref = refs
    index = lax.axis_index(axis)
    is_left = (lax.shift_right_logical(index, level) & 1) == 0
    pairs = [(mine[k], theirs[k]) for k in range(2)]
    left = [jnp.where(is_left, m, t) for m, t in pairs]
    right = [jnp.where(is_left, t, m) for m, t in pairs]
    flow = (left[1] - right[0]) * joint[0]
    flow_ref[0] = flow
    low, high = left[0] - joint[1] * flow, right[1] + joint[2] * flow
    if not ports:
        out[0] = low
        out[1] = high
        return
    ports = ports[0]
    next_left = (lax.shift_right_logical(index, level + 1) & 1) == 0
    out[0] = jnp.where(next_left, high, low)
    out[1] = jnp.where(next_left, ports[2], ports[0])
    out[2] = jnp.where(next_left, ports[4], ports[3])


def join_sources(mine, theirs, joint, ports, axis, level):
    _, lines, band = mine.shape
    last = [ports] if level + 2 == levels_of(axis) else []

    def kernel(*refs):
        source_kernel(axis, level, *refs)

    outs = [near(3 if last else 2, lines, band), near(1, lines, band)]
    return call(kernel, "join_sources", outs, [mine, theirs, joint, *last], cycles=100)


def end_currents(axis, mine, theirs, joints, flows):
    index = lax.axis_index(axis)
    level = len(joints)
    is_left = (lax.shift_right_logical(index, level) & 1) == 0
    d = reciprocal(reciprocal((0.5 * RATE) * (mine[2] + theirs[2])) + mine[1] + theirs[1])
    flow = (mine[0] - theirs[0]) * d
    zero = jnp.zeros_like(flow)
    low, high = jnp.where(is_left, zero, -flow), jnp.where(is_left, -flow, zero)
    for level in range(level - 1, -1, -1):
        joint = joints[level]
        is_left = (lax.shift_right_logical(index, level) & 1) == 0
        flow = flows[level][0] + (joint[1] * low - joint[2] * high) * joint[0]
        low, high = jnp.where(is_left, low, flow), jnp.where(is_left, -flow, high)
    return low, high


def solve_open(values, phi, psi, scale, base, ports):
    count = base.shape[0]
    total = jnp.zeros(base.shape[1:], F32)
    following = (values[0], phi[0], psi[0])
    for j in range(count):
        value, low, high = following
        if j + 1 < count:
            following = (values[j + 1], phi[j + 1], psi[j + 1])
        total = total + low * value
        base[j] = high * total
    ports[1] = scale * total
    total = jnp.zeros(base.shape[1:], F32)
    following = (base[count - 1], values[count - 1], phi[count - 1], psi[count - 1])
    for j in range(count - 1, -1, -1):
        below, value, low, high = following
        if j > 0:
            following = (base[j - 1], values[j - 1], phi[j - 1], psi[j - 1])
        base[j] = scale * (below + low * total)
        total = total + high * value
    ports[0] = scale * total


def advect_kernel(
    tracer, y_speed, z_speed, a, b, o, e, corner, ab, e_mine, r_y_far, r_z_far, ports_z,
    base, sources, r_y, r_z, ports_out, c, ys, zs, sy, sz, phi, psi, kept, sem,
):
    z, y, z_count, y_count = place()
    depth, width, band = tracer.shape
    rows, cols = depth + 8, width + 8
    copies = [
        pltpu.make_async_copy(own, field.at[pl.ds(4, depth), pl.ds(0, width), :], sem.at[k])
        for k, (field, own) in enumerate(((ys, y_speed), (zs, z_speed), (c, tracer)))
    ]
    y_copy = pltpu.make_async_copy(r_y_far, r_y, sem.at[3])
    z_copy = pltpu.make_async_copy(r_z_far, r_z, sem.at[4])
    y_copy.start()
    for copy in copies:
        copy.start()
    z_copy.start()
    ports_out[...] = ports_z[...]
    z_odd, y_odd = lax.rem(z, 2), lax.rem(y, 2)
    keep_b = jnp.where((z_odd == 0) & (z == 0) | (z_odd == 1) & (z == z_count - 1), 0.0, 1.0)
    keep_o = jnp.where((y_odd == 0) & (y == 0) | (y_odd == 1) & (y == y_count - 1), 0.0, 1.0)
    keep_below = keep_o * jnp.where(z_odd == 0, keep_b, 1.0)
    keep_above = keep_o * jnp.where(z_odd == 1, keep_b, 1.0)
    column = lax.broadcasted_iota(jnp.int32, (8, band), 0)
    outside = (column < 4) & (y == y_count - 1) | (column >= 4) & (y == 0)
    inside = jnp.where(outside, 0.0, 1.0)

    for field in (c, ys, zs):
        field[0:4, width:cols, :] = jnp.zeros((4, 8, band), F32)
        field[4 + depth : rows, width:cols, :] = jnp.zeros((4, 8, band), F32)
    ys[0:1, 0:width, :] = jnp.zeros((1, width, band), F32)
    ys[rows - 1 : rows, 0:width, :] = jnp.zeros((1, width, band), F32)
    for ref, low, keep in ((a, z_odd, None), (b, 1 - z_odd, keep_b)):
        scale = (lambda v: v) if keep is None else (lambda v: v * keep)
        four = jnp.where(low == 1, 0, depth + 4)
        three = jnp.where(low == 1, 1, depth + 4)
        c[pl.ds(four, 4), 0:width, :] = scale(ref[0:4])
        zs[pl.ds(four, 4), 0:width, :] = scale(ref[4:8])
        ys[pl.ds(three, 3), 0:width, :] = scale(ref[8:11])

    def sides(o_low):
        def columns(first, count):
            other, pair = o[first : first + count] * keep_o, e[first : first + count]
            above, below = (pair, other) if o_low else (other, pair)
            empty = [jnp.zeros((4 - count, depth, band), F32)] if count < 4 else []
            return turned(jnp.concatenate([above, *empty, *empty, below], axis=0))

        c[4 : 4 + depth, width:cols, :] = columns(0, 4)
        ys[4 : 4 + depth, width:cols, :] = columns(4, 4)
        zs[4 : 4 + depth, width:cols, :] = columns(8, 3)

        def from_pair(half, z_low):
            start = width if o_low else width + 4
            first = 0 if o_low else 4
            zr = 0 if z_low else depth + 4
            z3 = 1 if z_low else depth + 4
            keep = 1.0 if half == 0 else keep_b
            for k in range(11):
                field, row = ((c, zr + k), (zs, zr + k - 4), (ys, z3 + k - 8))[k // 4]
                field[row, start : start + 4, :] = ab[11 * half + k, first : first + 4, :] * keep

        start = width + (5 if o_low else 0)
        for f, (field, count) in enumerate(((c, 4), (ys, 3), (zs, 4))):
            for k in range(3):
                below, above = corner[3 * f + k, 4 - count : 4, :], corner[3 * f + k, 4 : 4 + count, :]
                field[4 - count : 4, start + k, :] = below * keep_below
                field[depth + 4 : depth + 4 + count, start + k, :] = above * keep_above

        @pl.when(z_odd == 0)
        def _():
            from_pair(0, False)
            from_pair(1, True)

        @pl.when(z_odd == 1)
        def _():
            from_pair(0, True)
            from_pair(1, False)

    @pl.when(y_odd == 0)
    def _():
        sides(True)

    @pl.when(y_odd == 1)
    def _():
        sides(False)

    y_copy.wait()
    factor(((lambda j: r_y[j], width, *outer(e_mine.at[11:16], y, y_count), (phi, psi), None),))
    for copy in copies[:2]:
        copy.wait()

    def up(v):
        return pltpu.roll(v, cols - 1, 0)

    def down(v):
        return pltpu.roll(v, 1, 0)

    def flux(speed, here, after):
        return speed * jnp.where(speed > 0.0, here, after)

    def faces(r, before):
        v = ys[r]
        sy[r] = 0.5 * (v + up(v))
        after = zs[r + 1]
        sz[r] = 0.5 * (before + after)
        return after

    lax.fori_loop(0, rows - 1, faces, zs[0], unroll=3)
    copies[2].wait()

    keep_low = jnp.where(z == 0, 0.0, 1.0)
    keep_high = jnp.where(z == z_count - 1, 0.0, 1.0)
    for step in range(1, NSUB + 1):
        here = c[step]

        def row(r, carry):
            here, below = carry
            after = c[r + 1]
            above = flux(sz[r], here, after)
            across = flux(sy[r], here, up(here))
            new = here - (across - down(across)) - (above - below)
            c[r, 0:width, :] = new[0:width]
            c[r, width:cols, :] = new[width:cols] * inside
            return after, above

        lax.fori_loop(step, rows - step, row, (here, flux(sz[step - 1], c[step - 1], here)), unroll=4)
        if step < NSUB:
            c[3] = c[3] * keep_low
            c[4 + depth] = c[4 + depth] * keep_high

    z_copy.wait()
    kept[...] = turned(c[4 : 4 + depth, 0:width, :])
    solve_open(kept, phi, psi, e_mine[12], base, sources)


def advect(tracer, y_speed, z_speed, halos, ports_y, r_y, r_z, ports_z):
    depth, width, band = tracer.shape
    padded = near(depth + 8, width + 8, band)
    along_y, along_z = near(width, depth, band), near(depth, width, band)
    return call(
        advect_kernel,
        "advect",
        [along_y, near(2, depth, band), along_y, along_z, near(5, width, band)],
        [("far", x) for x in (tracer, y_speed, z_speed)]
        + list(halos)
        + [ports_y, ("far", r_y), ("far", r_z), ports_z],
        scratch=[padded] * 5 + [along_y] * 3 + [pltpu.SemaphoreType.DMA((5,))],
        cycles=5000,
    )


def turn_kernel(levels, *refs):
    mine, theirs = refs[0:2]
    joints, flows = refs[2 : 2 + levels], refs[2 + levels : 2 + 2 * levels]
    ports_y, base_y, r_y, ports_z, r_z, _, base, sources, phi, psi, u, kept = refs[2 + 2 * levels :]
    z, y, z_count, y_count = place()
    width, depth = base_y.shape[0], base.shape[0]
    ports_y = ports_y.at[11:16]
    low, high = end_currents("gy", mine, theirs, joints, flows)
    edge, _ = outer(ports_y, y, y_count)
    value = low * ports_y[0] + high * ports_y[1]
    current = (1.0 + edge) * value - low
    u[0] = base_y[0] + value
    following = (r_y[1], base_y[1])
    for j in range(1, width):
        (r, own), following = following, (r_y[j + 1], base_y[j + 1]) if j + 1 < width else None
        value = value + r * current
        current = current + value
        u[j] = own + value
    factor(((lambda k: r_z[k], depth, *outer(ports_z, z, z_count), (phi, psi), None),))
    kept[...] = turned(u[...])
    solve_open(kept, phi, psi, ports_z[1], base, sources)


def turn(mine, theirs, joints, flows, ports_y, base_y, r_y, ports_z, r_z, after):
    width, depth, band = base_y.shape
    along_z = near(depth, width, band)

    def kernel(*refs):
        turn_kernel(len(joints), *refs)

    return call(
        kernel,
        "turn",
        [along_z, near(2, width, band), along_z, along_z],
        [mine, theirs, *joints, *flows, ports_y, base_y, r_y, ports_z, r_z, after],
        scratch=[near(width, depth, band), along_z],
        cycles=1500,
    )


def finish_kernel(levels, *refs):
    mine, theirs = refs[0:2]
    joints, flows = refs[2 : 2 + levels], refs[2 + levels : 2 + 2 * levels]
    ports_z, base, phi, psi, out, u, sem = refs[2 + 2 * levels :]
    low, high = end_currents("gz", mine, theirs, joints, flows)
    scale = ports_z[1]
    low, high = low * scale, high * scale
    depth = base.shape[0]
    part = depth // 4
    copies = []
    for p in range(4):
        for k in range(p * part, (p + 1) * part):
            u[k] = base[k] + low * psi[k] + high * phi[k]
        block = pl.ds(p * part, part)
        copies.append(pltpu.make_async_copy(u.at[block], out.at[block], sem.at[p]))
        copies[-1].start()
    for copy in copies:
        copy.wait()


def finish(mine, theirs, joints, flows, ports_z, base, phi, psi):
    def kernel(*refs):
        finish_kernel(len(joints), *refs)

    return call(
        kernel,
        "finish",
        [("far", jax.ShapeDtypeStruct(base.shape, F32))],
        [mine, theirs, *joints, *flows, ports_z, base, phi, psi],
        scratch=[near(*base.shape), pltpu.SemaphoreType.DMA((4,))],
        cycles=1000,
    )


def exchange_sources(sources, ports, joints, axis):
    flows = []
    for level, joint in enumerate(joints):
        theirs = swap(sources, axis, level)
        sources, flow = join_sources(sources, theirs, joint, ports, axis, level)
        flows.append(flow)
    return sources, swap(sources, axis, len(joints)), flows


def local(tracer, y_speed, z_speed, kappa):
    a, b, o, e_mine = begin(tracer, y_speed, z_speed, kappa)
    e = swap(e_mine, "gy", 0)
    a = send(a, z_partner=pair_up)
    b = send(b, z_partner=z_other)
    o = send(o, y_partner=y_other)
    r_y, r_z, ports_z = factor_lines(kappa)
    for_pair, for_other = rim(a, b, ports_z)
    corner = send(for_other, y_partner=y_other)
    ab = swap(for_pair, "gy", 0)

    joined_y, joint_y = join_ports(e_mine, e, "gy", 0, first_row=11)
    joined_y, joints = join_levels(joined_y, "gy", 1)
    joints_y = [joint_y] + joints

    base, sources, r_y, r_z, ports_z = advect(
        tracer, y_speed, z_speed, (a, b, o, e, corner, ab), e_mine, r_y, r_z, ports_z
    )
    joined_z, joints_z = join_levels(ports_z, "gz", 0)
    mine, theirs, flows = exchange_sources(sources, joined_y, joints_y, "gy")
    base, sources, phi_z, psi_z = turn(
        mine, theirs, joints_y, flows, e_mine, base, r_y, ports_z, r_z, joints_z[-1]
    )
    mine, theirs, flows = exchange_sources(sources, joined_z, joints_z, "gz")
    return finish(mine, theirs, joints_z, flows, ports_z, base, phi_z, psi_z)


def solution(mesh):
    spec = P("gz", "gy", None)
    return jax.shard_map(
        local, mesh=mesh, in_specs=(spec,) * 4, out_specs=spec, check_vma=False
    )
```

time: 40.4 us -> 38.7 us (0.958)
  Pallas kernels: 11.7 us -> 7.81 us
  starting transfers between devices: 15.4 us -> 18.4 us
  waiting for transfers between devices: 13.1 us -> 12.2 us
    pallas_call x12, Pallas kernels: 11.7 us -> 7.81 us  [call(): pl.pallas_call(kernel, out_shape=[out[1] if isinstance(out, tuple) else o...]
    ppermute x7 -> x9, starting transfers between devices: 7.33 us -> 10.5 us  [swap(): lax.ppermute(x, axis, [(i, i ^ step) for i in range(lax.axis_size(axis))])]
    ppermute x7 -> x9, waiting for transfers between devices: 11.2 us -> 9.42 us  [swap(): lax.ppermute(x, axis, [(i, i ^ step) for i in range(lax.axis_size(axis))])]
    ppermute x6 -> x4, waiting for transfers between devices: 1.99 us -> 2.78 us  [send(): return lax.ppermute(x, AXES, permutation(z_partner, y_partner))]
    ppermute x6 -> x4, starting transfers between devices: 8.02 us -> 7.94 us  [send(): return lax.ppermute(x, AXES, permutation(z_partner, y_partner))]
  transfers between devices with their start and end apart: 13 -> 13, of which waited for: 7 -> 7; matrix products, arithmetic and copies ran while one was open for 0% -> 0% of each run, Pallas kernels for 16% -> 12%
where the time goes in v4:
time: 38.7 us; the launch traced here: 38.5 us
  starting transfers between devices  18.4 us (48%)
  waiting for transfers between devices  12.2 us (32%)
  Pallas kernels  7.81 us (20%)
    ppermute x9, starting transfers between devices, swap(): lax.ppermute(x, axis, [(i, i ^ step) for i in range(lax.axis_size(axis))])  10.5 us
    ppermute x9, waiting for transfers between devices, swap(): lax.ppermute(x, axis, [(i, i ^ step) for i in range(lax.axis_size(axis))])  9.42 us
    ppermute x4, starting transfers between devices, send(): return lax.ppermute(x, AXES, permutation(z_partner, y_partner))  7.94 us
    pallas_call x12, Pallas kernels, call(): pl.pallas_call(kernel, out_shape=[out[1] if isinstance(out, tuple) else o...  7.81 us
    ppermute x4, waiting for transfers between devices, send(): return lax.ppermute(x, AXES, permutation(z_partner, y_partner))  2.78 us
  transfers between devices with their start and end apart: 13, of which 7 were waited for; matrix products, arithmetic and copies ran while one was open for 0% of the time, Pallas kernels for 12%

profile of v4, /device:TPU:0, one launch (start us, length us, event | category | flops | bytes accessed | tf_op | source)
XLA Modules:
  0.0 38.5 jit_solution(11799092977253162826)
XLA Ops:
  0.0 0.0 copy-start
  0.0 1.7 %begin.1 = (f32[11,32,128]{2,1,0:T(8,128)S(1)}, f32[11,32,128]{2,1,0:T(8,128)S(1)}, f32[11,32,128]{2,1,0:T(8,128)S(1)}, f32[16,32,128]{2,1,0:T(8,128)S(1)}) custom-call(f32[32,32,128]{2,1,0:T(8,128)} %tracer.3, f32[32,32,128]{2,1,0:T(8,128)} %y_speed.3, f32[32,32,128]{2,1,0:T(8,128)} %z_speed.3, f32[32,32,128]{2,1,0:T(8,128)} %kappa.1), custom_call_target="tpu_custom_call" | custom-call | bytes 2048000 | tf_op jit(solution)/shard_map/begin/pallas_call | solution.py:33
  1.7 0.5 %collective-permute-start.3 = (f32[16,32,128]{2,1,0:T(8,128)S(1)}, f32[16,32,128]{2,1,0:T(8,128)S(1)}, u32[]{:S(2)}, u32[]{:S(2)}) collective-permute-start(f32[16,32,128]{2,1,0:T(8,128)S(1)} %get-tuple-element.38.e_mine.refs_0_.refs_6_), channel_id=1, source_target_pairs={{0,1},{1,0},{2,3},{3,2},{4,5},{5,4},{6,7},{7,6},{8,9},{9,8},{10,11... | collective-permute-start | bytes 786440 | tf_op jit(solution)/shard_map/ppermute | solution.py:91
  2.3 2.6 %collective-permute-start = (f32[11,32,128]{2,1,0:T(8,128)S(1)}, f32[11,32,128]{2,1,0:T(8,128)S(1)}, u32[]{:S(2)}, u32[]{:S(2)}) collective-permute-start(f32[11,32,128]{2,1,0:T(8,128)S(1)} %get-tuple-element.35), channel_id=1, source_target_pairs={{0,8},{1,9},{2,10},{3,11},{4,12},{5,13},{6,14},{7,15},{8,0},{9,1},... | collective-permute-start | bytes 540680 | tf_op jit(solution)/shard_map/ppermute | solution.py:84
  4.9 0.2 collective-permute-start.1
  5.1 2.4 %collective-permute-start.2 = (f32[11,32,128]{2,1,0:T(8,128)S(1)}, f32[11,32,128]{2,1,0:T(8,128)S(1)}, u32[]{:S(2)}, u32[]{:S(2)}) collective-permute-start(f32[11,32,128]{2,1,0:T(8,128)S(1)} %get-tuple-element.37), channel_id=1, source_target_pairs={{0,7},{1,2},{2,1},{3,4},{4,3},{5,6},{6,5},{7,0},{8,15},{9,10},{10,... | collective-permute-start | bytes 540680 | tf_op jit(solution)/shard_map/ppermute | solution.py:84
  7.5 0.0 copy-done
  7.5 1.1 %factor.1 = (f32[32,32,128]{2,1,0:T(8,128)}, f32[32,32,128]{2,1,0:T(8,128)}, f32[5,32,128]{2,1,0:T(8,128)S(1)}) custom-call(f32[32,32,128]{2,1,0:T(8,128)S(1)} %copy-done), custom_call_target="tpu_custom_call" | custom-call | bytes 4096000 | tf_op jit(solution)/shard_map/factor/pallas_call | solution.py:33
  8.6 1.5 %collective-permute-done.a = f32[11,32,128]{2,1,0:T(8,128)S(1)} collective-permute-done((f32[11,32,128]{2,1,0:T(8,128)S(1)}, f32[11,32,128]{2,1,0:T(8,128)S(1)}, u32[]{:S(2)}, u32[]{:S(2)}) %collective-permute-start) | collective-permute-done | bytes 180256 | tf_op jit(solution)/shard_map/ppermute | solution.py:84
  10.1 0.0 collective-permute-done.1.b
  10.1 0.1 collective-permute-start.5
  10.2 2.7 %collective-permute-start.4 = (f32[9,8,128]{2,1,0:T(8,128)S(1)}, f32[9,8,128]{2,1,0:T(8,128)S(1)}, u32[]{:S(2)}, u32[]{:S(2)}) collective-permute-start(f32[9,8,128]{2,1,0:T(8,128)S(1)} %get-tuple-element.40), channel_id=1, source_target_pairs={{0,7},{1,2},{2,1},{3,4},{4,3},{5,6},{6,5},{7,0},{8,15},{9,10},{10,... | collective-permute-start | bytes 110600 | tf_op jit(solution)/shard_map/ppermute | solution.py:84
  12.9 0.0 collective-permute-done.3.e.refs_1_
  13.0 0.3 collective-permute-start.8
  13.2 0.0 collective-permute-done.2.o
  13.2 1.3 %collective-permute-done.4.corner = f32[9,8,128]{2,1,0:T(8,128)S(1)} collective-permute-done((f32[9,8,128]{2,1,0:T(8,128)S(1)}, f32[9,8,128]{2,1,0:T(8,128)S(1)}, u32[]{:S(2)}, u32[]{:S(2)}) %collective-permute-start.4) | collective-permute-done | bytes 36896 | tf_op jit(solution)/shard_map/ppermute | solution.py:84
  14.6 0.0 collective-permute-done.5.ab
  14.6 3.4 %advect.1 = (f32[32,32,128]{2,1,0:T(8,128)S(1)}, f32[2,32,128]{2,1,0:T(8,128)S(1)}, f32[32,32,128]{2,1,0:T(8,128)S(1)}, f32[32,32,128]{2,1,0:T(8,128)S(1)}, f32[5,32,128]{2,1,0:T(8,128)S(1)}) custom-call(f32[32,32,128]{2,1,0:T(8,128)} %tracer.3, f32[32,32,128]{2,1,0:T(8,128)} %y_speed.3, f32[32,32,128]{2,1,0:T(8,128)} %z_speed.3, ...), custom_call_target="tpu_custom_call" | custom-call | bytes 5120000 | tf_op jit(solution)/shard_map/advect/pallas_call | solution.py:33
  18.0 0.1 collective-permute-start.6
  18.1 1.2 %collective-permute-done.6.refs_1_ = f32[2,32,128]{2,1,0:T(8,128)S(1)} collective-permute-done((f32[2,32,128]{2,1,0:T(8,128)S(1)}, f32[2,32,128]{2,1,0:T(8,128)S(1)}, u32[]{:S(2)}, u32[]{:S(2)}) %collective-permute-start.6) | collective-permute-done | bytes 32800 | tf_op jit(solution)/shard_map/ppermute | solution.py:91
  19.3 2.0 %collective-permute-start.7 = (f32[2,32,128]{2,1,0:T(8,128)S(1)}, f32[2,32,128]{2,1,0:T(8,128)S(1)}, u32[]{:S(2)}, u32[]{:S(2)}) collective-permute-start(f32[2,32,128]{2,1,0:T(8,128)S(1)} %get-tuple-element.46.refs_0_), channel_id=1, source_target_pairs={{0,3},{1,2},{2,1},{3,0},{4,7},{5,6},{6,5},{7,4},{8,11},{9,10},{10,... | collective-permute-start | bytes 98312 | tf_op jit(solution)/shard_map/ppermute | solution.py:91
  21.3 2.7 %collective-permute-start.10 = (f32[5,32,128]{2,1,0:T(8,128)S(1)}, f32[5,32,128]{2,1,0:T(8,128)S(1)}, u32[]{:S(2)}, u32[]{:S(2)}) collective-permute-start(f32[5,32,128]{2,1,0:T(8,128)S(1)} %get-tuple-element.55.refs_0_.refs_9_.refs_4_), channel_id=1, source_target_pairs={{0,8},{8,0},{16,24},{24,16},{1,9},{9,1},{17,25},{25,17},{2,10},{10... | collective-permute-start | bytes 245768 | tf_op jit(solution)/shard_map/ppermute | solution.py:91
  24.0 0.0 collective-permute-done.8.refs_1_
  24.0 0.0 collective-permute-done.7.refs_1_
  24.1 0.8 %collective-permute-start.9 = (f32[3,32,128]{2,1,0:T(8,128)S(1)}, f32[3,32,128]{2,1,0:T(8,128)S(1)}, u32[]{:S(2)}, u32[]{:S(2)}) collective-permute-start(f32[3,32,128]{2,1,0:T(8,128)S(1)} %get-tuple-element.50.refs_0_), channel_id=1, source_target_pairs={{0,5},{1,4},{2,7},{3,6},{4,1},{5,0},{6,3},{7,2},{8,13},{9,12},{10,... | collective-permute-start | bytes 147464 | tf_op jit(solution)/shard_map/ppermute | solution.py:91
  24.9 1.9 %collective-permute-done.10.refs_1_ = f32[5,32,128]{2,1,0:T(8,128)S(1)} collective-permute-done((f32[5,32,128]{2,1,0:T(8,128)S(1)}, f32[5,32,128]{2,1,0:T(8,128)S(1)}, u32[]{:S(2)}, u32[]{:S(2)}) %collective-permute-start.10) | collective-permute-done | bytes 81952 | tf_op jit(solution)/shard_map/ppermute | solution.py:91
  26.8 1.3 %collective-permute-done.9.refs_1_ = f32[3,32,128]{2,1,0:T(8,128)S(1)} collective-permute-done((f32[3,32,128]{2,1,0:T(8,128)S(1)}, f32[3,32,128]{2,1,0:T(8,128)S(1)}, u32[]{:S(2)}, u32[]{:S(2)}) %collective-permute-start.9) | collective-permute-done | bytes 49184 | tf_op jit(solution)/shard_map/ppermute | solution.py:91
  28.1 0.5 %turn.1 = (f32[32,32,128]{2,1,0:T(8,128)S(1)}, f32[2,32,128]{2,1,0:T(8,128)S(1)}, f32[32,32,128]{2,1,0:T(8,128)S(1)}, f32[32,32,128]{2,1,0:T(8,128)S(1)}) custom-call(f32[3,32,128]{2,1,0:T(8,128)S(1)} %get-tuple-element.50.refs_0_, f32[3,32,128]{2,1,0:T(8,128)S(1)} %collective-permute-done.9.refs_1_, f32[3,32,128]{2,1,0:T(8,128)S(1)} %get-tuple-element.45.refs_2_, ...), custom_call_target="tpu_custom_call" | custom-call | bytes 1536000 | tf_op jit(solution)/shard_map/turn/pallas_call | solution.py:33
  28.6 1.4 %collective-permute-start.11 = (f32[2,32,128]{2,1,0:T(8,128)S(1)}, f32[2,32,128]{2,1,0:T(8,128)S(1)}, u32[]{:S(2)}, u32[]{:S(2)}) collective-permute-start(f32[2,32,128]{2,1,0:T(8,128)S(1)} %get-tuple-element.58.refs_0_), channel_id=1, source_target_pairs={{0,8},{8,0},{16,24},{24,16},{1,9},{9,1},{17,25},{25,17},{2,10},{10... | collective-permute-start | bytes 98312 | tf_op jit(solution)/shard_map/ppermute | solution.py:91
  30.0 2.6 %collective-permute-done.11.refs_1_ = f32[2,32,128]{2,1,0:T(8,128)S(1)} collective-permute-done((f32[2,32,128]{2,1,0:T(8,128)S(1)}, f32[2,32,128]{2,1,0:T(8,128)S(1)}, u32[]{:S(2)}, u32[]{:S(2)}) %collective-permute-start.11) | collective-permute-done | bytes 32800 | tf_op jit(solution)/shard_map/ppermute | solution.py:91
  32.6 2.6 %collective-permute-start.12 = (f32[3,32,128]{2,1,0:T(8,128)S(1)}, f32[3,32,128]{2,1,0:T(8,128)S(1)}, u32[]{:S(2)}, u32[]{:S(2)}) collective-permute-start(f32[3,32,128]{2,1,0:T(8,128)S(1)} %get-tuple-element.60.refs_0_), channel_id=1, source_target_pairs={{0,16},{8,24},{16,0},{24,8},{1,17},{9,25},{17,1},{25,9},{2,18},{10... | collective-permute-start | bytes 147464 | tf_op jit(solution)/shard_map/ppermute | solution.py:91
  35.2 2.5 %collective-permute-done.12.refs_1_ = f32[3,32,128]{2,1,0:T(8,128)S(1)} collective-permute-done((f32[3,32,128]{2,1,0:T(8,128)S(1)}, f32[3,32,128]{2,1,0:T(8,128)S(1)}, u32[]{:S(2)}, u32[]{:S(2)}) %collective-permute-start.12) | collective-permute-done | bytes 49184 | tf_op jit(solution)/shard_map/ppermute | solution.py:91
  37.7 0.9 %finish.1 = f32[32,32,128]{2,1,0:T(8,128)} custom-call(f32[3,32,128]{2,1,0:T(8,128)S(1)} %get-tuple-element.60.refs_0_, f32[3,32,128]{2,1,0:T(8,128)S(1)} %collective-permute-done.12.refs_1_, f32[3,32,128]{2,1,0:T(8,128)S(1)} %get-tuple-element.57.refs_11_.refs_2_, f32[1,32,128]{2,1,0:T(8,128)S(1)} %get-tuple-element.61.refs_3_, ...), custom_call_target="tpu_custom_call" | custom-call | bytes 1024000 | tf_op jit(solution)/shard_map/finish/pallas_call | solution.py:33
  (7 shorter events, 0.2 us)
Async XLA Ops:
  0.0 7.5 %copy-start = (f32[32,32,128]{2,1,0:T(8,128)S(1)}, f32[32,32,128]{2,1,0:T(8,128)}, u32[]{:S(2)}) copy-start(f32[32,32,128]{2,1,0:T(8,128)} %kappa.1) | copy-start | bytes 1572868
  1.7 11.2 %collective-permute-start.3 = (f32[16,32,128]{2,1,0:T(8,128)S(1)}, f32[16,32,128]{2,1,0:T(8,128)S(1)}, u32[]{:S(2)}, u32[]{:S(2)}) collective-permute-start(f32[16,32,128]{2,1,0:T(8,128)S(1)} %get-tuple-element.38.e_mine.refs_0_.refs_6_), channel_id=1, source_target_pairs={{0,1},{1,0},{2,3},{3,2},{4,5},{5,4},{6,7},{7,6},{8,9},{9,8},{10,11... | collective-permute-start | bytes 786440 | tf_op jit(solution)/shard_map/ppermute | solution.py:91
  2.3 7.8 %collective-permute-start = (f32[11,32,128]{2,1,0:T(8,128)S(1)}, f32[11,32,128]{2,1,0:T(8,128)S(1)}, u32[]{:S(2)}, u32[]{:S(2)}) collective-permute-start(f32[11,32,128]{2,1,0:T(8,128)S(1)} %get-tuple-element.35), channel_id=1, source_target_pairs={{0,8},{1,9},{2,10},{3,11},{4,12},{5,13},{6,14},{7,15},{8,0},{9,1},... | collective-permute-start | bytes 540680 | tf_op jit(solution)/shard_map/ppermute | solution.py:84
  4.9 5.1 %collective-permute-start.1 = (f32[11,32,128]{2,1,0:T(8,128)S(1)}, f32[11,32,128]{2,1,0:T(8,128)S(1)}, u32[]{:S(2)}, u32[]{:S(2)}) collective-permute-start(f32[11,32,128]{2,1,0:T(8,128)S(1)} %get-tuple-element.36), channel_id=1, source_target_pairs={{0,1},{1,0},{2,3},{3,2},{4,5},{5,4},{6,7},{7,6},{8,16},{9,17},{10,... | collective-permute-start | bytes 540680 | tf_op jit(solution)/shard_map/ppermute | solution.py:84
  5.1 8.2 %collective-permute-start.2 = (f32[11,32,128]{2,1,0:T(8,128)S(1)}, f32[11,32,128]{2,1,0:T(8,128)S(1)}, u32[]{:S(2)}, u32[]{:S(2)}) collective-permute-start(f32[11,32,128]{2,1,0:T(8,128)S(1)} %get-tuple-element.37), channel_id=1, source_target_pairs={{0,7},{1,2},{2,1},{3,4},{4,3},{5,6},{6,5},{7,0},{8,15},{9,10},{10,... | collective-permute-start | bytes 540680 | tf_op jit(solution)/shard_map/ppermute | solution.py:84
  10.1 4.5 %collective-permute-start.5 = (f32[22,8,128]{2,1,0:T(8,128)S(1)}, f32[22,8,128]{2,1,0:T(8,128)S(1)}, u32[]{:S(2)}, u32[]{:S(2)}) collective-permute-start(f32[22,8,128]{2,1,0:T(8,128)S(1)} %get-tuple-element.41), channel_id=1, source_target_pairs={{0,1},{1,0},{2,3},{3,2},{4,5},{5,4},{6,7},{7,6},{8,9},{9,8},{10,11... | collective-permute-start | bytes 270344 | tf_op jit(solution)/shard_map/ppermute | solution.py:91
  10.2 4.4 %collective-permute-start.4 = (f32[9,8,128]{2,1,0:T(8,128)S(1)}, f32[9,8,128]{2,1,0:T(8,128)S(1)}, u32[]{:S(2)}, u32[]{:S(2)}) collective-permute-start(f32[9,8,128]{2,1,0:T(8,128)S(1)} %get-tuple-element.40), channel_id=1, source_target_pairs={{0,7},{1,2},{2,1},{3,4},{4,3},{5,6},{6,5},{7,0},{8,15},{9,10},{10,... | collective-permute-start | bytes 110600 | tf_op jit(solution)/shard_map/ppermute | solution.py:84
  13.0 11.0 %collective-permute-start.8 = (f32[5,32,128]{2,1,0:T(8,128)S(1)}, f32[5,32,128]{2,1,0:T(8,128)S(1)}, u32[]{:S(2)}, u32[]{:S(2)}) collective-permute-start(f32[5,32,128]{2,1,0:T(8,128)S(1)} %get-tuple-element.47.refs_0_), channel_id=1, source_target_pairs={{0,3},{1,2},{2,1},{3,0},{4,7},{5,6},{6,5},{7,4},{8,11},{9,10},{10,... | collective-permute-start | bytes 245768 | tf_op jit(solution)/shard_map/ppermute | solution.py:91
  18.0 1.3 %collective-permute-start.6 = (f32[2,32,128]{2,1,0:T(8,128)S(1)}, f32[2,32,128]{2,1,0:T(8,128)S(1)}, u32[]{:S(2)}, u32[]{:S(2)}) collective-permute-start(f32[2,32,128]{2,1,0:T(8,128)S(1)} %get-tuple-element.44.refs_0_), channel_id=1, source_target_pairs={{0,1},{1,0},{2,3},{3,2},{4,5},{5,4},{6,7},{7,6},{8,9},{9,8},{10,11... | collective-permute-start | bytes 98312 | tf_op jit(solution)/shard_map/ppermute | solution.py:91
  19.3 4.8 %collective-permute-start.7 = (f32[2,32,128]{2,1,0:T(8,128)S(1)}, f32[2,32,128]{2,1,0:T(8,128)S(1)}, u32[]{:S(2)}, u32[]{:S(2)}) collective-permute-start(f32[2,32,128]{2,1,0:T(8,128)S(1)} %get-tuple-element.46.refs_0_), channel_id=1, source_target_pairs={{0,3},{1,2},{2,1},{3,0},{4,7},{5,6},{6,5},{7,4},{8,11},{9,10},{10,... | collective-permute-start | bytes 98312 | tf_op jit(solution)/shard_map/ppermute | solution.py:91
  21.3 5.5 %collective-permute-start.10 = (f32[5,32,128]{2,1,0:T(8,128)S(1)}, f32[5,32,128]{2,1,0:T(8,128)S(1)}, u32[]{:S(2)}, u32[]{:S(2)}) collective-permute-start(f32[5,32,128]{2,1,0:T(8,128)S(1)} %get-tuple-element.55.refs_0_.refs_9_.refs_4_), channel_id=1, source_target_pairs={{0,8},{8,0},{16,24},{24,16},{1,9},{9,1},{17,25},{25,17},{2,10},{10... | collective-permute-start | bytes 245768 | tf_op jit(solution)/shard_map/ppermute | solution.py:91
  24.1 4.0 %collective-permute-start.9 = (f32[3,32,128]{2,1,0:T(8,128)S(1)}, f32[3,32,128]{2,1,0:T(8,128)S(1)}, u32[]{:S(2)}, u32[]{:S(2)}) collective-permute-start(f32[3,32,128]{2,1,0:T(8,128)S(1)} %get-tuple-element.50.refs_0_), channel_id=1, source_target_pairs={{0,5},{1,4},{2,7},{3,6},{4,1},{5,0},{6,3},{7,2},{8,13},{9,12},{10,... | collective-permute-start | bytes 147464 | tf_op jit(solution)/shard_map/ppermute | solution.py:91
  28.6 4.0 %collective-permute-start.11 = (f32[2,32,128]{2,1,0:T(8,128)S(1)}, f32[2,32,128]{2,1,0:T(8,128)S(1)}, u32[]{:S(2)}, u32[]{:S(2)}) collective-permute-start(f32[2,32,128]{2,1,0:T(8,128)S(1)} %get-tuple-element.58.refs_0_), channel_id=1, source_target_pairs={{0,8},{8,0},{16,24},{24,16},{1,9},{9,1},{17,25},{25,17},{2,10},{10... | collective-permute-start | bytes 98312 | tf_op jit(solution)/shard_map/ppermute | solution.py:91
  32.6 5.1 %collective-permute-start.12 = (f32[3,32,128]{2,1,0:T(8,128)S(1)}, f32[3,32,128]{2,1,0:T(8,128)S(1)}, u32[]{:S(2)}, u32[]{:S(2)}) collective-permute-start(f32[3,32,128]{2,1,0:T(8,128)S(1)} %get-tuple-element.60.refs_0_), channel_id=1, source_target_pairs={{0,16},{8,24},{16,0},{24,8},{1,17},{9,25},{17,1},{25,9},{2,18},{10... | collective-permute-start | bytes 147464 | tf_op jit(solution)/shard_map/ppermute | solution.py:91

commit v5 on v4

--- a/solution.py
+++ b/solution.py
@@ -95,28 +95,52 @@
     return (lax.axis_size(axis) - 1).bit_length()
 
 
-def begin_kernel(tracer, y_speed, z_speed, kappa_far, a_ref, b_ref, o_ref, e_ref, c, ys, zs, kappa, kappa_y, r_y, sem):
+def z_rims_kernel(tracer, y_speed, z_speed, a_ref, b_ref, sem):
+    z, _, _, _ = place()
+    depth = tracer.shape[0]
+    z_odd = lax.rem(z, 2)
+    copies = []
+    for ref, low in ((a_ref, z_odd), (b_ref, 1 - z_odd)):
+        four, three = (1 - low) * (depth - 4), (1 - low) * (depth - 3)
+        for source, start, count, row in ((tracer, four, 4, 0), (z_speed, four, 4, 4), (y_speed, three, 3, 8)):
+            copies.append(
+                pltpu.make_async_copy(
+                    source.at[pl.ds(start, count)], ref.at[pl.ds(row, count)], sem.at[len(copies)]
+                )
+            )
+            copies[-1].start()
+    for copy in copies:
+        copy.wait()
+
+
+def z_rims(tracer, y_speed, z_speed):
+    _, width, band = tracer.shape
+    return call(
+        z_rims_kernel,
+        "z_rims",
+        [near(11, width, band)] * 2,
+        [("far", x) for x in (tracer, y_speed, z_speed)],
+        scratch=[pltpu.SemaphoreType.DMA((6,))],
+        cycles=1000,
+    )
+
+
+def begin_kernel(tracer, y_speed, z_speed, kappa_far, _, o_ref, e_ref, ports, c, ys, zs, kappa, kappa_y, r_y, sem):
     arrivals = [
         pltpu.make_async_copy(source, target, sem.at[k])
         for k, (source, target) in enumerate(((kappa_far, kappa), (tracer, c), (z_speed, zs), (y_speed, ys)))
     ]
     for copy in arrivals:
         copy.start()
-    z, y, _, y_count = place()
-    depth, width, _ = c.shape
-    z_odd, y_odd = lax.rem(z, 2), lax.rem(y, 2)
+    _, y, _, y_count = place()
+    width = c.shape[1]
+    y_odd = lax.rem(y, 2)
     arrivals[0].wait()
-    ports = e_ref.at[11:16]
     kappa_y[...] = turned(kappa[...])
     ports[3], ports[4] = resistances(kappa_y, r_y)
     factor(((lambda j: r_y[j], width, *outer(ports, y, y_count), None, ports),))
     for copy in arrivals[1:]:
         copy.wait()
-    for ref, low in ((a_ref, z_odd), (b_ref, 1 - z_odd)):
-        four, three = (1 - low) * (depth - 4), (1 - low) * (depth - 3)
-        ref[0:4] = c[pl.ds(four, 4)]
-        ref[4:8] = zs[pl.ds(four, 4)]
-        ref[8:11] = ys[pl.ds(three, 3)]
 
     def rims(o_low):
         for ref, low in ((o_ref, o_low), (e_ref, not o_low)):
@@ -135,53 +159,50 @@
         rims(False)
 
 
-def begin(tracer, y_speed, z_speed, kappa):
+def begin(tracer, y_speed, z_speed, kappa, after):
     depth, width, band = tracer.shape
     return call(
         begin_kernel,
         "begin",
-        [near(11, width, band)] * 2 + [near(11, depth, band), near(16, depth, band)],
-        [("far", x) for x in (tracer, y_speed, z_speed, kappa)],
+        [near(11, depth, band)] * 2 + [near(5, depth, band)],
+        [("far", x) for x in (tracer, y_speed, z_speed, kappa)] + [after],
         scratch=[near(depth, width, band)] * 4 + [near(width, depth, band)] * 2 + [pltpu.SemaphoreType.DMA((4,))],
         cycles=2000,
     )
 
 
-RIM_ROWS = 22
+PAD_TILES = 3
 
 
 def rim_kernel(a, b, _, for_pair, for_other):
     z, y, _, _ = place()
     width = a.shape[1]
     z_odd, y_odd = lax.rem(z, 2) == 1, lax.rem(y, 2)
-    start = pl.multiple_of((1 - y_odd) * (width - 8), 8)
-
-    def corners(first):
+
+    def corners(out, low):
+        tile, first = (slice(0, 8), 0) if low else (slice(width - 8, width), 5)
         for f, (row, count) in enumerate(((0, 4), (8, 3), (4, 4))):
-            for k in range(3):
-                column_a, column_b = (ref[row : row + count, first + k, :] for ref in (a, b))
-                for_other[3 * f + k, 4 - count : 4, :] = jnp.where(z_odd, column_a, column_b)
-                for_other[3 * f + k, 4 : 4 + count, :] = jnp.where(z_odd, column_b, column_a)
-
-    for tile in range(3, 6):
-        for_other[tile] = jnp.zeros(for_other.shape[1:], F32)
+            empty = [jnp.zeros((3, 4 - count, out.shape[2]), F32)] if count < 4 else []
+            side_a, side_b = (turned(ref[row : row + count, tile, :])[first : first + 3] for ref in (a, b))
+            below, above = jnp.where(z_odd, side_a, side_b), jnp.where(z_odd, side_b, side_a)
+            out[3 * f : 3 * f + 3] = jnp.concatenate([*empty, below, above, *empty], axis=1)
 
     @pl.when(y_odd == 0)
     def _():
-        corners(0)
+        corners(for_other, True)
+        corners(for_pair, False)
 
     @pl.when(y_odd == 1)
     def _():
-        corners(width - 3)
-
-    for half, ref in enumerate((a, b)):
-        for k in range(11):
-            for_pair[11 * half + k] = ref[k, pl.ds(start, 8), :]
+        corners(for_other, False)
+        corners(for_pair, True)
+
+    for_other[9:] = jnp.zeros((PAD_TILES, 8, for_other.shape[2]), F32)
 
 
 def rim(a, b, after):
     band = a.shape[2]
-    return call(rim_kernel, "rim", [near(22, 8, band), near(9, 8, band)], [a, b, after], cycles=200)
+    return call(rim_kernel, "rim", [near(9, 8, band), near(9 + PAD_TILES, 8, band)], [a, b, after], cycles=200)
 
 
 def reciprocal(x):
@@ -272,41 +293,49 @@
     )
 
 
-def ports_kernel(axis, level, first_row, mine, theirs, out, joint):
-    is_left = (lax.shift_right_logical(lax.axis_index(axis), level) & 1) == 0
-    pairs = [(mine[first_row + k], theirs[first_row + k]) for k in range(5)]
+def ports_kernel(axis, level, mine, theirs, joint, out):
+    index = lax.axis_index(axis)
+    is_left = (lax.shift_right_logical(index, level) & 1) == 0
+    pairs = [(mine[k], theirs[k]) for k in range(5)]
     left = [jnp.where(is_left, m, t) for m, t in pairs]
     right = [jnp.where(is_left, t, m) for m, t in pairs]
     d = reciprocal(reciprocal((0.5 * RATE) * (left[4] + right[3])) + left[2] + right[0])
-    out[0] = left[0] - left[1] * left[1] * d
-    out[1] = left[1] * right[1] * d
-    out[2] = right[2] - right[1] * right[1] * d
-    out[3] = left[3]
-    out[4] = right[4]
+    low, high = left[0] - left[1] * left[1] * d, right[2] - right[1] * right[1] * d
     joint[0] = d
     joint[1] = left[1]
     joint[2] = right[1]
-
-
-def join_ports(mine, theirs, axis, level, first_row=0):
+    if level + 2 == levels_of(axis):
+        next_left = (lax.shift_right_logical(index, level + 1) & 1) == 0
+        out[0] = jnp.where(next_left, high, low)
+        out[1] = jnp.where(next_left, right[4], left[3])
+    else:
+        out[0] = low
+        out[1] = left[1] * right[1] * d
+        out[2] = high
+        out[3] = left[3]
+        out[4] = right[4]
+
+
+def join_ports(mine, theirs, axis, level):
     _, lines, band = mine.shape
 
     def kernel(*refs):
-        ports_kernel(axis, level, first_row, *refs)
-
-    return call(kernel, "join_ports", [near(5, lines, band), near(3, lines, band)], [mine, theirs], cycles=100)
-
-
-def join_levels(ports, axis, done):
+        ports_kernel(axis, level, *refs)
+
+    last = level + 2 == levels_of(axis)
+    outs = [near(3, lines, band), near(2 if last else 5, lines, band)]
+    return call(kernel, "join_ports", outs, [mine, theirs], cycles=100)
+
+
+def join_all(ports, axis):
     joints = []
-    for level in range(done, levels_of(axis) - 1):
-        ports, joint = join_ports(ports, swap(ports, axis, level), axis, level)
+    for level in range(levels_of(axis) - 1):
+        joint, ports = join_ports(ports, swap(ports, axis, level), axis, level)
         joints.append(joint)
-    return ports, joints
-
-
-def source_kernel(axis, level, mine, theirs, joint, *refs):
-    *ports, out, flow_ref = refs
+    return joints, ports, swap(ports, axis, len(joints))
+
+
+def source_kernel(axis, level, last, mine, theirs, joint, out, flow_ref):
     index = lax.axis_index(axis)
     is_left = (lax.shift_right_logical(index, level) & 1) == 0
     pairs = [(mine[k], theirs[k]) for k in range(2)]
@@ -315,33 +344,30 @@
     flow = (left[1] - right[0]) * joint[0]
     flow_ref[0] = flow
     low, high = left[0] - joint[1] * flow, right[1] + joint[2] * flow
-    if not ports:
+    if last:
+        next_left = (lax.shift_right_logical(index, level + 1) & 1) == 0
+        out[0] = jnp.where(next_left, high, low)
+    else:
         out[0] = low
         out[1] = high
-        return
-    ports = ports[0]
-    next_left = (lax.shift_right_logical(index, level + 1) & 1) == 0
-    out[0] = jnp.where(next_left, high, low)
-    out[1] = jnp.where(next_left, ports[2], ports[0])
-    out[2] = jnp.where(next_left, ports[4], ports[3])
-
-
-def join_sources(mine, theirs, joint, ports, axis, level):
+
+
+def join_sources(mine, theirs, joint, axis, level):
     _, lines, band = mine.shape
-    last = [ports] if level + 2 == levels_of(axis) else []
+    last = level + 2 == levels_of(axis)
 
     def kernel(*refs):
-        source_kernel(axis, level, *refs)
-
-    outs = [near(3 if last else 2, lines, band), near(1, lines, band)]
-    return call(kernel, "join_sources", outs, [mine, theirs, joint, *last], cycles=100)
-
-
-def end_currents(axis, mine, theirs, joints, flows):
+        source_kernel(axis, level, last, *refs)
+
+    outs = [near(1 if last else 2, lines, band), near(1, lines, band)]
+    return call(kernel, "join_sources", outs, [mine, theirs, joint], cycles=100)
+
+
+def end_currents(axis, mine, theirs, edge, edge_theirs, joints, flows):
     index = lax.axis_index(axis)
     level = len(joints)
     is_left = (lax.shift_right_logical(index, level) & 1) == 0
-    d = reciprocal(reciprocal((0.5 * RATE) * (mine[2] + theirs[2])) + mine[1] + theirs[1])
+    d = reciprocal(reciprocal((0.5 * RATE) * (edge[1] + edge_theirs[1])) + edge[0] + edge_theirs[0])
     flow = (mine[0] - theirs[0]) * d
     zero = jnp.zeros_like(flow)
     low, high = jnp.where(is_left, zero, -flow), jnp.where(is_left, -flow, zero)
@@ -376,7 +402,7 @@
 
 
 def advect_kernel(
-    tracer, y_speed, z_speed, a, b, o, e, corner, ab, e_mine, r_y_far, r_z_far, ports_z,
+    tracer, y_speed, z_speed, a, b, o, e, corner, ab, ports_y, r_y_far, r_z_far, ports_z,
     base, sources, r_y, r_z, ports_out, c, ys, zs, sy, sz, phi, psi, kept, sem,
 ):
     z, y, z_count, y_count = place()
@@ -388,16 +414,16 @@
     ]
     y_copy = pltpu.make_async_copy(r_y_far, r_y, sem.at[3])
     z_copy = pltpu.make_async_copy(r_z_far, r_z, sem.at[4])
-    y_copy.start()
     for copy in copies:
         copy.start()
+    y_copy.start()
     z_copy.start()
     ports_out[...] = ports_z[...]
     z_odd, y_odd = lax.rem(z, 2), lax.rem(y, 2)
     keep_b = jnp.where((z_odd == 0) & (z == 0) | (z_odd == 1) & (z == z_count - 1), 0.0, 1.0)
     keep_o = jnp.where((y_odd == 0) & (y == 0) | (y_odd == 1) & (y == y_count - 1), 0.0, 1.0)
-    keep_below = keep_o * jnp.where(z_odd == 0, keep_b, 1.0)
-    keep_above = keep_o * jnp.where(z_odd == 1, keep_b, 1.0)
+    keep_below = jnp.where(z_odd == 0, keep_b, 1.0)
+    keep_above = jnp.where(z_odd == 1, keep_b, 1.0)
     column = lax.broadcasted_iota(jnp.int32, (8, band), 0)
     outside = (column < 4) & (y == y_count - 1) | (column >= 4) & (y == 0)
     inside = jnp.where(outside, 0.0, 1.0)
@@ -426,32 +452,16 @@
         ys[4 : 4 + depth, width:cols, :] = columns(4, 4)
         zs[4 : 4 + depth, width:cols, :] = columns(8, 3)
 
-        def from_pair(half, z_low):
-            start = width if o_low else width + 4
-            first = 0 if o_low else 4
-            zr = 0 if z_low else depth + 4
-            z3 = 1 if z_low else depth + 4
-            keep = 1.0 if half == 0 else keep_b
-            for k in range(11):
-                field, row = ((c, zr + k), (zs, zr + k - 4), (ys, z3 + k - 8))[k // 4]
-                field[row, start : start + 4, :] = ab[11 * half + k, first : first + 4, :] * keep
-
-        start = width + (5 if o_low else 0)
-        for f, (field, count) in enumerate(((c, 4), (ys, 3), (zs, 4))):
-            for k in range(3):
-                below, above = corner[3 * f + k, 4 - count : 4, :], corner[3 * f + k, 4 : 4 + count, :]
-                field[4 - count : 4, start + k, :] = below * keep_below
-                field[depth + 4 : depth + 4 + count, start + k, :] = above * keep_above
-
-        @pl.when(z_odd == 0)
-        def _():
-            from_pair(0, False)
-            from_pair(1, True)
-
-        @pl.when(z_odd == 1)
-        def _():
-            from_pair(0, True)
-            from_pair(1, False)
+        def corners(ref, low, keep):
+            start = width + (5 if low else 0)
+            for f, (field, count) in enumerate(((c, 4), (ys, 3), (zs, 4))):
+                for k in range(3):
+                    below, above = ref[3 * f + k, 4 - count : 4, :], ref[3 * f + k, 4 : 4 + count, :]
+                    field[4 - count : 4, start + k, :] = below * (keep * keep_below)
+                    field[depth + 4 : depth + 4 + count, start + k, :] = above * (keep * keep_above)
+
+        corners(corner, o_low, keep_o)
+        corners(ab, not o_low, 1.0)
 
     @pl.when(y_odd == 0)
     def _():
@@ -461,8 +471,6 @@
     def _():
         sides(False)
 
-    y_copy.wait()
-    factor(((lambda j: r_y[j], width, *outer(e_mine.at[11:16], y, y_count), (phi, psi), None),))
     for copy in copies[:2]:
         copy.wait()
 
@@ -482,7 +490,7 @@
         sz[r] = 0.5 * (before + after)
         return after
 
-    lax.fori_loop(0, rows - 1, faces, zs[0], unroll=3)
+    lax.fori_loop(0, rows - 1, faces, zs[0], unroll=13)
     copies[2].wait()
 
     keep_low = jnp.where(z == 0, 0.0, 1.0)
@@ -500,14 +508,16 @@
             c[r, width:cols, :] = new[width:cols] * inside
             return after, above
 
-        lax.fori_loop(step, rows - step, row, (here, flux(sz[step - 1], c[step - 1], here)), unroll=4)
+        lax.fori_loop(step, rows - step, row, (here, flux(sz[step - 1], c[step - 1], here)), unroll=16)
         if step < NSUB:
             c[3] = c[3] * keep_low
             c[4 + depth] = c[4 + depth] * keep_high
 
     z_copy.wait()
+    y_copy.wait()
+    factor(((lambda j: r_y[j], width, *outer(ports_y, y, y_count), (phi, psi), None),))
     kept[...] = turned(c[4 : 4 + depth, 0:width, :])
-    solve_open(kept, phi, psi, e_mine[12], base, sources)
+    solve_open(kept, phi, psi, ports_y[1], base, sources)
 
 
 def advect(tracer, y_speed, z_speed, halos, ports_y, r_y, r_z, ports_z):
@@ -527,13 +537,12 @@
 
 
 def turn_kernel(levels, *refs):
-    mine, theirs = refs[0:2]
-    joints, flows = refs[2 : 2 + levels], refs[2 + levels : 2 + 2 * levels]
-    ports_y, base_y, r_y, ports_z, r_z, _, base, sources, phi, psi, u, kept = refs[2 + 2 * levels :]
+    last, refs = refs[0:4], refs[4:]
+    joints, flows = refs[0:levels], refs[levels : 2 * levels]
+    ports_y, base_y, r_y, ports_z, r_z, _, base, sources, phi, psi, u, kept = refs[2 * levels :]
     z, y, z_count, y_count = place()
     width, depth = base_y.shape[0], base.shape[0]
-    ports_y = ports_y.at[11:16]
-    low, high = end_currents("gy", mine, theirs, joints, flows)
+    low, high = end_currents("gy", *last, joints, flows)
     edge, _ = outer(ports_y, y, y_count)
     value = low * ports_y[0] + high * ports_y[1]
     current = (1.0 + edge) * value - low
@@ -549,7 +558,7 @@
     solve_open(kept, phi, psi, ports_z[1], base, sources)
 
 
-def turn(mine, theirs, joints, flows, ports_y, base_y, r_y, ports_z, r_z, after):
+def turn(last, joints, flows, ports_y, base_y, r_y, ports_z, r_z, after):
     width, depth, band = base_y.shape
     along_z = near(depth, width, band)
 
@@ -560,17 +569,17 @@
         kernel,
         "turn",
         [along_z, near(2, width, band), along_z, along_z],
-        [mine, theirs, *joints, *flows, ports_y, base_y, r_y, ports_z, r_z, after],
+        [*last, *joints, *flows, ports_y, base_y, r_y, ports_z, r_z, after],
         scratch=[near(width, depth, band), along_z],
         cycles=1500,
     )
 
 
 def finish_kernel(levels, *refs):
-    mine, theirs = refs[0:2]
-    joints, flows = refs[2 : 2 + levels], refs[2 + levels : 2 + 2 * levels]
-    ports_z, base, phi, psi, out, u, sem = refs[2 + 2 * levels :]
-    low, high = end_currents("gz", mine, theirs, joints, flows)
+    last, refs = refs[0:4], refs[4:]
+    joints, flows = refs[0:levels], refs[levels : 2 * levels]
+    ports_z, base, phi, psi, out, u, sem = refs[2 * levels :]
+    low, high = end_currents("gz", *last, joints, flows)
     scale = ports_z[1]
     low, high = low * scale, high * scale
     depth = base.shape[0]
@@ -586,7 +595,7 @@
         copy.wait()
 
 
-def finish(mine, theirs, joints, flows, ports_z, base, phi, psi):
+def finish(last, joints, flows, ports_z, base, phi, psi):
     def kernel(*refs):
         finish_kernel(len(joints), *refs)
 
@@ -594,46 +603,43 @@
         kernel,
         "finish",
         [("far", jax.ShapeDtypeStruct(base.shape, F32))],
-        [mine, theirs, *joints, *flows, ports_z, base, phi, psi],
+        [*last, *joints, *flows, ports_z, base, phi, psi],
         scratch=[near(*base.shape), pltpu.SemaphoreType.DMA((4,))],
         cycles=1000,
     )
 
 
-def exchange_sources(sources, ports, joints, axis):
+def exchange_sources(sources, joints, axis):
     flows = []
     for level, joint in enumerate(joints):
-        theirs = swap(sources, axis, level)
-        sources, flow = join_sources(sources, theirs, joint, ports, axis, level)
+        sources, flow = join_sources(sources, swap(sources, axis, level), joint, axis, level)
         flows.append(flow)
     return sources, swap(sources, axis, len(joints)), flows
 
 
 def local(tracer, y_speed, z_speed, kappa):
-    a, b, o, e_mine = begin(tracer, y_speed, z_speed, kappa)
-    e = swap(e_mine, "gy", 0)
+    a, b = z_rims(tracer, y_speed, z_speed)
+    o, e, ports_y = begin(tracer, y_speed, z_speed, kappa, a)
     a = send(a, z_partner=pair_up)
     b = send(b, z_partner=z_other)
+    e = swap(e, "gy", 0)
     o = send(o, y_partner=y_other)
     r_y, r_z, ports_z = factor_lines(kappa)
     for_pair, for_other = rim(a, b, ports_z)
     corner = send(for_other, y_partner=y_other)
     ab = swap(for_pair, "gy", 0)
-
-    joined_y, joint_y = join_ports(e_mine, e, "gy", 0, first_row=11)
-    joined_y, joints = join_levels(joined_y, "gy", 1)
-    joints_y = [joint_y] + joints
+    joints_y, edge_y, edge_y_theirs = join_all(ports_y, "gy")
 
     base, sources, r_y, r_z, ports_z = advect(
-        tracer, y_speed, z_speed, (a, b, o, e, corner, ab), e_mine, r_y, r_z, ports_z
-    )
-    joined_z, joints_z = join_levels(ports_z, "gz", 0)
-    mine, theirs, flows = exchange_sources(sources, joined_y, joints_y, "gy")
+        tracer, y_speed, z_speed, (a, b, o, e, corner, ab), ports_y, r_y, r_z, ports_z
+    )
+    joints_z, edge_z, edge_z_theirs = join_all(ports_z, "gz")
+    mine, theirs, flows = exchange_sources(sources, joints_y, "gy")
     base, sources, phi_z, psi_z = turn(
-        mine, theirs, joints_y, flows, e_mine, base, r_y, ports_z, r_z, joints_z[-1]
-    )
-    mine, theirs, flows = exchange_sources(sources, joined_z, joints_z, "gz")
-    return finish(mine, theirs, joints_z, flows, ports_z, base, phi_z, psi_z)
+        (mine, theirs, edge_y, edge_y_theirs), joints_y, flows, ports_y, base, r_y, ports_z, r_z, joints_z[-1]
+    )
+    mine, theirs, flows = exchange_sources(sources, joints_z, "gz")
+    return finish((mine, theirs, edge_z, edge_z_theirs), joints_z, flows, ports_z, base, phi_z, psi_z)
 
 
 def solution(mesh):

time: 38.7 us -> 38 us (0.982)
  starting transfers between devices: 18.4 us -> 17.2 us
  Pallas kernels: 7.81 us -> 8.61 us
    ppermute x4, starting transfers between devices: 7.94 us -> 5.87 us  [send(): return lax.ppermute(x, AXES, permutation(z_partner, y_partner))]
    pallas_call x12 -> x13, Pallas kernels: 7.81 us -> 8.61 us  [call(): pl.pallas_call(kernel, out_shape=[out[1] if isinstance(out, tuple) else o...]
    ppermute x9 -> x12, starting transfers between devices: 10.5 us -> 11.3 us  [swap(): lax.ppermute(x, axis, [(i, i ^ step) for i in range(lax.axis_size(axis))])]
    ppermute x9 -> x12, waiting for transfers between devices: 9.42 us -> 9.25 us  [swap(): lax.ppermute(x, axis, [(i, i ^ step) for i in range(lax.axis_size(axis))])]
  transfers between devices with their start and end apart: 13 -> 16, of which waited for: 7 -> 7; matrix products, arithmetic and copies ran while one was open for 0% -> 0% of each run, Pallas kernels for 12% -> 16%
where the time goes in v5:
time: 38 us; the launch traced here: 37.8 us
  starting transfers between devices  17.2 us (45%)
  waiting for transfers between devices  11.9 us (31%)
  Pallas kernels  8.61 us (23%)
    ppermute x12, starting transfers between devices, swap(): lax.ppermute(x, axis, [(i, i ^ step) for i in range(lax.axis_size(axis))])  11.3 us
    ppermute x12, waiting for transfers between devices, swap(): lax.ppermute(x, axis, [(i, i ^ step) for i in range(lax.axis_size(axis))])  9.25 us
    pallas_call x13, Pallas kernels, call(): pl.pallas_call(kernel, out_shape=[out[1] if isinstance(out, tuple) else o...  8.61 us
    ppermute x4, starting transfers between devices, send(): return lax.ppermute(x, AXES, permutation(z_partner, y_partner))  5.87 us
    ppermute x4, waiting for transfers between devices, send(): return lax.ppermute(x, AXES, permutation(z_partner, y_partner))  2.67 us
  transfers between devices with their start and end apart: 16, of which 7 were waited for; matrix products, arithmetic and copies ran while one was open for 0% of the time, Pallas kernels for 16%

profile of v5, /device:TPU:0, one launch (start us, length us, event | category | flops | bytes accessed | tf_op | source)
XLA Modules:
  0.0 37.8 jit_solution(12900383734622525339)
XLA Ops:
  0.0 1.0 %z_rims.1 = (f32[11,32,128]{2,1,0:T(8,128)S(1)}, f32[11,32,128]{2,1,0:T(8,128)S(1)}) custom-call(f32[32,32,128]{2,1,0:T(8,128)} %tracer.5, f32[32,32,128]{2,1,0:T(8,128)} %y_speed.5, f32[32,32,128]{2,1,0:T(8,128)} %z_speed.5), custom_call_target="tpu_custom_call" | custom-call | bytes 1024000 | tf_op jit(solution)/shard_map/z_rims/pallas_call | solution.py:33
  1.0 3.1 %collective-permute-start = (f32[11,32,128]{2,1,0:T(8,128)S(1)}, f32[11,32,128]{2,1,0:T(8,128)S(1)}, u32[]{:S(2)}, u32[]{:S(2)}) collective-permute-start(f32[11,32,128]{2,1,0:T(8,128)S(1)} %get-tuple-element.36._), channel_id=1, source_target_pairs={{0,8},{1,9},{2,10},{3,11},{4,12},{5,13},{6,14},{7,15},{8,0},{9,1},... | collective-permute-start | bytes 540680 | tf_op jit(solution)/shard_map/ppermute | solution.py:84
  4.1 0.0 copy-start
  4.1 0.0 collective-permute-start.1
  4.1 1.7 %begin.1 = (f32[11,32,128]{2,1,0:T(8,128)S(1)}, f32[11,32,128]{2,1,0:T(8,128)S(1)}, f32[5,32,128]{2,1,0:T(8,128)S(1)}) custom-call(f32[32,32,128]{2,1,0:T(8,128)} %tracer.5, f32[32,32,128]{2,1,0:T(8,128)} %y_speed.5, f32[32,32,128]{2,1,0:T(8,128)} %z_speed.5, f32[32,32,128]{2,1,0:T(8,128)} %kappa.1, f32[11,32,128]{2,1,0:T(8,128)S(1)} %get-tuple-element.36._), custom_call_target="tpu_custom_call" | custom-call | bytes 2048000 | tf_op jit(solution)/shard_map/begin/pallas_call | solution.py:33
  5.8 2.6 %collective-permute-start.2 = (f32[11,32,128]{2,1,0:T(8,128)S(1)}, f32[11,32,128]{2,1,0:T(8,128)S(1)}, u32[]{:S(2)}, u32[]{:S(2)}) collective-permute-start(f32[11,32,128]{2,1,0:T(8,128)S(1)} %get-tuple-element.38), channel_id=1, source_target_pairs={{0,7},{1,2},{2,1},{3,4},{4,3},{5,6},{6,5},{7,0},{8,15},{9,10},{10,... | collective-permute-start | bytes 540680 | tf_op jit(solution)/shard_map/ppermute | solution.py:84
  8.4 0.0 collective-permute-start.3
  8.4 0.5 %collective-permute-start.7 = (f32[5,32,128]{2,1,0:T(8,128)S(1)}, f32[5,32,128]{2,1,0:T(8,128)S(1)}, u32[]{:S(2)}, u32[]{:S(2)}) collective-permute-start(f32[5,32,128]{2,1,0:T(8,128)S(1)} %get-tuple-element.43.ports_y.refs_0_.refs_8_), channel_id=1, source_target_pairs={{0,1},{1,0},{2,3},{3,2},{4,5},{5,4},{6,7},{7,6},{8,9},{9,8},{10,11... | collective-permute-start | bytes 245768 | tf_op jit(solution)/shard_map/ppermute | solution.py:91
  8.9 0.0 copy-done
  8.9 1.1 %factor.1 = (f32[32,32,128]{2,1,0:T(8,128)}, f32[32,32,128]{2,1,0:T(8,128)}, f32[5,32,128]{2,1,0:T(8,128)S(1)}) custom-call(f32[32,32,128]{2,1,0:T(8,128)S(1)} %copy-done), custom_call_target="tpu_custom_call" | custom-call | bytes 4096000 | tf_op jit(solution)/shard_map/factor/pallas_call | solution.py:33
  10.0 0.0 collective-permute-done.a
  10.0 0.0 collective-permute-done.1.b
  10.0 0.1 rim.1
  10.1 0.2 collective-permute-start.4
  10.3 0.2 collective-permute-start.5
  10.5 0.0 collective-permute-done.7.refs_1_
  10.6 1.4 %collective-permute-start.9 = (f32[5,32,128]{2,1,0:T(8,128)S(1)}, f32[5,32,128]{2,1,0:T(8,128)S(1)}, u32[]{:S(2)}, u32[]{:S(2)}) collective-permute-start(f32[5,32,128]{2,1,0:T(8,128)S(1)} %get-tuple-element.49.refs_0_), channel_id=1, source_target_pairs={{0,3},{1,2},{2,1},{3,0},{4,7},{5,6},{6,5},{7,4},{8,11},{9,10},{10,... | collective-permute-start | bytes 245768 | tf_op jit(solution)/shard_map/ppermute | solution.py:91
  12.0 1.0 %collective-permute-done.2.o = f32[11,32,128]{2,1,0:T(8,128)S(1)} collective-permute-done((f32[11,32,128]{2,1,0:T(8,128)S(1)}, f32[11,32,128]{2,1,0:T(8,128)S(1)}, u32[]{:S(2)}, u32[]{:S(2)}) %collective-permute-start.2) | collective-permute-done | bytes 180256 | tf_op jit(solution)/shard_map/ppermute | solution.py:84
  13.0 0.0 collective-permute-done.3.e
  13.0 0.0 collective-permute-done.5.ab
  13.0 1.7 %collective-permute-done.4.corner = f32[12,8,128]{2,1,0:T(8,128)S(1)} collective-permute-done((f32[12,8,128]{2,1,0:T(8,128)S(1)}, f32[12,8,128]{2,1,0:T(8,128)S(1)}, u32[]{:S(2)}, u32[]{:S(2)}) %collective-permute-start.4) | collective-permute-done | bytes 49184 | tf_op jit(solution)/shard_map/ppermute | solution.py:84
  14.7 3.2 %advect.1 = (f32[32,32,128]{2,1,0:T(8,128)S(1)}, f32[2,32,128]{2,1,0:T(8,128)S(1)}, f32[32,32,128]{2,1,0:T(8,128)S(1)}, f32[32,32,128]{2,1,0:T(8,128)S(1)}, f32[5,32,128]{2,1,0:T(8,128)S(1)}) custom-call(f32[32,32,128]{2,1,0:T(8,128)} %tracer.5, f32[32,32,128]{2,1,0:T(8,128)} %y_speed.5, f32[32,32,128]{2,1,0:T(8,128)} %z_speed.5, ...), custom_call_target="tpu_custom_call" | custom-call | bytes 5120000 | tf_op jit(solution)/shard_map/advect/pallas_call | solution.py:33
  17.9 0.1 collective-permute-start.6
  18.0 3.1 %collective-permute-start.12 = (f32[5,32,128]{2,1,0:T(8,128)S(1)}, f32[5,32,128]{2,1,0:T(8,128)S(1)}, u32[]{:S(2)}, u32[]{:S(2)}) collective-permute-start(f32[5,32,128]{2,1,0:T(8,128)S(1)} %get-tuple-element.57.refs_0_.refs_11_.refs_6_), channel_id=1, source_target_pairs={{0,8},{8,0},{16,24},{24,16},{1,9},{9,1},{17,25},{25,17},{2,10},{10... | collective-permute-start | bytes 245768 | tf_op jit(solution)/shard_map/ppermute | solution.py:91
  21.0 0.0 collective-permute-done.6.refs_1_
  21.1 0.6 %collective-permute-start.8 = (f32[2,32,128]{2,1,0:T(8,128)S(1)}, f32[2,32,128]{2,1,0:T(8,128)S(1)}, u32[]{:S(2)}, u32[]{:S(2)}) collective-permute-start(f32[2,32,128]{2,1,0:T(8,128)S(1)} %get-tuple-element.48.refs_0_), channel_id=1, source_target_pairs={{0,3},{1,2},{2,1},{3,0},{4,7},{5,6},{6,5},{7,4},{8,11},{9,10},{10,... | collective-permute-start | bytes 98312 | tf_op jit(solution)/shard_map/ppermute | solution.py:91
  21.6 0.0 collective-permute-done.9.refs_1_
  21.7 1.5 %collective-permute-start.11 = (f32[2,32,128]{2,1,0:T(8,128)S(1)}, f32[2,32,128]{2,1,0:T(8,128)S(1)}, u32[]{:S(2)}, u32[]{:S(2)}) collective-permute-start(f32[2,32,128]{2,1,0:T(8,128)S(1)} %get-tuple-element.52.refs_2_), channel_id=1, source_target_pairs={{0,5},{1,4},{2,7},{3,6},{4,1},{5,0},{6,3},{7,2},{8,13},{9,12},{10,... | collective-permute-start | bytes 98312 | tf_op jit(solution)/shard_map/ppermute | solution.py:91
  23.2 1.3 %collective-permute-done.8.refs_1_ = f32[2,32,128]{2,1,0:T(8,128)S(1)} collective-permute-done((f32[2,32,128]{2,1,0:T(8,128)S(1)}, f32[2,32,128]{2,1,0:T(8,128)S(1)}, u32[]{:S(2)}, u32[]{:S(2)}) %collective-permute-start.8) | collective-permute-done | bytes 32800 | tf_op jit(solution)/shard_map/ppermute | solution.py:91
  24.5 0.7 %collective-permute-start.10 = (f32[1,32,128]{2,1,0:T(8,128)S(1)}, f32[1,32,128]{2,1,0:T(8,128)S(1)}, u32[]{:S(2)}, u32[]{:S(2)}) collective-permute-start(f32[1,32,128]{2,1,0:T(8,128)S(1)} %get-tuple-element.51.refs_0_), channel_id=1, source_target_pairs={{0,5},{1,4},{2,7},{3,6},{4,1},{5,0},{6,3},{7,2},{8,13},{9,12},{10,... | collective-permute-start | bytes 49160 | tf_op jit(solution)/shard_map/ppermute | solution.py:91
  25.2 0.0 collective-permute-done.12.refs_1_
  25.2 0.0 collective-permute-done.11.refs_3_
  25.2 2.5 %collective-permute-done.10.refs_1_ = f32[1,32,128]{2,1,0:T(8,128)S(1)} collective-permute-done((f32[1,32,128]{2,1,0:T(8,128)S(1)}, f32[1,32,128]{2,1,0:T(8,128)S(1)}, u32[]{:S(2)}, u32[]{:S(2)}) %collective-permute-start.10) | collective-permute-done | bytes 16416 | tf_op jit(solution)/shard_map/ppermute | solution.py:91
  27.7 0.5 %turn.1 = (f32[32,32,128]{2,1,0:T(8,128)S(1)}, f32[2,32,128]{2,1,0:T(8,128)S(1)}, f32[32,32,128]{2,1,0:T(8,128)S(1)}, f32[32,32,128]{2,1,0:T(8,128)S(1)}) custom-call(f32[1,32,128]{2,1,0:T(8,128)S(1)} %get-tuple-element.51.refs_0_, f32[1,32,128]{2,1,0:T(8,128)S(1)} %collective-permute-done.10.refs_1_, f32[2,32,128]{2,1,0:T(8,128)S(1)} %get-tuple-element.52.refs_2_, ...), custom_call_target="tpu_custom_call" | custom-call | bytes 1536000 | tf_op jit(solution)/shard_map/turn/pallas_call | solution.py:33
  28.2 1.2 %collective-permute-start.13 = (f32[2,32,128]{2,1,0:T(8,128)S(1)}, f32[2,32,128]{2,1,0:T(8,128)S(1)}, u32[]{:S(2)}, u32[]{:S(2)}) collective-permute-start(f32[2,32,128]{2,1,0:T(8,128)S(1)} %get-tuple-element.60.refs_0_), channel_id=1, source_target_pairs={{0,8},{8,0},{16,24},{24,16},{1,9},{9,1},{17,25},{25,17},{2,10},{10... | collective-permute-start | bytes 98312 | tf_op jit(solution)/shard_map/ppermute | solution.py:91
  29.4 0.9 %collective-permute-start.15 = (f32[2,32,128]{2,1,0:T(8,128)S(1)}, f32[2,32,128]{2,1,0:T(8,128)S(1)}, u32[]{:S(2)}, u32[]{:S(2)}) collective-permute-start(f32[2,32,128]{2,1,0:T(8,128)S(1)} %get-tuple-element.62.refs_2_), channel_id=1, source_target_pairs={{0,16},{8,24},{16,0},{24,8},{1,17},{9,25},{17,1},{25,9},{2,18},{10... | collective-permute-start | bytes 98312 | tf_op jit(solution)/shard_map/ppermute | solution.py:91
  30.3 1.9 %collective-permute-done.13.refs_1_ = f32[2,32,128]{2,1,0:T(8,128)S(1)} collective-permute-done((f32[2,32,128]{2,1,0:T(8,128)S(1)}, f32[2,32,128]{2,1,0:T(8,128)S(1)}, u32[]{:S(2)}, u32[]{:S(2)}) %collective-permute-start.13) | collective-permute-done | bytes 32800 | tf_op jit(solution)/shard_map/ppermute | solution.py:91
  32.2 1.2 %collective-permute-start.14 = (f32[1,32,128]{2,1,0:T(8,128)S(1)}, f32[1,32,128]{2,1,0:T(8,128)S(1)}, u32[]{:S(2)}, u32[]{:S(2)}) collective-permute-start(f32[1,32,128]{2,1,0:T(8,128)S(1)} %get-tuple-element.61.refs_0_), channel_id=1, source_target_pairs={{0,16},{8,24},{16,0},{24,8},{1,17},{9,25},{17,1},{25,9},{2,18},{10... | collective-permute-start | bytes 49160 | tf_op jit(solution)/shard_map/ppermute | solution.py:91
  33.4 0.9 %collective-permute-done.15.refs_3_ = f32[2,32,128]{2,1,0:T(8,128)S(1)} collective-permute-done((f32[2,32,128]{2,1,0:T(8,128)S(1)}, f32[2,32,128]{2,1,0:T(8,128)S(1)}, u32[]{:S(2)}, u32[]{:S(2)}) %collective-permute-start.15) | collective-permute-done | bytes 32800 | tf_op jit(solution)/shard_map/ppermute | solution.py:91
  34.3 2.7 %collective-permute-done.14.refs_1_ = f32[1,32,128]{2,1,0:T(8,128)S(1)} collective-permute-done((f32[1,32,128]{2,1,0:T(8,128)S(1)}, f32[1,32,128]{2,1,0:T(8,128)S(1)}, u32[]{:S(2)}, u32[]{:S(2)}) %collective-permute-start.14) | collective-permute-done | bytes 16416 | tf_op jit(solution)/shard_map/ppermute | solution.py:91
  36.9 0.9 %finish.1 = f32[32,32,128]{2,1,0:T(8,128)} custom-call(f32[1,32,128]{2,1,0:T(8,128)S(1)} %get-tuple-element.61.refs_0_, f32[1,32,128]{2,1,0:T(8,128)S(1)} %collective-permute-done.14.refs_1_, f32[2,32,128]{2,1,0:T(8,128)S(1)} %get-tuple-element.62.refs_2_, f32[2,32,128]{2,1,0:T(8,128)S(1)} %collective-permute-done.15.refs_3_, ...), custom_call_target="tpu_custom_call" | custom-call | bytes 1024000 | tf_op jit(solution)/shard_map/finish/pallas_call | solution.py:33
  (6 shorter events, 0.1 us)
Async XLA Ops:
  1.0 9.0 %collective-permute-start = (f32[11,32,128]{2,1,0:T(8,128)S(1)}, f32[11,32,128]{2,1,0:T(8,128)S(1)}, u32[]{:S(2)}, u32[]{:S(2)}) collective-permute-start(f32[11,32,128]{2,1,0:T(8,128)S(1)} %get-tuple-element.36._), channel_id=1, source_target_pairs={{0,8},{1,9},{2,10},{3,11},{4,12},{5,13},{6,14},{7,15},{8,0},{9,1},... | collective-permute-start | bytes 540680 | tf_op jit(solution)/shard_map/ppermute | solution.py:84
  4.1 4.8 %copy-start = (f32[32,32,128]{2,1,0:T(8,128)S(1)}, f32[32,32,128]{2,1,0:T(8,128)}, u32[]{:S(2)}) copy-start(f32[32,32,128]{2,1,0:T(8,128)} %kappa.1) | copy-start | bytes 1572868
  4.1 5.9 %collective-permute-start.1 = (f32[11,32,128]{2,1,0:T(8,128)S(1)}, f32[11,32,128]{2,1,0:T(8,128)S(1)}, u32[]{:S(2)}, u32[]{:S(2)}) collective-permute-start(f32[11,32,128]{2,1,0:T(8,128)S(1)} %get-tuple-element.37), channel_id=1, source_target_pairs={{0,1},{1,0},{2,3},{3,2},{4,5},{5,4},{6,7},{7,6},{8,16},{9,17},{10,... | collective-permute-start | bytes 540680 | tf_op jit(solution)/shard_map/ppermute | solution.py:84
  5.8 7.2 %collective-permute-start.2 = (f32[11,32,128]{2,1,0:T(8,128)S(1)}, f32[11,32,128]{2,1,0:T(8,128)S(1)}, u32[]{:S(2)}, u32[]{:S(2)}) collective-permute-start(f32[11,32,128]{2,1,0:T(8,128)S(1)} %get-tuple-element.38), channel_id=1, source_target_pairs={{0,7},{1,2},{2,1},{3,4},{4,3},{5,6},{6,5},{7,0},{8,15},{9,10},{10,... | collective-permute-start | bytes 540680 | tf_op jit(solution)/shard_map/ppermute | solution.py:84
  8.4 4.6 %collective-permute-start.3 = (f32[11,32,128]{2,1,0:T(8,128)S(1)}, f32[11,32,128]{2,1,0:T(8,128)S(1)}, u32[]{:S(2)}, u32[]{:S(2)}) collective-permute-start(f32[11,32,128]{2,1,0:T(8,128)S(1)} %get-tuple-element.39), channel_id=1, source_target_pairs={{0,1},{1,0},{2,3},{3,2},{4,5},{5,4},{6,7},{7,6},{8,9},{9,8},{10,11... | collective-permute-start | bytes 540680 | tf_op jit(solution)/shard_map/ppermute | solution.py:91
  8.4 2.2 %collective-permute-start.7 = (f32[5,32,128]{2,1,0:T(8,128)S(1)}, f32[5,32,128]{2,1,0:T(8,128)S(1)}, u32[]{:S(2)}, u32[]{:S(2)}) collective-permute-start(f32[5,32,128]{2,1,0:T(8,128)S(1)} %get-tuple-element.43.ports_y.refs_0_.refs_8_), channel_id=1, source_target_pairs={{0,1},{1,0},{2,3},{3,2},{4,5},{5,4},{6,7},{7,6},{8,9},{9,8},{10,11... | collective-permute-start | bytes 245768 | tf_op jit(solution)/shard_map/ppermute | solution.py:91
  10.1 4.6 %collective-permute-start.4 = (f32[12,8,128]{2,1,0:T(8,128)S(1)}, f32[12,8,128]{2,1,0:T(8,128)S(1)}, u32[]{:S(2)}, u32[]{:S(2)}) collective-permute-start(f32[12,8,128]{2,1,0:T(8,128)S(1)} %get-tuple-element.41), channel_id=1, source_target_pairs={{0,7},{1,2},{2,1},{3,4},{4,3},{5,6},{6,5},{7,0},{8,15},{9,10},{10,... | collective-permute-start | bytes 147464 | tf_op jit(solution)/shard_map/ppermute | solution.py:84
  10.3 2.7 %collective-permute-start.5 = (f32[9,8,128]{2,1,0:T(8,128)S(1)}, f32[9,8,128]{2,1,0:T(8,128)S(1)}, u32[]{:S(2)}, u32[]{:S(2)}) collective-permute-start(f32[9,8,128]{2,1,0:T(8,128)S(1)} %get-tuple-element.42), channel_id=1, source_target_pairs={{0,1},{1,0},{2,3},{3,2},{4,5},{5,4},{6,7},{7,6},{8,9},{9,8},{10,11... | collective-permute-start | bytes 110600 | tf_op jit(solution)/shard_map/ppermute | solution.py:91
  10.6 11.1 %collective-permute-start.9 = (f32[5,32,128]{2,1,0:T(8,128)S(1)}, f32[5,32,128]{2,1,0:T(8,128)S(1)}, u32[]{:S(2)}, u32[]{:S(2)}) collective-permute-start(f32[5,32,128]{2,1,0:T(8,128)S(1)} %get-tuple-element.49.refs_0_), channel_id=1, source_target_pairs={{0,3},{1,2},{2,1},{3,0},{4,7},{5,6},{6,5},{7,4},{8,11},{9,10},{10,... | collective-permute-start | bytes 245768 | tf_op jit(solution)/shard_map/ppermute | solution.py:91
  17.9 3.1 %collective-permute-start.6 = (f32[2,32,128]{2,1,0:T(8,128)S(1)}, f32[2,32,128]{2,1,0:T(8,128)S(1)}, u32[]{:S(2)}, u32[]{:S(2)}) collective-permute-start(f32[2,32,128]{2,1,0:T(8,128)S(1)} %get-tuple-element.46.refs_0_), channel_id=1, source_target_pairs={{0,1},{1,0},{2,3},{3,2},{4,5},{5,4},{6,7},{7,6},{8,9},{9,8},{10,11... | collective-permute-start | bytes 98312 | tf_op jit(solution)/shard_map/ppermute | solution.py:91
  18.0 7.2 %collective-permute-start.12 = (f32[5,32,128]{2,1,0:T(8,128)S(1)}, f32[5,32,128]{2,1,0:T(8,128)S(1)}, u32[]{:S(2)}, u32[]{:S(2)}) collective-permute-start(f32[5,32,128]{2,1,0:T(8,128)S(1)} %get-tuple-element.57.refs_0_.refs_11_.refs_6_), channel_id=1, source_target_pairs={{0,8},{8,0},{16,24},{24,16},{1,9},{9,1},{17,25},{25,17},{2,10},{10... | collective-permute-start | bytes 245768 | tf_op jit(solution)/shard_map/ppermute | solution.py:91
  21.1 3.4 %collective-permute-start.8 = (f32[2,32,128]{2,1,0:T(8,128)S(1)}, f32[2,32,128]{2,1,0:T(8,128)S(1)}, u32[]{:S(2)}, u32[]{:S(2)}) collective-permute-start(f32[2,32,128]{2,1,0:T(8,128)S(1)} %get-tuple-element.48.refs_0_), channel_id=1, source_target_pairs={{0,3},{1,2},{2,1},{3,0},{4,7},{5,6},{6,5},{7,4},{8,11},{9,10},{10,... | collective-permute-start | bytes 98312 | tf_op jit(solution)/shard_map/ppermute | solution.py:91
  21.7 3.6 %collective-permute-start.11 = (f32[2,32,128]{2,1,0:T(8,128)S(1)}, f32[2,32,128]{2,1,0:T(8,128)S(1)}, u32[]{:S(2)}, u32[]{:S(2)}) collective-permute-start(f32[2,32,128]{2,1,0:T(8,128)S(1)} %get-tuple-element.52.refs_2_), channel_id=1, source_target_pairs={{0,5},{1,4},{2,7},{3,6},{4,1},{5,0},{6,3},{7,2},{8,13},{9,12},{10,... | collective-permute-start | bytes 98312 | tf_op jit(solution)/shard_map/ppermute | solution.py:91
  24.5 3.2 %collective-permute-start.10 = (f32[1,32,128]{2,1,0:T(8,128)S(1)}, f32[1,32,128]{2,1,0:T(8,128)S(1)}, u32[]{:S(2)}, u32[]{:S(2)}) collective-permute-start(f32[1,32,128]{2,1,0:T(8,128)S(1)} %get-tuple-element.51.refs_0_), channel_id=1, source_target_pairs={{0,5},{1,4},{2,7},{3,6},{4,1},{5,0},{6,3},{7,2},{8,13},{9,12},{10,... | collective-permute-start | bytes 49160 | tf_op jit(solution)/shard_map/ppermute | solution.py:91
  28.2 4.0 %collective-permute-start.13 = (f32[2,32,128]{2,1,0:T(8,128)S(1)}, f32[2,32,128]{2,1,0:T(8,128)S(1)}, u32[]{:S(2)}, u32[]{:S(2)}) collective-permute-start(f32[2,32,128]{2,1,0:T(8,128)S(1)} %get-tuple-element.60.refs_0_), channel_id=1, source_target_pairs={{0,8},{8,0},{16,24},{24,16},{1,9},{9,1},{17,25},{25,17},{2,10},{10... | collective-permute-start | bytes 98312 | tf_op jit(solution)/shard_map/ppermute | solution.py:91
  29.4 4.8 %collective-permute-start.15 = (f32[2,32,128]{2,1,0:T(8,128)S(1)}, f32[2,32,128]{2,1,0:T(8,128)S(1)}, u32[]{:S(2)}, u32[]{:S(2)}) collective-permute-start(f32[2,32,128]{2,1,0:T(8,128)S(1)} %get-tuple-element.62.refs_2_), channel_id=1, source_target_pairs={{0,16},{8,24},{16,0},{24,8},{1,17},{9,25},{17,1},{25,9},{2,18},{10... | collective-permute-start | bytes 98312 | tf_op jit(solution)/shard_map/ppermute | solution.py:91
  32.2 4.7 %collective-permute-start.14 = (f32[1,32,128]{2,1,0:T(8,128)S(1)}, f32[1,32,128]{2,1,0:T(8,128)S(1)}, u32[]{:S(2)}, u32[]{:S(2)}) collective-permute-start(f32[1,32,128]{2,1,0:T(8,128)S(1)} %get-tuple-element.61.refs_0_), channel_id=1, source_target_pairs={{0,16},{8,24},{16,0},{24,8},{1,17},{9,25},{17,1},{25,9},{2,18},{10... | collective-permute-start | bytes 49160 | tf_op jit(solution)/shard_map/ppermute | solution.py:91

commit v6 on v5

--- a/solution.py
+++ b/solution.py
@@ -65,7 +65,11 @@
 
 
 def y_other(index):
-    return (index + 1 if index % 2 else index - 1) % lax.axis_size("gy")
+    return index + 1 if index % 2 else index - 1
+
+
+def y_ring(index):
+    return y_other(index) % lax.axis_size("gy")
 
 
 def permutation(z_partner, y_partner):
@@ -76,6 +80,8 @@
             to_z, to_y = z_partner(z), y_partner(y)
             if not 0 <= to_z < z_count:
                 to_z, to_y = z, pair_up(y)
+            elif not 0 <= to_y < y_count:
+                to_z, to_y = pair_up(z), y
             pairs.append((z * y_count + y, to_z * y_count + to_y))
     return pairs
 
@@ -95,22 +101,33 @@
     return (lax.axis_size(axis) - 1).bit_length()
 
 
-def z_rims_kernel(tracer, y_speed, z_speed, a_ref, b_ref, sem):
+def flux(speed, lower, upper):
+    return speed * jnp.where(speed > 0.0, lower, upper)
+
+
+def z_rims_kernel(tracer, y_speed, z_speed, b_ref, a_ref, outer_rows, sem):
     z, _, _, _ = place()
     depth = tracer.shape[0]
     z_odd = lax.rem(z, 2)
+    sides = ((b_ref, 1 - z_odd), (a_ref, z_odd))
     copies = []
-    for ref, low in ((a_ref, z_odd), (b_ref, 1 - z_odd)):
-        four, three = (1 - low) * (depth - 4), (1 - low) * (depth - 3)
-        for source, start, count, row in ((tracer, four, 4, 0), (z_speed, four, 4, 4), (y_speed, three, 3, 8)):
-            copies.append(
-                pltpu.make_async_copy(
-                    source.at[pl.ds(start, count)], ref.at[pl.ds(row, count)], sem.at[len(copies)]
-                )
-            )
-            copies[-1].start()
+
+    def start(source, target):
+        copies.append(pltpu.make_async_copy(source, target, sem.at[len(copies)]))
+        copies[-1].start()
+
+    for side, (ref, low) in enumerate(sides):
+        near_rows, fourth = (1 - low) * (depth - 3), jnp.where(low == 1, 3, depth - 4)
+        for k, field in enumerate((tracer, z_speed)):
+            start(field.at[pl.ds(fourth, 1)], outer_rows.at[side, pl.ds(k, 1)])
+        for k, field in enumerate((tracer, z_speed, y_speed)):
+            start(field.at[pl.ds(near_rows, 3)], ref.at[pl.ds(3 * k, 3)])
     for copy in copies:
         copy.wait()
+    for side, (ref, low) in enumerate(sides):
+        third, fourth = ref[2 * low], outer_rows[side, 0]
+        speed = 0.5 * (ref[3 + 2 * low] + outer_rows[side, 1])
+        ref[9] = flux(speed, jnp.where(low == 1, third, fourth), jnp.where(low == 1, fourth, third))
 
 
 def z_rims(tracer, y_speed, z_speed):
@@ -118,9 +135,9 @@
     return call(
         z_rims_kernel,
         "z_rims",
-        [near(11, width, band)] * 2,
+        [near(10, width, band)] * 2,
         [("far", x) for x in (tracer, y_speed, z_speed)],
-        scratch=[pltpu.SemaphoreType.DMA((6,))],
+        scratch=[near(2, 2, width, band), pltpu.SemaphoreType.DMA((10,))],
         cycles=1000,
     )
 
@@ -145,10 +162,13 @@
     def rims(o_low):
         for ref, low in ((o_ref, o_low), (e_ref, not o_low)):
             tile = slice(0, 8) if low else slice(width - 8, width)
-            four, three = (0, 0) if low else (4, 5)
-            ref[0:4] = turned(c[:, tile, :])[four : four + 4]
-            ref[4:8] = turned(ys[:, tile, :])[four : four + 4]
-            ref[8:11] = turned(zs[:, tile, :])[three : three + 3]
+            tc, ty, tz = (turned(f[:, tile, :]) for f in (c, ys, zs))
+            three = 0 if low else 5
+            lower, upper = (2, 3) if low else (4, 5)
+            ref[0:3] = tc[three : three + 3]
+            ref[3:6] = ty[three : three + 3]
+            ref[6:9] = tz[three : three + 3]
+            ref[9] = flux(0.5 * (ty[lower] + ty[upper]), tc[lower], tc[upper])
 
     @pl.when(y_odd == 0)
     def _():
@@ -164,7 +184,7 @@
     return call(
         begin_kernel,
         "begin",
-        [near(11, depth, band)] * 2 + [near(5, depth, band)],
+        [near(10, depth, band)] * 2 + [near(5, depth, band)],
         [("far", x) for x in (tracer, y_speed, z_speed, kappa)] + [after],
         scratch=[near(depth, width, band)] * 4 + [near(width, depth, band)] * 2 + [pltpu.SemaphoreType.DMA((4,))],
         cycles=2000,
@@ -174,18 +194,18 @@
 PAD_TILES = 3
 
 
-def rim_kernel(a, b, _, for_pair, for_other):
+def rim_kernel(b, a, _, for_pair, for_other):
     z, y, _, _ = place()
     width = a.shape[1]
     z_odd, y_odd = lax.rem(z, 2) == 1, lax.rem(y, 2)
 
     def corners(out, low):
         tile, first = (slice(0, 8), 0) if low else (slice(width - 8, width), 5)
-        for f, (row, count) in enumerate(((0, 4), (8, 3), (4, 4))):
-            empty = [jnp.zeros((3, 4 - count, out.shape[2]), F32)] if count < 4 else []
-            side_a, side_b = (turned(ref[row : row + count, tile, :])[first : first + 3] for ref in (a, b))
+        empty = jnp.zeros((3, 1, out.shape[2]), F32)
+        for f, row in enumerate((0, 6, 3)):
+            side_a, side_b = (turned(ref[row : row + 3, tile, :])[first : first + 3] for ref in (a, b))
             below, above = jnp.where(z_odd, side_a, side_b), jnp.where(z_odd, side_b, side_a)
-            out[3 * f : 3 * f + 3] = jnp.concatenate([*empty, below, above, *empty], axis=1)
+            out[3 * f : 3 * f + 3] = jnp.concatenate([empty, below, above, empty], axis=1)
 
     @pl.when(y_odd == 0)
     def _():
@@ -202,7 +222,7 @@
 
 def rim(a, b, after):
     band = a.shape[2]
-    return call(rim_kernel, "rim", [near(9, 8, band), near(9 + PAD_TILES, 8, band)], [a, b, after], cycles=200)
+    return call(rim_kernel, "rim", [near(9, 8, band), near(9 + PAD_TILES, 8, band)], [b, a, after], cycles=200)
 
 
 def reciprocal(x):
@@ -402,8 +422,8 @@
 
 
 def advect_kernel(
-    tracer, y_speed, z_speed, a, b, o, e, corner, ab, ports_y, r_y_far, r_z_far, ports_z,
-    base, sources, r_y, r_z, ports_out, c, ys, zs, sy, sz, phi, psi, kept, sem,
+    tracer, y_speed, z_speed, b, a, o, e, corner, ab, ports_y, r_y_far, r_z_far, ports_z,
+    base, sources, r_y, r_z, ports_out, c, ys, zs, sy, sz, phi, psi, kept, flux_z, flux_y, sem,
 ):
     z, y, z_count, y_count = place()
     depth, width, band = tracer.shape
@@ -431,34 +451,30 @@
     for field in (c, ys, zs):
         field[0:4, width:cols, :] = jnp.zeros((4, 8, band), F32)
         field[4 + depth : rows, width:cols, :] = jnp.zeros((4, 8, band), F32)
-    ys[0:1, 0:width, :] = jnp.zeros((1, width, band), F32)
-    ys[rows - 1 : rows, 0:width, :] = jnp.zeros((1, width, band), F32)
-    for ref, low, keep in ((a, z_odd, None), (b, 1 - z_odd, keep_b)):
-        scale = (lambda v: v) if keep is None else (lambda v: v * keep)
-        four = jnp.where(low == 1, 0, depth + 4)
+    flux_z[:, width:cols, :] = jnp.zeros((2, 8, band), F32)
+    for ref, low, keep in ((a, z_odd, 1.0), (b, 1 - z_odd, keep_b)):
         three = jnp.where(low == 1, 1, depth + 4)
-        c[pl.ds(four, 4), 0:width, :] = scale(ref[0:4])
-        zs[pl.ds(four, 4), 0:width, :] = scale(ref[4:8])
-        ys[pl.ds(three, 3), 0:width, :] = scale(ref[8:11])
+        for k, field in enumerate((c, zs, ys)):
+            field[pl.ds(three, 3), 0:width, :] = ref[3 * k : 3 * k + 3] * keep
+        flux_z[1 - low, 0:width, :] = ref[9] * keep
 
     def sides(o_low):
-        def columns(first, count):
-            other, pair = o[first : first + count] * keep_o, e[first : first + count]
-            above, below = (pair, other) if o_low else (other, pair)
-            empty = [jnp.zeros((4 - count, depth, band), F32)] if count < 4 else []
-            return turned(jnp.concatenate([above, *empty, *empty, below], axis=0))
-
-        c[4 : 4 + depth, width:cols, :] = columns(0, 4)
-        ys[4 : 4 + depth, width:cols, :] = columns(4, 4)
-        zs[4 : 4 + depth, width:cols, :] = columns(8, 3)
+        other, pair = (o, keep_o), (e, 1.0)
+        (above, keep_up), (below, keep_down) = (pair, other) if o_low else (other, pair)
+        empty = jnp.zeros((2, depth, band), F32)
+        for k, field in enumerate((c, ys, zs)):
+            three = slice(3 * k, 3 * k + 3)
+            tile = jnp.concatenate([above[three] * keep_up, empty, below[three] * keep_down], axis=0)
+            field[4 : 4 + depth, width:cols, :] = turned(tile)
+        faces = [empty, above[9:10] * keep_up, empty[:1], below[9:10] * keep_down, empty, empty[:1]]
+        flux_y[...] = turned(jnp.concatenate(faces, axis=0))
 
         def corners(ref, low, keep):
             start = width + (5 if low else 0)
-            for f, (field, count) in enumerate(((c, 4), (ys, 3), (zs, 4))):
+            for f, field in enumerate((c, ys, zs)):
                 for k in range(3):
-                    below, above = ref[3 * f + k, 4 - count : 4, :], ref[3 * f + k, 4 : 4 + count, :]
-                    field[4 - count : 4, start + k, :] = below * (keep * keep_below)
-                    field[depth + 4 : depth + 4 + count, start + k, :] = above * (keep * keep_above)
+                    field[1:4, start + k, :] = ref[3 * f + k, 1:4, :] * (keep * keep_below)
+                    field[depth + 4 : depth + 7, start + k, :] = ref[3 * f + k, 4:7, :] * (keep * keep_above)
 
         corners(corner, o_low, keep_o)
         corners(ab, not o_low, 1.0)
@@ -479,9 +495,6 @@
 
     def down(v):
         return pltpu.roll(v, 1, 0)
-
-    def flux(speed, here, after):
-        return speed * jnp.where(speed > 0.0, here, after)
 
     def faces(r, before):
         v = ys[r]
@@ -495,20 +508,34 @@
 
     keep_low = jnp.where(z == 0, 0.0, 1.0)
     keep_high = jnp.where(z == z_count - 1, 0.0, 1.0)
+    given = (column == 2) | (column == 4)
     for step in range(1, NSUB + 1):
-        here = c[step]
-
-        def row(r, carry):
+
+        def row(r, carry, side=False, top=None):
             here, below = carry
             after = c[r + 1]
-            above = flux(sz[r], here, after)
+            above = flux(sz[r], here, after) if top is None else top
             across = flux(sy[r], here, up(here))
+            if side:
+                edge = jnp.where(given, flux_y[r - 4], across[width:cols])
+                across = jnp.concatenate([across[0:width], edge], axis=0)
             new = here - (across - down(across)) - (above - below)
             c[r, 0:width, :] = new[0:width]
             c[r, width:cols, :] = new[width:cols] * inside
             return after, above
 
-        lax.fori_loop(step, rows - step, row, (here, flux(sz[step - 1], c[step - 1], here)), unroll=16)
+        if step == 1:
+            carry = c[1], flux_z[0]
+            for r in range(1, 4):
+                carry = row(r, carry)
+            side_row = lambda r, carry: row(r, carry, side=True)
+            carry = lax.fori_loop(4, 4 + depth, side_row, carry, unroll=16)
+            for r in range(4 + depth, rows - 2):
+                carry = row(r, carry)
+            row(rows - 2, carry, top=flux_z[1])
+        else:
+            below = flux(sz[step - 1], c[step - 1], c[step])
+            lax.fori_loop(step, rows - step, row, (c[step], below), unroll=16)
         if step < NSUB:
             c[3] = c[3] * keep_low
             c[4 + depth] = c[4 + depth] * keep_high
@@ -531,7 +558,8 @@
         [("far", x) for x in (tracer, y_speed, z_speed)]
         + list(halos)
         + [ports_y, ("far", r_y), ("far", r_z), ports_z],
-        scratch=[padded] * 5 + [along_y] * 3 + [pltpu.SemaphoreType.DMA((5,))],
+        scratch=[padded] * 5 + [along_y] * 3
+        + [near(2, width + 8, band), near(depth, 8, band), pltpu.SemaphoreType.DMA((5,))],
         cycles=5000,
     )
 
@@ -618,12 +646,12 @@
 
 
 def local(tracer, y_speed, z_speed, kappa):
-    a, b = z_rims(tracer, y_speed, z_speed)
-    o, e, ports_y = begin(tracer, y_speed, z_speed, kappa, a)
+    b, a = z_rims(tracer, y_speed, z_speed)
+    o, e, ports_y = begin(tracer, y_speed, z_speed, kappa, b)
+    b = send(b, z_partner=z_other)
     a = send(a, z_partner=pair_up)
-    b = send(b, z_partner=z_other)
     e = swap(e, "gy", 0)
-    o = send(o, y_partner=y_other)
+    o = send(o, y_partner=y_ring)
     r_y, r_z, ports_z = factor_lines(kappa)
     for_pair, for_other = rim(a, b, ports_z)
     corner = send(for_other, y_partner=y_other)
@@ -631,7 +659,7 @@
     joints_y, edge_y, edge_y_theirs = join_all(ports_y, "gy")
 
     base, sources, r_y, r_z, ports_z = advect(
-        tracer, y_speed, z_speed, (a, b, o, e, corner, ab), ports_y, r_y, r_z, ports_z
+        tracer, y_speed, z_speed, (b, a, o, e, corner, ab), ports_y, r_y, r_z, ports_z
     )
     joints_z, edge_z, edge_z_theirs = join_all(ports_z, "gz")
     mine, theirs, flows = exchange_sources(sources, joints_y, "gy")

time: 38 us -> 36.5 us (0.961)
  waiting for transfers between devices: 11.9 us -> 8.93 us
  starting transfers between devices: 17.2 us -> 18.6 us
    ppermute x12, waiting for transfers between devices: 9.25 us -> 7.33 us  [swap(): lax.ppermute(x, axis, [(i, i ^ step) for i in range(lax.axis_size(axis))])]
    ppermute x4, starting transfers between devices: 5.87 us -> 7.05 us  [send(): return lax.ppermute(x, AXES, permutation(z_partner, y_partner))]
    ppermute x4, waiting for transfers between devices: 2.67 us -> 1.61 us  [send(): return lax.ppermute(x, AXES, permutation(z_partner, y_partner))]
  transfers between devices with their start and end apart: 16 -> 16, of which waited for: 7 -> 7; matrix products, arithmetic and copies ran while one was open for 0% -> 0% of each run, Pallas kernels for 16% -> 17%
where the time goes in v6:
time: 36.5 us; the launch traced here: 36.3 us
  starting transfers between devices  18.6 us (51%)
  waiting for transfers between devices  8.93 us (24%)
  Pallas kernels  8.62 us (24%)
    ppermute x12, starting transfers between devices, swap(): lax.ppermute(x, axis, [(i, i ^ step) for i in range(lax.axis_size(axis))])  11.5 us
    pallas_call x13, Pallas kernels, call(): pl.pallas_call(kernel, out_shape=[out[1] if isinstance(out, tuple) else o...  8.62 us
    ppermute x12, waiting for transfers between devices, swap(): lax.ppermute(x, axis, [(i, i ^ step) for i in range(lax.axis_size(axis))])  7.33 us
    ppermute x4, starting transfers between devices, send(): return lax.ppermute(x, AXES, permutation(z_partner, y_partner))  7.05 us
    ppermute x4, waiting for transfers between devices, send(): return lax.ppermute(x, AXES, permutation(z_partner, y_partner))  1.61 us
  transfers between devices with their start and end apart: 16, of which 7 were waited for; matrix products, arithmetic and copies ran while one was open for 0% of the time, Pallas kernels for 17%

profile of v6, /device:TPU:0, one launch (start us, length us, event | category | flops | bytes accessed | tf_op | source)
XLA Modules:
  0.0 36.3 jit_solution(12138974030171405393)
XLA Ops:
  0.0 1.1 %z_rims.1 = (f32[10,32,128]{2,1,0:T(8,128)S(1)}, f32[10,32,128]{2,1,0:T(8,128)S(1)}) custom-call(f32[32,32,128]{2,1,0:T(8,128)} %tracer.5, f32[32,32,128]{2,1,0:T(8,128)} %y_speed.5, f32[32,32,128]{2,1,0:T(8,128)} %z_speed.5), custom_call_target="tpu_custom_call" | custom-call | bytes 1024000 | tf_op jit(solution)/shard_map/z_rims/pallas_call | solution.py:33
  1.1 0.5 %collective-permute-start = (f32[10,32,128]{2,1,0:T(8,128)S(1)}, f32[10,32,128]{2,1,0:T(8,128)S(1)}, u32[]{:S(2)}, u32[]{:S(2)}) collective-permute-start(f32[10,32,128]{2,1,0:T(8,128)S(1)} %get-tuple-element.36._), channel_id=1, source_target_pairs={{0,1},{1,0},{2,3},{3,2},{4,5},{5,4},{6,7},{7,6},{8,16},{9,17},{10,... | collective-permute-start | bytes 491528 | tf_op jit(solution)/shard_map/ppermute | solution.py:90
  1.6 0.0 copy-start
  1.6 4.1 %collective-permute-start.1 = (f32[10,32,128]{2,1,0:T(8,128)S(1)}, f32[10,32,128]{2,1,0:T(8,128)S(1)}, u32[]{:S(2)}, u32[]{:S(2)}) collective-permute-start(f32[10,32,128]{2,1,0:T(8,128)S(1)} %get-tuple-element.37), channel_id=1, source_target_pairs={{0,8},{1,9},{2,10},{3,11},{4,12},{5,13},{6,14},{7,15},{8,0},{9,1},... | collective-permute-start | bytes 491528 | tf_op jit(solution)/shard_map/ppermute | solution.py:90
  5.8 1.7 %begin.1 = (f32[10,32,128]{2,1,0:T(8,128)S(1)}, f32[10,32,128]{2,1,0:T(8,128)S(1)}, f32[5,32,128]{2,1,0:T(8,128)S(1)}) custom-call(f32[32,32,128]{2,1,0:T(8,128)} %tracer.5, f32[32,32,128]{2,1,0:T(8,128)} %y_speed.5, f32[32,32,128]{2,1,0:T(8,128)} %z_speed.5, f32[32,32,128]{2,1,0:T(8,128)} %kappa.1, f32[10,32,128]{2,1,0:T(8,128)S(1)} %get-tuple-element.36._), custom_call_target="tpu_custom_call" | custom-call | bytes 2048000 | tf_op jit(solution)/shard_map/begin/pallas_call | solution.py:33
  7.4 1.4 %collective-permute-start.2 = (f32[10,32,128]{2,1,0:T(8,128)S(1)}, f32[10,32,128]{2,1,0:T(8,128)S(1)}, u32[]{:S(2)}, u32[]{:S(2)}) collective-permute-start(f32[10,32,128]{2,1,0:T(8,128)S(1)} %get-tuple-element.38), channel_id=1, source_target_pairs={{0,7},{1,2},{2,1},{3,4},{4,3},{5,6},{6,5},{7,0},{8,15},{9,10},{10,... | collective-permute-start | bytes 491528 | tf_op jit(solution)/shard_map/ppermute | solution.py:90
  8.8 0.3 collective-permute-start.3
  9.1 0.2 collective-permute-start.7
  9.3 0.0 copy-done
  9.3 1.1 %factor.1 = (f32[32,32,128]{2,1,0:T(8,128)}, f32[32,32,128]{2,1,0:T(8,128)}, f32[5,32,128]{2,1,0:T(8,128)S(1)}) custom-call(f32[32,32,128]{2,1,0:T(8,128)S(1)} %copy-done), custom_call_target="tpu_custom_call" | custom-call | bytes 4096000 | tf_op jit(solution)/shard_map/factor/pallas_call | solution.py:33
  10.4 0.0 collective-permute-done.b
  10.5 0.0 collective-permute-done.1.a
  10.5 0.1 rim.1
  10.5 1.0 %collective-permute-start.4 = (f32[12,8,128]{2,1,0:T(8,128)S(1)}, f32[12,8,128]{2,1,0:T(8,128)S(1)}, u32[]{:S(2)}, u32[]{:S(2)}) collective-permute-start(f32[12,8,128]{2,1,0:T(8,128)S(1)} %get-tuple-element.41), channel_id=1, source_target_pairs={{0,8},{1,2},{2,1},{3,4},{4,3},{5,6},{6,5},{7,15},{8,0},{9,10},{10,... | collective-permute-start | bytes 147464 | tf_op jit(solution)/shard_map/ppermute | solution.py:90
  11.5 0.4 %collective-permute-start.5 = (f32[9,8,128]{2,1,0:T(8,128)S(1)}, f32[9,8,128]{2,1,0:T(8,128)S(1)}, u32[]{:S(2)}, u32[]{:S(2)}) collective-permute-start(f32[9,8,128]{2,1,0:T(8,128)S(1)} %get-tuple-element.42), channel_id=1, source_target_pairs={{0,1},{1,0},{2,3},{3,2},{4,5},{5,4},{6,7},{7,6},{8,9},{9,8},{10,11... | collective-permute-start | bytes 110600 | tf_op jit(solution)/shard_map/ppermute | solution.py:97
  12.0 0.0 collective-permute-done.7.refs_1_
  12.0 1.2 %collective-permute-start.9 = (f32[5,32,128]{2,1,0:T(8,128)S(1)}, f32[5,32,128]{2,1,0:T(8,128)S(1)}, u32[]{:S(2)}, u32[]{:S(2)}) collective-permute-start(f32[5,32,128]{2,1,0:T(8,128)S(1)} %get-tuple-element.49.refs_0_), channel_id=1, source_target_pairs={{0,3},{1,2},{2,1},{3,0},{4,7},{5,6},{6,5},{7,4},{8,11},{9,10},{10,... | collective-permute-start | bytes 245768 | tf_op jit(solution)/shard_map/ppermute | solution.py:97
  13.2 1.6 %collective-permute-done.2.o = f32[10,32,128]{2,1,0:T(8,128)S(1)} collective-permute-done((f32[10,32,128]{2,1,0:T(8,128)S(1)}, f32[10,32,128]{2,1,0:T(8,128)S(1)}, u32[]{:S(2)}, u32[]{:S(2)}) %collective-permute-start.2) | collective-permute-done | bytes 163872 | tf_op jit(solution)/shard_map/ppermute | solution.py:90
  14.8 0.0 collective-permute-done.3.e
  14.8 0.0 collective-permute-done.5.ab
  14.8 0.0 collective-permute-done.4.corner
  14.8 3.2 %advect.1 = (f32[32,32,128]{2,1,0:T(8,128)S(1)}, f32[2,32,128]{2,1,0:T(8,128)S(1)}, f32[32,32,128]{2,1,0:T(8,128)S(1)}, f32[32,32,128]{2,1,0:T(8,128)S(1)}, f32[5,32,128]{2,1,0:T(8,128)S(1)}) custom-call(f32[32,32,128]{2,1,0:T(8,128)} %tracer.5, f32[32,32,128]{2,1,0:T(8,128)} %y_speed.5, f32[32,32,128]{2,1,0:T(8,128)} %z_speed.5, ...), custom_call_target="tpu_custom_call" | custom-call | bytes 5120000 | tf_op jit(solution)/shard_map/advect/pallas_call | solution.py:33
  18.0 0.2 collective-permute-start.6
  18.2 0.8 %collective-permute-start.12 = (f32[5,32,128]{2,1,0:T(8,128)S(1)}, f32[5,32,128]{2,1,0:T(8,128)S(1)}, u32[]{:S(2)}, u32[]{:S(2)}) collective-permute-start(f32[5,32,128]{2,1,0:T(8,128)S(1)} %get-tuple-element.57.refs_0_.refs_11_.refs_6_), channel_id=1, source_target_pairs={{0,8},{8,0},{16,24},{24,16},{1,9},{9,1},{17,25},{25,17},{2,10},{10... | collective-permute-start | bytes 245768 | tf_op jit(solution)/shard_map/ppermute | solution.py:97
  19.0 0.3 collective-permute-done.6.refs_1_
  19.3 2.0 %collective-permute-start.8 = (f32[2,32,128]{2,1,0:T(8,128)S(1)}, f32[2,32,128]{2,1,0:T(8,128)S(1)}, u32[]{:S(2)}, u32[]{:S(2)}) collective-permute-start(f32[2,32,128]{2,1,0:T(8,128)S(1)} %get-tuple-element.48.refs_0_), channel_id=1, source_target_pairs={{0,3},{1,2},{2,1},{3,0},{4,7},{5,6},{6,5},{7,4},{8,11},{9,10},{10,... | collective-permute-start | bytes 98312 | tf_op jit(solution)/shard_map/ppermute | solution.py:97
  21.3 0.0 collective-permute-done.9.refs_1_
  21.4 0.1 collective-permute-start.11
  21.5 1.5 %collective-permute-done.8.refs_1_ = f32[2,32,128]{2,1,0:T(8,128)S(1)} collective-permute-done((f32[2,32,128]{2,1,0:T(8,128)S(1)}, f32[2,32,128]{2,1,0:T(8,128)S(1)}, u32[]{:S(2)}, u32[]{:S(2)}) %collective-permute-start.8) | collective-permute-done | bytes 32800 | tf_op jit(solution)/shard_map/ppermute | solution.py:97
  23.0 1.6 %collective-permute-start.10 = (f32[1,32,128]{2,1,0:T(8,128)S(1)}, f32[1,32,128]{2,1,0:T(8,128)S(1)}, u32[]{:S(2)}, u32[]{:S(2)}) collective-permute-start(f32[1,32,128]{2,1,0:T(8,128)S(1)} %get-tuple-element.51.refs_0_), channel_id=1, source_target_pairs={{0,5},{1,4},{2,7},{3,6},{4,1},{5,0},{6,3},{7,2},{8,13},{9,12},{10,... | collective-permute-start | bytes 49160 | tf_op jit(solution)/shard_map/ppermute | solution.py:97
  24.6 0.0 collective-permute-done.12.refs_1_
  24.6 0.1 collective-permute-done.11.refs_3_
  24.8 1.4 %collective-permute-done.10.refs_1_ = f32[1,32,128]{2,1,0:T(8,128)S(1)} collective-permute-done((f32[1,32,128]{2,1,0:T(8,128)S(1)}, f32[1,32,128]{2,1,0:T(8,128)S(1)}, u32[]{:S(2)}, u32[]{:S(2)}) %collective-permute-start.10) | collective-permute-done | bytes 16416 | tf_op jit(solution)/shard_map/ppermute | solution.py:97
  26.2 0.5 %turn.1 = (f32[32,32,128]{2,1,0:T(8,128)S(1)}, f32[2,32,128]{2,1,0:T(8,128)S(1)}, f32[32,32,128]{2,1,0:T(8,128)S(1)}, f32[32,32,128]{2,1,0:T(8,128)S(1)}) custom-call(f32[1,32,128]{2,1,0:T(8,128)S(1)} %get-tuple-element.51.refs_0_, f32[1,32,128]{2,1,0:T(8,128)S(1)} %collective-permute-done.10.refs_1_, f32[2,32,128]{2,1,0:T(8,128)S(1)} %get-tuple-element.52.refs_2_, ...), custom_call_target="tpu_custom_call" | custom-call | bytes 1536000 | tf_op jit(solution)/shard_map/turn/pallas_call | solution.py:33
  26.7 0.8 %collective-permute-start.13 = (f32[2,32,128]{2,1,0:T(8,128)S(1)}, f32[2,32,128]{2,1,0:T(8,128)S(1)}, u32[]{:S(2)}, u32[]{:S(2)}) collective-permute-start(f32[2,32,128]{2,1,0:T(8,128)S(1)} %get-tuple-element.60.refs_0_), channel_id=1, source_target_pairs={{0,8},{8,0},{16,24},{24,16},{1,9},{9,1},{17,25},{25,17},{2,10},{10... | collective-permute-start | bytes 98312 | tf_op jit(solution)/shard_map/ppermute | solution.py:97
  27.5 2.1 %collective-permute-start.15 = (f32[2,32,128]{2,1,0:T(8,128)S(1)}, f32[2,32,128]{2,1,0:T(8,128)S(1)}, u32[]{:S(2)}, u32[]{:S(2)}) collective-permute-start(f32[2,32,128]{2,1,0:T(8,128)S(1)} %get-tuple-element.62.refs_2_), channel_id=1, source_target_pairs={{0,16},{8,24},{16,0},{24,8},{1,17},{9,25},{17,1},{25,9},{2,18},{10... | collective-permute-start | bytes 98312 | tf_op jit(solution)/shard_map/ppermute | solution.py:97
  29.6 1.1 %collective-permute-done.13.refs_1_ = f32[2,32,128]{2,1,0:T(8,128)S(1)} collective-permute-done((f32[2,32,128]{2,1,0:T(8,128)S(1)}, f32[2,32,128]{2,1,0:T(8,128)S(1)}, u32[]{:S(2)}, u32[]{:S(2)}) %collective-permute-start.13) | collective-permute-done | bytes 32800 | tf_op jit(solution)/shard_map/ppermute | solution.py:97
  30.7 1.8 %collective-permute-start.14 = (f32[1,32,128]{2,1,0:T(8,128)S(1)}, f32[1,32,128]{2,1,0:T(8,128)S(1)}, u32[]{:S(2)}, u32[]{:S(2)}) collective-permute-start(f32[1,32,128]{2,1,0:T(8,128)S(1)} %get-tuple-element.61.refs_0_), channel_id=1, source_target_pairs={{0,16},{8,24},{16,0},{24,8},{1,17},{9,25},{17,1},{25,9},{2,18},{10... | collective-permute-start | bytes 49160 | tf_op jit(solution)/shard_map/ppermute | solution.py:97
  32.5 0.0 collective-permute-done.15.refs_3_
  32.5 2.9 %collective-permute-done.14.refs_1_ = f32[1,32,128]{2,1,0:T(8,128)S(1)} collective-permute-done((f32[1,32,128]{2,1,0:T(8,128)S(1)}, f32[1,32,128]{2,1,0:T(8,128)S(1)}, u32[]{:S(2)}, u32[]{:S(2)}) %collective-permute-start.14) | collective-permute-done | bytes 16416 | tf_op jit(solution)/shard_map/ppermute | solution.py:97
  35.4 0.9 %finish.1 = f32[32,32,128]{2,1,0:T(8,128)} custom-call(f32[1,32,128]{2,1,0:T(8,128)S(1)} %get-tuple-element.61.refs_0_, f32[1,32,128]{2,1,0:T(8,128)S(1)} %collective-permute-done.14.refs_1_, f32[2,32,128]{2,1,0:T(8,128)S(1)} %get-tuple-element.62.refs_2_, f32[2,32,128]{2,1,0:T(8,128)S(1)} %collective-permute-done.15.refs_3_, ...), custom_call_target="tpu_custom_call" | custom-call | bytes 1024000 | tf_op jit(solution)/shard_map/finish/pallas_call | solution.py:33
  (6 shorter events, 0.1 us)
Async XLA Ops:
  1.1 9.4 %collective-permute-start = (f32[10,32,128]{2,1,0:T(8,128)S(1)}, f32[10,32,128]{2,1,0:T(8,128)S(1)}, u32[]{:S(2)}, u32[]{:S(2)}) collective-permute-start(f32[10,32,128]{2,1,0:T(8,128)S(1)} %get-tuple-element.36._), channel_id=1, source_target_pairs={{0,1},{1,0},{2,3},{3,2},{4,5},{5,4},{6,7},{7,6},{8,16},{9,17},{10,... | collective-permute-start | bytes 491528 | tf_op jit(solution)/shard_map/ppermute | solution.py:90
  1.6 7.7 %copy-start = (f32[32,32,128]{2,1,0:T(8,128)S(1)}, f32[32,32,128]{2,1,0:T(8,128)}, u32[]{:S(2)}) copy-start(f32[32,32,128]{2,1,0:T(8,128)} %kappa.1) | copy-start | bytes 1572868
  1.6 8.8 %collective-permute-start.1 = (f32[10,32,128]{2,1,0:T(8,128)S(1)}, f32[10,32,128]{2,1,0:T(8,128)S(1)}, u32[]{:S(2)}, u32[]{:S(2)}) collective-permute-start(f32[10,32,128]{2,1,0:T(8,128)S(1)} %get-tuple-element.37), channel_id=1, source_target_pairs={{0,8},{1,9},{2,10},{3,11},{4,12},{5,13},{6,14},{7,15},{8,0},{9,1},... | collective-permute-start | bytes 491528 | tf_op jit(solution)/shard_map/ppermute | solution.py:90
  7.4 7.4 %collective-permute-start.2 = (f32[10,32,128]{2,1,0:T(8,128)S(1)}, f32[10,32,128]{2,1,0:T(8,128)S(1)}, u32[]{:S(2)}, u32[]{:S(2)}) collective-permute-start(f32[10,32,128]{2,1,0:T(8,128)S(1)} %get-tuple-element.38), channel_id=1, source_target_pairs={{0,7},{1,2},{2,1},{3,4},{4,3},{5,6},{6,5},{7,0},{8,15},{9,10},{10,... | collective-permute-start | bytes 491528 | tf_op jit(solution)/shard_map/ppermute | solution.py:90
  8.8 6.0 %collective-permute-start.3 = (f32[10,32,128]{2,1,0:T(8,128)S(1)}, f32[10,32,128]{2,1,0:T(8,128)S(1)}, u32[]{:S(2)}, u32[]{:S(2)}) collective-permute-start(f32[10,32,128]{2,1,0:T(8,128)S(1)} %get-tuple-element.39), channel_id=1, source_target_pairs={{0,1},{1,0},{2,3},{3,2},{4,5},{5,4},{6,7},{7,6},{8,9},{9,8},{10,11... | collective-permute-start | bytes 491528 | tf_op jit(solution)/shard_map/ppermute | solution.py:97
  9.1 2.9 %collective-permute-start.7 = (f32[5,32,128]{2,1,0:T(8,128)S(1)}, f32[5,32,128]{2,1,0:T(8,128)S(1)}, u32[]{:S(2)}, u32[]{:S(2)}) collective-permute-start(f32[5,32,128]{2,1,0:T(8,128)S(1)} %get-tuple-element.43.ports_y.refs_0_.refs_8_), channel_id=1, source_target_pairs={{0,1},{1,0},{2,3},{3,2},{4,5},{5,4},{6,7},{7,6},{8,9},{9,8},{10,11... | collective-permute-start | bytes 245768 | tf_op jit(solution)/shard_map/ppermute | solution.py:97
  10.5 4.3 %collective-permute-start.4 = (f32[12,8,128]{2,1,0:T(8,128)S(1)}, f32[12,8,128]{2,1,0:T(8,128)S(1)}, u32[]{:S(2)}, u32[]{:S(2)}) collective-permute-start(f32[12,8,128]{2,1,0:T(8,128)S(1)} %get-tuple-element.41), channel_id=1, source_target_pairs={{0,8},{1,2},{2,1},{3,4},{4,3},{5,6},{6,5},{7,15},{8,0},{9,10},{10,... | collective-permute-start | bytes 147464 | tf_op jit(solution)/shard_map/ppermute | solution.py:90
  11.5 3.3 %collective-permute-start.5 = (f32[9,8,128]{2,1,0:T(8,128)S(1)}, f32[9,8,128]{2,1,0:T(8,128)S(1)}, u32[]{:S(2)}, u32[]{:S(2)}) collective-permute-start(f32[9,8,128]{2,1,0:T(8,128)S(1)} %get-tuple-element.42), channel_id=1, source_target_pairs={{0,1},{1,0},{2,3},{3,2},{4,5},{5,4},{6,7},{7,6},{8,9},{9,8},{10,11... | collective-permute-start | bytes 110600 | tf_op jit(solution)/shard_map/ppermute | solution.py:97
  12.0 9.3 %collective-permute-start.9 = (f32[5,32,128]{2,1,0:T(8,128)S(1)}, f32[5,32,128]{2,1,0:T(8,128)S(1)}, u32[]{:S(2)}, u32[]{:S(2)}) collective-permute-start(f32[5,32,128]{2,1,0:T(8,128)S(1)} %get-tuple-element.49.refs_0_), channel_id=1, source_target_pairs={{0,3},{1,2},{2,1},{3,0},{4,7},{5,6},{6,5},{7,4},{8,11},{9,10},{10,... | collective-permute-start | bytes 245768 | tf_op jit(solution)/shard_map/ppermute | solution.py:97
  18.0 1.3 %collective-permute-start.6 = (f32[2,32,128]{2,1,0:T(8,128)S(1)}, f32[2,32,128]{2,1,0:T(8,128)S(1)}, u32[]{:S(2)}, u32[]{:S(2)}) collective-permute-start(f32[2,32,128]{2,1,0:T(8,128)S(1)} %get-tuple-element.46.refs_0_), channel_id=1, source_target_pairs={{0,1},{1,0},{2,3},{3,2},{4,5},{5,4},{6,7},{7,6},{8,9},{9,8},{10,11... | collective-permute-start | bytes 98312 | tf_op jit(solution)/shard_map/ppermute | solution.py:97
  18.2 6.5 %collective-permute-start.12 = (f32[5,32,128]{2,1,0:T(8,128)S(1)}, f32[5,32,128]{2,1,0:T(8,128)S(1)}, u32[]{:S(2)}, u32[]{:S(2)}) collective-permute-start(f32[5,32,128]{2,1,0:T(8,128)S(1)} %get-tuple-element.57.refs_0_.refs_11_.refs_6_), channel_id=1, source_target_pairs={{0,8},{8,0},{16,24},{24,16},{1,9},{9,1},{17,25},{25,17},{2,10},{10... | collective-permute-start | bytes 245768 | tf_op jit(solution)/shard_map/ppermute | solution.py:97
  19.3 3.6 %collective-permute-start.8 = (f32[2,32,128]{2,1,0:T(8,128)S(1)}, f32[2,32,128]{2,1,0:T(8,128)S(1)}, u32[]{:S(2)}, u32[]{:S(2)}) collective-permute-start(f32[2,32,128]{2,1,0:T(8,128)S(1)} %get-tuple-element.48.refs_0_), channel_id=1, source_target_pairs={{0,3},{1,2},{2,1},{3,0},{4,7},{5,6},{6,5},{7,4},{8,11},{9,10},{10,... | collective-permute-start | bytes 98312 | tf_op jit(solution)/shard_map/ppermute | solution.py:97
  21.4 3.4 %collective-permute-start.11 = (f32[2,32,128]{2,1,0:T(8,128)S(1)}, f32[2,32,128]{2,1,0:T(8,128)S(1)}, u32[]{:S(2)}, u32[]{:S(2)}) collective-permute-start(f32[2,32,128]{2,1,0:T(8,128)S(1)} %get-tuple-element.52.refs_2_), channel_id=1, source_target_pairs={{0,5},{1,4},{2,7},{3,6},{4,1},{5,0},{6,3},{7,2},{8,13},{9,12},{10,... | collective-permute-start | bytes 98312 | tf_op jit(solution)/shard_map/ppermute | solution.py:97
  23.0 3.2 %collective-permute-start.10 = (f32[1,32,128]{2,1,0:T(8,128)S(1)}, f32[1,32,128]{2,1,0:T(8,128)S(1)}, u32[]{:S(2)}, u32[]{:S(2)}) collective-permute-start(f32[1,32,128]{2,1,0:T(8,128)S(1)} %get-tuple-element.51.refs_0_), channel_id=1, source_target_pairs={{0,5},{1,4},{2,7},{3,6},{4,1},{5,0},{6,3},{7,2},{8,13},{9,12},{10,... | collective-permute-start | bytes 49160 | tf_op jit(solution)/shard_map/ppermute | solution.py:97
  26.7 4.0 %collective-permute-start.13 = (f32[2,32,128]{2,1,0:T(8,128)S(1)}, f32[2,32,128]{2,1,0:T(8,128)S(1)}, u32[]{:S(2)}, u32[]{:S(2)}) collective-permute-start(f32[2,32,128]{2,1,0:T(8,128)S(1)} %get-tuple-element.60.refs_0_), channel_id=1, source_target_pairs={{0,8},{8,0},{16,24},{24,16},{1,9},{9,1},{17,25},{25,17},{2,10},{10... | collective-permute-start | bytes 98312 | tf_op jit(solution)/shard_map/ppermute | solution.py:97
  27.5 5.0 %collective-permute-start.15 = (f32[2,32,128]{2,1,0:T(8,128)S(1)}, f32[2,32,128]{2,1,0:T(8,128)S(1)}, u32[]{:S(2)}, u32[]{:S(2)}) collective-permute-start(f32[2,32,128]{2,1,0:T(8,128)S(1)} %get-tuple-element.62.refs_2_), channel_id=1, source_target_pairs={{0,16},{8,24},{16,0},{24,8},{1,17},{9,25},{17,1},{25,9},{2,18},{10... | collective-permute-start | bytes 98312 | tf_op jit(solution)/shard_map/ppermute | solution.py:97
  30.7 4.7 %collective-permute-start.14 = (f32[1,32,128]{2,1,0:T(8,128)S(1)}, f32[1,32,128]{2,1,0:T(8,128)S(1)}, u32[]{:S(2)}, u32[]{:S(2)}) collective-permute-start(f32[1,32,128]{2,1,0:T(8,128)S(1)} %get-tuple-element.61.refs_0_), channel_id=1, source_target_pairs={{0,16},{8,24},{16,0},{24,8},{1,17},{9,25},{17,1},{25,9},{2,18},{10... | collective-permute-start | bytes 49160 | tf_op jit(solution)/shard_map/ppermute | solution.py:97

commit v7 on v6

--- a/solution.py
+++ b/solution.py
@@ -142,21 +142,17 @@
     )
 
 
-def begin_kernel(tracer, y_speed, z_speed, kappa_far, _, o_ref, e_ref, ports, c, ys, zs, kappa, kappa_y, r_y, sem):
+def begin_kernel(tracer, y_speed, z_speed, _, o_ref, e_ref, c, ys, zs, sem):
     arrivals = [
         pltpu.make_async_copy(source, target, sem.at[k])
-        for k, (source, target) in enumerate(((kappa_far, kappa), (tracer, c), (z_speed, zs), (y_speed, ys)))
+        for k, (source, target) in enumerate(((tracer, c), (z_speed, zs), (y_speed, ys)))
     ]
     for copy in arrivals:
         copy.start()
-    _, y, _, y_count = place()
+    _, y, _, _ = place()
     width = c.shape[1]
     y_odd = lax.rem(y, 2)
-    arrivals[0].wait()
-    kappa_y[...] = turned(kappa[...])
-    ports[3], ports[4] = resistances(kappa_y, r_y)
-    factor(((lambda j: r_y[j], width, *outer(ports, y, y_count), None, ports),))
-    for copy in arrivals[1:]:
+    for copy in arrivals:
         copy.wait()
 
     def rims(o_low):
@@ -179,19 +175,19 @@
         rims(False)
 
 
-def begin(tracer, y_speed, z_speed, kappa, after):
+def begin(tracer, y_speed, z_speed, after):
     depth, width, band = tracer.shape
     return call(
         begin_kernel,
         "begin",
-        [near(10, depth, band)] * 2 + [near(5, depth, band)],
-        [("far", x) for x in (tracer, y_speed, z_speed, kappa)] + [after],
-        scratch=[near(depth, width, band)] * 4 + [near(width, depth, band)] * 2 + [pltpu.SemaphoreType.DMA((4,))],
+        [near(10, depth, band)] * 2,
+        [("far", x) for x in (tracer, y_speed, z_speed)] + [after],
+        scratch=[near(depth, width, band)] * 3 + [pltpu.SemaphoreType.DMA((3,))],
         cycles=2000,
     )
 
 
-PAD_TILES = 3
+PAD_TILES = 1
 
 
 def rim_kernel(b, a, _, for_pair, for_other):
@@ -285,17 +281,20 @@
     return jnp.where(index == 0, RATE, 0.0) * ports[3], jnp.where(index == count - 1, RATE, 0.0) * ports[4]
 
 
-def factor_kernel(kappa, r_y_far, r_z_far, ports_z, kappa_y, r_y, r_z, sem):
-    z, _, z_count, _ = place()
-    depth = kappa.shape[0]
+def factor_kernel(kappa, r_y_far, r_z_far, ports_y, ports_z, kappa_y, r_y, r_z, sem):
+    z, y, z_count, y_count = place()
+    depth, width, _ = kappa.shape
     y_copy = pltpu.make_async_copy(r_y, r_y_far, sem.at[0])
     z_copy = pltpu.make_async_copy(r_z, r_z_far, sem.at[1])
     ports_z[3], ports_z[4] = resistances(kappa, r_z)
     z_copy.start()
     kappa_y[...] = turned(kappa[...])
-    resistances(kappa_y, r_y)
+    ports_y[3], ports_y[4] = resistances(kappa_y, r_y)
     y_copy.start()
-    factor(((lambda j: r_z[j], depth, *outer(ports_z, z, z_count), None, ports_z),))
+    factor((
+        (lambda j: r_y[j], width, *outer(ports_y, y, y_count), None, ports_y),
+        (lambda j: r_z[j], depth, *outer(ports_z, z, z_count), None, ports_z),
+    ))
     y_copy.wait()
     z_copy.wait()
 
@@ -306,7 +305,7 @@
     return call(
         factor_kernel,
         "factor",
-        [("far", far(*along_y)), ("far", far(*along_z)), near(5, width, band)],
+        [("far", far(*along_y)), ("far", far(*along_z)), near(5, depth, band), near(5, width, band)],
         [("plain", kappa)],
         scratch=[near(*along_y), near(*along_y), near(*along_z), pltpu.SemaphoreType.DMA((2,))],
         cycles=4000,
@@ -647,12 +646,12 @@
 
 def local(tracer, y_speed, z_speed, kappa):
     b, a = z_rims(tracer, y_speed, z_speed)
-    o, e, ports_y = begin(tracer, y_speed, z_speed, kappa, b)
+    o, e = begin(tracer, y_speed, z_speed, b)
     b = send(b, z_partner=z_other)
     a = send(a, z_partner=pair_up)
     e = swap(e, "gy", 0)
     o = send(o, y_partner=y_ring)
-    r_y, r_z, ports_z = factor_lines(kappa)
+    r_y, r_z, ports_y, ports_z = factor_lines(kappa)
     for_pair, for_other = rim(a, b, ports_z)
     corner = send(for_other, y_partner=y_other)
     ab = swap(for_pair, "gy", 0)

time: 36.5 us -> 36.2 us (level)
  waiting for transfers between devices: 8.93 us -> 8.17 us
  starting transfers between devices: 18.6 us -> 19.2 us
    ppermute x12, waiting for transfers between devices: 7.33 us -> 6.64 us  [swap(): lax.ppermute(x, axis, [(i, i ^ step) for i in range(lax.axis_size(axis))])]
    ppermute x12, starting transfers between devices: 11.5 us -> 12.1 us  [swap(): lax.ppermute(x, axis, [(i, i ^ step) for i in range(lax.axis_size(axis))])]
where the time goes in v7:
time: 36.2 us; the launch traced here: 36 us
  starting transfers between devices  19.2 us (53%)
  Pallas kernels  8.42 us (23%)
  waiting for transfers between devices  8.17 us (23%)
    ppermute x12, starting transfers between devices, swap(): lax.ppermute(x, axis, [(i, i ^ step) for i in range(lax.axis_size(axis))])  12.1 us
    pallas_call x13, Pallas kernels, call(): pl.pallas_call(kernel, out_shape=[out[1] if isinstance(out, tuple) else o...  8.42 us
    ppermute x4, starting transfers between devices, send(): return lax.ppermute(x, AXES, permutation(z_partner, y_partner))  7.19 us
    ppermute x12, waiting for transfers between devices, swap(): lax.ppermute(x, axis, [(i, i ^ step) for i in range(lax.axis_size(axis))])  6.64 us
    ppermute x4, waiting for transfers between devices, send(): return lax.ppermute(x, AXES, permutation(z_partner, y_partner))  1.53 us
  transfers between devices with their start and end apart: 16, of which 7 were waited for; matrix products, arithmetic and copies ran while one was open for 0% of the time, Pallas kernels for 17%

profile of v7, /device:TPU:0, one launch (start us, length us, event | category | flops | bytes accessed | tf_op | source)
XLA Modules:
  0.0 36.0 jit_solution(10368618519278996227)
XLA Ops:
  0.0 1.1 %z_rims.1 = (f32[10,32,128]{2,1,0:T(8,128)S(1)}, f32[10,32,128]{2,1,0:T(8,128)S(1)}) custom-call(f32[32,32,128]{2,1,0:T(8,128)} %tracer.5, f32[32,32,128]{2,1,0:T(8,128)} %y_speed.5, f32[32,32,128]{2,1,0:T(8,128)} %z_speed.5), custom_call_target="tpu_custom_call" | custom-call | bytes 1024000 | tf_op jit(solution)/shard_map/z_rims/pallas_call | solution.py:33
  1.1 0.5 %collective-permute-start = (f32[10,32,128]{2,1,0:T(8,128)S(1)}, f32[10,32,128]{2,1,0:T(8,128)S(1)}, u32[]{:S(2)}, u32[]{:S(2)}) collective-permute-start(f32[10,32,128]{2,1,0:T(8,128)S(1)} %get-tuple-element.36._), channel_id=1, source_target_pairs={{0,1},{1,0},{2,3},{3,2},{4,5},{5,4},{6,7},{7,6},{8,16},{9,17},{10,... | collective-permute-start | bytes 491528 | tf_op jit(solution)/shard_map/ppermute | solution.py:90
  1.6 0.0 copy-start
  1.6 4.1 %collective-permute-start.1 = (f32[10,32,128]{2,1,0:T(8,128)S(1)}, f32[10,32,128]{2,1,0:T(8,128)S(1)}, u32[]{:S(2)}, u32[]{:S(2)}) collective-permute-start(f32[10,32,128]{2,1,0:T(8,128)S(1)} %get-tuple-element.37), channel_id=1, source_target_pairs={{0,8},{1,9},{2,10},{3,11},{4,12},{5,13},{6,14},{7,15},{8,0},{9,1},... | collective-permute-start | bytes 491528 | tf_op jit(solution)/shard_map/ppermute | solution.py:90
  5.8 1.5 %begin.1 = (f32[10,32,128]{2,1,0:T(8,128)S(1)}, f32[10,32,128]{2,1,0:T(8,128)S(1)}) custom-call(f32[32,32,128]{2,1,0:T(8,128)} %tracer.5, f32[32,32,128]{2,1,0:T(8,128)} %y_speed.5, f32[32,32,128]{2,1,0:T(8,128)} %z_speed.5, f32[10,32,128]{2,1,0:T(8,128)S(1)} %get-tuple-element.36._), custom_call_target="tpu_custom_call" | custom-call | bytes 2048000 | tf_op jit(solution)/shard_map/begin/pallas_call | solution.py:33
  7.3 1.4 %collective-permute-start.2 = (f32[10,32,128]{2,1,0:T(8,128)S(1)}, f32[10,32,128]{2,1,0:T(8,128)S(1)}, u32[]{:S(2)}, u32[]{:S(2)}) collective-permute-start(f32[10,32,128]{2,1,0:T(8,128)S(1)} %get-tuple-element.38), channel_id=1, source_target_pairs={{0,7},{1,2},{2,1},{3,4},{4,3},{5,6},{6,5},{7,0},{8,15},{9,10},{10,... | collective-permute-start | bytes 491528 | tf_op jit(solution)/shard_map/ppermute | solution.py:90
  8.6 0.3 collective-permute-start.3
  8.9 0.0 copy-done
  8.9 1.1 %factor.1 = (f32[32,32,128]{2,1,0:T(8,128)}, f32[32,32,128]{2,1,0:T(8,128)}, f32[5,32,128]{2,1,0:T(8,128)S(1)}, f32[5,32,128]{2,1,0:T(8,128)S(1)}) custom-call(f32[32,32,128]{2,1,0:T(8,128)S(1)} %copy-done), custom_call_target="tpu_custom_call" | custom-call | bytes 4096000 | tf_op jit(solution)/shard_map/factor/pallas_call | solution.py:33
  10.0 0.3 collective-permute-start.7
  10.3 0.0 collective-permute-done.b
  10.3 0.0 collective-permute-done.1.a
  10.4 1.1 %collective-permute-start.4 = (f32[10,8,128]{2,1,0:T(8,128)S(1)}, f32[10,8,128]{2,1,0:T(8,128)S(1)}, u32[]{:S(2)}, u32[]{:S(2)}) collective-permute-start(f32[10,8,128]{2,1,0:T(8,128)S(1)} %get-tuple-element.41), channel_id=1, source_target_pairs={{0,8},{1,2},{2,1},{3,4},{4,3},{5,6},{6,5},{7,15},{8,0},{9,10},{10,... | collective-permute-start | bytes 122888 | tf_op jit(solution)/shard_map/ppermute | solution.py:90
  11.5 0.4 collective-permute-start.5
  11.9 0.0 collective-permute-done.7.refs_1_
  11.9 1.2 %collective-permute-start.9 = (f32[5,32,128]{2,1,0:T(8,128)S(1)}, f32[5,32,128]{2,1,0:T(8,128)S(1)}, u32[]{:S(2)}, u32[]{:S(2)}) collective-permute-start(f32[5,32,128]{2,1,0:T(8,128)S(1)} %get-tuple-element.49.refs_0_), channel_id=1, source_target_pairs={{0,3},{1,2},{2,1},{3,0},{4,7},{5,6},{6,5},{7,4},{8,11},{9,10},{10,... | collective-permute-start | bytes 245768 | tf_op jit(solution)/shard_map/ppermute | solution.py:97
  13.1 1.5 %collective-permute-done.2.o = f32[10,32,128]{2,1,0:T(8,128)S(1)} collective-permute-done((f32[10,32,128]{2,1,0:T(8,128)S(1)}, f32[10,32,128]{2,1,0:T(8,128)S(1)}, u32[]{:S(2)}, u32[]{:S(2)}) %collective-permute-start.2) | collective-permute-done | bytes 163872 | tf_op jit(solution)/shard_map/ppermute | solution.py:90
  14.6 0.0 collective-permute-done.3.e
  14.6 0.0 collective-permute-done.5.ab
  14.6 0.0 collective-permute-done.4.corner
  14.6 3.2 %advect.1 = (f32[32,32,128]{2,1,0:T(8,128)S(1)}, f32[2,32,128]{2,1,0:T(8,128)S(1)}, f32[32,32,128]{2,1,0:T(8,128)S(1)}, f32[32,32,128]{2,1,0:T(8,128)S(1)}, f32[5,32,128]{2,1,0:T(8,128)S(1)}) custom-call(f32[32,32,128]{2,1,0:T(8,128)} %tracer.5, f32[32,32,128]{2,1,0:T(8,128)} %y_speed.5, f32[32,32,128]{2,1,0:T(8,128)} %z_speed.5, ...), custom_call_target="tpu_custom_call" | custom-call | bytes 5120000 | tf_op jit(solution)/shard_map/advect/pallas_call | solution.py:33
  17.8 0.1 collective-permute-start.6
  17.9 1.0 %collective-permute-start.12 = (f32[5,32,128]{2,1,0:T(8,128)S(1)}, f32[5,32,128]{2,1,0:T(8,128)S(1)}, u32[]{:S(2)}, u32[]{:S(2)}) collective-permute-start(f32[5,32,128]{2,1,0:T(8,128)S(1)} %get-tuple-element.57.refs_0_.refs_11_.refs_6_), channel_id=1, source_target_pairs={{0,8},{8,0},{16,24},{24,16},{1,9},{9,1},{17,25},{25,17},{2,10},{10... | collective-permute-start | bytes 245768 | tf_op jit(solution)/shard_map/ppermute | solution.py:97
  18.9 0.2 collective-permute-done.6.refs_1_
  19.1 1.9 %collective-permute-start.8 = (f32[2,32,128]{2,1,0:T(8,128)S(1)}, f32[2,32,128]{2,1,0:T(8,128)S(1)}, u32[]{:S(2)}, u32[]{:S(2)}) collective-permute-start(f32[2,32,128]{2,1,0:T(8,128)S(1)} %get-tuple-element.48.refs_0_), channel_id=1, source_target_pairs={{0,3},{1,2},{2,1},{3,0},{4,7},{5,6},{6,5},{7,4},{8,11},{9,10},{10,... | collective-permute-start | bytes 98312 | tf_op jit(solution)/shard_map/ppermute | solution.py:97
  21.0 0.0 collective-permute-done.9.refs_1_
  21.1 0.2 collective-permute-start.11
  21.2 1.4 %collective-permute-done.8.refs_1_ = f32[2,32,128]{2,1,0:T(8,128)S(1)} collective-permute-done((f32[2,32,128]{2,1,0:T(8,128)S(1)}, f32[2,32,128]{2,1,0:T(8,128)S(1)}, u32[]{:S(2)}, u32[]{:S(2)}) %collective-permute-start.8) | collective-permute-done | bytes 32800 | tf_op jit(solution)/shard_map/ppermute | solution.py:97
  22.6 1.7 %collective-permute-start.10 = (f32[1,32,128]{2,1,0:T(8,128)S(1)}, f32[1,32,128]{2,1,0:T(8,128)S(1)}, u32[]{:S(2)}, u32[]{:S(2)}) collective-permute-start(f32[1,32,128]{2,1,0:T(8,128)S(1)} %get-tuple-element.51.refs_0_), channel_id=1, source_target_pairs={{0,5},{1,4},{2,7},{3,6},{4,1},{5,0},{6,3},{7,2},{8,13},{9,12},{10,... | collective-permute-start | bytes 49160 | tf_op jit(solution)/shard_map/ppermute | solution.py:97
  24.3 0.0 collective-permute-done.12.refs_1_
  24.3 0.1 collective-permute-done.11.refs_3_
  24.5 1.4 %collective-permute-done.10.refs_1_ = f32[1,32,128]{2,1,0:T(8,128)S(1)} collective-permute-done((f32[1,32,128]{2,1,0:T(8,128)S(1)}, f32[1,32,128]{2,1,0:T(8,128)S(1)}, u32[]{:S(2)}, u32[]{:S(2)}) %collective-permute-start.10) | collective-permute-done | bytes 16416 | tf_op jit(solution)/shard_map/ppermute | solution.py:97
  25.9 0.5 %turn.1 = (f32[32,32,128]{2,1,0:T(8,128)S(1)}, f32[2,32,128]{2,1,0:T(8,128)S(1)}, f32[32,32,128]{2,1,0:T(8,128)S(1)}, f32[32,32,128]{2,1,0:T(8,128)S(1)}) custom-call(f32[1,32,128]{2,1,0:T(8,128)S(1)} %get-tuple-element.51.refs_0_, f32[1,32,128]{2,1,0:T(8,128)S(1)} %collective-permute-done.10.refs_1_, f32[2,32,128]{2,1,0:T(8,128)S(1)} %get-tuple-element.52.refs_2_, ...), custom_call_target="tpu_custom_call" | custom-call | bytes 1536000 | tf_op jit(solution)/shard_map/turn/pallas_call | solution.py:33
  26.4 1.1 %collective-permute-start.13 = (f32[2,32,128]{2,1,0:T(8,128)S(1)}, f32[2,32,128]{2,1,0:T(8,128)S(1)}, u32[]{:S(2)}, u32[]{:S(2)}) collective-permute-start(f32[2,32,128]{2,1,0:T(8,128)S(1)} %get-tuple-element.60.refs_0_), channel_id=1, source_target_pairs={{0,8},{8,0},{16,24},{24,16},{1,9},{9,1},{17,25},{25,17},{2,10},{10... | collective-permute-start | bytes 98312 | tf_op jit(solution)/shard_map/ppermute | solution.py:97
  27.4 2.0 %collective-permute-start.15 = (f32[2,32,128]{2,1,0:T(8,128)S(1)}, f32[2,32,128]{2,1,0:T(8,128)S(1)}, u32[]{:S(2)}, u32[]{:S(2)}) collective-permute-start(f32[2,32,128]{2,1,0:T(8,128)S(1)} %get-tuple-element.62.refs_2_), channel_id=1, source_target_pairs={{0,16},{8,24},{16,0},{24,8},{1,17},{9,25},{17,1},{25,9},{2,18},{10... | collective-permute-start | bytes 98312 | tf_op jit(solution)/shard_map/ppermute | solution.py:97
  29.4 0.9 %collective-permute-done.13.refs_1_ = f32[2,32,128]{2,1,0:T(8,128)S(1)} collective-permute-done((f32[2,32,128]{2,1,0:T(8,128)S(1)}, f32[2,32,128]{2,1,0:T(8,128)S(1)}, u32[]{:S(2)}, u32[]{:S(2)}) %collective-permute-start.13) | collective-permute-done | bytes 32800 | tf_op jit(solution)/shard_map/ppermute | solution.py:97
  30.4 2.2 %collective-permute-start.14 = (f32[1,32,128]{2,1,0:T(8,128)S(1)}, f32[1,32,128]{2,1,0:T(8,128)S(1)}, u32[]{:S(2)}, u32[]{:S(2)}) collective-permute-start(f32[1,32,128]{2,1,0:T(8,128)S(1)} %get-tuple-element.61.refs_0_), channel_id=1, source_target_pairs={{0,16},{8,24},{16,0},{24,8},{1,17},{9,25},{17,1},{25,9},{2,18},{10... | collective-permute-start | bytes 49160 | tf_op jit(solution)/shard_map/ppermute | solution.py:97
  32.6 0.0 collective-permute-done.15.refs_3_
  32.6 2.5 %collective-permute-done.14.refs_1_ = f32[1,32,128]{2,1,0:T(8,128)S(1)} collective-permute-done((f32[1,32,128]{2,1,0:T(8,128)S(1)}, f32[1,32,128]{2,1,0:T(8,128)S(1)}, u32[]{:S(2)}, u32[]{:S(2)}) %collective-permute-start.14) | collective-permute-done | bytes 16416 | tf_op jit(solution)/shard_map/ppermute | solution.py:97
  35.1 0.9 %finish.1 = f32[32,32,128]{2,1,0:T(8,128)} custom-call(f32[1,32,128]{2,1,0:T(8,128)S(1)} %get-tuple-element.61.refs_0_, f32[1,32,128]{2,1,0:T(8,128)S(1)} %collective-permute-done.14.refs_1_, f32[2,32,128]{2,1,0:T(8,128)S(1)} %get-tuple-element.62.refs_2_, f32[2,32,128]{2,1,0:T(8,128)S(1)} %collective-permute-done.15.refs_3_, ...), custom_call_target="tpu_custom_call" | custom-call | bytes 1024000 | tf_op jit(solution)/shard_map/finish/pallas_call | solution.py:33
  (7 shorter events, 0.2 us)
Async XLA Ops:
  1.1 9.3 %collective-permute-start = (f32[10,32,128]{2,1,0:T(8,128)S(1)}, f32[10,32,128]{2,1,0:T(8,128)S(1)}, u32[]{:S(2)}, u32[]{:S(2)}) collective-permute-start(f32[10,32,128]{2,1,0:T(8,128)S(1)} %get-tuple-element.36._), channel_id=1, source_target_pairs={{0,1},{1,0},{2,3},{3,2},{4,5},{5,4},{6,7},{7,6},{8,16},{9,17},{10,... | collective-permute-start | bytes 491528 | tf_op jit(solution)/shard_map/ppermute | solution.py:90
  1.6 7.3 %copy-start = (f32[32,32,128]{2,1,0:T(8,128)S(1)}, f32[32,32,128]{2,1,0:T(8,128)}, u32[]{:S(2)}) copy-start(f32[32,32,128]{2,1,0:T(8,128)} %kappa.1) | copy-start | bytes 1572868
  1.6 8.7 %collective-permute-start.1 = (f32[10,32,128]{2,1,0:T(8,128)S(1)}, f32[10,32,128]{2,1,0:T(8,128)S(1)}, u32[]{:S(2)}, u32[]{:S(2)}) collective-permute-start(f32[10,32,128]{2,1,0:T(8,128)S(1)} %get-tuple-element.37), channel_id=1, source_target_pairs={{0,8},{1,9},{2,10},{3,11},{4,12},{5,13},{6,14},{7,15},{8,0},{9,1},... | collective-permute-start | bytes 491528 | tf_op jit(solution)/shard_map/ppermute | solution.py:90
  7.3 7.4 %collective-permute-start.2 = (f32[10,32,128]{2,1,0:T(8,128)S(1)}, f32[10,32,128]{2,1,0:T(8,128)S(1)}, u32[]{:S(2)}, u32[]{:S(2)}) collective-permute-start(f32[10,32,128]{2,1,0:T(8,128)S(1)} %get-tuple-element.38), channel_id=1, source_target_pairs={{0,7},{1,2},{2,1},{3,4},{4,3},{5,6},{6,5},{7,0},{8,15},{9,10},{10,... | collective-permute-start | bytes 491528 | tf_op jit(solution)/shard_map/ppermute | solution.py:90
  8.6 6.0 %collective-permute-start.3 = (f32[10,32,128]{2,1,0:T(8,128)S(1)}, f32[10,32,128]{2,1,0:T(8,128)S(1)}, u32[]{:S(2)}, u32[]{:S(2)}) collective-permute-start(f32[10,32,128]{2,1,0:T(8,128)S(1)} %get-tuple-element.39), channel_id=1, source_target_pairs={{0,1},{1,0},{2,3},{3,2},{4,5},{5,4},{6,7},{7,6},{8,9},{9,8},{10,11... | collective-permute-start | bytes 491528 | tf_op jit(solution)/shard_map/ppermute | solution.py:97
  10.0 1.8 %collective-permute-start.7 = (f32[5,32,128]{2,1,0:T(8,128)S(1)}, f32[5,32,128]{2,1,0:T(8,128)S(1)}, u32[]{:S(2)}, u32[]{:S(2)}) collective-permute-start(f32[5,32,128]{2,1,0:T(8,128)S(1)} %get-tuple-element.43.ports_y.refs_0_.refs_8_), channel_id=1, source_target_pairs={{0,1},{1,0},{2,3},{3,2},{4,5},{5,4},{6,7},{7,6},{8,9},{9,8},{10,11... | collective-permute-start | bytes 245768 | tf_op jit(solution)/shard_map/ppermute | solution.py:97
  10.4 4.2 %collective-permute-start.4 = (f32[10,8,128]{2,1,0:T(8,128)S(1)}, f32[10,8,128]{2,1,0:T(8,128)S(1)}, u32[]{:S(2)}, u32[]{:S(2)}) collective-permute-start(f32[10,8,128]{2,1,0:T(8,128)S(1)} %get-tuple-element.41), channel_id=1, source_target_pairs={{0,8},{1,2},{2,1},{3,4},{4,3},{5,6},{6,5},{7,15},{8,0},{9,10},{10,... | collective-permute-start | bytes 122888 | tf_op jit(solution)/shard_map/ppermute | solution.py:90
  11.5 3.1 %collective-permute-start.5 = (f32[9,8,128]{2,1,0:T(8,128)S(1)}, f32[9,8,128]{2,1,0:T(8,128)S(1)}, u32[]{:S(2)}, u32[]{:S(2)}) collective-permute-start(f32[9,8,128]{2,1,0:T(8,128)S(1)} %get-tuple-element.42), channel_id=1, source_target_pairs={{0,1},{1,0},{2,3},{3,2},{4,5},{5,4},{6,7},{7,6},{8,9},{9,8},{10,11... | collective-permute-start | bytes 110600 | tf_op jit(solution)/shard_map/ppermute | solution.py:97
  11.9 9.1 %collective-permute-start.9 = (f32[5,32,128]{2,1,0:T(8,128)S(1)}, f32[5,32,128]{2,1,0:T(8,128)S(1)}, u32[]{:S(2)}, u32[]{:S(2)}) collective-permute-start(f32[5,32,128]{2,1,0:T(8,128)S(1)} %get-tuple-element.49.refs_0_), channel_id=1, source_target_pairs={{0,3},{1,2},{2,1},{3,0},{4,7},{5,6},{6,5},{7,4},{8,11},{9,10},{10,... | collective-permute-start | bytes 245768 | tf_op jit(solution)/shard_map/ppermute | solution.py:97
  17.8 1.3 %collective-permute-start.6 = (f32[2,32,128]{2,1,0:T(8,128)S(1)}, f32[2,32,128]{2,1,0:T(8,128)S(1)}, u32[]{:S(2)}, u32[]{:S(2)}) collective-permute-start(f32[2,32,128]{2,1,0:T(8,128)S(1)} %get-tuple-element.46.refs_0_), channel_id=1, source_target_pairs={{0,1},{1,0},{2,3},{3,2},{4,5},{5,4},{6,7},{7,6},{8,9},{9,8},{10,11... | collective-permute-start | bytes 98312 | tf_op jit(solution)/shard_map/ppermute | solution.py:97
  17.9 6.4 %collective-permute-start.12 = (f32[5,32,128]{2,1,0:T(8,128)S(1)}, f32[5,32,128]{2,1,0:T(8,128)S(1)}, u32[]{:S(2)}, u32[]{:S(2)}) collective-permute-start(f32[5,32,128]{2,1,0:T(8,128)S(1)} %get-tuple-element.57.refs_0_.refs_11_.refs_6_), channel_id=1, source_target_pairs={{0,8},{8,0},{16,24},{24,16},{1,9},{9,1},{17,25},{25,17},{2,10},{10... | collective-permute-start | bytes 245768 | tf_op jit(solution)/shard_map/ppermute | solution.py:97
  19.1 3.5 %collective-permute-start.8 = (f32[2,32,128]{2,1,0:T(8,128)S(1)}, f32[2,32,128]{2,1,0:T(8,128)S(1)}, u32[]{:S(2)}, u32[]{:S(2)}) collective-permute-start(f32[2,32,128]{2,1,0:T(8,128)S(1)} %get-tuple-element.48.refs_0_), channel_id=1, source_target_pairs={{0,3},{1,2},{2,1},{3,0},{4,7},{5,6},{6,5},{7,4},{8,11},{9,10},{10,... | collective-permute-start | bytes 98312 | tf_op jit(solution)/shard_map/ppermute | solution.py:97
  21.1 3.4 %collective-permute-start.11 = (f32[2,32,128]{2,1,0:T(8,128)S(1)}, f32[2,32,128]{2,1,0:T(8,128)S(1)}, u32[]{:S(2)}, u32[]{:S(2)}) collective-permute-start(f32[2,32,128]{2,1,0:T(8,128)S(1)} %get-tuple-element.52.refs_2_), channel_id=1, source_target_pairs={{0,5},{1,4},{2,7},{3,6},{4,1},{5,0},{6,3},{7,2},{8,13},{9,12},{10,... | collective-permute-start | bytes 98312 | tf_op jit(solution)/shard_map/ppermute | solution.py:97
  22.6 3.2 %collective-permute-start.10 = (f32[1,32,128]{2,1,0:T(8,128)S(1)}, f32[1,32,128]{2,1,0:T(8,128)S(1)}, u32[]{:S(2)}, u32[]{:S(2)}) collective-permute-start(f32[1,32,128]{2,1,0:T(8,128)S(1)} %get-tuple-element.51.refs_0_), channel_id=1, source_target_pairs={{0,5},{1,4},{2,7},{3,6},{4,1},{5,0},{6,3},{7,2},{8,13},{9,12},{10,... | collective-permute-start | bytes 49160 | tf_op jit(solution)/shard_map/ppermute | solution.py:97
  26.4 4.0 %collective-permute-start.13 = (f32[2,32,128]{2,1,0:T(8,128)S(1)}, f32[2,32,128]{2,1,0:T(8,128)S(1)}, u32[]{:S(2)}, u32[]{:S(2)}) collective-permute-start(f32[2,32,128]{2,1,0:T(8,128)S(1)} %get-tuple-element.60.refs_0_), channel_id=1, source_target_pairs={{0,8},{8,0},{16,24},{24,16},{1,9},{9,1},{17,25},{25,17},{2,10},{10... | collective-permute-start | bytes 98312 | tf_op jit(solution)/shard_map/ppermute | solution.py:97
  27.4 5.1 %collective-permute-start.15 = (f32[2,32,128]{2,1,0:T(8,128)S(1)}, f32[2,32,128]{2,1,0:T(8,128)S(1)}, u32[]{:S(2)}, u32[]{:S(2)}) collective-permute-start(f32[2,32,128]{2,1,0:T(8,128)S(1)} %get-tuple-element.62.refs_2_), channel_id=1, source_target_pairs={{0,16},{8,24},{16,0},{24,8},{1,17},{9,25},{17,1},{25,9},{2,18},{10... | collective-permute-start | bytes 98312 | tf_op jit(solution)/shard_map/ppermute | solution.py:97
  30.4 4.7 %collective-permute-start.14 = (f32[1,32,128]{2,1,0:T(8,128)S(1)}, f32[1,32,128]{2,1,0:T(8,128)S(1)}, u32[]{:S(2)}, u32[]{:S(2)}) collective-permute-start(f32[1,32,128]{2,1,0:T(8,128)S(1)} %get-tuple-element.61.refs_0_), channel_id=1, source_target_pairs={{0,16},{8,24},{16,0},{24,8},{1,17},{9,25},{17,1},{25,9},{2,18},{10... | collective-permute-start | bytes 49160 | tf_op jit(solution)/shard_map/ppermute | solution.py:97

commit v8 on v7

--- a/solution.py
+++ b/solution.py
@@ -142,19 +142,10 @@
     )
 
 
-def begin_kernel(tracer, y_speed, z_speed, _, o_ref, e_ref, c, ys, zs, sem):
-    arrivals = [
-        pltpu.make_async_copy(source, target, sem.at[k])
-        for k, (source, target) in enumerate(((tracer, c), (z_speed, zs), (y_speed, ys)))
-    ]
-    for copy in arrivals:
-        copy.start()
+def begin_kernel(c, ys, zs, _, o_ref, e_ref):
     _, y, _, _ = place()
     width = c.shape[1]
     y_odd = lax.rem(y, 2)
-    for copy in arrivals:
-        copy.wait()
-
     def rims(o_low):
         for ref, low in ((o_ref, o_low), (e_ref, not o_low)):
             tile = slice(0, 8) if low else slice(width - 8, width)
@@ -181,8 +172,7 @@
         begin_kernel,
         "begin",
         [near(10, depth, band)] * 2,
-        [("far", x) for x in (tracer, y_speed, z_speed)] + [after],
-        scratch=[near(depth, width, band)] * 3 + [pltpu.SemaphoreType.DMA((3,))],
+        [tracer, y_speed, z_speed, after],
         cycles=2000,
     )
 
@@ -427,14 +417,8 @@
     z, y, z_count, y_count = place()
     depth, width, band = tracer.shape
     rows, cols = depth + 8, width + 8
-    copies = [
-        pltpu.make_async_copy(own, field.at[pl.ds(4, depth), pl.ds(0, width), :], sem.at[k])
-        for k, (field, own) in enumerate(((ys, y_speed), (zs, z_speed), (c, tracer)))
-    ]
     y_copy = pltpu.make_async_copy(r_y_far, r_y, sem.at[3])
     z_copy = pltpu.make_async_copy(r_z_far, r_z, sem.at[4])
-    for copy in copies:
-        copy.start()
     y_copy.start()
     z_copy.start()
     ports_out[...] = ports_z[...]
@@ -486,8 +470,8 @@
     def _():
         sides(False)
 
-    for copy in copies[:2]:
-        copy.wait()
+    for field, own in ((ys, y_speed), (zs, z_speed), (c, tracer)):
+        field[4 : 4 + depth, 0:width, :] = own[...]
 
     def up(v):
         return pltpu.roll(v, cols - 1, 0)
@@ -503,7 +487,6 @@
         return after
 
     lax.fori_loop(0, rows - 1, faces, zs[0], unroll=13)
-    copies[2].wait()
 
     keep_low = jnp.where(z == 0, 0.0, 1.0)
     keep_high = jnp.where(z == z_count - 1, 0.0, 1.0)
@@ -554,7 +537,7 @@
         advect_kernel,
         "advect",
         [along_y, near(2, depth, band), along_y, along_z, near(5, width, band)],
-        [("far", x) for x in (tracer, y_speed, z_speed)]
+        [tracer, y_speed, z_speed]
         + list(halos)
         + [ports_y, ("far", r_y), ("far", r_z), ports_z],
         scratch=[padded] * 5 + [along_y] * 3

time: 36.2 us -> 35.2 us (0.972)
  Pallas kernels: 8.42 us -> 6.24 us
  starting transfers between devices: 19.2 us -> 21 us
  waiting for transfers between devices: 8.17 us -> 7.69 us
    pallas_call x13, Pallas kernels: 8.42 us -> 6.24 us  [call(): pl.pallas_call(kernel, out_shape=[out[1] if isinstance(out, tuple) else o...]
    ppermute x12, starting transfers between devices: 12.1 us -> 13.1 us  [swap(): lax.ppermute(x, axis, [(i, i ^ step) for i in range(lax.axis_size(axis))])]
    ppermute x12, waiting for transfers between devices: 6.64 us -> 5.81 us  [swap(): lax.ppermute(x, axis, [(i, i ^ step) for i in range(lax.axis_size(axis))])]
    ppermute x4, starting transfers between devices: 7.19 us -> 7.88 us  [send(): return lax.ppermute(x, AXES, permutation(z_partner, y_partner))]
  transfers between devices with their start and end apart: 16 -> 16, of which waited for: 7 -> 7; matrix products, arithmetic and copies ran while one was open for 0% -> 0% of each run, Pallas kernels for 17% -> 11%
where the time goes in v8:
time: 35.2 us; the launch traced here: 35 us
  starting transfers between devices  21 us (60%)
  waiting for transfers between devices  7.69 us (22%)
  Pallas kernels  6.24 us (18%)
    ppermute x12, starting transfers between devices, swap(): lax.ppermute(x, axis, [(i, i ^ step) for i in range(lax.axis_size(axis))])  13.1 us
    ppermute x4, starting transfers between devices, send(): return lax.ppermute(x, AXES, permutation(z_partner, y_partner))  7.88 us
    pallas_call x13, Pallas kernels, call(): pl.pallas_call(kernel, out_shape=[out[1] if isinstance(out, tuple) else o...  6.24 us
    ppermute x12, waiting for transfers between devices, swap(): lax.ppermute(x, axis, [(i, i ^ step) for i in range(lax.axis_size(axis))])  5.81 us
    ppermute x4, waiting for transfers between devices, send(): return lax.ppermute(x, AXES, permutation(z_partner, y_partner))  1.87 us
  transfers between devices with their start and end apart: 16, of which 7 were waited for; matrix products, arithmetic and copies ran while one was open for 0% of the time, Pallas kernels for 11%

profile of v8, /device:TPU:0, one launch (start us, length us, event | category | flops | bytes accessed | tf_op | source)
XLA Modules:
  0.0 35.0 jit_solution(17733444572867008937)
XLA Ops:
  0.0 0.0 copy-start
  0.0 0.0 copy-start.1
  0.0 0.0 copy-start.2
  0.0 1.2 %z_rims.1 = (f32[10,32,128]{2,1,0:T(8,128)S(1)}, f32[10,32,128]{2,1,0:T(8,128)S(1)}) custom-call(f32[32,32,128]{2,1,0:T(8,128)} %tracer.3, f32[32,32,128]{2,1,0:T(8,128)} %y_speed.3, f32[32,32,128]{2,1,0:T(8,128)} %z_speed.3), custom_call_target="tpu_custom_call" | custom-call | bytes 1024000 | tf_op jit(solution)/shard_map/z_rims/pallas_call | solution.py:33
  1.2 0.5 %collective-permute-start = (f32[10,32,128]{2,1,0:T(8,128)S(1)}, f32[10,32,128]{2,1,0:T(8,128)S(1)}, u32[]{:S(2)}, u32[]{:S(2)}) collective-permute-start(f32[10,32,128]{2,1,0:T(8,128)S(1)} %get-tuple-element.36._), channel_id=1, source_target_pairs={{0,1},{1,0},{2,3},{3,2},{4,5},{5,4},{6,7},{7,6},{8,16},{9,17},{10,... | collective-permute-start | bytes 491528 | tf_op jit(solution)/shard_map/ppermute | solution.py:90
  1.7 0.0 copy-start.3
  1.7 4.1 %collective-permute-start.1 = (f32[10,32,128]{2,1,0:T(8,128)S(1)}, f32[10,32,128]{2,1,0:T(8,128)S(1)}, u32[]{:S(2)}, u32[]{:S(2)}) collective-permute-start(f32[10,32,128]{2,1,0:T(8,128)S(1)} %get-tuple-element.37), channel_id=1, source_target_pairs={{0,8},{1,9},{2,10},{3,11},{4,12},{5,13},{6,14},{7,15},{8,0},{9,1},... | collective-permute-start | bytes 491528 | tf_op jit(solution)/shard_map/ppermute | solution.py:90
  5.9 0.0 copy-done
  5.9 0.0 copy-done.1
  5.9 0.0 copy-done.2
  5.9 0.1 begin.1
  6.0 1.4 %collective-permute-start.2 = (f32[10,32,128]{2,1,0:T(8,128)S(1)}, f32[10,32,128]{2,1,0:T(8,128)S(1)}, u32[]{:S(2)}, u32[]{:S(2)}) collective-permute-start(f32[10,32,128]{2,1,0:T(8,128)S(1)} %get-tuple-element.38), channel_id=1, source_target_pairs={{0,7},{1,2},{2,1},{3,4},{4,3},{5,6},{6,5},{7,0},{8,15},{9,10},{10,... | collective-permute-start | bytes 491528 | tf_op jit(solution)/shard_map/ppermute | solution.py:90
  7.4 0.3 collective-permute-start.3
  7.7 0.0 copy-done.3
  7.7 1.1 %factor.1 = (f32[32,32,128]{2,1,0:T(8,128)}, f32[32,32,128]{2,1,0:T(8,128)}, f32[5,32,128]{2,1,0:T(8,128)S(1)}, f32[5,32,128]{2,1,0:T(8,128)S(1)}) custom-call(f32[32,32,128]{2,1,0:T(8,128)S(1)} %copy-done.3), custom_call_target="tpu_custom_call" | custom-call | bytes 4096000 | tf_op jit(solution)/shard_map/factor/pallas_call | solution.py:33
  8.8 0.3 collective-permute-start.7
  9.1 0.0 collective-permute-done.b
  9.1 0.7 %collective-permute-done.1.a = f32[10,32,128]{2,1,0:T(8,128)S(1)} collective-permute-done((f32[10,32,128]{2,1,0:T(8,128)S(1)}, f32[10,32,128]{2,1,0:T(8,128)S(1)}, u32[]{:S(2)}, u32[]{:S(2)}) %collective-permute-start.1) | collective-permute-done | bytes 163872 | tf_op jit(solution)/shard_map/ppermute | solution.py:90
  9.8 1.8 %collective-permute-start.4 = (f32[10,8,128]{2,1,0:T(8,128)S(1)}, f32[10,8,128]{2,1,0:T(8,128)S(1)}, u32[]{:S(2)}, u32[]{:S(2)}) collective-permute-start(f32[10,8,128]{2,1,0:T(8,128)S(1)} %get-tuple-element.41), channel_id=1, source_target_pairs={{0,8},{1,2},{2,1},{3,4},{4,3},{5,6},{6,5},{7,15},{8,0},{9,10},{10,... | collective-permute-start | bytes 122888 | tf_op jit(solution)/shard_map/ppermute | solution.py:90
  11.6 0.0 collective-permute-start.5
  11.7 0.0 collective-permute-done.7.refs_1_
  11.7 1.0 %collective-permute-start.9 = (f32[5,32,128]{2,1,0:T(8,128)S(1)}, f32[5,32,128]{2,1,0:T(8,128)S(1)}, u32[]{:S(2)}, u32[]{:S(2)}) collective-permute-start(f32[5,32,128]{2,1,0:T(8,128)S(1)} %get-tuple-element.49.refs_0_), channel_id=1, source_target_pairs={{0,3},{1,2},{2,1},{3,0},{4,7},{5,6},{6,5},{7,4},{8,11},{9,10},{10,... | collective-permute-start | bytes 245768 | tf_op jit(solution)/shard_map/ppermute | solution.py:97
  12.7 0.7 %collective-permute-done.2.o = f32[10,32,128]{2,1,0:T(8,128)S(1)} collective-permute-done((f32[10,32,128]{2,1,0:T(8,128)S(1)}, f32[10,32,128]{2,1,0:T(8,128)S(1)}, u32[]{:S(2)}, u32[]{:S(2)}) %collective-permute-start.2) | collective-permute-done | bytes 163872 | tf_op jit(solution)/shard_map/ppermute | solution.py:90
  13.4 0.0 collective-permute-done.3.e
  13.4 0.0 collective-permute-done.5.ab
  13.4 0.5 %collective-permute-done.4.corner = f32[10,8,128]{2,1,0:T(8,128)S(1)} collective-permute-done((f32[10,8,128]{2,1,0:T(8,128)S(1)}, f32[10,8,128]{2,1,0:T(8,128)S(1)}, u32[]{:S(2)}, u32[]{:S(2)}) %collective-permute-start.4) | collective-permute-done | bytes 40992 | tf_op jit(solution)/shard_map/ppermute | solution.py:90
  13.9 2.3 %advect.1 = (f32[32,32,128]{2,1,0:T(8,128)S(1)}, f32[2,32,128]{2,1,0:T(8,128)S(1)}, f32[32,32,128]{2,1,0:T(8,128)S(1)}, f32[32,32,128]{2,1,0:T(8,128)S(1)}, f32[5,32,128]{2,1,0:T(8,128)S(1)}) custom-call(f32[32,32,128]{2,1,0:T(8,128)S(1)} %copy-done, f32[32,32,128]{2,1,0:T(8,128)S(1)} %copy-done.1, f32[32,32,128]{2,1,0:T(8,128)S(1)} %copy-done.2, ...), custom_call_target="tpu_custom_call" | custom-call | bytes 5120000 | tf_op jit(solution)/shard_map/advect/pallas_call | solution.py:33
  16.2 0.1 collective-permute-start.6
  16.3 1.8 %collective-permute-start.12 = (f32[5,32,128]{2,1,0:T(8,128)S(1)}, f32[5,32,128]{2,1,0:T(8,128)S(1)}, u32[]{:S(2)}, u32[]{:S(2)}) collective-permute-start(f32[5,32,128]{2,1,0:T(8,128)S(1)} %get-tuple-element.57.refs_0_.refs_11_.refs_6_), channel_id=1, source_target_pairs={{0,8},{8,0},{16,24},{24,16},{1,9},{9,1},{17,25},{25,17},{2,10},{10... | collective-permute-start | bytes 245768 | tf_op jit(solution)/shard_map/ppermute | solution.py:97
  18.1 0.0 collective-permute-done.6.refs_1_
  18.1 0.8 %collective-permute-start.8 = (f32[2,32,128]{2,1,0:T(8,128)S(1)}, f32[2,32,128]{2,1,0:T(8,128)S(1)}, u32[]{:S(2)}, u32[]{:S(2)}) collective-permute-start(f32[2,32,128]{2,1,0:T(8,128)S(1)} %get-tuple-element.48.refs_0_), channel_id=1, source_target_pairs={{0,3},{1,2},{2,1},{3,0},{4,7},{5,6},{6,5},{7,4},{8,11},{9,10},{10,... | collective-permute-start | bytes 98312 | tf_op jit(solution)/shard_map/ppermute | solution.py:97
  18.9 0.0 collective-permute-done.9.refs_1_
  18.9 1.5 %collective-permute-start.11 = (f32[2,32,128]{2,1,0:T(8,128)S(1)}, f32[2,32,128]{2,1,0:T(8,128)S(1)}, u32[]{:S(2)}, u32[]{:S(2)}) collective-permute-start(f32[2,32,128]{2,1,0:T(8,128)S(1)} %get-tuple-element.52.refs_2_), channel_id=1, source_target_pairs={{0,5},{1,4},{2,7},{3,6},{4,1},{5,0},{6,3},{7,2},{8,13},{9,12},{10,... | collective-permute-start | bytes 98312 | tf_op jit(solution)/shard_map/ppermute | solution.py:97
  20.4 1.1 %collective-permute-done.8.refs_1_ = f32[2,32,128]{2,1,0:T(8,128)S(1)} collective-permute-done((f32[2,32,128]{2,1,0:T(8,128)S(1)}, f32[2,32,128]{2,1,0:T(8,128)S(1)}, u32[]{:S(2)}, u32[]{:S(2)}) %collective-permute-start.8) | collective-permute-done | bytes 32800 | tf_op jit(solution)/shard_map/ppermute | solution.py:97
  21.5 2.0 %collective-permute-start.10 = (f32[1,32,128]{2,1,0:T(8,128)S(1)}, f32[1,32,128]{2,1,0:T(8,128)S(1)}, u32[]{:S(2)}, u32[]{:S(2)}) collective-permute-start(f32[1,32,128]{2,1,0:T(8,128)S(1)} %get-tuple-element.51.refs_0_), channel_id=1, source_target_pairs={{0,5},{1,4},{2,7},{3,6},{4,1},{5,0},{6,3},{7,2},{8,13},{9,12},{10,... | collective-permute-start | bytes 49160 | tf_op jit(solution)/shard_map/ppermute | solution.py:97
  23.5 0.0 collective-permute-done.12.refs_1_
  23.6 0.0 collective-permute-done.11.refs_3_
  23.6 1.4 %collective-permute-done.10.refs_1_ = f32[1,32,128]{2,1,0:T(8,128)S(1)} collective-permute-done((f32[1,32,128]{2,1,0:T(8,128)S(1)}, f32[1,32,128]{2,1,0:T(8,128)S(1)}, u32[]{:S(2)}, u32[]{:S(2)}) %collective-permute-start.10) | collective-permute-done | bytes 16416 | tf_op jit(solution)/shard_map/ppermute | solution.py:97
  25.0 0.5 %turn.1 = (f32[32,32,128]{2,1,0:T(8,128)S(1)}, f32[2,32,128]{2,1,0:T(8,128)S(1)}, f32[32,32,128]{2,1,0:T(8,128)S(1)}, f32[32,32,128]{2,1,0:T(8,128)S(1)}) custom-call(f32[1,32,128]{2,1,0:T(8,128)S(1)} %get-tuple-element.51.refs_0_, f32[1,32,128]{2,1,0:T(8,128)S(1)} %collective-permute-done.10.refs_1_, f32[2,32,128]{2,1,0:T(8,128)S(1)} %get-tuple-element.52.refs_2_, ...), custom_call_target="tpu_custom_call" | custom-call | bytes 1536000 | tf_op jit(solution)/shard_map/turn/pallas_call | solution.py:33
  25.5 1.2 %collective-permute-start.13 = (f32[2,32,128]{2,1,0:T(8,128)S(1)}, f32[2,32,128]{2,1,0:T(8,128)S(1)}, u32[]{:S(2)}, u32[]{:S(2)}) collective-permute-start(f32[2,32,128]{2,1,0:T(8,128)S(1)} %get-tuple-element.60.refs_0_), channel_id=1, source_target_pairs={{0,8},{8,0},{16,24},{24,16},{1,9},{9,1},{17,25},{25,17},{2,10},{10... | collective-permute-start | bytes 98312 | tf_op jit(solution)/shard_map/ppermute | solution.py:97
  26.7 2.0 %collective-permute-start.15 = (f32[2,32,128]{2,1,0:T(8,128)S(1)}, f32[2,32,128]{2,1,0:T(8,128)S(1)}, u32[]{:S(2)}, u32[]{:S(2)}) collective-permute-start(f32[2,32,128]{2,1,0:T(8,128)S(1)} %get-tuple-element.62.refs_2_), channel_id=1, source_target_pairs={{0,16},{8,24},{16,0},{24,8},{1,17},{9,25},{17,1},{25,9},{2,18},{10... | collective-permute-start | bytes 98312 | tf_op jit(solution)/shard_map/ppermute | solution.py:97
  28.6 0.8 %collective-permute-done.13.refs_1_ = f32[2,32,128]{2,1,0:T(8,128)S(1)} collective-permute-done((f32[2,32,128]{2,1,0:T(8,128)S(1)}, f32[2,32,128]{2,1,0:T(8,128)S(1)}, u32[]{:S(2)}, u32[]{:S(2)}) %collective-permute-start.13) | collective-permute-done | bytes 32800 | tf_op jit(solution)/shard_map/ppermute | solution.py:97
  29.5 2.2 %collective-permute-start.14 = (f32[1,32,128]{2,1,0:T(8,128)S(1)}, f32[1,32,128]{2,1,0:T(8,128)S(1)}, u32[]{:S(2)}, u32[]{:S(2)}) collective-permute-start(f32[1,32,128]{2,1,0:T(8,128)S(1)} %get-tuple-element.61.refs_0_), channel_id=1, source_target_pairs={{0,16},{8,24},{16,0},{24,8},{1,17},{9,25},{17,1},{25,9},{2,18},{10... | collective-permute-start | bytes 49160 | tf_op jit(solution)/shard_map/ppermute | solution.py:97
  31.7 0.0 collective-permute-done.15.refs_3_
  31.7 2.5 %collective-permute-done.14.refs_1_ = f32[1,32,128]{2,1,0:T(8,128)S(1)} collective-permute-done((f32[1,32,128]{2,1,0:T(8,128)S(1)}, f32[1,32,128]{2,1,0:T(8,128)S(1)}, u32[]{:S(2)}, u32[]{:S(2)}) %collective-permute-start.14) | collective-permute-done | bytes 16416 | tf_op jit(solution)/shard_map/ppermute | solution.py:97
  34.2 0.9 %finish.1 = f32[32,32,128]{2,1,0:T(8,128)} custom-call(f32[1,32,128]{2,1,0:T(8,128)S(1)} %get-tuple-element.61.refs_0_, f32[1,32,128]{2,1,0:T(8,128)S(1)} %collective-permute-done.14.refs_1_, f32[2,32,128]{2,1,0:T(8,128)S(1)} %get-tuple-element.62.refs_2_, f32[2,32,128]{2,1,0:T(8,128)S(1)} %collective-permute-done.15.refs_3_, ...), custom_call_target="tpu_custom_call" | custom-call | bytes 1024000 | tf_op jit(solution)/shard_map/finish/pallas_call | solution.py:33
  (7 shorter events, 0.2 us)
Async XLA Ops:
  0.0 5.9 %copy-start = (f32[32,32,128]{2,1,0:T(8,128)S(1)}, f32[32,32,128]{2,1,0:T(8,128)}, u32[]{:S(2)}) copy-start(f32[32,32,128]{2,1,0:T(8,128)} %tracer.3) | copy-start | bytes 1572868
  0.0 5.9 %copy-start.1 = (f32[32,32,128]{2,1,0:T(8,128)S(1)}, f32[32,32,128]{2,1,0:T(8,128)}, u32[]{:S(2)}) copy-start(f32[32,32,128]{2,1,0:T(8,128)} %y_speed.3) | copy-start | bytes 1572868
  0.0 5.9 %copy-start.2 = (f32[32,32,128]{2,1,0:T(8,128)S(1)}, f32[32,32,128]{2,1,0:T(8,128)}, u32[]{:S(2)}) copy-start(f32[32,32,128]{2,1,0:T(8,128)} %z_speed.3) | copy-start | bytes 1572868
  1.2 7.9 %collective-permute-start = (f32[10,32,128]{2,1,0:T(8,128)S(1)}, f32[10,32,128]{2,1,0:T(8,128)S(1)}, u32[]{:S(2)}, u32[]{:S(2)}) collective-permute-start(f32[10,32,128]{2,1,0:T(8,128)S(1)} %get-tuple-element.36._), channel_id=1, source_target_pairs={{0,1},{1,0},{2,3},{3,2},{4,5},{5,4},{6,7},{7,6},{8,16},{9,17},{10,... | collective-permute-start | bytes 491528 | tf_op jit(solution)/shard_map/ppermute | solution.py:90
  1.7 6.0 %copy-start.3 = (f32[32,32,128]{2,1,0:T(8,128)S(1)}, f32[32,32,128]{2,1,0:T(8,128)}, u32[]{:S(2)}) copy-start(f32[32,32,128]{2,1,0:T(8,128)} %kappa.1) | copy-start | bytes 1572868
  1.7 8.1 %collective-permute-start.1 = (f32[10,32,128]{2,1,0:T(8,128)S(1)}, f32[10,32,128]{2,1,0:T(8,128)S(1)}, u32[]{:S(2)}, u32[]{:S(2)}) collective-permute-start(f32[10,32,128]{2,1,0:T(8,128)S(1)} %get-tuple-element.37), channel_id=1, source_target_pairs={{0,8},{1,9},{2,10},{3,11},{4,12},{5,13},{6,14},{7,15},{8,0},{9,1},... | collective-permute-start | bytes 491528 | tf_op jit(solution)/shard_map/ppermute | solution.py:90
  6.0 7.4 %collective-permute-start.2 = (f32[10,32,128]{2,1,0:T(8,128)S(1)}, f32[10,32,128]{2,1,0:T(8,128)S(1)}, u32[]{:S(2)}, u32[]{:S(2)}) collective-permute-start(f32[10,32,128]{2,1,0:T(8,128)S(1)} %get-tuple-element.38), channel_id=1, source_target_pairs={{0,7},{1,2},{2,1},{3,4},{4,3},{5,6},{6,5},{7,0},{8,15},{9,10},{10,... | collective-permute-start | bytes 491528 | tf_op jit(solution)/shard_map/ppermute | solution.py:90
  7.4 6.0 %collective-permute-start.3 = (f32[10,32,128]{2,1,0:T(8,128)S(1)}, f32[10,32,128]{2,1,0:T(8,128)S(1)}, u32[]{:S(2)}, u32[]{:S(2)}) collective-permute-start(f32[10,32,128]{2,1,0:T(8,128)S(1)} %get-tuple-element.39), channel_id=1, source_target_pairs={{0,1},{1,0},{2,3},{3,2},{4,5},{5,4},{6,7},{7,6},{8,9},{9,8},{10,11... | collective-permute-start | bytes 491528 | tf_op jit(solution)/shard_map/ppermute | solution.py:97
  8.8 2.9 %collective-permute-start.7 = (f32[5,32,128]{2,1,0:T(8,128)S(1)}, f32[5,32,128]{2,1,0:T(8,128)S(1)}, u32[]{:S(2)}, u32[]{:S(2)}) collective-permute-start(f32[5,32,128]{2,1,0:T(8,128)S(1)} %get-tuple-element.43.ports_y.refs_0_.refs_8_), channel_id=1, source_target_pairs={{0,1},{1,0},{2,3},{3,2},{4,5},{5,4},{6,7},{7,6},{8,9},{9,8},{10,11... | collective-permute-start | bytes 245768 | tf_op jit(solution)/shard_map/ppermute | solution.py:97
  9.8 4.1 %collective-permute-start.4 = (f32[10,8,128]{2,1,0:T(8,128)S(1)}, f32[10,8,128]{2,1,0:T(8,128)S(1)}, u32[]{:S(2)}, u32[]{:S(2)}) collective-permute-start(f32[10,8,128]{2,1,0:T(8,128)S(1)} %get-tuple-element.41), channel_id=1, source_target_pairs={{0,8},{1,2},{2,1},{3,4},{4,3},{5,6},{6,5},{7,15},{8,0},{9,10},{10,... | collective-permute-start | bytes 122888 | tf_op jit(solution)/shard_map/ppermute | solution.py:90
  11.6 1.7 %collective-permute-start.5 = (f32[9,8,128]{2,1,0:T(8,128)S(1)}, f32[9,8,128]{2,1,0:T(8,128)S(1)}, u32[]{:S(2)}, u32[]{:S(2)}) collective-permute-start(f32[9,8,128]{2,1,0:T(8,128)S(1)} %get-tuple-element.42), channel_id=1, source_target_pairs={{0,1},{1,0},{2,3},{3,2},{4,5},{5,4},{6,7},{7,6},{8,9},{9,8},{10,11... | collective-permute-start | bytes 110600 | tf_op jit(solution)/shard_map/ppermute | solution.py:97
  11.7 7.2 %collective-permute-start.9 = (f32[5,32,128]{2,1,0:T(8,128)S(1)}, f32[5,32,128]{2,1,0:T(8,128)S(1)}, u32[]{:S(2)}, u32[]{:S(2)}) collective-permute-start(f32[5,32,128]{2,1,0:T(8,128)S(1)} %get-tuple-element.49.refs_0_), channel_id=1, source_target_pairs={{0,3},{1,2},{2,1},{3,0},{4,7},{5,6},{6,5},{7,4},{8,11},{9,10},{10,... | collective-permute-start | bytes 245768 | tf_op jit(solution)/shard_map/ppermute | solution.py:97
  16.2 1.9 %collective-permute-start.6 = (f32[2,32,128]{2,1,0:T(8,128)S(1)}, f32[2,32,128]{2,1,0:T(8,128)S(1)}, u32[]{:S(2)}, u32[]{:S(2)}) collective-permute-start(f32[2,32,128]{2,1,0:T(8,128)S(1)} %get-tuple-element.46.refs_0_), channel_id=1, source_target_pairs={{0,1},{1,0},{2,3},{3,2},{4,5},{5,4},{6,7},{7,6},{8,9},{9,8},{10,11... | collective-permute-start | bytes 98312 | tf_op jit(solution)/shard_map/ppermute | solution.py:97
  16.3 7.2 %collective-permute-start.12 = (f32[5,32,128]{2,1,0:T(8,128)S(1)}, f32[5,32,128]{2,1,0:T(8,128)S(1)}, u32[]{:S(2)}, u32[]{:S(2)}) collective-permute-start(f32[5,32,128]{2,1,0:T(8,128)S(1)} %get-tuple-element.57.refs_0_.refs_11_.refs_6_), channel_id=1, source_target_pairs={{0,8},{8,0},{16,24},{24,16},{1,9},{9,1},{17,25},{25,17},{2,10},{10... | collective-permute-start | bytes 245768 | tf_op jit(solution)/shard_map/ppermute | solution.py:97
  18.1 3.4 %collective-permute-start.8 = (f32[2,32,128]{2,1,0:T(8,128)S(1)}, f32[2,32,128]{2,1,0:T(8,128)S(1)}, u32[]{:S(2)}, u32[]{:S(2)}) collective-permute-start(f32[2,32,128]{2,1,0:T(8,128)S(1)} %get-tuple-element.48.refs_0_), channel_id=1, source_target_pairs={{0,3},{1,2},{2,1},{3,0},{4,7},{5,6},{6,5},{7,4},{8,11},{9,10},{10,... | collective-permute-start | bytes 98312 | tf_op jit(solution)/shard_map/ppermute | solution.py:97
  18.9 4.7 %collective-permute-start.11 = (f32[2,32,128]{2,1,0:T(8,128)S(1)}, f32[2,32,128]{2,1,0:T(8,128)S(1)}, u32[]{:S(2)}, u32[]{:S(2)}) collective-permute-start(f32[2,32,128]{2,1,0:T(8,128)S(1)} %get-tuple-element.52.refs_2_), channel_id=1, source_target_pairs={{0,5},{1,4},{2,7},{3,6},{4,1},{5,0},{6,3},{7,2},{8,13},{9,12},{10,... | collective-permute-start | bytes 98312 | tf_op jit(solution)/shard_map/ppermute | solution.py:97
  21.5 3.4 %collective-permute-start.10 = (f32[1,32,128]{2,1,0:T(8,128)S(1)}, f32[1,32,128]{2,1,0:T(8,128)S(1)}, u32[]{:S(2)}, u32[]{:S(2)}) collective-permute-start(f32[1,32,128]{2,1,0:T(8,128)S(1)} %get-tuple-element.51.refs_0_), channel_id=1, source_target_pairs={{0,5},{1,4},{2,7},{3,6},{4,1},{5,0},{6,3},{7,2},{8,13},{9,12},{10,... | collective-permute-start | bytes 49160 | tf_op jit(solution)/shard_map/ppermute | solution.py:97
  25.5 4.0 %collective-permute-start.13 = (f32[2,32,128]{2,1,0:T(8,128)S(1)}, f32[2,32,128]{2,1,0:T(8,128)S(1)}, u32[]{:S(2)}, u32[]{:S(2)}) collective-permute-start(f32[2,32,128]{2,1,0:T(8,128)S(1)} %get-tuple-element.60.refs_0_), channel_id=1, source_target_pairs={{0,8},{8,0},{16,24},{24,16},{1,9},{9,1},{17,25},{25,17},{2,10},{10... | collective-permute-start | bytes 98312 | tf_op jit(solution)/shard_map/ppermute | solution.py:97
  26.7 5.0 %collective-permute-start.15 = (f32[2,32,128]{2,1,0:T(8,128)S(1)}, f32[2,32,128]{2,1,0:T(8,128)S(1)}, u32[]{:S(2)}, u32[]{:S(2)}) collective-permute-start(f32[2,32,128]{2,1,0:T(8,128)S(1)} %get-tuple-element.62.refs_2_), channel_id=1, source_target_pairs={{0,16},{8,24},{16,0},{24,8},{1,17},{9,25},{17,1},{25,9},{2,18},{10... | collective-permute-start | bytes 98312 | tf_op jit(solution)/shard_map/ppermute | solution.py:97
  29.5 4.7 %collective-permute-start.14 = (f32[1,32,128]{2,1,0:T(8,128)S(1)}, f32[1,32,128]{2,1,0:T(8,128)S(1)}, u32[]{:S(2)}, u32[]{:S(2)}) collective-permute-start(f32[1,32,128]{2,1,0:T(8,128)S(1)} %get-tuple-element.61.refs_0_), channel_id=1, source_target_pairs={{0,16},{8,24},{16,0},{24,8},{1,17},{9,25},{17,1},{25,9},{2,18},{10... | collective-permute-start | bytes 49160 | tf_op jit(solution)/shard_map/ppermute | solution.py:97

commit v9 on v8

--- a/solution.py
+++ b/solution.py
@@ -177,9 +177,6 @@
     )
 
 
-PAD_TILES = 1
-
-
 def rim_kernel(b, a, _, for_pair, for_other):
     z, y, _, _ = place()
     width = a.shape[1]
@@ -203,12 +200,10 @@
         corners(for_other, False)
         corners(for_pair, True)
 
-    for_other[9:] = jnp.zeros((PAD_TILES, 8, for_other.shape[2]), F32)
-
 
 def rim(a, b, after):
     band = a.shape[2]
-    return call(rim_kernel, "rim", [near(9, 8, band), near(9 + PAD_TILES, 8, band)], [b, a, after], cycles=200)
+    return call(rim_kernel, "rim", [near(9, 8, band), near(9, 8, band)], [b, a, after], cycles=200)
 
 
 def reciprocal(x):
@@ -411,8 +406,8 @@
 
 
 def advect_kernel(
-    tracer, y_speed, z_speed, b, a, o, e, corner, ab, ports_y, r_y_far, r_z_far, ports_z,
-    base, sources, r_y, r_z, ports_out, c, ys, zs, sy, sz, phi, psi, kept, flux_z, flux_y, sem,
+    tracer, y_speed, z_speed, b, a, o, e, corner, ab, ports_y, r_y_far, r_z_far,
+    base, sources, r_y, r_z, c, ys, zs, sy, sz, phi, psi, kept, flux_z, flux_y, sem,
 ):
     z, y, z_count, y_count = place()
     depth, width, band = tracer.shape
@@ -421,7 +416,6 @@
     z_copy = pltpu.make_async_copy(r_z_far, r_z, sem.at[4])
     y_copy.start()
     z_copy.start()
-    ports_out[...] = ports_z[...]
     z_odd, y_odd = lax.rem(z, 2), lax.rem(y, 2)
     keep_b = jnp.where((z_odd == 0) & (z == 0) | (z_odd == 1) & (z == z_count - 1), 0.0, 1.0)
     keep_o = jnp.where((y_odd == 0) & (y == 0) | (y_odd == 1) & (y == y_count - 1), 0.0, 1.0)
@@ -486,7 +480,7 @@
         sz[r] = 0.5 * (before + after)
         return after
 
-    lax.fori_loop(0, rows - 1, faces, zs[0], unroll=13)
+    lax.fori_loop(0, rows - 1, faces, zs[0], unroll=39)
 
     keep_low = jnp.where(z == 0, 0.0, 1.0)
     keep_high = jnp.where(z == z_count - 1, 0.0, 1.0)
@@ -529,17 +523,17 @@
     solve_open(kept, phi, psi, ports_y[1], base, sources)
 
 
-def advect(tracer, y_speed, z_speed, halos, ports_y, r_y, r_z, ports_z):
+def advect(tracer, y_speed, z_speed, halos, ports_y, r_y, r_z):
     depth, width, band = tracer.shape
     padded = near(depth + 8, width + 8, band)
     along_y, along_z = near(width, depth, band), near(depth, width, band)
     return call(
         advect_kernel,
         "advect",
-        [along_y, near(2, depth, band), along_y, along_z, near(5, width, band)],
+        [along_y, near(2, depth, band), along_y, along_z],
         [tracer, y_speed, z_speed]
         + list(halos)
-        + [ports_y, ("far", r_y), ("far", r_z), ports_z],
+        + [ports_y, ("far", r_y), ("far", r_z)],
         scratch=[padded] * 5 + [along_y] * 3
         + [near(2, width + 8, band), near(depth, 8, band), pltpu.SemaphoreType.DMA((5,))],
         cycles=5000,
@@ -554,6 +548,7 @@
     width, depth = base_y.shape[0], base.shape[0]
     low, high = end_currents("gy", *last, joints, flows)
     edge, _ = outer(ports_y, y, y_count)
+    factor(((lambda k: r_z[k], depth, *outer(ports_z, z, z_count), (phi, psi), None),))
     value = low * ports_y[0] + high * ports_y[1]
     current = (1.0 + edge) * value - low
     u[0] = base_y[0] + value
@@ -563,7 +558,6 @@
         value = value + r * current
         current = current + value
         u[j] = own + value
-    factor(((lambda k: r_z[k], depth, *outer(ports_z, z, z_count), (phi, psi), None),))
     kept[...] = turned(u[...])
     solve_open(kept, phi, psi, ports_z[1], base, sources)
 
@@ -640,8 +634,8 @@
     ab = swap(for_pair, "gy", 0)
     joints_y, edge_y, edge_y_theirs = join_all(ports_y, "gy")
 
-    base, sources, r_y, r_z, ports_z = advect(
-        tracer, y_speed, z_speed, (b, a, o, e, corner, ab), ports_y, r_y, r_z, ports_z
+    base, sources, r_y, r_z = advect(
+        tracer, y_speed, z_speed, (b, a, o, e, corner, ab), ports_y, r_y, r_z
     )
     joints_z, edge_z, edge_z_theirs = join_all(ports_z, "gz")
     mine, theirs, flows = exchange_sources(sources, joints_y, "gy")

time: 35.2 us -> 34.9 us (level)
  waiting for transfers between devices: 7.69 us -> 7.23 us
    ppermute x4, starting transfers between devices: 7.88 us -> 8.38 us  [send(): return lax.ppermute(x, AXES, permutation(z_partner, y_partner))]
    ppermute x12, waiting for transfers between devices: 5.81 us -> 5.42 us  [swap(): lax.ppermute(x, axis, [(i, i ^ step) for i in range(lax.axis_size(axis))])]
  transfers between devices with their start and end apart: 16 -> 16, of which waited for: 7 -> 5; matrix products, arithmetic and copies ran while one was open for 0% -> 0% of each run, Pallas kernels for 11% -> 11%
where the time goes in v9:
time: 34.9 us; the launch traced here: 34.8 us
  starting transfers between devices  21.2 us (61%)
  waiting for transfers between devices  7.23 us (21%)
  Pallas kernels  6.2 us (18%)
    ppermute x12, starting transfers between devices, swap(): lax.ppermute(x, axis, [(i, i ^ step) for i in range(lax.axis_size(axis))])  12.8 us
    ppermute x4, starting transfers between devices, send(): return lax.ppermute(x, AXES, permutation(z_partner, y_partner))  8.38 us
    pallas_call x13, Pallas kernels, call(): pl.pallas_call(kernel, out_shape=[out[1] if isinstance(out, tuple) else o...  6.2 us
    ppermute x12, waiting for transfers between devices, swap(): lax.ppermute(x, axis, [(i, i ^ step) for i in range(lax.axis_size(axis))])  5.42 us
    ppermute x4, waiting for transfers between devices, send(): return lax.ppermute(x, AXES, permutation(z_partner, y_partner))  1.8 us
  transfers between devices with their start and end apart: 16, of which 5 were waited for; matrix products, arithmetic and copies ran while one was open for 0% of the time, Pallas kernels for 11%

profile of v9, /device:TPU:0, one launch (start us, length us, event | category | flops | bytes accessed | tf_op | source)
XLA Modules:
  0.0 34.8 jit_solution(16007440143954433669)
XLA Ops:
  0.0 0.0 copy-start.2
  0.0 0.0 copy-start.1
  0.0 0.0 copy-start
  0.0 1.2 %z_rims.1 = (f32[10,32,128]{2,1,0:T(8,128)S(1)}, f32[10,32,128]{2,1,0:T(8,128)S(1)}) custom-call(f32[32,32,128]{2,1,0:T(8,128)} %tracer.3, f32[32,32,128]{2,1,0:T(8,128)} %y_speed.3, f32[32,32,128]{2,1,0:T(8,128)} %z_speed.3), custom_call_target="tpu_custom_call" | custom-call | bytes 1024000 | tf_op jit(solution)/shard_map/z_rims/pallas_call | solution.py:33
  1.2 3.1 %collective-permute-start.1 = (f32[10,32,128]{2,1,0:T(8,128)S(1)}, f32[10,32,128]{2,1,0:T(8,128)S(1)}, u32[]{:S(2)}, u32[]{:S(2)}) collective-permute-start(f32[10,32,128]{2,1,0:T(8,128)S(1)} %get-tuple-element.36), channel_id=1, source_target_pairs={{0,8},{1,9},{2,10},{3,11},{4,12},{5,13},{6,14},{7,15},{8,0},{9,1},... | collective-permute-start | bytes 491528 | tf_op jit(solution)/shard_map/ppermute | solution.py:90
  4.3 0.0 copy-start.3
  4.3 0.0 collective-permute-start
  4.3 0.0 copy-done.2
  4.3 0.0 copy-done.1
  4.3 0.0 copy-done
  4.3 0.1 begin.1
  4.5 2.6 %collective-permute-start.2 = (f32[10,32,128]{2,1,0:T(8,128)S(1)}, f32[10,32,128]{2,1,0:T(8,128)S(1)}, u32[]{:S(2)}, u32[]{:S(2)}) collective-permute-start(f32[10,32,128]{2,1,0:T(8,128)S(1)} %get-tuple-element.37), channel_id=1, source_target_pairs={{0,7},{1,2},{2,1},{3,4},{4,3},{5,6},{6,5},{7,0},{8,15},{9,10},{10,... | collective-permute-start | bytes 491528 | tf_op jit(solution)/shard_map/ppermute | solution.py:90
  7.1 0.0 collective-permute-start.3
  7.1 0.0 copy-done.3
  7.1 1.1 %factor.1 = (f32[32,32,128]{2,1,0:T(8,128)}, f32[32,32,128]{2,1,0:T(8,128)}, f32[5,32,128]{2,1,0:T(8,128)S(1)}, f32[5,32,128]{2,1,0:T(8,128)S(1)}) custom-call(f32[32,32,128]{2,1,0:T(8,128)S(1)} %copy-done.3), custom_call_target="tpu_custom_call" | custom-call | bytes 4096000 | tf_op jit(solution)/shard_map/factor/pallas_call | solution.py:33
  8.2 0.6 %collective-permute-start.7 = (f32[5,32,128]{2,1,0:T(8,128)S(1)}, f32[5,32,128]{2,1,0:T(8,128)S(1)}, u32[]{:S(2)}, u32[]{:S(2)}) collective-permute-start(f32[5,32,128]{2,1,0:T(8,128)S(1)} %get-tuple-element.42.ports_y.refs_0_.refs_8_), channel_id=1, source_target_pairs={{0,1},{1,0},{2,3},{3,2},{4,5},{5,4},{6,7},{7,6},{8,9},{9,8},{10,11... | collective-permute-start | bytes 245768 | tf_op jit(solution)/shard_map/ppermute | solution.py:97
  8.8 0.0 collective-permute-done.1.a
  8.8 0.0 collective-permute-done.b
  8.8 2.7 %collective-permute-start.4 = (f32[9,8,128]{2,1,0:T(8,128)S(1)}, f32[9,8,128]{2,1,0:T(8,128)S(1)}, u32[]{:S(2)}, u32[]{:S(2)}) collective-permute-start(f32[9,8,128]{2,1,0:T(8,128)S(1)} %get-tuple-element.40), channel_id=1, source_target_pairs={{0,8},{1,2},{2,1},{3,4},{4,3},{5,6},{6,5},{7,15},{8,0},{9,10},{10,... | collective-permute-start | bytes 110600 | tf_op jit(solution)/shard_map/ppermute | solution.py:90
  11.5 0.0 collective-permute-start.5
  11.5 0.0 collective-permute-done.7.refs_1_
  11.5 0.1 collective-permute-start.9
  11.6 0.0 collective-permute-done.2.o
  11.6 0.0 collective-permute-done.3.e
  11.6 1.8 %collective-permute-done.4.corner = f32[9,8,128]{2,1,0:T(8,128)S(1)} collective-permute-done((f32[9,8,128]{2,1,0:T(8,128)S(1)}, f32[9,8,128]{2,1,0:T(8,128)S(1)}, u32[]{:S(2)}, u32[]{:S(2)}) %collective-permute-start.4) | collective-permute-done | bytes 36896 | tf_op jit(solution)/shard_map/ppermute | solution.py:90
  13.4 0.0 collective-permute-done.5.ab
  13.4 2.3 %advect.1 = (f32[32,32,128]{2,1,0:T(8,128)S(1)}, f32[2,32,128]{2,1,0:T(8,128)S(1)}, f32[32,32,128]{2,1,0:T(8,128)S(1)}, f32[32,32,128]{2,1,0:T(8,128)S(1)}) custom-call(f32[32,32,128]{2,1,0:T(8,128)S(1)} %copy-done, f32[32,32,128]{2,1,0:T(8,128)S(1)} %copy-done.1, f32[32,32,128]{2,1,0:T(8,128)S(1)} %copy-done.2, f32[10,32,128]{2,1,0:T(8,128)S(1)} %collective-permute-done.b, ...), custom_call_target="tpu_custom_call" | custom-call | bytes 5120000 | tf_op jit(solution)/shard_map/advect/pallas_call | solution.py:33
  15.7 0.1 collective-permute-start.6
  15.8 2.1 %collective-permute-start.12 = (f32[5,32,128]{2,1,0:T(8,128)S(1)}, f32[5,32,128]{2,1,0:T(8,128)S(1)}, u32[]{:S(2)}, u32[]{:S(2)}) collective-permute-start(f32[5,32,128]{2,1,0:T(8,128)S(1)} %get-tuple-element.39._.refs_0_.refs_11_.refs_6_), channel_id=1, source_target_pairs={{0,8},{8,0},{16,24},{24,16},{1,9},{9,1},{17,25},{25,17},{2,10},{10... | collective-permute-start | bytes 245768 | tf_op jit(solution)/shard_map/ppermute | solution.py:97
  17.9 0.0 collective-permute-done.6.refs_1_
  17.9 0.9 %collective-permute-start.8 = (f32[2,32,128]{2,1,0:T(8,128)S(1)}, f32[2,32,128]{2,1,0:T(8,128)S(1)}, u32[]{:S(2)}, u32[]{:S(2)}) collective-permute-start(f32[2,32,128]{2,1,0:T(8,128)S(1)} %get-tuple-element.47.refs_0_), channel_id=1, source_target_pairs={{0,3},{1,2},{2,1},{3,0},{4,7},{5,6},{6,5},{7,4},{8,11},{9,10},{10,... | collective-permute-start | bytes 98312 | tf_op jit(solution)/shard_map/ppermute | solution.py:97
  18.8 0.0 collective-permute-done.9.refs_1_
  18.8 1.5 %collective-permute-start.11 = (f32[2,32,128]{2,1,0:T(8,128)S(1)}, f32[2,32,128]{2,1,0:T(8,128)S(1)}, u32[]{:S(2)}, u32[]{:S(2)}) collective-permute-start(f32[2,32,128]{2,1,0:T(8,128)S(1)} %get-tuple-element.51.refs_2_), channel_id=1, source_target_pairs={{0,5},{1,4},{2,7},{3,6},{4,1},{5,0},{6,3},{7,2},{8,13},{9,12},{10,... | collective-permute-start | bytes 98312 | tf_op jit(solution)/shard_map/ppermute | solution.py:97
  20.3 1.0 %collective-permute-done.8.refs_1_ = f32[2,32,128]{2,1,0:T(8,128)S(1)} collective-permute-done((f32[2,32,128]{2,1,0:T(8,128)S(1)}, f32[2,32,128]{2,1,0:T(8,128)S(1)}, u32[]{:S(2)}, u32[]{:S(2)}) %collective-permute-start.8) | collective-permute-done | bytes 32800 | tf_op jit(solution)/shard_map/ppermute | solution.py:97
  21.3 2.0 %collective-permute-start.10 = (f32[1,32,128]{2,1,0:T(8,128)S(1)}, f32[1,32,128]{2,1,0:T(8,128)S(1)}, u32[]{:S(2)}, u32[]{:S(2)}) collective-permute-start(f32[1,32,128]{2,1,0:T(8,128)S(1)} %get-tuple-element.50.refs_0_), channel_id=1, source_target_pairs={{0,5},{1,4},{2,7},{3,6},{4,1},{5,0},{6,3},{7,2},{8,13},{9,12},{10,... | collective-permute-start | bytes 49160 | tf_op jit(solution)/shard_map/ppermute | solution.py:97
  23.3 0.0 collective-permute-done.12.refs_1_
  23.3 0.0 collective-permute-done.11.refs_3_
  23.3 1.4 %collective-permute-done.10.refs_1_ = f32[1,32,128]{2,1,0:T(8,128)S(1)} collective-permute-done((f32[1,32,128]{2,1,0:T(8,128)S(1)}, f32[1,32,128]{2,1,0:T(8,128)S(1)}, u32[]{:S(2)}, u32[]{:S(2)}) %collective-permute-start.10) | collective-permute-done | bytes 16416 | tf_op jit(solution)/shard_map/ppermute | solution.py:97
  24.7 0.5 %turn.1 = (f32[32,32,128]{2,1,0:T(8,128)S(1)}, f32[2,32,128]{2,1,0:T(8,128)S(1)}, f32[32,32,128]{2,1,0:T(8,128)S(1)}, f32[32,32,128]{2,1,0:T(8,128)S(1)}) custom-call(f32[1,32,128]{2,1,0:T(8,128)S(1)} %get-tuple-element.50.refs_0_, f32[1,32,128]{2,1,0:T(8,128)S(1)} %collective-permute-done.10.refs_1_, f32[2,32,128]{2,1,0:T(8,128)S(1)} %get-tuple-element.51.refs_2_, ...), custom_call_target="tpu_custom_call" | custom-call | bytes 1536000 | tf_op jit(solution)/shard_map/turn/pallas_call | solution.py:33
  25.2 1.2 %collective-permute-start.13 = (f32[2,32,128]{2,1,0:T(8,128)S(1)}, f32[2,32,128]{2,1,0:T(8,128)S(1)}, u32[]{:S(2)}, u32[]{:S(2)}) collective-permute-start(f32[2,32,128]{2,1,0:T(8,128)S(1)} %get-tuple-element.58.refs_0_), channel_id=1, source_target_pairs={{0,8},{8,0},{16,24},{24,16},{1,9},{9,1},{17,25},{25,17},{2,10},{10... | collective-permute-start | bytes 98312 | tf_op jit(solution)/shard_map/ppermute | solution.py:97
  26.4 2.1 %collective-permute-start.15 = (f32[2,32,128]{2,1,0:T(8,128)S(1)}, f32[2,32,128]{2,1,0:T(8,128)S(1)}, u32[]{:S(2)}, u32[]{:S(2)}) collective-permute-start(f32[2,32,128]{2,1,0:T(8,128)S(1)} %get-tuple-element.60.refs_2_), channel_id=1, source_target_pairs={{0,16},{8,24},{16,0},{24,8},{1,17},{9,25},{17,1},{25,9},{2,18},{10... | collective-permute-start | bytes 98312 | tf_op jit(solution)/shard_map/ppermute | solution.py:97
  28.5 0.7 %collective-permute-done.13.refs_1_ = f32[2,32,128]{2,1,0:T(8,128)S(1)} collective-permute-done((f32[2,32,128]{2,1,0:T(8,128)S(1)}, f32[2,32,128]{2,1,0:T(8,128)S(1)}, u32[]{:S(2)}, u32[]{:S(2)}) %collective-permute-start.13) | collective-permute-done | bytes 32800 | tf_op jit(solution)/shard_map/ppermute | solution.py:97
  29.2 2.4 %collective-permute-start.14 = (f32[1,32,128]{2,1,0:T(8,128)S(1)}, f32[1,32,128]{2,1,0:T(8,128)S(1)}, u32[]{:S(2)}, u32[]{:S(2)}) collective-permute-start(f32[1,32,128]{2,1,0:T(8,128)S(1)} %get-tuple-element.59.refs_0_), channel_id=1, source_target_pairs={{0,16},{8,24},{16,0},{24,8},{1,17},{9,25},{17,1},{25,9},{2,18},{10... | collective-permute-start | bytes 49160 | tf_op jit(solution)/shard_map/ppermute | solution.py:97
  31.6 0.0 collective-permute-done.15.refs_3_
  31.6 2.3 %collective-permute-done.14.refs_1_ = f32[1,32,128]{2,1,0:T(8,128)S(1)} collective-permute-done((f32[1,32,128]{2,1,0:T(8,128)S(1)}, f32[1,32,128]{2,1,0:T(8,128)S(1)}, u32[]{:S(2)}, u32[]{:S(2)}) %collective-permute-start.14) | collective-permute-done | bytes 16416 | tf_op jit(solution)/shard_map/ppermute | solution.py:97
  33.9 0.9 %finish.1 = f32[32,32,128]{2,1,0:T(8,128)} custom-call(f32[1,32,128]{2,1,0:T(8,128)S(1)} %get-tuple-element.59.refs_0_, f32[1,32,128]{2,1,0:T(8,128)S(1)} %collective-permute-done.14.refs_1_, f32[2,32,128]{2,1,0:T(8,128)S(1)} %get-tuple-element.60.refs_2_, f32[2,32,128]{2,1,0:T(8,128)S(1)} %collective-permute-done.15.refs_3_, ...), custom_call_target="tpu_custom_call" | custom-call | bytes 1024000 | tf_op jit(solution)/shard_map/finish/pallas_call | solution.py:33
  (7 shorter events, 0.2 us)
Async XLA Ops:
  0.0 4.3 %copy-start.2 = (f32[32,32,128]{2,1,0:T(8,128)S(1)}, f32[32,32,128]{2,1,0:T(8,128)}, u32[]{:S(2)}) copy-start(f32[32,32,128]{2,1,0:T(8,128)} %z_speed.3) | copy-start | bytes 1572868
  0.0 4.3 %copy-start.1 = (f32[32,32,128]{2,1,0:T(8,128)S(1)}, f32[32,32,128]{2,1,0:T(8,128)}, u32[]{:S(2)}) copy-start(f32[32,32,128]{2,1,0:T(8,128)} %y_speed.3) | copy-start | bytes 1572868
  0.0 4.3 %copy-start = (f32[32,32,128]{2,1,0:T(8,128)S(1)}, f32[32,32,128]{2,1,0:T(8,128)}, u32[]{:S(2)}) copy-start(f32[32,32,128]{2,1,0:T(8,128)} %tracer.3) | copy-start | bytes 1572868
  1.2 7.6 %collective-permute-start.1 = (f32[10,32,128]{2,1,0:T(8,128)S(1)}, f32[10,32,128]{2,1,0:T(8,128)S(1)}, u32[]{:S(2)}, u32[]{:S(2)}) collective-permute-start(f32[10,32,128]{2,1,0:T(8,128)S(1)} %get-tuple-element.36), channel_id=1, source_target_pairs={{0,8},{1,9},{2,10},{3,11},{4,12},{5,13},{6,14},{7,15},{8,0},{9,1},... | collective-permute-start | bytes 491528 | tf_op jit(solution)/shard_map/ppermute | solution.py:90
  4.3 2.8 %copy-start.3 = (f32[32,32,128]{2,1,0:T(8,128)S(1)}, f32[32,32,128]{2,1,0:T(8,128)}, u32[]{:S(2)}) copy-start(f32[32,32,128]{2,1,0:T(8,128)} %kappa.1) | copy-start | bytes 1572868
  4.3 4.5 %collective-permute-start = (f32[10,32,128]{2,1,0:T(8,128)S(1)}, f32[10,32,128]{2,1,0:T(8,128)S(1)}, u32[]{:S(2)}, u32[]{:S(2)}) collective-permute-start(f32[10,32,128]{2,1,0:T(8,128)S(1)} %get-tuple-element.35._), channel_id=1, source_target_pairs={{0,1},{1,0},{2,3},{3,2},{4,5},{5,4},{6,7},{7,6},{8,16},{9,17},{10,... | collective-permute-start | bytes 491528 | tf_op jit(solution)/shard_map/ppermute | solution.py:90
  4.5 7.2 %collective-permute-start.2 = (f32[10,32,128]{2,1,0:T(8,128)S(1)}, f32[10,32,128]{2,1,0:T(8,128)S(1)}, u32[]{:S(2)}, u32[]{:S(2)}) collective-permute-start(f32[10,32,128]{2,1,0:T(8,128)S(1)} %get-tuple-element.37), channel_id=1, source_target_pairs={{0,7},{1,2},{2,1},{3,4},{4,3},{5,6},{6,5},{7,0},{8,15},{9,10},{10,... | collective-permute-start | bytes 491528 | tf_op jit(solution)/shard_map/ppermute | solution.py:90
  7.1 4.6 %collective-permute-start.3 = (f32[10,32,128]{2,1,0:T(8,128)S(1)}, f32[10,32,128]{2,1,0:T(8,128)S(1)}, u32[]{:S(2)}, u32[]{:S(2)}) collective-permute-start(f32[10,32,128]{2,1,0:T(8,128)S(1)} %get-tuple-element.38), channel_id=1, source_target_pairs={{0,1},{1,0},{2,3},{3,2},{4,5},{5,4},{6,7},{7,6},{8,9},{9,8},{10,11... | collective-permute-start | bytes 491528 | tf_op jit(solution)/shard_map/ppermute | solution.py:97
  8.2 3.3 %collective-permute-start.7 = (f32[5,32,128]{2,1,0:T(8,128)S(1)}, f32[5,32,128]{2,1,0:T(8,128)S(1)}, u32[]{:S(2)}, u32[]{:S(2)}) collective-permute-start(f32[5,32,128]{2,1,0:T(8,128)S(1)} %get-tuple-element.42.ports_y.refs_0_.refs_8_), channel_id=1, source_target_pairs={{0,1},{1,0},{2,3},{3,2},{4,5},{5,4},{6,7},{7,6},{8,9},{9,8},{10,11... | collective-permute-start | bytes 245768 | tf_op jit(solution)/shard_map/ppermute | solution.py:97
  8.8 4.6 %collective-permute-start.4 = (f32[9,8,128]{2,1,0:T(8,128)S(1)}, f32[9,8,128]{2,1,0:T(8,128)S(1)}, u32[]{:S(2)}, u32[]{:S(2)}) collective-permute-start(f32[9,8,128]{2,1,0:T(8,128)S(1)} %get-tuple-element.40), channel_id=1, source_target_pairs={{0,8},{1,2},{2,1},{3,4},{4,3},{5,6},{6,5},{7,15},{8,0},{9,10},{10,... | collective-permute-start | bytes 110600 | tf_op jit(solution)/shard_map/ppermute | solution.py:90
  11.5 1.9 %collective-permute-start.5 = (f32[9,8,128]{2,1,0:T(8,128)S(1)}, f32[9,8,128]{2,1,0:T(8,128)S(1)}, u32[]{:S(2)}, u32[]{:S(2)}) collective-permute-start(f32[9,8,128]{2,1,0:T(8,128)S(1)} %get-tuple-element.41), channel_id=1, source_target_pairs={{0,1},{1,0},{2,3},{3,2},{4,5},{5,4},{6,7},{7,6},{8,9},{9,8},{10,11... | collective-permute-start | bytes 110600 | tf_op jit(solution)/shard_map/ppermute | solution.py:97
  11.5 7.3 %collective-permute-start.9 = (f32[5,32,128]{2,1,0:T(8,128)S(1)}, f32[5,32,128]{2,1,0:T(8,128)S(1)}, u32[]{:S(2)}, u32[]{:S(2)}) collective-permute-start(f32[5,32,128]{2,1,0:T(8,128)S(1)} %get-tuple-element.48.refs_0_), channel_id=1, source_target_pairs={{0,3},{1,2},{2,1},{3,0},{4,7},{5,6},{6,5},{7,4},{8,11},{9,10},{10,... | collective-permute-start | bytes 245768 | tf_op jit(solution)/shard_map/ppermute | solution.py:97
  15.7 2.2 %collective-permute-start.6 = (f32[2,32,128]{2,1,0:T(8,128)S(1)}, f32[2,32,128]{2,1,0:T(8,128)S(1)}, u32[]{:S(2)}, u32[]{:S(2)}) collective-permute-start(f32[2,32,128]{2,1,0:T(8,128)S(1)} %get-tuple-element.45.refs_0_), channel_id=1, source_target_pairs={{0,1},{1,0},{2,3},{3,2},{4,5},{5,4},{6,7},{7,6},{8,9},{9,8},{10,11... | collective-permute-start | bytes 98312 | tf_op jit(solution)/shard_map/ppermute | solution.py:97
  15.8 7.5 %collective-permute-start.12 = (f32[5,32,128]{2,1,0:T(8,128)S(1)}, f32[5,32,128]{2,1,0:T(8,128)S(1)}, u32[]{:S(2)}, u32[]{:S(2)}) collective-permute-start(f32[5,32,128]{2,1,0:T(8,128)S(1)} %get-tuple-element.39._.refs_0_.refs_11_.refs_6_), channel_id=1, source_target_pairs={{0,8},{8,0},{16,24},{24,16},{1,9},{9,1},{17,25},{25,17},{2,10},{10... | collective-permute-start | bytes 245768 | tf_op jit(solution)/shard_map/ppermute | solution.py:97
  17.9 3.4 %collective-permute-start.8 = (f32[2,32,128]{2,1,0:T(8,128)S(1)}, f32[2,32,128]{2,1,0:T(8,128)S(1)}, u32[]{:S(2)}, u32[]{:S(2)}) collective-permute-start(f32[2,32,128]{2,1,0:T(8,128)S(1)} %get-tuple-element.47.refs_0_), channel_id=1, source_target_pairs={{0,3},{1,2},{2,1},{3,0},{4,7},{5,6},{6,5},{7,4},{8,11},{9,10},{10,... | collective-permute-start | bytes 98312 | tf_op jit(solution)/shard_map/ppermute | solution.py:97
  18.8 4.5 %collective-permute-start.11 = (f32[2,32,128]{2,1,0:T(8,128)S(1)}, f32[2,32,128]{2,1,0:T(8,128)S(1)}, u32[]{:S(2)}, u32[]{:S(2)}) collective-permute-start(f32[2,32,128]{2,1,0:T(8,128)S(1)} %get-tuple-element.51.refs_2_), channel_id=1, source_target_pairs={{0,5},{1,4},{2,7},{3,6},{4,1},{5,0},{6,3},{7,2},{8,13},{9,12},{10,... | collective-permute-start | bytes 98312 | tf_op jit(solution)/shard_map/ppermute | solution.py:97
  21.3 3.4 %collective-permute-start.10 = (f32[1,32,128]{2,1,0:T(8,128)S(1)}, f32[1,32,128]{2,1,0:T(8,128)S(1)}, u32[]{:S(2)}, u32[]{:S(2)}) collective-permute-start(f32[1,32,128]{2,1,0:T(8,128)S(1)} %get-tuple-element.50.refs_0_), channel_id=1, source_target_pairs={{0,5},{1,4},{2,7},{3,6},{4,1},{5,0},{6,3},{7,2},{8,13},{9,12},{10,... | collective-permute-start | bytes 49160 | tf_op jit(solution)/shard_map/ppermute | solution.py:97
  25.2 4.0 %collective-permute-start.13 = (f32[2,32,128]{2,1,0:T(8,128)S(1)}, f32[2,32,128]{2,1,0:T(8,128)S(1)}, u32[]{:S(2)}, u32[]{:S(2)}) collective-permute-start(f32[2,32,128]{2,1,0:T(8,128)S(1)} %get-tuple-element.58.refs_0_), channel_id=1, source_target_pairs={{0,8},{8,0},{16,24},{24,16},{1,9},{9,1},{17,25},{25,17},{2,10},{10... | collective-permute-start | bytes 98312 | tf_op jit(solution)/shard_map/ppermute | solution.py:97
  26.4 5.2 %collective-permute-start.15 = (f32[2,32,128]{2,1,0:T(8,128)S(1)}, f32[2,32,128]{2,1,0:T(8,128)S(1)}, u32[]{:S(2)}, u32[]{:S(2)}) collective-permute-start(f32[2,32,128]{2,1,0:T(8,128)S(1)} %get-tuple-element.60.refs_2_), channel_id=1, source_target_pairs={{0,16},{8,24},{16,0},{24,8},{1,17},{9,25},{17,1},{25,9},{2,18},{10... | collective-permute-start | bytes 98312 | tf_op jit(solution)/shard_map/ppermute | solution.py:97
  29.2 4.7 %collective-permute-start.14 = (f32[1,32,128]{2,1,0:T(8,128)S(1)}, f32[1,32,128]{2,1,0:T(8,128)S(1)}, u32[]{:S(2)}, u32[]{:S(2)}) collective-permute-start(f32[1,32,128]{2,1,0:T(8,128)S(1)} %get-tuple-element.59.refs_0_), channel_id=1, source_target_pairs={{0,16},{8,24},{16,0},{24,8},{1,17},{9,25},{17,1},{25,9},{2,18},{10... | collective-permute-start | bytes 49160 | tf_op jit(solution)/shard_map/ppermute | solution.py:97

commit v10 on v9

--- a/solution.py
+++ b/solution.py
@@ -184,11 +184,17 @@
 
     def corners(out, low):
         tile, first = (slice(0, 8), 0) if low else (slice(width - 8, width), 5)
-        empty = jnp.zeros((3, 1, out.shape[2]), F32)
+        one, two, three = (0, 1, 2) if low else (2, 1, 0)
+        empty = jnp.zeros((1, out.shape[2]), F32)
         for f, row in enumerate((0, 6, 3)):
             side_a, side_b = (turned(ref[row : row + 3, tile, :])[first : first + 3] for ref in (a, b))
             below, above = jnp.where(z_odd, side_a, side_b), jnp.where(z_odd, side_b, side_a)
-            out[3 * f : 3 * f + 3] = jnp.concatenate([empty, below, above, empty], axis=1)
+            out[2 * f] = jnp.concatenate([empty, below[one], above[one], empty], axis=0)
+            out[2 * f + 1] = jnp.concatenate(
+                [empty, below[three, 2:3], below[two, 1:3], above[two, 0:2], above[three, 0:1], empty], axis=0
+            )
+
+    for_other[6:] = jnp.zeros((2, 8, for_other.shape[2]), F32)
 
     @pl.when(y_odd == 0)
     def _():
@@ -203,7 +209,7 @@
 
 def rim(a, b, after):
     band = a.shape[2]
-    return call(rim_kernel, "rim", [near(9, 8, band), near(9, 8, band)], [b, a, after], cycles=200)
+    return call(rim_kernel, "rim", [near(6, 8, band), near(8, 8, band)], [b, a, after], cycles=200)
 
 
 def reciprocal(x):
@@ -447,11 +453,16 @@
         flux_y[...] = turned(jnp.concatenate(faces, axis=0))
 
         def corners(ref, low, keep):
-            start = width + (5 if low else 0)
+            one, two, three = (width + 7, width + 6, width + 5) if low else (width, width + 1, width + 2)
+            top = 4 + depth
             for f, field in enumerate((c, ys, zs)):
-                for k in range(3):
-                    field[1:4, start + k, :] = ref[3 * f + k, 1:4, :] * (keep * keep_below)
-                    field[depth + 4 : depth + 7, start + k, :] = ref[3 * f + k, 4:7, :] * (keep * keep_above)
+                near_tile, far_tile = ref.at[2 * f], ref.at[2 * f + 1]
+                field[1:4, one, :] = near_tile[1:4] * (keep * keep_below)
+                field[top : top + 3, one, :] = near_tile[4:7] * (keep * keep_above)
+                field[2:4, two, :] = far_tile[2:4] * (keep * keep_below)
+                field[top : top + 2, two, :] = far_tile[4:6] * (keep * keep_above)
+                field[3:4, three, :] = far_tile[1:2] * (keep * keep_below)
+                field[top : top + 1, three, :] = far_tile[6:7] * (keep * keep_above)
 
         corners(corner, o_low, keep_o)
         corners(ab, not o_low, 1.0)

time: 34.9 us -> 35 us (level)
  waiting for transfers between devices: 7.23 us -> 7.65 us
  starting transfers between devices: 21.2 us -> 20.8 us
    ppermute x12, waiting for transfers between devices: 5.42 us -> 7.13 us  [swap(): lax.ppermute(x, axis, [(i, i ^ step) for i in range(lax.axis_size(axis))])]
    ppermute x4, waiting for transfers between devices: 1.8 us -> 0.52 us  [send(): return lax.ppermute(x, AXES, permutation(z_partner, y_partner))]
    ppermute x12, starting transfers between devices: 12.8 us -> 12.4 us  [swap(): lax.ppermute(x, axis, [(i, i ^ step) for i in range(lax.axis_size(axis))])]
  transfers between devices with their start and end apart: 16 -> 16, of which waited for: 5 -> 6; matrix products, arithmetic and copies ran while one was open for 0% -> 0% of each run, Pallas kernels for 11% -> 11%
where the time goes in v10:
time: 35 us; the launch traced here: 34.8 us
  starting transfers between devices  20.8 us (59%)
  waiting for transfers between devices  7.65 us (22%)
  Pallas kernels  6.19 us (18%)
    ppermute x12, starting transfers between devices, swap(): lax.ppermute(x, axis, [(i, i ^ step) for i in range(lax.axis_size(axis))])  12.4 us
    ppermute x4, starting transfers between devices, send(): return lax.ppermute(x, AXES, permutation(z_partner, y_partner))  8.38 us
    ppermute x12, waiting for transfers between devices, swap(): lax.ppermute(x, axis, [(i, i ^ step) for i in range(lax.axis_size(axis))])  7.13 us
    pallas_call x13, Pallas kernels, call(): pl.pallas_call(kernel, out_shape=[out[1] if isinstance(out, tuple) else o...  6.19 us
  transfers between devices with their start and end apart: 16, of which 6 were waited for; matrix products, arithmetic and copies ran while one was open for 0% of the time, Pallas kernels for 11%

profile of v10, /device:TPU:0, one launch (start us, length us, event | category | flops | bytes accessed | tf_op | source)
XLA Modules:
  0.0 34.8 jit_solution(12662521612429008697)
XLA Ops:
  0.0 0.0 copy-start.2
  0.0 0.0 copy-start.1
  0.0 0.0 copy-start
  0.0 1.2 %z_rims.1 = (f32[10,32,128]{2,1,0:T(8,128)S(1)}, f32[10,32,128]{2,1,0:T(8,128)S(1)}) custom-call(f32[32,32,128]{2,1,0:T(8,128)} %tracer.3, f32[32,32,128]{2,1,0:T(8,128)} %y_speed.3, f32[32,32,128]{2,1,0:T(8,128)} %z_speed.3), custom_call_target="tpu_custom_call" | custom-call | bytes 1024000 | tf_op jit(solution)/shard_map/z_rims/pallas_call | solution.py:33
  1.2 3.1 %collective-permute-start.1 = (f32[10,32,128]{2,1,0:T(8,128)S(1)}, f32[10,32,128]{2,1,0:T(8,128)S(1)}, u32[]{:S(2)}, u32[]{:S(2)}) collective-permute-start(f32[10,32,128]{2,1,0:T(8,128)S(1)} %get-tuple-element.36), channel_id=1, source_target_pairs={{0,8},{1,9},{2,10},{3,11},{4,12},{5,13},{6,14},{7,15},{8,0},{9,1},... | collective-permute-start | bytes 491528 | tf_op jit(solution)/shard_map/ppermute | solution.py:90
  4.3 0.0 copy-start.3
  4.3 0.0 collective-permute-start
  4.3 0.0 copy-done.2
  4.3 0.0 copy-done.1
  4.3 0.0 copy-done
  4.3 0.1 begin.1
  4.5 2.6 %collective-permute-start.2 = (f32[10,32,128]{2,1,0:T(8,128)S(1)}, f32[10,32,128]{2,1,0:T(8,128)S(1)}, u32[]{:S(2)}, u32[]{:S(2)}) collective-permute-start(f32[10,32,128]{2,1,0:T(8,128)S(1)} %get-tuple-element.37), channel_id=1, source_target_pairs={{0,7},{1,2},{2,1},{3,4},{4,3},{5,6},{6,5},{7,0},{8,15},{9,10},{10,... | collective-permute-start | bytes 491528 | tf_op jit(solution)/shard_map/ppermute | solution.py:90
  7.1 0.0 collective-permute-start.3
  7.1 0.0 copy-done.3
  7.1 1.1 %factor.1 = (f32[32,32,128]{2,1,0:T(8,128)}, f32[32,32,128]{2,1,0:T(8,128)}, f32[5,32,128]{2,1,0:T(8,128)S(1)}, f32[5,32,128]{2,1,0:T(8,128)S(1)}) custom-call(f32[32,32,128]{2,1,0:T(8,128)S(1)} %copy-done.3), custom_call_target="tpu_custom_call" | custom-call | bytes 4096000 | tf_op jit(solution)/shard_map/factor/pallas_call | solution.py:33
  8.2 0.6 %collective-permute-start.7 = (f32[5,32,128]{2,1,0:T(8,128)S(1)}, f32[5,32,128]{2,1,0:T(8,128)S(1)}, u32[]{:S(2)}, u32[]{:S(2)}) collective-permute-start(f32[5,32,128]{2,1,0:T(8,128)S(1)} %get-tuple-element.42.ports_y.refs_0_.refs_8_), channel_id=1, source_target_pairs={{0,1},{1,0},{2,3},{3,2},{4,5},{5,4},{6,7},{7,6},{8,9},{9,8},{10,11... | collective-permute-start | bytes 245768 | tf_op jit(solution)/shard_map/ppermute | solution.py:97
  8.8 0.0 collective-permute-done.1.a
  8.8 0.0 collective-permute-done.b
  8.8 2.7 %collective-permute-start.4 = (f32[8,8,128]{2,1,0:T(8,128)S(1)}, f32[8,8,128]{2,1,0:T(8,128)S(1)}, u32[]{:S(2)}, u32[]{:S(2)}) collective-permute-start(f32[8,8,128]{2,1,0:T(8,128)S(1)} %get-tuple-element.40), channel_id=1, source_target_pairs={{0,8},{1,2},{2,1},{3,4},{4,3},{5,6},{6,5},{7,15},{8,0},{9,10},{10,... | collective-permute-start | bytes 98312 | tf_op jit(solution)/shard_map/ppermute | solution.py:90
  11.5 0.0 collective-permute-done.7.refs_1_
  11.5 0.1 collective-permute-start.9
  11.6 0.1 collective-permute-start.5
  11.7 0.0 collective-permute-done.2.o
  11.7 0.0 collective-permute-done.3.e
  11.7 1.2 %collective-permute-done.5.ab = f32[6,8,128]{2,1,0:T(8,128)S(1)} collective-permute-done((f32[6,8,128]{2,1,0:T(8,128)S(1)}, f32[6,8,128]{2,1,0:T(8,128)S(1)}, u32[]{:S(2)}, u32[]{:S(2)}) %collective-permute-start.5) | collective-permute-done | bytes 24608 | tf_op jit(solution)/shard_map/ppermute | solution.py:97
  12.9 0.5 %collective-permute-done.4.corner = f32[8,8,128]{2,1,0:T(8,128)S(1)} collective-permute-done((f32[8,8,128]{2,1,0:T(8,128)S(1)}, f32[8,8,128]{2,1,0:T(8,128)S(1)}, u32[]{:S(2)}, u32[]{:S(2)}) %collective-permute-start.4) | collective-permute-done | bytes 32800 | tf_op jit(solution)/shard_map/ppermute | solution.py:90
  13.4 2.2 %advect.1 = (f32[32,32,128]{2,1,0:T(8,128)S(1)}, f32[2,32,128]{2,1,0:T(8,128)S(1)}, f32[32,32,128]{2,1,0:T(8,128)S(1)}, f32[32,32,128]{2,1,0:T(8,128)S(1)}) custom-call(f32[32,32,128]{2,1,0:T(8,128)S(1)} %copy-done, f32[32,32,128]{2,1,0:T(8,128)S(1)} %copy-done.1, f32[32,32,128]{2,1,0:T(8,128)S(1)} %copy-done.2, f32[10,32,128]{2,1,0:T(8,128)S(1)} %collective-permute-done.b, ...), custom_call_target="tpu_custom_call" | custom-call | bytes 5120000 | tf_op jit(solution)/shard_map/advect/pallas_call | solution.py:33
  15.6 0.1 collective-permute-start.6
  15.7 2.3 %collective-permute-start.12 = (f32[5,32,128]{2,1,0:T(8,128)S(1)}, f32[5,32,128]{2,1,0:T(8,128)S(1)}, u32[]{:S(2)}, u32[]{:S(2)}) collective-permute-start(f32[5,32,128]{2,1,0:T(8,128)S(1)} %get-tuple-element.39._.refs_0_.refs_11_.refs_6_), channel_id=1, source_target_pairs={{0,8},{8,0},{16,24},{24,16},{1,9},{9,1},{17,25},{25,17},{2,10},{10... | collective-permute-start | bytes 245768 | tf_op jit(solution)/shard_map/ppermute | solution.py:97
  18.0 0.0 collective-permute-done.6.refs_1_
  18.0 0.7 %collective-permute-start.8 = (f32[2,32,128]{2,1,0:T(8,128)S(1)}, f32[2,32,128]{2,1,0:T(8,128)S(1)}, u32[]{:S(2)}, u32[]{:S(2)}) collective-permute-start(f32[2,32,128]{2,1,0:T(8,128)S(1)} %get-tuple-element.47.refs_0_), channel_id=1, source_target_pairs={{0,3},{1,2},{2,1},{3,0},{4,7},{5,6},{6,5},{7,4},{8,11},{9,10},{10,... | collective-permute-start | bytes 98312 | tf_op jit(solution)/shard_map/ppermute | solution.py:97
  18.7 0.0 collective-permute-done.9.refs_1_
  18.7 1.8 %collective-permute-start.11 = (f32[2,32,128]{2,1,0:T(8,128)S(1)}, f32[2,32,128]{2,1,0:T(8,128)S(1)}, u32[]{:S(2)}, u32[]{:S(2)}) collective-permute-start(f32[2,32,128]{2,1,0:T(8,128)S(1)} %get-tuple-element.51.refs_2_), channel_id=1, source_target_pairs={{0,5},{1,4},{2,7},{3,6},{4,1},{5,0},{6,3},{7,2},{8,13},{9,12},{10,... | collective-permute-start | bytes 98312 | tf_op jit(solution)/shard_map/ppermute | solution.py:97
  20.5 1.0 %collective-permute-done.8.refs_1_ = f32[2,32,128]{2,1,0:T(8,128)S(1)} collective-permute-done((f32[2,32,128]{2,1,0:T(8,128)S(1)}, f32[2,32,128]{2,1,0:T(8,128)S(1)}, u32[]{:S(2)}, u32[]{:S(2)}) %collective-permute-start.8) | collective-permute-done | bytes 32800 | tf_op jit(solution)/shard_map/ppermute | solution.py:97
  21.5 1.4 %collective-permute-start.10 = (f32[1,32,128]{2,1,0:T(8,128)S(1)}, f32[1,32,128]{2,1,0:T(8,128)S(1)}, u32[]{:S(2)}, u32[]{:S(2)}) collective-permute-start(f32[1,32,128]{2,1,0:T(8,128)S(1)} %get-tuple-element.50.refs_0_), channel_id=1, source_target_pairs={{0,5},{1,4},{2,7},{3,6},{4,1},{5,0},{6,3},{7,2},{8,13},{9,12},{10,... | collective-permute-start | bytes 49160 | tf_op jit(solution)/shard_map/ppermute | solution.py:97
  22.9 0.0 collective-permute-done.12.refs_1_
  23.0 0.0 collective-permute-done.11.refs_3_
  23.0 1.8 %collective-permute-done.10.refs_1_ = f32[1,32,128]{2,1,0:T(8,128)S(1)} collective-permute-done((f32[1,32,128]{2,1,0:T(8,128)S(1)}, f32[1,32,128]{2,1,0:T(8,128)S(1)}, u32[]{:S(2)}, u32[]{:S(2)}) %collective-permute-start.10) | collective-permute-done | bytes 16416 | tf_op jit(solution)/shard_map/ppermute | solution.py:97
  24.8 0.5 %turn.1 = (f32[32,32,128]{2,1,0:T(8,128)S(1)}, f32[2,32,128]{2,1,0:T(8,128)S(1)}, f32[32,32,128]{2,1,0:T(8,128)S(1)}, f32[32,32,128]{2,1,0:T(8,128)S(1)}) custom-call(f32[1,32,128]{2,1,0:T(8,128)S(1)} %get-tuple-element.50.refs_0_, f32[1,32,128]{2,1,0:T(8,128)S(1)} %collective-permute-done.10.refs_1_, f32[2,32,128]{2,1,0:T(8,128)S(1)} %get-tuple-element.51.refs_2_, ...), custom_call_target="tpu_custom_call" | custom-call | bytes 1536000 | tf_op jit(solution)/shard_map/turn/pallas_call | solution.py:33
  25.3 1.0 %collective-permute-start.13 = (f32[2,32,128]{2,1,0:T(8,128)S(1)}, f32[2,32,128]{2,1,0:T(8,128)S(1)}, u32[]{:S(2)}, u32[]{:S(2)}) collective-permute-start(f32[2,32,128]{2,1,0:T(8,128)S(1)} %get-tuple-element.58.refs_0_), channel_id=1, source_target_pairs={{0,8},{8,0},{16,24},{24,16},{1,9},{9,1},{17,25},{25,17},{2,10},{10... | collective-permute-start | bytes 98312 | tf_op jit(solution)/shard_map/ppermute | solution.py:97
  26.2 2.3 %collective-permute-start.15 = (f32[2,32,128]{2,1,0:T(8,128)S(1)}, f32[2,32,128]{2,1,0:T(8,128)S(1)}, u32[]{:S(2)}, u32[]{:S(2)}) collective-permute-start(f32[2,32,128]{2,1,0:T(8,128)S(1)} %get-tuple-element.60.refs_2_), channel_id=1, source_target_pairs={{0,16},{8,24},{16,0},{24,8},{1,17},{9,25},{17,1},{25,9},{2,18},{10... | collective-permute-start | bytes 98312 | tf_op jit(solution)/shard_map/ppermute | solution.py:97
  28.5 0.7 %collective-permute-done.13.refs_1_ = f32[2,32,128]{2,1,0:T(8,128)S(1)} collective-permute-done((f32[2,32,128]{2,1,0:T(8,128)S(1)}, f32[2,32,128]{2,1,0:T(8,128)S(1)}, u32[]{:S(2)}, u32[]{:S(2)}) %collective-permute-start.13) | collective-permute-done | bytes 32800 | tf_op jit(solution)/shard_map/ppermute | solution.py:97
  29.3 2.2 %collective-permute-start.14 = (f32[1,32,128]{2,1,0:T(8,128)S(1)}, f32[1,32,128]{2,1,0:T(8,128)S(1)}, u32[]{:S(2)}, u32[]{:S(2)}) collective-permute-start(f32[1,32,128]{2,1,0:T(8,128)S(1)} %get-tuple-element.59.refs_0_), channel_id=1, source_target_pairs={{0,16},{8,24},{16,0},{24,8},{1,17},{9,25},{17,1},{25,9},{2,18},{10... | collective-permute-start | bytes 49160 | tf_op jit(solution)/shard_map/ppermute | solution.py:97
  31.5 0.0 collective-permute-done.15.refs_3_
  31.5 2.5 %collective-permute-done.14.refs_1_ = f32[1,32,128]{2,1,0:T(8,128)S(1)} collective-permute-done((f32[1,32,128]{2,1,0:T(8,128)S(1)}, f32[1,32,128]{2,1,0:T(8,128)S(1)}, u32[]{:S(2)}, u32[]{:S(2)}) %collective-permute-start.14) | collective-permute-done | bytes 16416 | tf_op jit(solution)/shard_map/ppermute | solution.py:97
  34.0 0.9 %finish.1 = f32[32,32,128]{2,1,0:T(8,128)} custom-call(f32[1,32,128]{2,1,0:T(8,128)S(1)} %get-tuple-element.59.refs_0_, f32[1,32,128]{2,1,0:T(8,128)S(1)} %collective-permute-done.14.refs_1_, f32[2,32,128]{2,1,0:T(8,128)S(1)} %get-tuple-element.60.refs_2_, f32[2,32,128]{2,1,0:T(8,128)S(1)} %collective-permute-done.15.refs_3_, ...), custom_call_target="tpu_custom_call" | custom-call | bytes 1024000 | tf_op jit(solution)/shard_map/finish/pallas_call | solution.py:33
  (7 shorter events, 0.2 us)
Async XLA Ops:
  0.0 4.3 %copy-start.2 = (f32[32,32,128]{2,1,0:T(8,128)S(1)}, f32[32,32,128]{2,1,0:T(8,128)}, u32[]{:S(2)}) copy-start(f32[32,32,128]{2,1,0:T(8,128)} %z_speed.3) | copy-start | bytes 1572868
  0.0 4.3 %copy-start.1 = (f32[32,32,128]{2,1,0:T(8,128)S(1)}, f32[32,32,128]{2,1,0:T(8,128)}, u32[]{:S(2)}) copy-start(f32[32,32,128]{2,1,0:T(8,128)} %y_speed.3) | copy-start | bytes 1572868
  0.0 4.3 %copy-start = (f32[32,32,128]{2,1,0:T(8,128)S(1)}, f32[32,32,128]{2,1,0:T(8,128)}, u32[]{:S(2)}) copy-start(f32[32,32,128]{2,1,0:T(8,128)} %tracer.3) | copy-start | bytes 1572868
  1.2 7.6 %collective-permute-start.1 = (f32[10,32,128]{2,1,0:T(8,128)S(1)}, f32[10,32,128]{2,1,0:T(8,128)S(1)}, u32[]{:S(2)}, u32[]{:S(2)}) collective-permute-start(f32[10,32,128]{2,1,0:T(8,128)S(1)} %get-tuple-element.36), channel_id=1, source_target_pairs={{0,8},{1,9},{2,10},{3,11},{4,12},{5,13},{6,14},{7,15},{8,0},{9,1},... | collective-permute-start | bytes 491528 | tf_op jit(solution)/shard_map/ppermute | solution.py:90
  4.3 2.8 %copy-start.3 = (f32[32,32,128]{2,1,0:T(8,128)S(1)}, f32[32,32,128]{2,1,0:T(8,128)}, u32[]{:S(2)}) copy-start(f32[32,32,128]{2,1,0:T(8,128)} %kappa.1) | copy-start | bytes 1572868
  4.3 4.5 %collective-permute-start = (f32[10,32,128]{2,1,0:T(8,128)S(1)}, f32[10,32,128]{2,1,0:T(8,128)S(1)}, u32[]{:S(2)}, u32[]{:S(2)}) collective-permute-start(f32[10,32,128]{2,1,0:T(8,128)S(1)} %get-tuple-element.35._), channel_id=1, source_target_pairs={{0,1},{1,0},{2,3},{3,2},{4,5},{5,4},{6,7},{7,6},{8,16},{9,17},{10,... | collective-permute-start | bytes 491528 | tf_op jit(solution)/shard_map/ppermute | solution.py:90
  4.5 7.2 %collective-permute-start.2 = (f32[10,32,128]{2,1,0:T(8,128)S(1)}, f32[10,32,128]{2,1,0:T(8,128)S(1)}, u32[]{:S(2)}, u32[]{:S(2)}) collective-permute-start(f32[10,32,128]{2,1,0:T(8,128)S(1)} %get-tuple-element.37), channel_id=1, source_target_pairs={{0,7},{1,2},{2,1},{3,4},{4,3},{5,6},{6,5},{7,0},{8,15},{9,10},{10,... | collective-permute-start | bytes 491528 | tf_op jit(solution)/shard_map/ppermute | solution.py:90
  7.1 4.6 %collective-permute-start.3 = (f32[10,32,128]{2,1,0:T(8,128)S(1)}, f32[10,32,128]{2,1,0:T(8,128)S(1)}, u32[]{:S(2)}, u32[]{:S(2)}) collective-permute-start(f32[10,32,128]{2,1,0:T(8,128)S(1)} %get-tuple-element.38), channel_id=1, source_target_pairs={{0,1},{1,0},{2,3},{3,2},{4,5},{5,4},{6,7},{7,6},{8,9},{9,8},{10,11... | collective-permute-start | bytes 491528 | tf_op jit(solution)/shard_map/ppermute | solution.py:97
  8.2 3.3 %collective-permute-start.7 = (f32[5,32,128]{2,1,0:T(8,128)S(1)}, f32[5,32,128]{2,1,0:T(8,128)S(1)}, u32[]{:S(2)}, u32[]{:S(2)}) collective-permute-start(f32[5,32,128]{2,1,0:T(8,128)S(1)} %get-tuple-element.42.ports_y.refs_0_.refs_8_), channel_id=1, source_target_pairs={{0,1},{1,0},{2,3},{3,2},{4,5},{5,4},{6,7},{7,6},{8,9},{9,8},{10,11... | collective-permute-start | bytes 245768 | tf_op jit(solution)/shard_map/ppermute | solution.py:97
  8.8 4.6 %collective-permute-start.4 = (f32[8,8,128]{2,1,0:T(8,128)S(1)}, f32[8,8,128]{2,1,0:T(8,128)S(1)}, u32[]{:S(2)}, u32[]{:S(2)}) collective-permute-start(f32[8,8,128]{2,1,0:T(8,128)S(1)} %get-tuple-element.40), channel_id=1, source_target_pairs={{0,8},{1,2},{2,1},{3,4},{4,3},{5,6},{6,5},{7,15},{8,0},{9,10},{10,... | collective-permute-start | bytes 98312 | tf_op jit(solution)/shard_map/ppermute | solution.py:90
  11.5 7.2 %collective-permute-start.9 = (f32[5,32,128]{2,1,0:T(8,128)S(1)}, f32[5,32,128]{2,1,0:T(8,128)S(1)}, u32[]{:S(2)}, u32[]{:S(2)}) collective-permute-start(f32[5,32,128]{2,1,0:T(8,128)S(1)} %get-tuple-element.48.refs_0_), channel_id=1, source_target_pairs={{0,3},{1,2},{2,1},{3,0},{4,7},{5,6},{6,5},{7,4},{8,11},{9,10},{10,... | collective-permute-start | bytes 245768 | tf_op jit(solution)/shard_map/ppermute | solution.py:97
  11.6 1.3 %collective-permute-start.5 = (f32[6,8,128]{2,1,0:T(8,128)S(1)}, f32[6,8,128]{2,1,0:T(8,128)S(1)}, u32[]{:S(2)}, u32[]{:S(2)}) collective-permute-start(f32[6,8,128]{2,1,0:T(8,128)S(1)} %get-tuple-element.41), channel_id=1, source_target_pairs={{0,1},{1,0},{2,3},{3,2},{4,5},{5,4},{6,7},{7,6},{8,9},{9,8},{10,11... | collective-permute-start | bytes 73736 | tf_op jit(solution)/shard_map/ppermute | solution.py:97
  15.6 2.4 %collective-permute-start.6 = (f32[2,32,128]{2,1,0:T(8,128)S(1)}, f32[2,32,128]{2,1,0:T(8,128)S(1)}, u32[]{:S(2)}, u32[]{:S(2)}) collective-permute-start(f32[2,32,128]{2,1,0:T(8,128)S(1)} %get-tuple-element.45.refs_0_), channel_id=1, source_target_pairs={{0,1},{1,0},{2,3},{3,2},{4,5},{5,4},{6,7},{7,6},{8,9},{9,8},{10,11... | collective-permute-start | bytes 98312 | tf_op jit(solution)/shard_map/ppermute | solution.py:97
  15.7 7.2 %collective-permute-start.12 = (f32[5,32,128]{2,1,0:T(8,128)S(1)}, f32[5,32,128]{2,1,0:T(8,128)S(1)}, u32[]{:S(2)}, u32[]{:S(2)}) collective-permute-start(f32[5,32,128]{2,1,0:T(8,128)S(1)} %get-tuple-element.39._.refs_0_.refs_11_.refs_6_), channel_id=1, source_target_pairs={{0,8},{8,0},{16,24},{24,16},{1,9},{9,1},{17,25},{25,17},{2,10},{10... | collective-permute-start | bytes 245768 | tf_op jit(solution)/shard_map/ppermute | solution.py:97
  18.0 3.5 %collective-permute-start.8 = (f32[2,32,128]{2,1,0:T(8,128)S(1)}, f32[2,32,128]{2,1,0:T(8,128)S(1)}, u32[]{:S(2)}, u32[]{:S(2)}) collective-permute-start(f32[2,32,128]{2,1,0:T(8,128)S(1)} %get-tuple-element.47.refs_0_), channel_id=1, source_target_pairs={{0,3},{1,2},{2,1},{3,0},{4,7},{5,6},{6,5},{7,4},{8,11},{9,10},{10,... | collective-permute-start | bytes 98312 | tf_op jit(solution)/shard_map/ppermute | solution.py:97
  18.7 4.3 %collective-permute-start.11 = (f32[2,32,128]{2,1,0:T(8,128)S(1)}, f32[2,32,128]{2,1,0:T(8,128)S(1)}, u32[]{:S(2)}, u32[]{:S(2)}) collective-permute-start(f32[2,32,128]{2,1,0:T(8,128)S(1)} %get-tuple-element.51.refs_2_), channel_id=1, source_target_pairs={{0,5},{1,4},{2,7},{3,6},{4,1},{5,0},{6,3},{7,2},{8,13},{9,12},{10,... | collective-permute-start | bytes 98312 | tf_op jit(solution)/shard_map/ppermute | solution.py:97
  21.5 3.2 %collective-permute-start.10 = (f32[1,32,128]{2,1,0:T(8,128)S(1)}, f32[1,32,128]{2,1,0:T(8,128)S(1)}, u32[]{:S(2)}, u32[]{:S(2)}) collective-permute-start(f32[1,32,128]{2,1,0:T(8,128)S(1)} %get-tuple-element.50.refs_0_), channel_id=1, source_target_pairs={{0,5},{1,4},{2,7},{3,6},{4,1},{5,0},{6,3},{7,2},{8,13},{9,12},{10,... | collective-permute-start | bytes 49160 | tf_op jit(solution)/shard_map/ppermute | solution.py:97
  25.3 4.0 %collective-permute-start.13 = (f32[2,32,128]{2,1,0:T(8,128)S(1)}, f32[2,32,128]{2,1,0:T(8,128)S(1)}, u32[]{:S(2)}, u32[]{:S(2)}) collective-permute-start(f32[2,32,128]{2,1,0:T(8,128)S(1)} %get-tuple-element.58.refs_0_), channel_id=1, source_target_pairs={{0,8},{8,0},{16,24},{24,16},{1,9},{9,1},{17,25},{25,17},{2,10},{10... | collective-permute-start | bytes 98312 | tf_op jit(solution)/shard_map/ppermute | solution.py:97
  26.2 5.3 %collective-permute-start.15 = (f32[2,32,128]{2,1,0:T(8,128)S(1)}, f32[2,32,128]{2,1,0:T(8,128)S(1)}, u32[]{:S(2)}, u32[]{:S(2)}) collective-permute-start(f32[2,32,128]{2,1,0:T(8,128)S(1)} %get-tuple-element.60.refs_2_), channel_id=1, source_target_pairs={{0,16},{8,24},{16,0},{24,8},{1,17},{9,25},{17,1},{25,9},{2,18},{10... | collective-permute-start | bytes 98312 | tf_op jit(solution)/shard_map/ppermute | solution.py:97
  29.3 4.7 %collective-permute-start.14 = (f32[1,32,128]{2,1,0:T(8,128)S(1)}, f32[1,32,128]{2,1,0:T(8,128)S(1)}, u32[]{:S(2)}, u32[]{:S(2)}) collective-permute-start(f32[1,32,128]{2,1,0:T(8,128)S(1)} %get-tuple-element.59.refs_0_), channel_id=1, source_target_pairs={{0,16},{8,24},{16,0},{24,8},{1,17},{9,25},{17,1},{25,9},{2,18},{10... | collective-permute-start | bytes 49160 | tf_op jit(solution)/shard_map/ppermute | solution.py:97

commit v11 on v10

--- a/solution.py
+++ b/solution.py
@@ -177,7 +177,7 @@
     )
 
 
-def rim_kernel(b, a, _, for_pair, for_other):
+def rim_kernel(b, a, for_pair, for_other):
     z, y, _, _ = place()
     width = a.shape[1]
     z_odd, y_odd = lax.rem(z, 2) == 1, lax.rem(y, 2)
@@ -207,9 +207,9 @@
         corners(for_pair, True)
 
 
-def rim(a, b, after):
+def rim(a, b):
     band = a.shape[2]
-    return call(rim_kernel, "rim", [near(6, 8, band), near(8, 8, band)], [b, a, after], cycles=200)
+    return call(rim_kernel, "rim", [near(6, 8, band), near(8, 8, band)], [b, a], cycles=200)
 
 
 def reciprocal(x):
@@ -640,7 +640,7 @@
     e = swap(e, "gy", 0)
     o = send(o, y_partner=y_ring)
     r_y, r_z, ports_y, ports_z = factor_lines(kappa)
-    for_pair, for_other = rim(a, b, ports_z)
+    for_pair, for_other = rim(a, b)
     corner = send(for_other, y_partner=y_other)
     ab = swap(for_pair, "gy", 0)
     joints_y, edge_y, edge_y_theirs = join_all(ports_y, "gy")

time: 35 us -> 35 us (level)
  no operation moved by 1% of the time
where the time goes in v11:
time: 35 us; the launch traced here: 34.8 us
  starting transfers between devices  20.8 us (59%)
  waiting for transfers between devices  7.65 us (22%)
  Pallas kernels  6.19 us (18%)
    ppermute x12, starting transfers between devices, swap(): lax.ppermute(x, axis, [(i, i ^ step) for i in range(lax.axis_size(axis))])  12.4 us
    ppermute x4, starting transfers between devices, send(): return lax.ppermute(x, AXES, permutation(z_partner, y_partner))  8.38 us
    ppermute x12, waiting for transfers between devices, swap(): lax.ppermute(x, axis, [(i, i ^ step) for i in range(lax.axis_size(axis))])  7.13 us
    pallas_call x13, Pallas kernels, call(): pl.pallas_call(kernel, out_shape=[out[1] if isinstance(out, tuple) else o...  6.19 us
  transfers between devices with their start and end apart: 16, of which 6 were waited for; matrix products, arithmetic and copies ran while one was open for 0% of the time, Pallas kernels for 11%

profile of v11, /device:TPU:0, one launch (start us, length us, event | category | flops | bytes accessed | tf_op | source)
XLA Modules:
  0.0 34.8 jit_solution(2071919235578968159)
XLA Ops:
  0.0 0.0 copy-start.2
  0.0 0.0 copy-start.1
  0.0 0.0 copy-start
  0.0 1.2 %z_rims.1 = (f32[10,32,128]{2,1,0:T(8,128)S(1)}, f32[10,32,128]{2,1,0:T(8,128)S(1)}) custom-call(f32[32,32,128]{2,1,0:T(8,128)} %tracer.3, f32[32,32,128]{2,1,0:T(8,128)} %y_speed.3, f32[32,32,128]{2,1,0:T(8,128)} %z_speed.3), custom_call_target="tpu_custom_call" | custom-call | bytes 1024000 | tf_op jit(solution)/shard_map/z_rims/pallas_call | solution.py:33
  1.2 3.1 %collective-permute-start.1 = (f32[10,32,128]{2,1,0:T(8,128)S(1)}, f32[10,32,128]{2,1,0:T(8,128)S(1)}, u32[]{:S(2)}, u32[]{:S(2)}) collective-permute-start(f32[10,32,128]{2,1,0:T(8,128)S(1)} %get-tuple-element.36), channel_id=1, source_target_pairs={{0,8},{1,9},{2,10},{3,11},{4,12},{5,13},{6,14},{7,15},{8,0},{9,1},... | collective-permute-start | bytes 491528 | tf_op jit(solution)/shard_map/ppermute | solution.py:90
  4.3 0.0 copy-start.3
  4.3 0.0 collective-permute-start
  4.3 0.0 copy-done.2
  4.3 0.0 copy-done.1
  4.3 0.0 copy-done
  4.3 0.1 begin.1
  4.5 2.6 %collective-permute-start.2 = (f32[10,32,128]{2,1,0:T(8,128)S(1)}, f32[10,32,128]{2,1,0:T(8,128)S(1)}, u32[]{:S(2)}, u32[]{:S(2)}) collective-permute-start(f32[10,32,128]{2,1,0:T(8,128)S(1)} %get-tuple-element.37), channel_id=1, source_target_pairs={{0,7},{1,2},{2,1},{3,4},{4,3},{5,6},{6,5},{7,0},{8,15},{9,10},{10,... | collective-permute-start | bytes 491528 | tf_op jit(solution)/shard_map/ppermute | solution.py:90
  7.1 0.0 collective-permute-start.3
  7.1 0.0 copy-done.3
  7.1 1.1 %factor.1 = (f32[32,32,128]{2,1,0:T(8,128)}, f32[32,32,128]{2,1,0:T(8,128)}, f32[5,32,128]{2,1,0:T(8,128)S(1)}, f32[5,32,128]{2,1,0:T(8,128)S(1)}) custom-call(f32[32,32,128]{2,1,0:T(8,128)S(1)} %copy-done.3), custom_call_target="tpu_custom_call" | custom-call | bytes 4096000 | tf_op jit(solution)/shard_map/factor/pallas_call | solution.py:33
  8.2 0.6 %collective-permute-start.7 = (f32[5,32,128]{2,1,0:T(8,128)S(1)}, f32[5,32,128]{2,1,0:T(8,128)S(1)}, u32[]{:S(2)}, u32[]{:S(2)}) collective-permute-start(f32[5,32,128]{2,1,0:T(8,128)S(1)} %get-tuple-element.41.ports_y.refs_0_.refs_8_), channel_id=1, source_target_pairs={{0,1},{1,0},{2,3},{3,2},{4,5},{5,4},{6,7},{7,6},{8,9},{9,8},{10,11... | collective-permute-start | bytes 245768 | tf_op jit(solution)/shard_map/ppermute | solution.py:97
  8.8 0.0 collective-permute-done.1.a
  8.8 0.0 collective-permute-done.b
  8.8 2.7 %collective-permute-start.4 = (f32[8,8,128]{2,1,0:T(8,128)S(1)}, f32[8,8,128]{2,1,0:T(8,128)S(1)}, u32[]{:S(2)}, u32[]{:S(2)}) collective-permute-start(f32[8,8,128]{2,1,0:T(8,128)S(1)} %get-tuple-element.39), channel_id=1, source_target_pairs={{0,8},{1,2},{2,1},{3,4},{4,3},{5,6},{6,5},{7,15},{8,0},{9,10},{10,... | collective-permute-start | bytes 98312 | tf_op jit(solution)/shard_map/ppermute | solution.py:90
  11.5 0.0 collective-permute-done.7.refs_1_
  11.5 0.1 collective-permute-start.9
  11.6 0.1 collective-permute-start.5
  11.7 0.0 collective-permute-done.2.o
  11.7 0.0 collective-permute-done.3.e
  11.7 1.2 %collective-permute-done.5.ab = f32[6,8,128]{2,1,0:T(8,128)S(1)} collective-permute-done((f32[6,8,128]{2,1,0:T(8,128)S(1)}, f32[6,8,128]{2,1,0:T(8,128)S(1)}, u32[]{:S(2)}, u32[]{:S(2)}) %collective-permute-start.5) | collective-permute-done | bytes 24608 | tf_op jit(solution)/shard_map/ppermute | solution.py:97
  12.9 0.5 %collective-permute-done.4.corner = f32[8,8,128]{2,1,0:T(8,128)S(1)} collective-permute-done((f32[8,8,128]{2,1,0:T(8,128)S(1)}, f32[8,8,128]{2,1,0:T(8,128)S(1)}, u32[]{:S(2)}, u32[]{:S(2)}) %collective-permute-start.4) | collective-permute-done | bytes 32800 | tf_op jit(solution)/shard_map/ppermute | solution.py:90
  13.4 2.2 %advect.1 = (f32[32,32,128]{2,1,0:T(8,128)S(1)}, f32[2,32,128]{2,1,0:T(8,128)S(1)}, f32[32,32,128]{2,1,0:T(8,128)S(1)}, f32[32,32,128]{2,1,0:T(8,128)S(1)}) custom-call(f32[32,32,128]{2,1,0:T(8,128)S(1)} %copy-done, f32[32,32,128]{2,1,0:T(8,128)S(1)} %copy-done.1, f32[32,32,128]{2,1,0:T(8,128)S(1)} %copy-done.2, f32[10,32,128]{2,1,0:T(8,128)S(1)} %collective-permute-done.b, ...), custom_call_target="tpu_custom_call" | custom-call | bytes 5120000 | tf_op jit(solution)/shard_map/advect/pallas_call | solution.py:33
  15.6 0.1 collective-permute-start.6
  15.7 2.3 %collective-permute-start.12 = (f32[5,32,128]{2,1,0:T(8,128)S(1)}, f32[5,32,128]{2,1,0:T(8,128)S(1)}, u32[]{:S(2)}, u32[]{:S(2)}) collective-permute-start(f32[5,32,128]{2,1,0:T(8,128)S(1)} %get-tuple-element.55.refs_0_.refs_11_.refs_6_), channel_id=1, source_target_pairs={{0,8},{8,0},{16,24},{24,16},{1,9},{9,1},{17,25},{25,17},{2,10},{10... | collective-permute-start | bytes 245768 | tf_op jit(solution)/shard_map/ppermute | solution.py:97
  18.0 0.0 collective-permute-done.6.refs_1_
  18.0 0.7 %collective-permute-start.8 = (f32[2,32,128]{2,1,0:T(8,128)S(1)}, f32[2,32,128]{2,1,0:T(8,128)S(1)}, u32[]{:S(2)}, u32[]{:S(2)}) collective-permute-start(f32[2,32,128]{2,1,0:T(8,128)S(1)} %get-tuple-element.46.refs_0_), channel_id=1, source_target_pairs={{0,3},{1,2},{2,1},{3,0},{4,7},{5,6},{6,5},{7,4},{8,11},{9,10},{10,... | collective-permute-start | bytes 98312 | tf_op jit(solution)/shard_map/ppermute | solution.py:97
  18.7 0.0 collective-permute-done.9.refs_1_
  18.7 1.8 %collective-permute-start.11 = (f32[2,32,128]{2,1,0:T(8,128)S(1)}, f32[2,32,128]{2,1,0:T(8,128)S(1)}, u32[]{:S(2)}, u32[]{:S(2)}) collective-permute-start(f32[2,32,128]{2,1,0:T(8,128)S(1)} %get-tuple-element.50.refs_2_), channel_id=1, source_target_pairs={{0,5},{1,4},{2,7},{3,6},{4,1},{5,0},{6,3},{7,2},{8,13},{9,12},{10,... | collective-permute-start | bytes 98312 | tf_op jit(solution)/shard_map/ppermute | solution.py:97
  20.5 1.0 %collective-permute-done.8.refs_1_ = f32[2,32,128]{2,1,0:T(8,128)S(1)} collective-permute-done((f32[2,32,128]{2,1,0:T(8,128)S(1)}, f32[2,32,128]{2,1,0:T(8,128)S(1)}, u32[]{:S(2)}, u32[]{:S(2)}) %collective-permute-start.8) | collective-permute-done | bytes 32800 | tf_op jit(solution)/shard_map/ppermute | solution.py:97
  21.5 1.4 %collective-permute-start.10 = (f32[1,32,128]{2,1,0:T(8,128)S(1)}, f32[1,32,128]{2,1,0:T(8,128)S(1)}, u32[]{:S(2)}, u32[]{:S(2)}) collective-permute-start(f32[1,32,128]{2,1,0:T(8,128)S(1)} %get-tuple-element.49.refs_0_), channel_id=1, source_target_pairs={{0,5},{1,4},{2,7},{3,6},{4,1},{5,0},{6,3},{7,2},{8,13},{9,12},{10,... | collective-permute-start | bytes 49160 | tf_op jit(solution)/shard_map/ppermute | solution.py:97
  22.9 0.0 collective-permute-done.12.refs_1_
  23.0 0.0 collective-permute-done.11.refs_3_
  23.0 1.8 %collective-permute-done.10.refs_1_ = f32[1,32,128]{2,1,0:T(8,128)S(1)} collective-permute-done((f32[1,32,128]{2,1,0:T(8,128)S(1)}, f32[1,32,128]{2,1,0:T(8,128)S(1)}, u32[]{:S(2)}, u32[]{:S(2)}) %collective-permute-start.10) | collective-permute-done | bytes 16416 | tf_op jit(solution)/shard_map/ppermute | solution.py:97
  24.8 0.5 %turn.1 = (f32[32,32,128]{2,1,0:T(8,128)S(1)}, f32[2,32,128]{2,1,0:T(8,128)S(1)}, f32[32,32,128]{2,1,0:T(8,128)S(1)}, f32[32,32,128]{2,1,0:T(8,128)S(1)}) custom-call(f32[1,32,128]{2,1,0:T(8,128)S(1)} %get-tuple-element.49.refs_0_, f32[1,32,128]{2,1,0:T(8,128)S(1)} %collective-permute-done.10.refs_1_, f32[2,32,128]{2,1,0:T(8,128)S(1)} %get-tuple-element.50.refs_2_, ...), custom_call_target="tpu_custom_call" | custom-call | bytes 1536000 | tf_op jit(solution)/shard_map/turn/pallas_call | solution.py:33
  25.3 1.0 %collective-permute-start.13 = (f32[2,32,128]{2,1,0:T(8,128)S(1)}, f32[2,32,128]{2,1,0:T(8,128)S(1)}, u32[]{:S(2)}, u32[]{:S(2)}) collective-permute-start(f32[2,32,128]{2,1,0:T(8,128)S(1)} %get-tuple-element.58.refs_0_), channel_id=1, source_target_pairs={{0,8},{8,0},{16,24},{24,16},{1,9},{9,1},{17,25},{25,17},{2,10},{10... | collective-permute-start | bytes 98312 | tf_op jit(solution)/shard_map/ppermute | solution.py:97
  26.2 2.3 %collective-permute-start.15 = (f32[2,32,128]{2,1,0:T(8,128)S(1)}, f32[2,32,128]{2,1,0:T(8,128)S(1)}, u32[]{:S(2)}, u32[]{:S(2)}) collective-permute-start(f32[2,32,128]{2,1,0:T(8,128)S(1)} %get-tuple-element.60.refs_2_), channel_id=1, source_target_pairs={{0,16},{8,24},{16,0},{24,8},{1,17},{9,25},{17,1},{25,9},{2,18},{10... | collective-permute-start | bytes 98312 | tf_op jit(solution)/shard_map/ppermute | solution.py:97
  28.5 0.7 %collective-permute-done.13.refs_1_ = f32[2,32,128]{2,1,0:T(8,128)S(1)} collective-permute-done((f32[2,32,128]{2,1,0:T(8,128)S(1)}, f32[2,32,128]{2,1,0:T(8,128)S(1)}, u32[]{:S(2)}, u32[]{:S(2)}) %collective-permute-start.13) | collective-permute-done | bytes 32800 | tf_op jit(solution)/shard_map/ppermute | solution.py:97
  29.3 2.2 %collective-permute-start.14 = (f32[1,32,128]{2,1,0:T(8,128)S(1)}, f32[1,32,128]{2,1,0:T(8,128)S(1)}, u32[]{:S(2)}, u32[]{:S(2)}) collective-permute-start(f32[1,32,128]{2,1,0:T(8,128)S(1)} %get-tuple-element.59.refs_0_), channel_id=1, source_target_pairs={{0,16},{8,24},{16,0},{24,8},{1,17},{9,25},{17,1},{25,9},{2,18},{10... | collective-permute-start | bytes 49160 | tf_op jit(solution)/shard_map/ppermute | solution.py:97
  31.5 0.0 collective-permute-done.15.refs_3_
  31.5 2.5 %collective-permute-done.14.refs_1_ = f32[1,32,128]{2,1,0:T(8,128)S(1)} collective-permute-done((f32[1,32,128]{2,1,0:T(8,128)S(1)}, f32[1,32,128]{2,1,0:T(8,128)S(1)}, u32[]{:S(2)}, u32[]{:S(2)}) %collective-permute-start.14) | collective-permute-done | bytes 16416 | tf_op jit(solution)/shard_map/ppermute | solution.py:97
  34.0 0.9 %finish.1 = f32[32,32,128]{2,1,0:T(8,128)} custom-call(f32[1,32,128]{2,1,0:T(8,128)S(1)} %get-tuple-element.59.refs_0_, f32[1,32,128]{2,1,0:T(8,128)S(1)} %collective-permute-done.14.refs_1_, f32[2,32,128]{2,1,0:T(8,128)S(1)} %get-tuple-element.60.refs_2_, f32[2,32,128]{2,1,0:T(8,128)S(1)} %collective-permute-done.15.refs_3_, ...), custom_call_target="tpu_custom_call" | custom-call | bytes 1024000 | tf_op jit(solution)/shard_map/finish/pallas_call | solution.py:33
  (7 shorter events, 0.2 us)
Async XLA Ops:
  0.0 4.3 %copy-start.2 = (f32[32,32,128]{2,1,0:T(8,128)S(1)}, f32[32,32,128]{2,1,0:T(8,128)}, u32[]{:S(2)}) copy-start(f32[32,32,128]{2,1,0:T(8,128)} %z_speed.3) | copy-start | bytes 1572868
  0.0 4.3 %copy-start.1 = (f32[32,32,128]{2,1,0:T(8,128)S(1)}, f32[32,32,128]{2,1,0:T(8,128)}, u32[]{:S(2)}) copy-start(f32[32,32,128]{2,1,0:T(8,128)} %y_speed.3) | copy-start | bytes 1572868
  0.0 4.3 %copy-start = (f32[32,32,128]{2,1,0:T(8,128)S(1)}, f32[32,32,128]{2,1,0:T(8,128)}, u32[]{:S(2)}) copy-start(f32[32,32,128]{2,1,0:T(8,128)} %tracer.3) | copy-start | bytes 1572868
  1.2 7.6 %collective-permute-start.1 = (f32[10,32,128]{2,1,0:T(8,128)S(1)}, f32[10,32,128]{2,1,0:T(8,128)S(1)}, u32[]{:S(2)}, u32[]{:S(2)}) collective-permute-start(f32[10,32,128]{2,1,0:T(8,128)S(1)} %get-tuple-element.36), channel_id=1, source_target_pairs={{0,8},{1,9},{2,10},{3,11},{4,12},{5,13},{6,14},{7,15},{8,0},{9,1},... | collective-permute-start | bytes 491528 | tf_op jit(solution)/shard_map/ppermute | solution.py:90
  4.3 2.8 %copy-start.3 = (f32[32,32,128]{2,1,0:T(8,128)S(1)}, f32[32,32,128]{2,1,0:T(8,128)}, u32[]{:S(2)}) copy-start(f32[32,32,128]{2,1,0:T(8,128)} %kappa.1) | copy-start | bytes 1572868
  4.3 4.5 %collective-permute-start = (f32[10,32,128]{2,1,0:T(8,128)S(1)}, f32[10,32,128]{2,1,0:T(8,128)S(1)}, u32[]{:S(2)}, u32[]{:S(2)}) collective-permute-start(f32[10,32,128]{2,1,0:T(8,128)S(1)} %get-tuple-element.35._), channel_id=1, source_target_pairs={{0,1},{1,0},{2,3},{3,2},{4,5},{5,4},{6,7},{7,6},{8,16},{9,17},{10,... | collective-permute-start | bytes 491528 | tf_op jit(solution)/shard_map/ppermute | solution.py:90
  4.5 7.2 %collective-permute-start.2 = (f32[10,32,128]{2,1,0:T(8,128)S(1)}, f32[10,32,128]{2,1,0:T(8,128)S(1)}, u32[]{:S(2)}, u32[]{:S(2)}) collective-permute-start(f32[10,32,128]{2,1,0:T(8,128)S(1)} %get-tuple-element.37), channel_id=1, source_target_pairs={{0,7},{1,2},{2,1},{3,4},{4,3},{5,6},{6,5},{7,0},{8,15},{9,10},{10,... | collective-permute-start | bytes 491528 | tf_op jit(solution)/shard_map/ppermute | solution.py:90
  7.1 4.6 %collective-permute-start.3 = (f32[10,32,128]{2,1,0:T(8,128)S(1)}, f32[10,32,128]{2,1,0:T(8,128)S(1)}, u32[]{:S(2)}, u32[]{:S(2)}) collective-permute-start(f32[10,32,128]{2,1,0:T(8,128)S(1)} %get-tuple-element.38), channel_id=1, source_target_pairs={{0,1},{1,0},{2,3},{3,2},{4,5},{5,4},{6,7},{7,6},{8,9},{9,8},{10,11... | collective-permute-start | bytes 491528 | tf_op jit(solution)/shard_map/ppermute | solution.py:97
  8.2 3.3 %collective-permute-start.7 = (f32[5,32,128]{2,1,0:T(8,128)S(1)}, f32[5,32,128]{2,1,0:T(8,128)S(1)}, u32[]{:S(2)}, u32[]{:S(2)}) collective-permute-start(f32[5,32,128]{2,1,0:T(8,128)S(1)} %get-tuple-element.41.ports_y.refs_0_.refs_8_), channel_id=1, source_target_pairs={{0,1},{1,0},{2,3},{3,2},{4,5},{5,4},{6,7},{7,6},{8,9},{9,8},{10,11... | collective-permute-start | bytes 245768 | tf_op jit(solution)/shard_map/ppermute | solution.py:97
  8.8 4.6 %collective-permute-start.4 = (f32[8,8,128]{2,1,0:T(8,128)S(1)}, f32[8,8,128]{2,1,0:T(8,128)S(1)}, u32[]{:S(2)}, u32[]{:S(2)}) collective-permute-start(f32[8,8,128]{2,1,0:T(8,128)S(1)} %get-tuple-element.39), channel_id=1, source_target_pairs={{0,8},{1,2},{2,1},{3,4},{4,3},{5,6},{6,5},{7,15},{8,0},{9,10},{10,... | collective-permute-start | bytes 98312 | tf_op jit(solution)/shard_map/ppermute | solution.py:90
  11.5 7.2 %collective-permute-start.9 = (f32[5,32,128]{2,1,0:T(8,128)S(1)}, f32[5,32,128]{2,1,0:T(8,128)S(1)}, u32[]{:S(2)}, u32[]{:S(2)}) collective-permute-start(f32[5,32,128]{2,1,0:T(8,128)S(1)} %get-tuple-element.47.refs_0_), channel_id=1, source_target_pairs={{0,3},{1,2},{2,1},{3,0},{4,7},{5,6},{6,5},{7,4},{8,11},{9,10},{10,... | collective-permute-start | bytes 245768 | tf_op jit(solution)/shard_map/ppermute | solution.py:97
  11.6 1.3 %collective-permute-start.5 = (f32[6,8,128]{2,1,0:T(8,128)S(1)}, f32[6,8,128]{2,1,0:T(8,128)S(1)}, u32[]{:S(2)}, u32[]{:S(2)}) collective-permute-start(f32[6,8,128]{2,1,0:T(8,128)S(1)} %get-tuple-element.40), channel_id=1, source_target_pairs={{0,1},{1,0},{2,3},{3,2},{4,5},{5,4},{6,7},{7,6},{8,9},{9,8},{10,11... | collective-permute-start | bytes 73736 | tf_op jit(solution)/shard_map/ppermute | solution.py:97
  15.6 2.4 %collective-permute-start.6 = (f32[2,32,128]{2,1,0:T(8,128)S(1)}, f32[2,32,128]{2,1,0:T(8,128)S(1)}, u32[]{:S(2)}, u32[]{:S(2)}) collective-permute-start(f32[2,32,128]{2,1,0:T(8,128)S(1)} %get-tuple-element.44.refs_0_), channel_id=1, source_target_pairs={{0,1},{1,0},{2,3},{3,2},{4,5},{5,4},{6,7},{7,6},{8,9},{9,8},{10,11... | collective-permute-start | bytes 98312 | tf_op jit(solution)/shard_map/ppermute | solution.py:97
  15.7 7.2 %collective-permute-start.12 = (f32[5,32,128]{2,1,0:T(8,128)S(1)}, f32[5,32,128]{2,1,0:T(8,128)S(1)}, u32[]{:S(2)}, u32[]{:S(2)}) collective-permute-start(f32[5,32,128]{2,1,0:T(8,128)S(1)} %get-tuple-element.55.refs_0_.refs_11_.refs_6_), channel_id=1, source_target_pairs={{0,8},{8,0},{16,24},{24,16},{1,9},{9,1},{17,25},{25,17},{2,10},{10... | collective-permute-start | bytes 245768 | tf_op jit(solution)/shard_map/ppermute | solution.py:97
  18.0 3.5 %collective-permute-start.8 = (f32[2,32,128]{2,1,0:T(8,128)S(1)}, f32[2,32,128]{2,1,0:T(8,128)S(1)}, u32[]{:S(2)}, u32[]{:S(2)}) collective-permute-start(f32[2,32,128]{2,1,0:T(8,128)S(1)} %get-tuple-element.46.refs_0_), channel_id=1, source_target_pairs={{0,3},{1,2},{2,1},{3,0},{4,7},{5,6},{6,5},{7,4},{8,11},{9,10},{10,... | collective-permute-start | bytes 98312 | tf_op jit(solution)/shard_map/ppermute | solution.py:97
  18.7 4.3 %collective-permute-start.11 = (f32[2,32,128]{2,1,0:T(8,128)S(1)}, f32[2,32,128]{2,1,0:T(8,128)S(1)}, u32[]{:S(2)}, u32[]{:S(2)}) collective-permute-start(f32[2,32,128]{2,1,0:T(8,128)S(1)} %get-tuple-element.50.refs_2_), channel_id=1, source_target_pairs={{0,5},{1,4},{2,7},{3,6},{4,1},{5,0},{6,3},{7,2},{8,13},{9,12},{10,... | collective-permute-start | bytes 98312 | tf_op jit(solution)/shard_map/ppermute | solution.py:97
  21.5 3.2 %collective-permute-start.10 = (f32[1,32,128]{2,1,0:T(8,128)S(1)}, f32[1,32,128]{2,1,0:T(8,128)S(1)}, u32[]{:S(2)}, u32[]{:S(2)}) collective-permute-start(f32[1,32,128]{2,1,0:T(8,128)S(1)} %get-tuple-element.49.refs_0_), channel_id=1, source_target_pairs={{0,5},{1,4},{2,7},{3,6},{4,1},{5,0},{6,3},{7,2},{8,13},{9,12},{10,... | collective-permute-start | bytes 49160 | tf_op jit(solution)/shard_map/ppermute | solution.py:97
  25.3 4.0 %collective-permute-start.13 = (f32[2,32,128]{2,1,0:T(8,128)S(1)}, f32[2,32,128]{2,1,0:T(8,128)S(1)}, u32[]{:S(2)}, u32[]{:S(2)}) collective-permute-start(f32[2,32,128]{2,1,0:T(8,128)S(1)} %get-tuple-element.58.refs_0_), channel_id=1, source_target_pairs={{0,8},{8,0},{16,24},{24,16},{1,9},{9,1},{17,25},{25,17},{2,10},{10... | collective-permute-start | bytes 98312 | tf_op jit(solution)/shard_map/ppermute | solution.py:97
  26.2 5.3 %collective-permute-start.15 = (f32[2,32,128]{2,1,0:T(8,128)S(1)}, f32[2,32,128]{2,1,0:T(8,128)S(1)}, u32[]{:S(2)}, u32[]{:S(2)}) collective-permute-start(f32[2,32,128]{2,1,0:T(8,128)S(1)} %get-tuple-element.60.refs_2_), channel_id=1, source_target_pairs={{0,16},{8,24},{16,0},{24,8},{1,17},{9,25},{17,1},{25,9},{2,18},{10... | collective-permute-start | bytes 98312 | tf_op jit(solution)/shard_map/ppermute | solution.py:97
  29.3 4.7 %collective-permute-start.14 = (f32[1,32,128]{2,1,0:T(8,128)S(1)}, f32[1,32,128]{2,1,0:T(8,128)S(1)}, u32[]{:S(2)}, u32[]{:S(2)}) collective-permute-start(f32[1,32,128]{2,1,0:T(8,128)S(1)} %get-tuple-element.59.refs_0_), channel_id=1, source_target_pairs={{0,16},{8,24},{16,0},{24,8},{1,17},{9,25},{17,1},{25,9},{2,18},{10... | collective-permute-start | bytes 49160 | tf_op jit(solution)/shard_map/ppermute | solution.py:97
